TPU v7x, 32 devices: a whole 2x2x4 slice. The times are simulated.
32 devices in a mesh: groups: 2 (over y), dp: 16 (over z, x, core).
Axes of the slice: x: 2, y: 2, z: 4, core: 2. Of those that a mesh axis runs over, the one named last changes fastest.
Arguments:
- activations: bfloat16 [128, 64, 8192], P(('groups', 'dp')), parts along dimension 0, may hold values from -6 to 6
- out_grads: bfloat16 [128, 64, 8192], P(('groups', 'dp')), parts along dimension 0, may hold values from -6 to 6
- project_in: bfloat16 [8192, 32], replicated, may hold values from -0.0625 to 0.0625
- project_out: bfloat16 [8192, 32], replicated, may hold values from -0.0625 to 0.0625
- lengths: int32 [128], P(('groups', 'dp')), parts along dimension 0, may hold values from 16 to 64, as said below
- query_index: int32 [32], P('groups'), parts along dimension 0, may hold values from 0 to 63, as said below
Outputs:
- scores: float32 [128, 16], P(('groups', 'dp')), parts along dimension 0
There are 2 independent parts, one for each index of `groups`. A program takes and returns all parts, laid end to end along the dimension named above; an argument that names none is the same for every part. Nothing has to cross between parts.
Inputs may be any that keep to these rules, and one draw needn't show every extreme that they name: `lengths`: some examples have exactly 64 live positions and some exactly 16. `query_index`: distinct example numbers; 0 and 63 are always among them.
All inputs are finite; a program needn't handle non-finite values.
Results may differ from a plain program's by a relative error of at most 0.0003.
Values sent between devices are 32-bit elements; how exact they have to be, the bound alone decides.
No kernel may reach another device: no remote copies, remote signals or barrier semaphores. Data moves between devices by JAX's collectives and lax.ppermute only.
A program may use at most 128 MiB of HBM per device.

v0:
```python
import jax
import jax.numpy as jnp
from jax import lax
from jax.sharding import PartitionSpec as P

damp_ratio = 0.5


def sketch_rows(activations, out_grads, project_in, project_out, lengths):
    count, seq_len, width = activations.shape
    rank_dim = project_in.shape[1]
    feat = jnp.dot(
        activations.reshape(count * seq_len, width), project_in, preferred_element_type=jnp.float32
    ).reshape(count, seq_len, rank_dim)
    grad = jnp.dot(
        out_grads.reshape(count * seq_len, width), project_out, preferred_element_type=jnp.float32
    ).reshape(count, seq_len, rank_dim)
    padding = (jnp.arange(seq_len, dtype=jnp.int32)[None, :] < lengths[:, None]).astype(jnp.float32)
    grad = grad * padding[:, :, None]
    outer = jnp.einsum("esi,esj->eij", grad, feat, precision=lax.Precision.HIGHEST)
    return outer.reshape(count, rank_dim * rank_dim)


def dense_solve(system, right_hand):
    lower_factor = jnp.linalg.cholesky(system)
    middle = lax.linalg.triangular_solve(lower_factor, right_hand, left_side=True, lower=True)
    return lax.linalg.triangular_solve(
        lower_factor, middle, left_side=True, lower=True, transpose_a=True
    )


def selector_for(query_index, first_row, row_count):
    numbers = first_row + jnp.arange(row_count, dtype=jnp.int32)
    return (query_index[:, None] == numbers[None, :]).astype(jnp.float32)


def local(activations, out_grads, project_in, project_out, lengths, query_index):
    sketches = sketch_rows(activations, out_grads, project_in, project_out, lengths)
    ex_dev, fisher_dim = sketches.shape
    identity = jnp.eye(fisher_dim, dtype=jnp.float32)
    row_shares = lax.psum_scatter(
        jnp.dot(sketches.T, sketches, precision=lax.Precision.HIGHEST),
        "dp",
        scatter_dimension=0,
        tiled=True,
    )
    fisher = lax.all_gather(row_shares, "dp", axis=0, tiled=True)
    first_row = lax.axis_index("dp") * ex_dev
    selector = selector_for(query_index, first_row, ex_dev)
    chosen = jnp.dot(selector, sketches, precision=lax.Precision.HIGHEST)
    queries, sum_squares = lax.psum((chosen, jnp.sum(sketches * sketches)), "dp")
    damping = damp_ratio * sum_squares / fisher_dim
    solved = dense_solve(fisher + damping * identity, queries.T)
    return jnp.dot(sketches, solved, precision=lax.Precision.HIGHEST)


def solution(mesh):
    return jax.shard_map(
        local,
        mesh=mesh,
        in_specs=(
            P(("groups", "dp"), None, None),
            P(("groups", "dp"), None, None),
            P(),
            P(),
            P(("groups", "dp")),
            P("groups"),
        ),
        out_specs=P(("groups", "dp"), None),
        check_vma=False,
    )
```

profile of v0, /device:TPU:0, one launch (start us, length us, event | category | flops | bytes accessed | tf_op | source)
XLA Modules:
  0.0 514.0 jit_solution(9964654597216682301)
XLA Ops:
  7.6 4.7 fusion.6
  12.3 2.0 convolution_multiply_fusion
  15.3 5.1 fusion.103
  20.5 75.5 %reduce-scatter.4.cloned.1.call-done = f32[64,1024]{1,0:T(8,128)} async-done(((f32[1024,1024]{1,0:T(8,128)}), f32[64,1024]{1,0:T(8,128)}) %reduce-scatter.4.cloned.1.call-update) | async-done | bytes 262160 | tf_op jit(solution)/shard_map/reduce_scatter | solution.py:41
  96.9 31.0 %psum.14 = f32[]{:T(128)} all-reduce(f32[]{:T(128)} %get-tuple-element.62), channel_id=1, replica_groups=mesh['groups'=2,'dp'=16] {'dp'}, use_global_device_ids=true, to_apply=%region_2.0 | all-reduce | flops 1 | bytes 8 | tf_op jit(solution)/shard_map/psum | solution.py:51
  128.6 19.7 %all-gather.2.cloned.1.call-done = f32[1024,1024]{1,0:T(8,128)} async-done(((f32[64,1024]{1,0:T(8,128)}), f32[1024,1024]{1,0:T(8,128)}) %all-gather.2.cloned.1.call-update) | async-done | bytes 4194320 | tf_op jit(solution)/shard_map/all_gather | solution.py:47
  148.3 5.3 %copy.27 = f32[1024,1024]{0,1:T(8,128)} copy(f32[1024,1024]{1,0:T(8,128)} %all-gather.2.cloned.1.call-done) | data formatting | bytes 8388608 | tf_op jit(solution)/shard_map/all_gather | solution.py:47
  153.7 4.8 select_add_fusion
  158.5 5.5 %copy.28 = f32[1024,1024]{1,0:T(8,128)} copy(f32[1024,1024]{0,1:T(8,128)} %select_add_fusion) | data formatting | bytes 8388608 | tf_op jit(solution)/shard_map/add | solution.py:53
  164.0 4.5 fusion
  168.5 1.9 copy-done.2
  170.5 11.7 %cholesky.222 = f32[128,128]{1,0:T(8,128)S(1)} custom-call(f32[128,128]{1,0:T(8,128)S(1)} %cholesky.577), custom_call_target="Cholesky" | custom-call | tf_op jit(solution)/shard_map/jit(cholesky)/cholesky | solution.py:25
  182.3 9.8 %custom-call.64 = f32[1,128,128]{1,2,0:T(8,128)S(1)} custom-call(f32[1,128,128]{2,1,0:T(8,128)S(1)} %get-tuple-element.44), custom_call_target="InvertDiagBlocksLowerTriangular" | custom-call | tf_op jit(solution)/shard_map/jit(cholesky)/cholesky | solution.py:25
  192.1 1.5 fusion.12
  193.9 1.6 convolution_subtract_fusion
  195.4 11.7 %cholesky.243 = f32[128,128]{1,0:T(8,128)S(1)} custom-call(f32[128,128]{1,0:T(8,128)S(1)} %cholesky.581), custom_call_target="Cholesky" | custom-call | tf_op jit(solution)/shard_map/jit(cholesky)/cholesky | solution.py:25
  207.5 9.8 %custom-call.65 = f32[1,128,128]{1,2,0:T(8,128)S(1)} custom-call(f32[1,128,128]{2,1,0:T(8,128)S(1)} %get-tuple-element.42), custom_call_target="InvertDiagBlocksLowerTriangular" | custom-call | tf_op jit(solution)/shard_map/jit(cholesky)/cholesky | solution.py:25
  218.4 2.0 copy-done.1
  220.4 2.4 convolution_subtract_fusion.1
  222.8 11.7 %cholesky.466 = f32[128,128]{1,0:T(8,128)S(1)} custom-call(f32[128,128]{1,0:T(8,128)S(1)} %cholesky.586), custom_call_target="Cholesky" | custom-call | tf_op jit(solution)/shard_map/jit(cholesky)/cholesky | solution.py:25
  235.3 9.8 %custom-call.66 = f32[1,128,128]{1,2,0:T(8,128)S(1)} custom-call(f32[1,128,128]{2,1,0:T(8,128)S(1)} %get-tuple-element.40), custom_call_target="InvertDiagBlocksLowerTriangular" | custom-call | tf_op jit(solution)/shard_map/jit(cholesky)/cholesky | solution.py:25
  245.1 1.3 convolution_dynamic-update-slice_fusion.1
  246.4 3.5 convolution_subtract_fusion.2
  249.9 11.7 %cholesky.485 = f32[128,128]{1,0:T(8,128)S(1)} custom-call(f32[128,128]{1,0:T(8,128)S(1)} %cholesky.591), custom_call_target="Cholesky" | custom-call | tf_op jit(solution)/shard_map/jit(cholesky)/cholesky | solution.py:25
  262.4 9.8 %custom-call.67 = f32[1,128,128]{1,2,0:T(8,128)S(1)} custom-call(f32[1,128,128]{2,1,0:T(8,128)S(1)} %get-tuple-element.38), custom_call_target="InvertDiagBlocksLowerTriangular" | custom-call | tf_op jit(solution)/shard_map/jit(cholesky)/cholesky | solution.py:25
  272.2 1.1 convolution_dynamic-update-slice_fusion.2
  273.3 3.2 convolution_subtract_fusion.3
  276.5 11.9 %cholesky.504 = f32[128,128]{1,0:T(8,128)S(1)} custom-call(f32[128,128]{1,0:T(8,128)S(1)} %cholesky.596), custom_call_target="Cholesky" | custom-call | tf_op jit(solution)/shard_map/jit(cholesky)/cholesky | solution.py:25
  289.2 9.8 %custom-call.68 = f32[1,128,128]{1,2,0:T(8,128)S(1)} custom-call(f32[1,128,128]{2,1,0:T(8,128)S(1)} %get-tuple-element.36), custom_call_target="InvertDiagBlocksLowerTriangular" | custom-call | tf_op jit(solution)/shard_map/jit(cholesky)/cholesky | solution.py:25
  299.0 1.1 convolution_dynamic-update-slice_fusion.3
  300.1 3.1 convolution_subtract_fusion.4
  303.2 11.7 %cholesky.524 = f32[128,128]{1,0:T(8,128)S(1)} custom-call(f32[128,128]{1,0:T(8,128)S(1)} %cholesky.601), custom_call_target="Cholesky" | custom-call | tf_op jit(solution)/shard_map/jit(cholesky)/cholesky | solution.py:25
  315.7 9.8 %custom-call.69 = f32[1,128,128]{1,2,0:T(8,128)S(1)} custom-call(f32[1,128,128]{2,1,0:T(8,128)S(1)} %get-tuple-element.34), custom_call_target="InvertDiagBlocksLowerTriangular" | custom-call | tf_op jit(solution)/shard_map/jit(cholesky)/cholesky | solution.py:25
  325.5 1.0 convolution_dynamic-update-slice_fusion.4
  326.5 2.9 convolution_subtract_fusion.5
  329.4 11.7 %cholesky.544 = f32[128,128]{1,0:T(8,128)S(1)} custom-call(f32[128,128]{1,0:T(8,128)S(1)} %cholesky.606), custom_call_target="Cholesky" | custom-call | tf_op jit(solution)/shard_map/jit(cholesky)/cholesky | solution.py:25
  341.9 9.8 %custom-call.70 = f32[1,128,128]{1,2,0:T(8,128)S(1)} custom-call(f32[1,128,128]{2,1,0:T(8,128)S(1)} %get-tuple-element.32), custom_call_target="InvertDiagBlocksLowerTriangular" | custom-call | tf_op jit(solution)/shard_map/jit(cholesky)/cholesky | solution.py:25
  352.6 2.1 convolution_subtract_fusion.6
  354.7 11.7 %cholesky.562 = f32[128,128]{1,0:T(8,128)S(1)} custom-call(f32[128,128]{1,0:T(8,128)S(1)} %convolution_subtract_fusion.6), custom_call_target="Cholesky" | custom-call | tf_op jit(solution)/shard_map/jit(cholesky)/cholesky | solution.py:25
  376.8 4.8 select_select_fusion
  381.6 23.9 %while.1 = (s32[]{:T(128)}, f32[1024,1024]{0,1:T(8,128)}, s32[8,2]{0,1:T(2,128)S(1)}, f32[8,128,128]{2,1,0:T(8,128)S(1)}, s32[]{:T(128)}) while((s32[]{:T(128)}, f32[1024,1024]{0,1:T(8,128)}, s32[8,2]{0,1:T(2,128)S(1)}, f32[8,128,128]{2,1,0:T(8,128)S(1)}, s32[]{:T(128)}) %tuple.51), condition=%wide.while_cond, body=%wide.while_body.sunk | while | flops 2 | bytes 393329 | solution.py:27
  382.2 2.3 dynamic-slice.7
  385.2 2.3 dynamic-slice.7
  388.2 2.3 dynamic-slice.7
  391.2 2.3 dynamic-slice.7
  394.2 2.3 dynamic-slice.7
  397.2 2.3 dynamic-slice.7
  400.2 2.3 dynamic-slice.7
  403.2 2.2 dynamic-slice.7
  405.5 78.8 %custom-call.71 = f32[8,128,128]{1,2,0:T(8,128)S(1)} custom-call(f32[8,128,128]{2,1,0:T(8,128)S(1)} %get-tuple-element.12), custom_call_target="InvertDiagBlocksLowerTriangular" | custom-call | tf_op jit(solution)/shard_map/triangular_solve | solution.py:27
  485.2 1.0 convolution_subtract_fusion.14
  486.4 1.1 convolution_subtract_fusion.13
  487.7 1.2 convolution_subtract_fusion.12
  489.0 1.2 convolution_subtract_fusion.11
  490.4 1.3 convolution_subtract_fusion.20
  491.9 1.3 convolution_subtract_fusion.19
  493.4 1.4 convolution_subtract_fusion.18
  495.3 1.1 convolution_subtract_fusion.10
  496.6 1.1 convolution_subtract_fusion.9
  498.0 1.3 convolution_subtract_fusion.8
  499.4 1.3 convolution_subtract_fusion.7
  501.0 1.4 convolution_subtract_fusion.17
  502.7 1.4 convolution_subtract_fusion.16
  504.4 1.5 convolution_subtract_fusion.15
  (138 shorter events, 25.4 us)
Async XLA Ops:
  6.5 1.0 copy-start
  6.5 5.8 %copy-start.4 = (bf16[8192,32]{0,1:T(8,128)(2,1)S(1)}, bf16[8192,32]{0,1:T(8,128)(2,1)}, u32[]{:S(2)}) copy-start(bf16[8192,32]{0,1:T(8,128)(2,1)} %param.9) | copy-start | bytes 1572868
  6.5 89.4 %reduce-scatter.4.cloned.1.call-start = ((), (), s32[]{:S(2)}) async-start(), calls=%async_computation.3 | async-start | bytes 4456448 | tf_op jit(solution)/shard_map/reduce_scatter | solution.py:41
  6.5 5.8 %copy-start.3 = (bf16[4,64,8192]{2,1,0:T(8,128)(2,1)S(1)}, bf16[4,64,8192]{2,1,0:T(8,128)(2,1)}, u32[]{:S(2)}) copy-start(bf16[4,64,8192]{2,1,0:T(8,128)(2,1)} %param.7) | copy-start | bytes 12582916
  15.3 80.7 %copy-start.5 = (s32[16]{0:T(128)S(1)}, s32[16]{0:T(128)}, u32[]{:S(2)}) copy-start(s32[16]{0:T(128)} %param.11) | copy-start | bytes 196
  20.4 127.9 %all-gather.2.cloned.1.call-start = ((), (), s32[]{:S(2)}) async-start(), calls=%async_computation.1 | async-start | bytes 4456448 | tf_op jit(solution)/shard_map/all_gather | solution.py:47
  96.0 388.4 %all-reduce.3.cloned.1.call-start = ((), (), s32[]{:S(2)}) async-start(), calls=%async_computation.2 | async-start | bytes 131072 | tf_op jit(solution)/shard_map/psum | solution.py:51
  168.5 1.9 copy-start.2
  218.4 2.0 copy-start.1
Sparse Core Ops, SparseCore 0:
  20.5 75.3 reduce-scatter.3
  98.3 49.9 all-gather.1
  152.2 83.8 all-reduce.2
where the time goes:
time: 519 us; the launch traced here: 514 us
  other arithmetic  261 us (50%)
  waiting for transfers between devices  95.2 us (18%)
  matrix products  61.8 us (12%)
  local copies, waits for them, and re-layouts  44.5 us (9%)
  blocking collectives  31 us (6%)
  between operations  19.7 us (4%)
    another operation x30, other arithmetic, dense_solve(): lower_factor = jnp.linalg.cholesky(system)  167 us
    another operation x3, other arithmetic, dense_solve(): lax.linalg.triangular_solve(lower_factor, middle, left_side=True, lower=T...  83.7 us
    reduce_scatter x1, waiting for transfers between devices, local(): lax.psum_scatter(jnp.dot(sketches.T, sketches, precision=lax.Precision.HI...  75.5 us
    psum x1, blocking collectives, local(): lax.psum((chosen, jnp.sum(sketches * sketches)), 'dp')  31 us
    another operation x14, matrix products, dense_solve(): lower_factor = jnp.linalg.cholesky(system)  26.2 us
    another operation x40, local copies, waits for them, and re-layouts  23.6 us
    all_gather x1, waiting for transfers between devices, local(): fisher = lax.all_gather(row_shares, 'dp', axis=0, tiled=True)  19.7 us
    another operation x15, matrix products, dense_solve(): lax.linalg.triangular_solve(lower_factor, middle, left_side=True, lower=T...  10.7 us
  transfers between devices with their start and end apart: 3, of which 2 were waited for; matrix products, arithmetic and copies ran while one was open for 64% of the time, Pallas kernels for 0%

commit v1 on v0

v1 whole, which is shorter than its diff:
```python
import functools

import jax
import jax.numpy as jnp
from jax import lax
from jax.experimental import pallas as pl
from jax.experimental.pallas import tpu as pltpu
from jax.sharding import PartitionSpec as P

damp_ratio = 0.5
LANES = 128
SUBLANES = 8
NT = (((1,), (1,)), ((), ()))


def sketch_kernel(chunks, seq_len, act_hbm, out_hbm, pin_hbm, pout_hbm, lengths_ref, sketch_ref, act, out, pin, pout, sems):
    rows, width = act.shape
    rank_dim = pin.shape[0]
    step = width // chunks
    copies = []
    for c in range(chunks):
        cols = pl.ds(c * step, step)
        copies.append(
            [
                pltpu.make_async_copy(src.at[:, cols], dst.at[:, cols], sems.at[n, c])
                for n, (src, dst) in enumerate(
                    ((pin_hbm, pin), (act_hbm, act), (pout_hbm, pout), (out_hbm, out))
                )
            ]
        )
        for copy in copies[-1]:
            copy.start()
    feat = jnp.zeros((rank_dim, rows), jnp.float32)
    grad = jnp.zeros((rank_dim, rows), jnp.float32)
    for c in range(chunks):
        cols = slice(c * step, (c + 1) * step)
        for copy in copies[c]:
            copy.wait()
        feat = feat + lax.dot_general(pin[:, cols], act[:, cols], NT, preferred_element_type=jnp.float32)
        grad = grad + lax.dot_general(pout[:, cols], out[:, cols], NT, preferred_element_type=jnp.float32)
    count = rows // seq_len
    reps = LANES // rank_dim
    position = lax.broadcasted_iota(jnp.int32, (rank_dim, rows), 1)
    masked = []
    for e in range(count):
        first = e * seq_len
        live = (position >= first) & (position < first + lengths_ref[e])
        masked.append(jnp.where(live, grad, 0.0))
    outer = lax.dot_general(
        jnp.concatenate(masked, axis=0),
        jnp.concatenate([feat] * reps, axis=0),
        NT,
        precision=lax.Precision.HIGHEST,
        preferred_element_type=jnp.float32,
    )
    band = lax.broadcasted_iota(jnp.int32, (SUBLANES, LANES), 1) // rank_dim
    for e in range(count):
        entry = outer[e * rank_dim : e * rank_dim + SUBLANES]
        for b in range(1, reps):
            first = e * rank_dim + b * SUBLANES
            entry = jnp.where(band == b, outer[first : first + SUBLANES], entry)
        sketch_ref[e * SUBLANES : (e + 1) * SUBLANES] = entry


def sketch_rows(activations, out_grads, project_in, project_out, lengths):
    count, seq_len, width = activations.shape
    rank_dim = project_in.shape[1]
    rows = count * seq_len
    chunks = 8
    return pl.pallas_call(
        functools.partial(sketch_kernel, chunks, seq_len),
        out_shape=jax.ShapeDtypeStruct((count * SUBLANES, LANES), jnp.float32),
        in_specs=[pl.BlockSpec(memory_space=pl.ANY)] * 4 + [pl.BlockSpec(memory_space=pltpu.SMEM)],
        out_specs=pl.BlockSpec(memory_space=pltpu.VMEM),
        scratch_shapes=[
            pltpu.VMEM((rows, width), jnp.bfloat16),
            pltpu.VMEM((rows, width), jnp.bfloat16),
            pltpu.VMEM((rank_dim, width), jnp.bfloat16),
            pltpu.VMEM((rank_dim, width), jnp.bfloat16),
            pltpu.SemaphoreType.DMA((4, chunks)),
        ],
        compiler_params=pltpu.CompilerParams(vmem_limit_bytes=24 * 2**20),
    )(
        activations.reshape(rows, width),
        out_grads.reshape(rows, width),
        project_in.T,
        project_out.T,
        lengths,
    )


def solve_kernel(nq, per_dev, axis, tiles_ref, query_ref, scores_ref, extended, solved):
    examples = tiles_ref.shape[0] // SUBLANES
    wide = examples + nq
    fisher_dim = SUBLANES * LANES
    extended[: examples * SUBLANES] = tiles_ref[...]
    for q in range(nq):
        first = pl.multiple_of(query_ref[q] * SUBLANES, SUBLANES)
        extended[(examples + q) * SUBLANES : (examples + q + 1) * SUBLANES] = tiles_ref[pl.ds(first, SUBLANES)]
    extended[wide * SUBLANES :] = jnp.zeros((LANES * SUBLANES - wide * SUBLANES, LANES), jnp.float32)
    right = jnp.concatenate([extended[pl.ds(s, LANES, stride=SUBLANES)] for s in range(SUBLANES)], axis=1)
    system = lax.dot_general(
        right[:examples], right, NT, precision=lax.Precision.HIGHEST, preferred_element_type=jnp.float32
    )
    row = lax.broadcasted_iota(jnp.int32, system.shape, 0)
    col = lax.broadcasted_iota(jnp.int32, system.shape, 1)
    diagonal = row == col
    trace = jnp.sum(jnp.where(diagonal, system, 0.0))
    damping = damp_ratio * trace / fisher_dim
    system = jnp.where(diagonal, system + damping, system)
    for k in range(examples):
        pivot_row = system[k : k + 1]
        scaled = pivot_row / system[k : k + 1, k : k + 1]
        system = jnp.where(row == k, scaled, system - system[:, k : k + 1] * scaled)
    solved[...] = system
    first = lax.axis_index(axis) * per_dev
    mine = solved[pl.ds(first, per_dev)]
    scores_ref[...] = mine[:, examples : examples + nq]


def gram_scores(tiles, query_index, per_dev, axis):
    examples = tiles.shape[0] // SUBLANES
    nq = query_index.shape[0]
    return pl.pallas_call(
        functools.partial(solve_kernel, nq, per_dev, axis),
        out_shape=jax.ShapeDtypeStruct((per_dev, nq), jnp.float32),
        in_specs=[pl.BlockSpec(memory_space=pltpu.VMEM), pl.BlockSpec(memory_space=pltpu.SMEM)],
        out_specs=pl.BlockSpec(memory_space=pltpu.VMEM),
        scratch_shapes=[
            pltpu.VMEM((LANES * SUBLANES, LANES), jnp.float32),
            pltpu.VMEM((examples, LANES), jnp.float32),
        ],
    )(tiles, query_index)


def large_scores(tiles, query_index, per_dev, axis):
    sketches = tiles.reshape(-1, SUBLANES * LANES)
    gram = jnp.dot(sketches, sketches.T, precision=lax.Precision.HIGHEST)
    examples, fisher_dim = sketches.shape
    damping = damp_ratio * jnp.trace(gram) / fisher_dim
    factor = jnp.linalg.cholesky(gram + damping * jnp.eye(examples, dtype=jnp.float32))
    mine = lax.dynamic_slice_in_dim(gram, lax.axis_index(axis) * per_dev, per_dev, 0)
    half = lax.linalg.triangular_solve(factor, mine.T, left_side=True, lower=True)
    solved = lax.linalg.triangular_solve(factor, half, left_side=True, lower=True, transpose_a=True)
    selector = (query_index[:, None] == jnp.arange(examples, dtype=jnp.int32)[None, :]).astype(jnp.float32)
    return jnp.dot(selector, solved, precision=lax.Precision.HIGHEST).T


def local(activations, out_grads, project_in, project_out, lengths, query_index):
    per_dev = activations.shape[0]
    tiles = sketch_rows(activations, out_grads, project_in, project_out, lengths)
    every = lax.all_gather(tiles, "dp", axis=0, tiled=True)
    examples = every.shape[0] // SUBLANES
    if examples + query_index.shape[0] <= LANES:
        return gram_scores(every, query_index, per_dev, "dp")
    return large_scores(every, query_index, per_dev, "dp")


def solution(mesh):
    return jax.shard_map(
        local,
        mesh=mesh,
        in_specs=(
            P(("groups", "dp"), None, None),
            P(("groups", "dp"), None, None),
            P(),
            P(),
            P(("groups", "dp")),
            P("groups"),
        ),
        out_specs=P(("groups", "dp"), None),
        check_vma=False,
    )
```

time: 519 us -> 45.5 us (0.09)
  other arithmetic: 261 us -> 0 us
  waiting for transfers between devices: 95.2 us -> 0 us
  matrix products: 61.8 us -> 0 us
  local copies, waits for them, and re-layouts: 44.5 us -> 7.11 us
  between operations: 19.7 us -> 0.01 us
  Pallas kernels: 0 us -> 12.9 us
  blocking collectives: 31 us -> 25.2 us
    another operation x33 -> x0, other arithmetic: 251 us -> none  [the longest x30 167 us: dense_solve(): lower_factor = jnp.linalg.cholesky(system)]
    reduce_scatter x1 -> x0, waiting for transfers between devices: 75.5 us -> none  [local(): lax.psum_scatter(jnp.dot(sketches.T, sketches, precision=lax.Precision.HI...]
    another operation x44 -> x0, matrix products: 47.6 us -> none  [the longest x14 26.2 us: dense_solve(): lower_factor = jnp.linalg.cholesky(system)]
    psum x1 -> x0, blocking collectives: 31 us -> none  [local(): lax.psum((chosen, jnp.sum(sketches * sketches)), 'dp')]
    another operation x70 -> x0, local copies, waits for them, and re-layouts: 29.2 us -> none
    all_gather x0 -> x1, blocking collectives: none -> 25.2 us  [local(): every = lax.all_gather(tiles, 'dp', axis=0, tiled=True)]
    all_gather x1 -> x0, waiting for transfers between devices: 19.7 us -> none  [local(): fisher = lax.all_gather(row_shares, 'dp', axis=0, tiled=True)]
    pallas_call x0 -> x2, Pallas kernels: none -> 12.9 us  [the longest x1 7.87 us: gram_scores(): pl.pallas_call(functools.partial(solve_kernel, nq, per_dev, axis), out_sh...]
  transfers between devices with their start and end apart: 3 -> 0, of which waited for: 2 -> 0; matrix products, arithmetic and copies ran while one was open for 64% -> 0% of each run, Pallas kernels for 0% -> 0%
where the time goes in v1:
time: 45.5 us; the launch traced here: 45.2 us
  blocking collectives  25.2 us (55%)
  Pallas kernels  12.9 us (28%)
  local copies, waits for them, and re-layouts  7.11 us (16%)
    all_gather x1, blocking collectives, local(): every = lax.all_gather(tiles, 'dp', axis=0, tiled=True)  25.2 us
    pallas_call x1, Pallas kernels, gram_scores(): pl.pallas_call(functools.partial(solve_kernel, nq, per_dev, axis), out_sh...  7.87 us
    unnamed x10, local copies, waits for them, and re-layouts  7.11 us
    pallas_call x1, Pallas kernels, sketch_rows(): pl.pallas_call(functools.partial(sketch_kernel, chunks, seq_len), out_sha...  5.02 us

profile of v1, /device:TPU:0, one launch (start us, length us, event | category | flops | bytes accessed | tf_op | source)
XLA Modules:
  0.0 45.2 jit_solution(12894256373560527180)
XLA Ops:
  0.0 0.0 copy-start
  0.0 2.2 %copy-done = bf16[4,64,8192]{2,1,0:T(8,128)(2,1)S(1)} copy-done((bf16[4,64,8192]{2,1,0:T(8,128)(2,1)S(1)}, bf16[4,64,8192]{2,1,0:T(8,128)(2,1)}, u32[]{:S(2)}) %copy-start) | copy-done | bytes 4194328
  2.2 0.0 copy-start.1
  2.2 2.2 %copy-done.1 = bf16[4,64,8192]{2,1,0:T(8,128)(2,1)S(1)} copy-done((bf16[4,64,8192]{2,1,0:T(8,128)(2,1)S(1)}, bf16[4,64,8192]{2,1,0:T(8,128)(2,1)}, u32[]{:S(2)}) %copy-start.1) | copy-done | bytes 4194328
  4.4 0.0 copy-start.2
  4.4 1.0 %copy-done.2 = bf16[8192,32]{0,1:T(8,128)(2,1)S(1)} copy-done((bf16[8192,32]{0,1:T(8,128)(2,1)S(1)}, bf16[8192,32]{0,1:T(8,128)(2,1)}, u32[]{:S(2)}) %copy-start.2) | copy-done | bytes 524312
  5.4 0.0 copy-start.3
  5.4 1.0 %copy-done.3 = bf16[8192,32]{0,1:T(8,128)(2,1)S(1)} copy-done((bf16[8192,32]{0,1:T(8,128)(2,1)S(1)}, bf16[8192,32]{0,1:T(8,128)(2,1)}, u32[]{:S(2)}) %copy-start.3) | copy-done | bytes 524312
  6.5 0.0 copy-start.4
  6.5 0.7 %copy-done.4 = s32[4]{0:T(128)S(1)} copy-done((s32[4]{0:T(128)S(1)}, s32[4]{0:T(128)}, u32[]{:S(2)}) %copy-start.4) | copy-done | bytes 40
  7.1 5.0 %shard_map.64 = f32[32,128]{1,0:T(8,128)S(1)} custom-call(bf16[256,8192]{1,0:T(8,128)(2,1)S(1)} %bitcast.4, bf16[256,8192]{1,0:T(8,128)(2,1)S(1)} %bitcast.5, bf16[32,8192]{1,0:T(8,128)(2,1)S(1)} %bitcast.6, bf16[32,8192]{1,0:T(8,128)(2,1)S(1)} %bitcast.7, s32[4]{0:T(128)S(1)} %copy-done.4), custom_call_target="tpu_custom_call" | custom-call | tf_op jit(solution)/shard_map/pallas_call | solution.py:70
  12.1 25.2 %all_gather.3.tiles_ref = f32[512,128]{1,0:T(8,128)} all-gather(f32[32,128]{1,0:T(8,128)S(1)} %shard_map.64), channel_id=1, replica_groups=mesh['groups'=2,'dp'=16] {'dp'}, dimensions={0}, use_global_device_ids=true | all-gather | bytes 278528 | tf_op jit(solution)/shard_map/all_gather | solution.py:152
  37.4 7.9 %shard_map.65 = f32[4,16]{1,0:T(4,128)} custom-call(f32[512,128]{1,0:T(8,128)} %all_gather.3.tiles_ref, s32[16]{0:T(128)} %query_ref.1), custom_call_target="tpu_custom_call" | custom-call | tf_op jit(solution)/shard_map/pallas_call | solution.py:124
Async XLA Ops:
  0.0 2.2 %copy-start = (bf16[4,64,8192]{2,1,0:T(8,128)(2,1)S(1)}, bf16[4,64,8192]{2,1,0:T(8,128)(2,1)}, u32[]{:S(2)}) copy-start(bf16[4,64,8192]{2,1,0:T(8,128)(2,1)} %param.6) | copy-start | bytes 12582916
  2.2 2.2 %copy-start.1 = (bf16[4,64,8192]{2,1,0:T(8,128)(2,1)S(1)}, bf16[4,64,8192]{2,1,0:T(8,128)(2,1)}, u32[]{:S(2)}) copy-start(bf16[4,64,8192]{2,1,0:T(8,128)(2,1)} %param.7) | copy-start | bytes 12582916
  4.4 1.0 %copy-start.2 = (bf16[8192,32]{0,1:T(8,128)(2,1)S(1)}, bf16[8192,32]{0,1:T(8,128)(2,1)}, u32[]{:S(2)}) copy-start(bf16[8192,32]{0,1:T(8,128)(2,1)} %param.8) | copy-start | bytes 1572868
  5.4 1.0 %copy-start.3 = (bf16[8192,32]{0,1:T(8,128)(2,1)S(1)}, bf16[8192,32]{0,1:T(8,128)(2,1)}, u32[]{:S(2)}) copy-start(bf16[8192,32]{0,1:T(8,128)(2,1)} %param.9) | copy-start | bytes 1572868
  6.5 0.7 %copy-start.4 = (s32[4]{0:T(128)S(1)}, s32[4]{0:T(128)}, u32[]{:S(2)}) copy-start(s32[4]{0:T(128)} %lengths_ref.1) | copy-start | bytes 52

commit v2 on v1

--- a/solution.py
+++ b/solution.py
@@ -70,7 +70,7 @@
     return pl.pallas_call(
         functools.partial(sketch_kernel, chunks, seq_len),
         out_shape=jax.ShapeDtypeStruct((count * SUBLANES, LANES), jnp.float32),
-        in_specs=[pl.BlockSpec(memory_space=pl.ANY)] * 4 + [pl.BlockSpec(memory_space=pltpu.SMEM)],
+        in_specs=[pl.BlockSpec(memory_space=pltpu.HBM)] * 4 + [pl.BlockSpec(memory_space=pltpu.SMEM)],
         out_specs=pl.BlockSpec(memory_space=pltpu.VMEM),
         scratch_shapes=[
             pltpu.VMEM((rows, width), jnp.bfloat16),
@@ -79,7 +79,6 @@
             pltpu.VMEM((rank_dim, width), jnp.bfloat16),
             pltpu.SemaphoreType.DMA((4, chunks)),
         ],
-        compiler_params=pltpu.CompilerParams(vmem_limit_bytes=24 * 2**20),
     )(
         activations.reshape(rows, width),
         out_grads.reshape(rows, width),
@@ -89,14 +88,20 @@
     )
 
 
-def solve_kernel(nq, per_dev, axis, tiles_ref, query_ref, scores_ref, extended, solved):
-    examples = tiles_ref.shape[0] // SUBLANES
+def solve_kernel(nq, per_dev, axis, *refs):
+    tiles, (query_ref, scores_ref, extended) = refs[:-3], refs[-3:]
+    block = per_dev * SUBLANES
+    examples = len(tiles) * per_dev
     wide = examples + nq
     fisher_dim = SUBLANES * LANES
-    extended[: examples * SUBLANES] = tiles_ref[...]
+    me = lax.axis_index(axis)
+    for slot, tile in enumerate(tiles):
+        extended[slot * block : (slot + 1) * block] = tile[...]
     for q in range(nq):
-        first = pl.multiple_of(query_ref[q] * SUBLANES, SUBLANES)
-        extended[(examples + q) * SUBLANES : (examples + q + 1) * SUBLANES] = tiles_ref[pl.ds(first, SUBLANES)]
+        number = query_ref[q]
+        place = (number // per_dev ^ me) * per_dev + number % per_dev
+        first = pl.multiple_of(place * SUBLANES, SUBLANES)
+        extended[(examples + q) * SUBLANES : (examples + q + 1) * SUBLANES] = extended[pl.ds(first, SUBLANES)]
     extended[wide * SUBLANES :] = jnp.zeros((LANES * SUBLANES - wide * SUBLANES, LANES), jnp.float32)
     right = jnp.concatenate([extended[pl.ds(s, LANES, stride=SUBLANES)] for s in range(SUBLANES)], axis=1)
     system = lax.dot_general(
@@ -112,25 +117,24 @@
         pivot_row = system[k : k + 1]
         scaled = pivot_row / system[k : k + 1, k : k + 1]
         system = jnp.where(row == k, scaled, system - system[:, k : k + 1] * scaled)
-    solved[...] = system
-    first = lax.axis_index(axis) * per_dev
-    mine = solved[pl.ds(first, per_dev)]
-    scores_ref[...] = mine[:, examples : examples + nq]
+    scores_ref[...] = system[:per_dev, examples : examples + nq]
 
 
-def gram_scores(tiles, query_index, per_dev, axis):
-    examples = tiles.shape[0] // SUBLANES
+def gram_scores(tiles, query_index, axis):
+    block = tiles[0].shape[0]
+    per_dev = block // SUBLANES
     nq = query_index.shape[0]
     return pl.pallas_call(
         functools.partial(solve_kernel, nq, per_dev, axis),
         out_shape=jax.ShapeDtypeStruct((per_dev, nq), jnp.float32),
-        in_specs=[pl.BlockSpec(memory_space=pltpu.VMEM), pl.BlockSpec(memory_space=pltpu.SMEM)],
+        in_specs=[pl.BlockSpec(memory_space=pltpu.VMEM)] * len(tiles) + [pl.BlockSpec(memory_space=pltpu.SMEM)],
         out_specs=pl.BlockSpec(memory_space=pltpu.VMEM),
-        scratch_shapes=[
-            pltpu.VMEM((LANES * SUBLANES, LANES), jnp.float32),
-            pltpu.VMEM((examples, LANES), jnp.float32),
-        ],
-    )(tiles, query_index)
+        scratch_shapes=[pltpu.VMEM((LANES * SUBLANES, LANES), jnp.float32)],
+    )(*tiles, query_index)
+
+
+def gather_xor(tiles, axis, size):
+    return [tiles] + [lax.ppermute(tiles, axis, [(i, i ^ s) for i in range(size)]) for s in range(1, size)]
 
 
 def large_scores(tiles, query_index, per_dev, axis):
@@ -149,11 +153,10 @@
 def local(activations, out_grads, project_in, project_out, lengths, query_index):
     per_dev = activations.shape[0]
     tiles = sketch_rows(activations, out_grads, project_in, project_out, lengths)
-    every = lax.all_gather(tiles, "dp", axis=0, tiled=True)
-    examples = every.shape[0] // SUBLANES
-    if examples + query_index.shape[0] <= LANES:
-        return gram_scores(every, query_index, per_dev, "dp")
-    return large_scores(every, query_index, per_dev, "dp")
+    size = lax.axis_size("dp")
+    if size * per_dev + query_index.shape[0] <= LANES:
+        return gram_scores(gather_xor(tiles, "dp", size), query_index, "dp")
+    return large_scores(lax.all_gather(tiles, "dp", axis=0, tiled=True), query_index, per_dev, "dp")
 
 
 def solution(mesh):

time: 45.5 us -> 40.6 us (0.89)
  blocking collectives: 25.2 us -> 0 us
  starting transfers between devices: 0 us -> 22 us
  local copies, waits for them, and re-layouts: 7.11 us -> 1.11 us
  waiting for transfers between devices: 0 us -> 3.1 us
  Pallas kernels: 12.9 us -> 14 us
    all_gather x1 -> x0, blocking collectives: 25.2 us -> none  [local(): every = lax.all_gather(tiles, 'dp', axis=0, tiled=True)]
    ppermute x0 -> x15, starting transfers between devices: none -> 22 us  [gather_xor(): lax.ppermute(tiles, axis, [(i, i ^ s) for i in range(size)])]
    unnamed x10 -> x30, local copies, waits for them, and re-layouts: 7.11 us -> 1.11 us
    ppermute x0 -> x15, waiting for transfers between devices: none -> 3.1 us  [gather_xor(): lax.ppermute(tiles, axis, [(i, i ^ s) for i in range(size)])]
    pallas_call x1, Pallas kernels: 5.02 us -> 6.15 us  [sketch_rows(): pl.pallas_call(functools.partial(sketch_kernel, chunks, seq_len), out_sha...]
  transfers between devices with their start and end apart: 0 -> 15, of which waited for: 0 -> 3; matrix products, arithmetic and copies ran while one was open for 0% -> 0% of each run, Pallas kernels for 0% -> 0%
where the time goes in v2:
time: 40.6 us; the launch traced here: 40.4 us
  starting transfers between devices  22 us (54%)
  Pallas kernels  14 us (34%)
  waiting for transfers between devices  3.1 us (8%)
  local copies, waits for them, and re-layouts  1.11 us (3%)
    ppermute x15, starting transfers between devices, gather_xor(): lax.ppermute(tiles, axis, [(i, i ^ s) for i in range(size)])  22 us
    pallas_call x1, Pallas kernels, gram_scores(): pl.pallas_call(functools.partial(solve_kernel, nq, per_dev, axis), out_sh...  7.87 us
    pallas_call x1, Pallas kernels, sketch_rows(): pl.pallas_call(functools.partial(sketch_kernel, chunks, seq_len), out_sha...  6.15 us
    ppermute x15, waiting for transfers between devices, gather_xor(): lax.ppermute(tiles, axis, [(i, i ^ s) for i in range(size)])  3.1 us
    unnamed x30, local copies, waits for them, and re-layouts  1.11 us
  transfers between devices with their start and end apart: 15, of which 3 were waited for; matrix products, arithmetic and copies ran while one was open for 0% of the time, Pallas kernels for 0%

profile of v2, /device:TPU:0, one launch (start us, length us, event | category | flops | bytes accessed | tf_op | source)
XLA Modules:
  0.0 40.4 jit_solution(15675174281893657393)
XLA Ops:
  0.0 6.1 %shard_map.64.refs_0_ = f32[32,128]{1,0:T(8,128)} custom-call(bf16[256,8192]{1,0:T(8,128)(2,1)} %bitcast.4, bf16[256,8192]{1,0:T(8,128)(2,1)} %bitcast.5, bf16[32,8192]{1,0:T(8,128)(2,1)} %bitcast.6, bf16[32,8192]{1,0:T(8,128)(2,1)} %bitcast.7, s32[4]{0:T(128)} %lengths_ref.1), custom_call_target="tpu_custom_call" | custom-call | tf_op jit(solution)/shard_map/pallas_call | solution.py:70
  6.2 5.5 %collective-permute-start.14 = (f32[32,128]{1,0:T(8,128)}, f32[32,128]{1,0:T(8,128)S(1)}, u32[]{:S(2)}, u32[]{:S(2)}) collective-permute-start(f32[32,128]{1,0:T(8,128)} %shard_map.64.refs_0_), channel_id=1, source_target_pairs={{0,15},{1,14},{2,13},{3,12},{4,11},{5,10},{6,9},{7,8},{8,7},{9,6},... | collective-permute-start | bytes 49160 | tf_op jit(solution)/shard_map/ppermute | solution.py:137
  11.6 0.6 %collective-permute-start.13 = (f32[32,128]{1,0:T(8,128)}, f32[32,128]{1,0:T(8,128)S(1)}, u32[]{:S(2)}, u32[]{:S(2)}) collective-permute-start(f32[32,128]{1,0:T(8,128)} %shard_map.64.refs_0_), channel_id=1, source_target_pairs={{0,14},{1,15},{2,12},{3,13},{4,10},{5,11},{6,8},{7,9},{8,6},{9,7},... | collective-permute-start | bytes 49160 | tf_op jit(solution)/shard_map/ppermute | solution.py:137
  12.3 3.2 %collective-permute-start.12 = (f32[32,128]{1,0:T(8,128)}, f32[32,128]{1,0:T(8,128)S(1)}, u32[]{:S(2)}, u32[]{:S(2)}) collective-permute-start(f32[32,128]{1,0:T(8,128)} %shard_map.64.refs_0_), channel_id=1, source_target_pairs={{0,13},{1,12},{2,15},{3,14},{4,9},{5,8},{6,11},{7,10},{8,5},{9,4},... | collective-permute-start | bytes 49160 | tf_op jit(solution)/shard_map/ppermute | solution.py:137
  15.4 0.3 collective-permute-start.11
  15.7 0.0 collective-permute-start.10
  15.8 0.0 collective-permute-done.14.refs_15_
  15.8 0.0 copy-start
  15.8 3.6 %collective-permute-start.9 = (f32[32,128]{1,0:T(8,128)}, f32[32,128]{1,0:T(8,128)S(1)}, u32[]{:S(2)}, u32[]{:S(2)}) collective-permute-start(f32[32,128]{1,0:T(8,128)} %shard_map.64.refs_0_), channel_id=1, source_target_pairs={{0,10},{1,11},{2,8},{3,9},{4,14},{5,15},{6,12},{7,13},{8,2},{9,3},... | collective-permute-start | bytes 49160 | tf_op jit(solution)/shard_map/ppermute | solution.py:137
  19.4 0.0 collective-permute-done.13.refs_14_
  19.4 0.0 copy-start.1
  19.4 0.0 collective-permute-start.8
  19.4 0.0 collective-permute-done.12.refs_13_
  19.4 0.0 copy-start.2
  19.4 2.5 %collective-permute-start.7 = (f32[32,128]{1,0:T(8,128)}, f32[32,128]{1,0:T(8,128)S(1)}, u32[]{:S(2)}, u32[]{:S(2)}) collective-permute-start(f32[32,128]{1,0:T(8,128)} %shard_map.64.refs_0_), channel_id=1, source_target_pairs={{0,8},{1,9},{2,10},{3,11},{4,12},{5,13},{6,14},{7,15},{8,0},{9,1},... | collective-permute-start | bytes 49160 | tf_op jit(solution)/shard_map/ppermute | solution.py:137
  22.0 0.0 collective-permute-done.11.refs_12_
  22.0 0.0 copy-start.3
  22.0 1.9 %collective-permute-start.6 = (f32[32,128]{1,0:T(8,128)}, f32[32,128]{1,0:T(8,128)S(1)}, u32[]{:S(2)}, u32[]{:S(2)}) collective-permute-start(f32[32,128]{1,0:T(8,128)} %shard_map.64.refs_0_), channel_id=1, source_target_pairs={{0,7},{1,6},{2,5},{3,4},{4,3},{5,2},{6,1},{7,0},{8,15},{9,14},{10,... | collective-permute-start | bytes 49160 | tf_op jit(solution)/shard_map/ppermute | solution.py:137
  23.9 0.0 collective-permute-done.10.refs_11_
  23.9 0.0 copy-start.4
  23.9 0.8 %collective-permute-start.5 = (f32[32,128]{1,0:T(8,128)}, f32[32,128]{1,0:T(8,128)S(1)}, u32[]{:S(2)}, u32[]{:S(2)}) collective-permute-start(f32[32,128]{1,0:T(8,128)} %shard_map.64.refs_0_), channel_id=1, source_target_pairs={{0,6},{1,7},{2,4},{3,5},{4,2},{5,3},{6,0},{7,1},{8,14},{9,15},{10,... | collective-permute-start | bytes 49160 | tf_op jit(solution)/shard_map/ppermute | solution.py:137
  24.7 0.0 collective-permute-done.9.refs_10_
  24.7 0.0 copy-start.5
  24.7 1.2 %collective-permute-start.4 = (f32[32,128]{1,0:T(8,128)}, f32[32,128]{1,0:T(8,128)S(1)}, u32[]{:S(2)}, u32[]{:S(2)}) collective-permute-start(f32[32,128]{1,0:T(8,128)} %shard_map.64.refs_0_), channel_id=1, source_target_pairs={{0,5},{1,4},{2,7},{3,6},{4,1},{5,0},{6,3},{7,2},{8,13},{9,12},{10,... | collective-permute-start | bytes 49160 | tf_op jit(solution)/shard_map/ppermute | solution.py:137
  25.9 0.0 collective-permute-done.8.refs_9_
  25.9 0.0 copy-start.6
  25.9 0.4 %collective-permute-start.3 = (f32[32,128]{1,0:T(8,128)}, f32[32,128]{1,0:T(8,128)S(1)}, u32[]{:S(2)}, u32[]{:S(2)}) collective-permute-start(f32[32,128]{1,0:T(8,128)} %shard_map.64.refs_0_), channel_id=1, source_target_pairs={{0,4},{1,5},{2,6},{3,7},{4,0},{5,1},{6,2},{7,3},{8,12},{9,13},{10,... | collective-permute-start | bytes 49160 | tf_op jit(solution)/shard_map/ppermute | solution.py:137
  26.4 0.0 collective-permute-done.7.refs_8_
  26.4 0.0 copy-start.7
  26.4 1.0 %collective-permute-start.2 = (f32[32,128]{1,0:T(8,128)}, f32[32,128]{1,0:T(8,128)S(1)}, u32[]{:S(2)}, u32[]{:S(2)}) collective-permute-start(f32[32,128]{1,0:T(8,128)} %shard_map.64.refs_0_), channel_id=1, source_target_pairs={{0,3},{1,2},{2,1},{3,0},{4,7},{5,6},{6,5},{7,4},{8,11},{9,10},{10,... | collective-permute-start | bytes 49160 | tf_op jit(solution)/shard_map/ppermute | solution.py:137
  27.3 0.0 collective-permute-done.6.refs_7_
  27.3 0.0 copy-start.8
  27.3 0.9 %collective-permute-start.1 = (f32[32,128]{1,0:T(8,128)}, f32[32,128]{1,0:T(8,128)S(1)}, u32[]{:S(2)}, u32[]{:S(2)}) collective-permute-start(f32[32,128]{1,0:T(8,128)} %shard_map.64.refs_0_), channel_id=1, source_target_pairs={{0,2},{1,3},{2,0},{3,1},{4,6},{5,7},{6,4},{7,5},{8,10},{9,11},{10,... | collective-permute-start | bytes 49160 | tf_op jit(solution)/shard_map/ppermute | solution.py:137
  28.2 0.6 %collective-permute-done.5.refs_6_ = f32[32,128]{1,0:T(8,128)S(1)} collective-permute-done((f32[32,128]{1,0:T(8,128)}, f32[32,128]{1,0:T(8,128)S(1)}, u32[]{:S(2)}, u32[]{:S(2)}) %collective-permute-start.5) | collective-permute-done | bytes 16416 | tf_op jit(solution)/shard_map/ppermute | solution.py:137
  28.9 0.0 copy-start.9
  28.9 0.0 collective-permute-start
  28.9 0.0 collective-permute-done.4.refs_5_
  28.9 0.0 copy-start.10
  28.9 1.0 %collective-permute-done.3.refs_4_ = f32[32,128]{1,0:T(8,128)S(1)} collective-permute-done((f32[32,128]{1,0:T(8,128)}, f32[32,128]{1,0:T(8,128)S(1)}, u32[]{:S(2)}, u32[]{:S(2)}) %collective-permute-start.3) | collective-permute-done | bytes 16416 | tf_op jit(solution)/shard_map/ppermute | solution.py:137
  29.9 0.0 copy-start.11
  29.9 0.0 collective-permute-done.2.refs_3_
  29.9 0.0 copy-start.12
  29.9 1.4 %collective-permute-done.1.refs_2_ = f32[32,128]{1,0:T(8,128)S(1)} collective-permute-done((f32[32,128]{1,0:T(8,128)}, f32[32,128]{1,0:T(8,128)S(1)}, u32[]{:S(2)}, u32[]{:S(2)}) %collective-permute-start.1) | collective-permute-done | bytes 16416 | tf_op jit(solution)/shard_map/ppermute | solution.py:137
  31.3 0.0 copy-start.13
  31.3 0.0 collective-permute-done.refs_1_
  31.3 0.0 copy-done
  31.3 0.0 copy-done.1
  31.3 0.0 copy-done.2
  31.3 0.0 copy-done.3
  31.3 0.0 copy-done.4
  31.4 0.0 copy-done.5
  31.4 0.0 copy-done.6
  31.4 0.0 copy-done.7
  31.4 0.0 copy-done.8
  31.4 0.0 copy-done.9
  31.4 0.0 copy-done.10
  31.4 0.0 copy-done.11
  31.4 0.0 copy-done.12
  31.4 0.5 %copy-done.13 = f32[32,128]{1,0:T(8,128)} copy-done((f32[32,128]{1,0:T(8,128)}, f32[32,128]{1,0:T(8,128)S(1)}, u32[]{:S(2)}) %copy-start.13) | copy-done | bytes 16408
  31.9 0.0 copy-start.14
  31.9 0.6 %copy-done.14 = f32[32,128]{1,0:T(8,128)} copy-done((f32[32,128]{1,0:T(8,128)}, f32[32,128]{1,0:T(8,128)S(1)}, u32[]{:S(2)}) %copy-start.14) | copy-done | bytes 16408
  32.5 7.9 %shard_map.65 = f32[4,16]{1,0:T(4,128)} custom-call(f32[32,128]{1,0:T(8,128)} %shard_map.64.refs_0_, f32[32,128]{1,0:T(8,128)} %copy-done.14, f32[32,128]{1,0:T(8,128)} %copy-done.13, f32[32,128]{1,0:T(8,128)} %copy-done.12, f32[32,128]{1,0:T(8,128)} %copy-done.11, f32[32,128]{1,0:T(8,128)} %copy-done.10, f32[32,128]{1,0:T(8,128)} %copy-done.9, ...), custom_call_target="tpu_custom_call" | custom-call | tf_op jit(solution)/shard_map/pallas_call | solution.py:127
Async XLA Ops:
  6.2 9.6 %collective-permute-start.14 = (f32[32,128]{1,0:T(8,128)}, f32[32,128]{1,0:T(8,128)S(1)}, u32[]{:S(2)}, u32[]{:S(2)}) collective-permute-start(f32[32,128]{1,0:T(8,128)} %shard_map.64.refs_0_), channel_id=1, source_target_pairs={{0,15},{1,14},{2,13},{3,12},{4,11},{5,10},{6,9},{7,8},{8,7},{9,6},... | collective-permute-start | bytes 49160 | tf_op jit(solution)/shard_map/ppermute | solution.py:137
  11.6 7.7 %collective-permute-start.13 = (f32[32,128]{1,0:T(8,128)}, f32[32,128]{1,0:T(8,128)S(1)}, u32[]{:S(2)}, u32[]{:S(2)}) collective-permute-start(f32[32,128]{1,0:T(8,128)} %shard_map.64.refs_0_), channel_id=1, source_target_pairs={{0,14},{1,15},{2,12},{3,13},{4,10},{5,11},{6,8},{7,9},{8,6},{9,7},... | collective-permute-start | bytes 49160 | tf_op jit(solution)/shard_map/ppermute | solution.py:137
  12.3 7.1 %collective-permute-start.12 = (f32[32,128]{1,0:T(8,128)}, f32[32,128]{1,0:T(8,128)S(1)}, u32[]{:S(2)}, u32[]{:S(2)}) collective-permute-start(f32[32,128]{1,0:T(8,128)} %shard_map.64.refs_0_), channel_id=1, source_target_pairs={{0,13},{1,12},{2,15},{3,14},{4,9},{5,8},{6,11},{7,10},{8,5},{9,4},... | collective-permute-start | bytes 49160 | tf_op jit(solution)/shard_map/ppermute | solution.py:137
  15.4 6.5 %collective-permute-start.11 = (f32[32,128]{1,0:T(8,128)}, f32[32,128]{1,0:T(8,128)S(1)}, u32[]{:S(2)}, u32[]{:S(2)}) collective-permute-start(f32[32,128]{1,0:T(8,128)} %shard_map.64.refs_0_), channel_id=1, source_target_pairs={{0,12},{1,13},{2,14},{3,15},{4,8},{5,9},{6,10},{7,11},{8,4},{9,5},... | collective-permute-start | bytes 49160 | tf_op jit(solution)/shard_map/ppermute | solution.py:137
  15.7 8.1 %collective-permute-start.10 = (f32[32,128]{1,0:T(8,128)}, f32[32,128]{1,0:T(8,128)S(1)}, u32[]{:S(2)}, u32[]{:S(2)}) collective-permute-start(f32[32,128]{1,0:T(8,128)} %shard_map.64.refs_0_), channel_id=1, source_target_pairs={{0,11},{1,10},{2,9},{3,8},{4,15},{5,14},{6,13},{7,12},{8,3},{9,2},... | collective-permute-start | bytes 49160 | tf_op jit(solution)/shard_map/ppermute | solution.py:137
  15.8 15.6 %copy-start = (f32[32,128]{1,0:T(8,128)}, f32[32,128]{1,0:T(8,128)S(1)}, u32[]{:S(2)}) copy-start(f32[32,128]{1,0:T(8,128)S(1)} %collective-permute-done.14.refs_15_) | copy-start | bytes 49156
  15.8 8.9 %collective-permute-start.9 = (f32[32,128]{1,0:T(8,128)}, f32[32,128]{1,0:T(8,128)S(1)}, u32[]{:S(2)}, u32[]{:S(2)}) collective-permute-start(f32[32,128]{1,0:T(8,128)} %shard_map.64.refs_0_), channel_id=1, source_target_pairs={{0,10},{1,11},{2,8},{3,9},{4,14},{5,15},{6,12},{7,13},{8,2},{9,3},... | collective-permute-start | bytes 49160 | tf_op jit(solution)/shard_map/ppermute | solution.py:137
  19.4 11.9 %copy-start.1 = (f32[32,128]{1,0:T(8,128)}, f32[32,128]{1,0:T(8,128)S(1)}, u32[]{:S(2)}) copy-start(f32[32,128]{1,0:T(8,128)S(1)} %collective-permute-done.13.refs_14_) | copy-start | bytes 49156
  19.4 6.5 %collective-permute-start.8 = (f32[32,128]{1,0:T(8,128)}, f32[32,128]{1,0:T(8,128)S(1)}, u32[]{:S(2)}, u32[]{:S(2)}) collective-permute-start(f32[32,128]{1,0:T(8,128)} %shard_map.64.refs_0_), channel_id=1, source_target_pairs={{0,9},{1,8},{2,11},{3,10},{4,13},{5,12},{6,15},{7,14},{8,1},{9,0},... | collective-permute-start | bytes 49160 | tf_op jit(solution)/shard_map/ppermute | solution.py:137
  19.4 11.9 %copy-start.2 = (f32[32,128]{1,0:T(8,128)}, f32[32,128]{1,0:T(8,128)S(1)}, u32[]{:S(2)}) copy-start(f32[32,128]{1,0:T(8,128)S(1)} %collective-permute-done.12.refs_13_) | copy-start | bytes 49156
  19.4 7.0 %collective-permute-start.7 = (f32[32,128]{1,0:T(8,128)}, f32[32,128]{1,0:T(8,128)S(1)}, u32[]{:S(2)}, u32[]{:S(2)}) collective-permute-start(f32[32,128]{1,0:T(8,128)} %shard_map.64.refs_0_), channel_id=1, source_target_pairs={{0,8},{1,9},{2,10},{3,11},{4,12},{5,13},{6,14},{7,15},{8,0},{9,1},... | collective-permute-start | bytes 49160 | tf_op jit(solution)/shard_map/ppermute | solution.py:137
  22.0 9.4 %copy-start.3 = (f32[32,128]{1,0:T(8,128)}, f32[32,128]{1,0:T(8,128)S(1)}, u32[]{:S(2)}) copy-start(f32[32,128]{1,0:T(8,128)S(1)} %collective-permute-done.11.refs_12_) | copy-start | bytes 49156
  22.0 5.4 %collective-permute-start.6 = (f32[32,128]{1,0:T(8,128)}, f32[32,128]{1,0:T(8,128)S(1)}, u32[]{:S(2)}, u32[]{:S(2)}) collective-permute-start(f32[32,128]{1,0:T(8,128)} %shard_map.64.refs_0_), channel_id=1, source_target_pairs={{0,7},{1,6},{2,5},{3,4},{4,3},{5,2},{6,1},{7,0},{8,15},{9,14},{10,... | collective-permute-start | bytes 49160 | tf_op jit(solution)/shard_map/ppermute | solution.py:137
  23.9 7.4 %copy-start.4 = (f32[32,128]{1,0:T(8,128)}, f32[32,128]{1,0:T(8,128)S(1)}, u32[]{:S(2)}) copy-start(f32[32,128]{1,0:T(8,128)S(1)} %collective-permute-done.10.refs_11_) | copy-start | bytes 49156
  23.9 5.0 %collective-permute-start.5 = (f32[32,128]{1,0:T(8,128)}, f32[32,128]{1,0:T(8,128)S(1)}, u32[]{:S(2)}, u32[]{:S(2)}) collective-permute-start(f32[32,128]{1,0:T(8,128)} %shard_map.64.refs_0_), channel_id=1, source_target_pairs={{0,6},{1,7},{2,4},{3,5},{4,2},{5,3},{6,0},{7,1},{8,14},{9,15},{10,... | collective-permute-start | bytes 49160 | tf_op jit(solution)/shard_map/ppermute | solution.py:137
  24.7 6.7 %copy-start.5 = (f32[32,128]{1,0:T(8,128)}, f32[32,128]{1,0:T(8,128)S(1)}, u32[]{:S(2)}) copy-start(f32[32,128]{1,0:T(8,128)S(1)} %collective-permute-done.9.refs_10_) | copy-start | bytes 49156
  24.7 4.2 %collective-permute-start.4 = (f32[32,128]{1,0:T(8,128)}, f32[32,128]{1,0:T(8,128)S(1)}, u32[]{:S(2)}, u32[]{:S(2)}) collective-permute-start(f32[32,128]{1,0:T(8,128)} %shard_map.64.refs_0_), channel_id=1, source_target_pairs={{0,5},{1,4},{2,7},{3,6},{4,1},{5,0},{6,3},{7,2},{8,13},{9,12},{10,... | collective-permute-start | bytes 49160 | tf_op jit(solution)/shard_map/ppermute | solution.py:137
  25.9 5.4 %copy-start.6 = (f32[32,128]{1,0:T(8,128)}, f32[32,128]{1,0:T(8,128)S(1)}, u32[]{:S(2)}) copy-start(f32[32,128]{1,0:T(8,128)S(1)} %collective-permute-done.8.refs_9_) | copy-start | bytes 49156
  25.9 4.0 %collective-permute-start.3 = (f32[32,128]{1,0:T(8,128)}, f32[32,128]{1,0:T(8,128)S(1)}, u32[]{:S(2)}, u32[]{:S(2)}) collective-permute-start(f32[32,128]{1,0:T(8,128)} %shard_map.64.refs_0_), channel_id=1, source_target_pairs={{0,4},{1,5},{2,6},{3,7},{4,0},{5,1},{6,2},{7,3},{8,12},{9,13},{10,... | collective-permute-start | bytes 49160 | tf_op jit(solution)/shard_map/ppermute | solution.py:137
  26.4 5.0 %copy-start.7 = (f32[32,128]{1,0:T(8,128)}, f32[32,128]{1,0:T(8,128)S(1)}, u32[]{:S(2)}) copy-start(f32[32,128]{1,0:T(8,128)S(1)} %collective-permute-done.7.refs_8_) | copy-start | bytes 49156
  26.4 3.5 %collective-permute-start.2 = (f32[32,128]{1,0:T(8,128)}, f32[32,128]{1,0:T(8,128)S(1)}, u32[]{:S(2)}, u32[]{:S(2)}) collective-permute-start(f32[32,128]{1,0:T(8,128)} %shard_map.64.refs_0_), channel_id=1, source_target_pairs={{0,3},{1,2},{2,1},{3,0},{4,7},{5,6},{6,5},{7,4},{8,11},{9,10},{10,... | collective-permute-start | bytes 49160 | tf_op jit(solution)/shard_map/ppermute | solution.py:137
  27.3 4.0 %copy-start.8 = (f32[32,128]{1,0:T(8,128)}, f32[32,128]{1,0:T(8,128)S(1)}, u32[]{:S(2)}) copy-start(f32[32,128]{1,0:T(8,128)S(1)} %collective-permute-done.6.refs_7_) | copy-start | bytes 49156
  27.3 4.0 %collective-permute-start.1 = (f32[32,128]{1,0:T(8,128)}, f32[32,128]{1,0:T(8,128)S(1)}, u32[]{:S(2)}, u32[]{:S(2)}) collective-permute-start(f32[32,128]{1,0:T(8,128)} %shard_map.64.refs_0_), channel_id=1, source_target_pairs={{0,2},{1,3},{2,0},{3,1},{4,6},{5,7},{6,4},{7,5},{8,10},{9,11},{10,... | collective-permute-start | bytes 49160 | tf_op jit(solution)/shard_map/ppermute | solution.py:137
  28.9 2.5 %copy-start.9 = (f32[32,128]{1,0:T(8,128)}, f32[32,128]{1,0:T(8,128)S(1)}, u32[]{:S(2)}) copy-start(f32[32,128]{1,0:T(8,128)S(1)} %collective-permute-done.5.refs_6_) | copy-start | bytes 49156
  28.9 2.5 %collective-permute-start = (f32[32,128]{1,0:T(8,128)}, f32[32,128]{1,0:T(8,128)S(1)}, u32[]{:S(2)}, u32[]{:S(2)}) collective-permute-start(f32[32,128]{1,0:T(8,128)} %shard_map.64.refs_0_), channel_id=1, source_target_pairs={{0,1},{1,0},{2,3},{3,2},{4,5},{5,4},{6,7},{7,6},{8,9},{9,8},{10,11... | collective-permute-start | bytes 49160 | tf_op jit(solution)/shard_map/ppermute | solution.py:137
  28.9 2.5 %copy-start.10 = (f32[32,128]{1,0:T(8,128)}, f32[32,128]{1,0:T(8,128)S(1)}, u32[]{:S(2)}) copy-start(f32[32,128]{1,0:T(8,128)S(1)} %collective-permute-done.4.refs_5_) | copy-start | bytes 49156
  29.9 1.5 %copy-start.11 = (f32[32,128]{1,0:T(8,128)}, f32[32,128]{1,0:T(8,128)S(1)}, u32[]{:S(2)}) copy-start(f32[32,128]{1,0:T(8,128)S(1)} %collective-permute-done.3.refs_4_) | copy-start | bytes 49156
  29.9 1.5 %copy-start.12 = (f32[32,128]{1,0:T(8,128)}, f32[32,128]{1,0:T(8,128)S(1)}, u32[]{:S(2)}) copy-start(f32[32,128]{1,0:T(8,128)S(1)} %collective-permute-done.2.refs_3_) | copy-start | bytes 49156
  31.3 0.6 %copy-start.13 = (f32[32,128]{1,0:T(8,128)}, f32[32,128]{1,0:T(8,128)S(1)}, u32[]{:S(2)}) copy-start(f32[32,128]{1,0:T(8,128)S(1)} %collective-permute-done.1.refs_2_) | copy-start | bytes 49156
  31.9 0.6 %copy-start.14 = (f32[32,128]{1,0:T(8,128)}, f32[32,128]{1,0:T(8,128)S(1)}, u32[]{:S(2)}) copy-start(f32[32,128]{1,0:T(8,128)S(1)} %collective-permute-done.refs_1_) | copy-start | bytes 49156

commit v3 on v2

--- a/solution.py
+++ b/solution.py
@@ -13,7 +13,7 @@
 NT = (((1,), (1,)), ((), ()))
 
 
-def sketch_kernel(chunks, seq_len, act_hbm, out_hbm, pin_hbm, pout_hbm, lengths_ref, sketch_ref, act, out, pin, pout, sems):
+def sketch_kernel(chunks, seq_len, copies_out, act_hbm, out_hbm, pin_hbm, pout_hbm, lengths_ref, sketch_ref, act, out, pin, pout, sems):
     rows, width = act.shape
     rank_dim = pin.shape[0]
     step = width // chunks
@@ -59,17 +59,19 @@
         for b in range(1, reps):
             first = e * rank_dim + b * SUBLANES
             entry = jnp.where(band == b, outer[first : first + SUBLANES], entry)
-        sketch_ref[e * SUBLANES : (e + 1) * SUBLANES] = entry
+        for n in range(copies_out):
+            first = (n * count + e) * SUBLANES
+            sketch_ref[first : first + SUBLANES] = entry
 
 
-def sketch_rows(activations, out_grads, project_in, project_out, lengths):
+def sketch_rows(activations, out_grads, project_in, project_out, lengths, copies_out):
     count, seq_len, width = activations.shape
     rank_dim = project_in.shape[1]
     rows = count * seq_len
     chunks = 8
     return pl.pallas_call(
-        functools.partial(sketch_kernel, chunks, seq_len),
-        out_shape=jax.ShapeDtypeStruct((count * SUBLANES, LANES), jnp.float32),
+        functools.partial(sketch_kernel, chunks, seq_len, copies_out),
+        out_shape=jax.ShapeDtypeStruct((copies_out * count * SUBLANES, LANES), jnp.float32),
         in_specs=[pl.BlockSpec(memory_space=pltpu.HBM)] * 4 + [pl.BlockSpec(memory_space=pltpu.SMEM)],
         out_specs=pl.BlockSpec(memory_space=pltpu.VMEM),
         scratch_shapes=[
@@ -88,20 +90,20 @@
     )
 
 
-def solve_kernel(nq, per_dev, axis, *refs):
-    tiles, (query_ref, scores_ref, extended) = refs[:-3], refs[-3:]
+def solve_kernel(nq, per_dev, axis, tiles_ref, query_ref, scores_ref, extended):
     block = per_dev * SUBLANES
-    examples = len(tiles) * per_dev
+    size = tiles_ref.shape[0] // block
+    examples = size * per_dev
     wide = examples + nq
     fisher_dim = SUBLANES * LANES
     me = lax.axis_index(axis)
-    for slot, tile in enumerate(tiles):
-        extended[slot * block : (slot + 1) * block] = tile[...]
+    for slot in range(size):
+        first = pl.multiple_of((me ^ slot) * block, block)
+        extended[slot * block : (slot + 1) * block] = tiles_ref[pl.ds(first, block)]
     for q in range(nq):
         number = query_ref[q]
-        place = (number // per_dev ^ me) * per_dev + number % per_dev
-        first = pl.multiple_of(place * SUBLANES, SUBLANES)
-        extended[(examples + q) * SUBLANES : (examples + q + 1) * SUBLANES] = extended[pl.ds(first, SUBLANES)]
+        first = pl.multiple_of(number * SUBLANES, SUBLANES)
+        extended[(examples + q) * SUBLANES : (examples + q + 1) * SUBLANES] = tiles_ref[pl.ds(first, SUBLANES)]
     extended[wide * SUBLANES :] = jnp.zeros((LANES * SUBLANES - wide * SUBLANES, LANES), jnp.float32)
     right = jnp.concatenate([extended[pl.ds(s, LANES, stride=SUBLANES)] for s in range(SUBLANES)], axis=1)
     system = lax.dot_general(
@@ -120,21 +122,16 @@
     scores_ref[...] = system[:per_dev, examples : examples + nq]
 
 
-def gram_scores(tiles, query_index, axis):
-    block = tiles[0].shape[0]
-    per_dev = block // SUBLANES
+def gram_scores(tiles, query_index, per_dev, axis):
     nq = query_index.shape[0]
     return pl.pallas_call(
         functools.partial(solve_kernel, nq, per_dev, axis),
         out_shape=jax.ShapeDtypeStruct((per_dev, nq), jnp.float32),
-        in_specs=[pl.BlockSpec(memory_space=pltpu.VMEM)] * len(tiles) + [pl.BlockSpec(memory_space=pltpu.SMEM)],
+        in_specs=[pl.BlockSpec(memory_space=pltpu.VMEM), pl.BlockSpec(memory_space=pltpu.SMEM)],
         out_specs=pl.BlockSpec(memory_space=pltpu.VMEM),
         scratch_shapes=[pltpu.VMEM((LANES * SUBLANES, LANES), jnp.float32)],
-    )(*tiles, query_index)
-
-
-def gather_xor(tiles, axis, size):
-    return [tiles] + [lax.ppermute(tiles, axis, [(i, i ^ s) for i in range(size)]) for s in range(1, size)]
+        compiler_params=pltpu.CompilerParams(vmem_limit_bytes=8 * 2**20),
+    )(tiles, query_index)
 
 
 def large_scores(tiles, query_index, per_dev, axis):
@@ -152,10 +149,13 @@
 
 def local(activations, out_grads, project_in, project_out, lengths, query_index):
     per_dev = activations.shape[0]
-    tiles = sketch_rows(activations, out_grads, project_in, project_out, lengths)
     size = lax.axis_size("dp")
-    if size * per_dev + query_index.shape[0] <= LANES:
-        return gram_scores(gather_xor(tiles, "dp", size), query_index, "dp")
+    small = size * per_dev + query_index.shape[0] <= LANES
+    copies_out = size if small else 1
+    tiles = sketch_rows(activations, out_grads, project_in, project_out, lengths, copies_out)
+    if small:
+        every = lax.all_to_all(tiles, "dp", split_axis=0, concat_axis=0, tiled=True)
+        return gram_scores(every, query_index, per_dev, "dp")
     return large_scores(lax.all_gather(tiles, "dp", axis=0, tiled=True), query_index, per_dev, "dp")
 
 

time: 40.6 us -> 31.5 us (0.78)
  starting transfers between devices: 22 us -> 0 us
  blocking collectives: 0 us -> 17.4 us
  waiting for transfers between devices: 3.1 us -> 0 us
  local copies, waits for them, and re-layouts: 1.11 us -> 0.01 us
    ppermute x15 -> x0, starting transfers between devices: 22 us -> none  [gather_xor(): lax.ppermute(tiles, axis, [(i, i ^ s) for i in range(size)])]
    all_to_all x0 -> x1, blocking collectives: none -> 17.4 us  [local(): every = lax.all_to_all(tiles, 'dp', split_axis=0, concat_axis=0, tiled=True)]
    ppermute x15 -> x0, waiting for transfers between devices: 3.1 us -> none  [gather_xor(): lax.ppermute(tiles, axis, [(i, i ^ s) for i in range(size)])]
    unnamed x30 -> x2, local copies, waits for them, and re-layouts: 1.11 us -> 0.01 us
    pallas_call x1, Pallas kernels: 7.87 us -> 7.44 us  [gram_scores(): pl.pallas_call(functools.partial(solve_kernel, nq, per_dev, axis), out_sh...]
  transfers between devices with their start and end apart: 15 -> 0, of which waited for: 3 -> 0; matrix products, arithmetic and copies ran while one was open for 0% -> 0% of each run, Pallas kernels for 0% -> 0%
where the time goes in v3:
time: 31.5 us; the launch traced here: 31.3 us
  blocking collectives  17.4 us (55%)
  Pallas kernels  13.8 us (44%)
    all_to_all x1, blocking collectives, local(): every = lax.all_to_all(tiles, 'dp', split_axis=0, concat_axis=0, tiled=True)  17.4 us
    pallas_call x1, Pallas kernels, gram_scores(): pl.pallas_call(functools.partial(solve_kernel, nq, per_dev, axis), out_sh...  7.44 us
    pallas_call x1, Pallas kernels, sketch_rows(): pl.pallas_call(functools.partial(sketch_kernel, chunks, seq_len, copies_o...  6.39 us

profile of v3, /device:TPU:0, one launch (start us, length us, event | category | flops | bytes accessed | tf_op | source)
XLA Modules:
  0.0 31.3 jit_solution(12256966373413551117)
XLA Ops:
  0.0 0.0 copy-start
  0.0 6.4 %shard_map.64 = f32[512,128]{1,0:T(8,128)} custom-call(bf16[256,8192]{1,0:T(8,128)(2,1)} %bitcast.7, bf16[256,8192]{1,0:T(8,128)(2,1)} %bitcast.8, bf16[32,8192]{1,0:T(8,128)(2,1)} %bitcast.10, bf16[32,8192]{1,0:T(8,128)(2,1)} %bitcast.11, s32[4]{0:T(128)} %lengths_ref.1), custom_call_target="tpu_custom_call" | custom-call | tf_op jit(solution)/shard_map/pallas_call | solution.py:72
  6.4 17.4 %all_to_all.11 = f32[16,32,128]{2,1,0:T(8,128)S(1)} all-to-all(f32[16,32,128]{2,1,0:T(8,128)} %bitcast.9), channel_id=1, replica_groups=mesh['groups'=2,'dp'=16] {'dp'}, dimensions={0} | all-to-all | bytes 524288 | tf_op jit(solution)/shard_map/all_to_all | solution.py:157
  23.8 0.0 copy-done
  23.8 7.4 %shard_map.65 = f32[4,16]{1,0:T(4,128)} custom-call(f32[512,128]{1,0:T(8,128)S(1)} %bitcast.6, s32[16]{0:T(128)S(1)} %copy-done), custom_call_target="tpu_custom_call" | custom-call | tf_op jit(solution)/shard_map/pallas_call | solution.py:127
Async XLA Ops:
  0.0 23.8 %copy-start = (s32[16]{0:T(128)S(1)}, s32[16]{0:T(128)}, u32[]{:S(2)}) copy-start(s32[16]{0:T(128)} %query_ref.1) | copy-start | bytes 196

commit v4 on v2

--- a/solution.py
+++ b/solution.py
@@ -88,10 +88,11 @@
     )
 
 
-def solve_kernel(nq, per_dev, axis, *refs):
+def solve_kernel(nq, per_dev, inner, axis, *refs):
     tiles, (query_ref, scores_ref, extended) = refs[:-3], refs[-3:]
-    block = per_dev * SUBLANES
-    examples = len(tiles) * per_dev
+    block = tiles[0].shape[0]
+    examples = len(tiles) * block // SUBLANES
+    outer = examples // (inner * per_dev)
     wide = examples + nq
     fisher_dim = SUBLANES * LANES
     me = lax.axis_index(axis)
@@ -99,7 +100,8 @@
         extended[slot * block : (slot + 1) * block] = tile[...]
     for q in range(nq):
         number = query_ref[q]
-        place = (number // per_dev ^ me) * per_dev + number % per_dev
+        slot = (number // per_dev) ^ me
+        place = ((slot % inner) * outer + slot // inner) * per_dev + number % per_dev
         first = pl.multiple_of(place * SUBLANES, SUBLANES)
         extended[(examples + q) * SUBLANES : (examples + q + 1) * SUBLANES] = extended[pl.ds(first, SUBLANES)]
     extended[wide * SUBLANES :] = jnp.zeros((LANES * SUBLANES - wide * SUBLANES, LANES), jnp.float32)
@@ -120,21 +122,24 @@
     scores_ref[...] = system[:per_dev, examples : examples + nq]
 
 
-def gram_scores(tiles, query_index, axis):
-    block = tiles[0].shape[0]
-    per_dev = block // SUBLANES
+def gram_scores(tiles, query_index, per_dev, inner, axis):
     nq = query_index.shape[0]
     return pl.pallas_call(
-        functools.partial(solve_kernel, nq, per_dev, axis),
+        functools.partial(solve_kernel, nq, per_dev, inner, axis),
         out_shape=jax.ShapeDtypeStruct((per_dev, nq), jnp.float32),
         in_specs=[pl.BlockSpec(memory_space=pltpu.VMEM)] * len(tiles) + [pl.BlockSpec(memory_space=pltpu.SMEM)],
         out_specs=pl.BlockSpec(memory_space=pltpu.VMEM),
         scratch_shapes=[pltpu.VMEM((LANES * SUBLANES, LANES), jnp.float32)],
+        compiler_params=pltpu.CompilerParams(vmem_limit_bytes=8 * 2**20),
     )(*tiles, query_index)
 
 
-def gather_xor(tiles, axis, size):
-    return [tiles] + [lax.ppermute(tiles, axis, [(i, i ^ s) for i in range(size)]) for s in range(1, size)]
+def gather_xor(tiles, axis, size, inner):
+    def swap(block, slot):
+        return lax.ppermute(block, axis, [(i, i ^ slot) for i in range(size)])
+
+    column = jnp.concatenate([tiles] + [swap(tiles, slot) for slot in range(inner, size, inner)], axis=0)
+    return [column] + [swap(column, slot) for slot in range(1, inner)]
 
 
 def large_scores(tiles, query_index, per_dev, axis):
@@ -152,10 +157,11 @@
 
 def local(activations, out_grads, project_in, project_out, lengths, query_index):
     per_dev = activations.shape[0]
+    size = lax.axis_size("dp")
     tiles = sketch_rows(activations, out_grads, project_in, project_out, lengths)
-    size = lax.axis_size("dp")
     if size * per_dev + query_index.shape[0] <= LANES:
-        return gram_scores(gather_xor(tiles, "dp", size), query_index, "dp")
+        inner = 4
+        return gram_scores(gather_xor(tiles, "dp", size, inner), query_index, per_dev, inner, "dp")
     return large_scores(lax.all_gather(tiles, "dp", axis=0, tiled=True), query_index, per_dev, "dp")
 
 

time: 40.6 us -> 30.6 us (0.75)
  starting transfers between devices: 22 us -> 7.61 us
  waiting for transfers between devices: 3.1 us -> 8.14 us
  local copies, waits for them, and re-layouts: 1.11 us -> 0.01 us
  other arithmetic: 0 us -> 0.72 us
    ppermute x15 -> x6, starting transfers between devices: 22 us -> 7.61 us  [swap(): return lax.ppermute(block, axis, [(i, i ^ slot) for i in range(size)])]
    ppermute x15 -> x6, waiting for transfers between devices: 3.1 us -> 8.14 us  [swap(): return lax.ppermute(block, axis, [(i, i ^ slot) for i in range(size)])]
    unnamed x30 -> x2, local copies, waits for them, and re-layouts: 1.11 us -> 0.01 us
    concatenate x0 -> x1, other arithmetic: none -> 0.72 us  [gather_xor(): jnp.concatenate([tiles] + [swap(tiles, slot) for slot in range(inner, siz...]
  transfers between devices with their start and end apart: 15 -> 6, of which waited for: 3 -> 4; matrix products, arithmetic and copies ran while one was open for 0% -> 0% of each run, Pallas kernels for 0% -> 0%
where the time goes in v4:
time: 30.6 us; the launch traced here: 30.4 us
  Pallas kernels  13.9 us (45%)
  waiting for transfers between devices  8.14 us (27%)
  starting transfers between devices  7.61 us (25%)
  other arithmetic  0.72 us (2%)
    ppermute x6, waiting for transfers between devices, swap(): return lax.ppermute(block, axis, [(i, i ^ slot) for i in range(size)])  8.14 us
    ppermute x6, starting transfers between devices, swap(): return lax.ppermute(block, axis, [(i, i ^ slot) for i in range(size)])  7.61 us
    pallas_call x1, Pallas kernels, gram_scores(): pl.pallas_call(functools.partial(solve_kernel, nq, per_dev, inner, axis),...  7.61 us
    pallas_call x1, Pallas kernels, sketch_rows(): pl.pallas_call(functools.partial(sketch_kernel, chunks, seq_len), out_sha...  6.29 us
    concatenate x1, other arithmetic, gather_xor(): jnp.concatenate([tiles] + [swap(tiles, slot) for slot in range(inner, siz...  0.72 us
  transfers between devices with their start and end apart: 6, of which 4 were waited for; matrix products, arithmetic and copies ran while one was open for 0% of the time, Pallas kernels for 0%

profile of v4, /device:TPU:0, one launch (start us, length us, event | category | flops | bytes accessed | tf_op | source)
XLA Modules:
  0.0 30.4 jit_solution(10615223712117573879)
XLA Ops:
  0.0 0.0 copy-start
  0.0 6.3 %shard_map.64 = f32[32,128]{1,0:T(8,128)} custom-call(bf16[256,8192]{1,0:T(8,128)(2,1)} %bitcast.4, bf16[256,8192]{1,0:T(8,128)(2,1)} %bitcast.5, bf16[32,8192]{1,0:T(8,128)(2,1)} %bitcast.6, bf16[32,8192]{1,0:T(8,128)(2,1)} %bitcast.7, s32[4]{0:T(128)} %lengths_ref.1), custom_call_target="tpu_custom_call" | custom-call | tf_op jit(solution)/shard_map/pallas_call | solution.py:70
  6.3 5.1 %collective-permute-start.2 = (f32[32,128]{1,0:T(8,128)}, f32[32,128]{1,0:T(8,128)S(1)}, u32[]{:S(2)}, u32[]{:S(2)}) collective-permute-start(f32[32,128]{1,0:T(8,128)} %shard_map.64), channel_id=1, source_target_pairs={{0,12},{1,13},{2,14},{3,15},{4,8},{5,9},{6,10},{7,11},{8,4},{9,5},... | collective-permute-start | bytes 49160 | tf_op jit(solution)/shard_map/ppermute | solution.py:139
  11.4 0.0 collective-permute-start.1
  11.4 0.6 %collective-permute-start = (f32[32,128]{1,0:T(8,128)}, f32[32,128]{1,0:T(8,128)S(1)}, u32[]{:S(2)}, u32[]{:S(2)}) collective-permute-start(f32[32,128]{1,0:T(8,128)} %shard_map.64), channel_id=1, source_target_pairs={{0,4},{1,5},{2,6},{3,7},{4,0},{5,1},{6,2},{7,3},{8,12},{9,13},{10,... | collective-permute-start | bytes 49160 | tf_op jit(solution)/shard_map/ppermute | solution.py:139
  12.1 1.3 %collective-permute-done.2 = f32[32,128]{1,0:T(8,128)S(1)} collective-permute-done((f32[32,128]{1,0:T(8,128)}, f32[32,128]{1,0:T(8,128)S(1)}, u32[]{:S(2)}, u32[]{:S(2)}) %collective-permute-start.2) | collective-permute-done | bytes 16416 | tf_op jit(solution)/shard_map/ppermute | solution.py:139
  13.3 2.9 %collective-permute-done.1 = f32[32,128]{1,0:T(8,128)S(1)} collective-permute-done((f32[32,128]{1,0:T(8,128)}, f32[32,128]{1,0:T(8,128)S(1)}, u32[]{:S(2)}, u32[]{:S(2)}) %collective-permute-start.1) | collective-permute-done | bytes 16416 | tf_op jit(solution)/shard_map/ppermute | solution.py:139
  16.3 0.0 collective-permute-done
  16.3 0.7 %pad_maximum_fusion.refs_0_ = f32[128,128]{1,0:T(8,128)S(1)} fusion(f32[32,128]{1,0:T(8,128)S(1)} %collective-permute-done.2, f32[32,128]{1,0:T(8,128)S(1)} %collective-permute-done.1, f32[32,128]{1,0:T(8,128)S(1)} %collective-permute-done, f32[32,128]{1,0:T(8,128)} %shard_map.64), kind=kLoop, calls=%fused_computation | loop fusion | flops 49152 | bytes 131072 | tf_op jit(solution)/shard_map/concatenate | solution.py:141
  17.0 0.0 collective-permute-start.5
  17.0 1.5 %collective-permute-start.4 = (f32[128,128]{1,0:T(8,128)S(1)}, f32[128,128]{1,0:T(8,128)S(1)}, u32[]{:S(2)}, u32[]{:S(2)}) collective-permute-start(f32[128,128]{1,0:T(8,128)S(1)} %pad_maximum_fusion.refs_0_), channel_id=1, source_target_pairs={{0,2},{1,3},{2,0},{3,1},{4,6},{5,7},{6,4},{7,5},{8,10},{9,11},{10,... | collective-permute-start | bytes 196616 | tf_op jit(solution)/shard_map/ppermute | solution.py:139
  18.5 0.3 %collective-permute-start.3 = (f32[128,128]{1,0:T(8,128)S(1)}, f32[128,128]{1,0:T(8,128)S(1)}, u32[]{:S(2)}, u32[]{:S(2)}) collective-permute-start(f32[128,128]{1,0:T(8,128)S(1)} %pad_maximum_fusion.refs_0_), channel_id=1, source_target_pairs={{0,1},{1,0},{2,3},{3,2},{4,5},{5,4},{6,7},{7,6},{8,9},{9,8},{10,11... | collective-permute-start | bytes 196616 | tf_op jit(solution)/shard_map/ppermute | solution.py:139
  18.8 2.5 %collective-permute-done.5.refs_3_ = f32[128,128]{1,0:T(8,128)S(1)} collective-permute-done((f32[128,128]{1,0:T(8,128)S(1)}, f32[128,128]{1,0:T(8,128)S(1)}, u32[]{:S(2)}, u32[]{:S(2)}) %collective-permute-start.5) | collective-permute-done | bytes 65568 | tf_op jit(solution)/shard_map/ppermute | solution.py:139
  21.3 1.5 %collective-permute-done.4.refs_2_ = f32[128,128]{1,0:T(8,128)S(1)} collective-permute-done((f32[128,128]{1,0:T(8,128)S(1)}, f32[128,128]{1,0:T(8,128)S(1)}, u32[]{:S(2)}, u32[]{:S(2)}) %collective-permute-start.4) | collective-permute-done | bytes 65568 | tf_op jit(solution)/shard_map/ppermute | solution.py:139
  22.8 0.0 collective-permute-done.3.refs_1_
  22.8 0.0 copy-done
  22.8 7.6 %shard_map.65 = f32[4,16]{1,0:T(4,128)} custom-call(f32[128,128]{1,0:T(8,128)S(1)} %pad_maximum_fusion.refs_0_, f32[128,128]{1,0:T(8,128)S(1)} %collective-permute-done.3.refs_1_, f32[128,128]{1,0:T(8,128)S(1)} %collective-permute-done.4.refs_2_, f32[128,128]{1,0:T(8,128)S(1)} %collective-permute-done.5.refs_3_, s32[16]{0:T(128)S(1)} %copy-done), custom_call_target="tpu_custom_call" | custom-call | tf_op jit(solution)/shard_map/pallas_call | solution.py:127
Async XLA Ops:
  0.0 22.8 %copy-start = (s32[16]{0:T(128)S(1)}, s32[16]{0:T(128)}, u32[]{:S(2)}) copy-start(s32[16]{0:T(128)} %refs_4_.1) | copy-start | bytes 196
  6.3 7.0 %collective-permute-start.2 = (f32[32,128]{1,0:T(8,128)}, f32[32,128]{1,0:T(8,128)S(1)}, u32[]{:S(2)}, u32[]{:S(2)}) collective-permute-start(f32[32,128]{1,0:T(8,128)} %shard_map.64), channel_id=1, source_target_pairs={{0,12},{1,13},{2,14},{3,15},{4,8},{5,9},{6,10},{7,11},{8,4},{9,5},... | collective-permute-start | bytes 49160 | tf_op jit(solution)/shard_map/ppermute | solution.py:139
  11.4 4.8 %collective-permute-start.1 = (f32[32,128]{1,0:T(8,128)}, f32[32,128]{1,0:T(8,128)S(1)}, u32[]{:S(2)}, u32[]{:S(2)}) collective-permute-start(f32[32,128]{1,0:T(8,128)} %shard_map.64), channel_id=1, source_target_pairs={{0,8},{1,9},{2,10},{3,11},{4,12},{5,13},{6,14},{7,15},{8,0},{9,1},... | collective-permute-start | bytes 49160 | tf_op jit(solution)/shard_map/ppermute | solution.py:139
  11.4 4.8 %collective-permute-start = (f32[32,128]{1,0:T(8,128)}, f32[32,128]{1,0:T(8,128)S(1)}, u32[]{:S(2)}, u32[]{:S(2)}) collective-permute-start(f32[32,128]{1,0:T(8,128)} %shard_map.64), channel_id=1, source_target_pairs={{0,4},{1,5},{2,6},{3,7},{4,0},{5,1},{6,2},{7,3},{8,12},{9,13},{10,... | collective-permute-start | bytes 49160 | tf_op jit(solution)/shard_map/ppermute | solution.py:139
  17.0 4.3 %collective-permute-start.5 = (f32[128,128]{1,0:T(8,128)S(1)}, f32[128,128]{1,0:T(8,128)S(1)}, u32[]{:S(2)}, u32[]{:S(2)}) collective-permute-start(f32[128,128]{1,0:T(8,128)S(1)} %pad_maximum_fusion.refs_0_), channel_id=1, source_target_pairs={{0,3},{1,2},{2,1},{3,0},{4,7},{5,6},{6,5},{7,4},{8,11},{9,10},{10,... | collective-permute-start | bytes 196616 | tf_op jit(solution)/shard_map/ppermute | solution.py:139
  17.0 5.8 %collective-permute-start.4 = (f32[128,128]{1,0:T(8,128)S(1)}, f32[128,128]{1,0:T(8,128)S(1)}, u32[]{:S(2)}, u32[]{:S(2)}) collective-permute-start(f32[128,128]{1,0:T(8,128)S(1)} %pad_maximum_fusion.refs_0_), channel_id=1, source_target_pairs={{0,2},{1,3},{2,0},{3,1},{4,6},{5,7},{6,4},{7,5},{8,10},{9,11},{10,... | collective-permute-start | bytes 196616 | tf_op jit(solution)/shard_map/ppermute | solution.py:139
  18.5 4.3 %collective-permute-start.3 = (f32[128,128]{1,0:T(8,128)S(1)}, f32[128,128]{1,0:T(8,128)S(1)}, u32[]{:S(2)}, u32[]{:S(2)}) collective-permute-start(f32[128,128]{1,0:T(8,128)S(1)} %pad_maximum_fusion.refs_0_), channel_id=1, source_target_pairs={{0,1},{1,0},{2,3},{3,2},{4,5},{5,4},{6,7},{7,6},{8,9},{9,8},{10,11... | collective-permute-start | bytes 196616 | tf_op jit(solution)/shard_map/ppermute | solution.py:139

commit v5 on v1

--- a/solution.py
+++ b/solution.py
@@ -8,6 +8,7 @@
 from jax.sharding import PartitionSpec as P
 
 damp_ratio = 0.5
+AXES = ("outer", "inner")
 LANES = 128
 SUBLANES = 8
 NT = (((1,), (1,)), ((), ()))
@@ -70,7 +71,7 @@
     return pl.pallas_call(
         functools.partial(sketch_kernel, chunks, seq_len),
         out_shape=jax.ShapeDtypeStruct((count * SUBLANES, LANES), jnp.float32),
-        in_specs=[pl.BlockSpec(memory_space=pl.ANY)] * 4 + [pl.BlockSpec(memory_space=pltpu.SMEM)],
+        in_specs=[pl.BlockSpec(memory_space=pltpu.HBM)] * 4 + [pl.BlockSpec(memory_space=pltpu.SMEM)],
         out_specs=pl.BlockSpec(memory_space=pltpu.VMEM),
         scratch_shapes=[
             pltpu.VMEM((rows, width), jnp.bfloat16),
@@ -79,7 +80,6 @@
             pltpu.VMEM((rank_dim, width), jnp.bfloat16),
             pltpu.SemaphoreType.DMA((4, chunks)),
         ],
-        compiler_params=pltpu.CompilerParams(vmem_limit_bytes=24 * 2**20),
     )(
         activations.reshape(rows, width),
         out_grads.reshape(rows, width),
@@ -89,13 +89,15 @@
     )
 
 
-def solve_kernel(nq, per_dev, axis, tiles_ref, query_ref, scores_ref, extended, solved):
+def solve_kernel(nq, per_dev, place_of, tiles_ref, query_ref, scores_ref, extended, solved):
     examples = tiles_ref.shape[0] // SUBLANES
     wide = examples + nq
     fisher_dim = SUBLANES * LANES
     extended[: examples * SUBLANES] = tiles_ref[...]
     for q in range(nq):
-        first = pl.multiple_of(query_ref[q] * SUBLANES, SUBLANES)
+        number = query_ref[q]
+        place = place_of(number // per_dev) * per_dev + number % per_dev
+        first = pl.multiple_of(place * SUBLANES, SUBLANES)
         extended[(examples + q) * SUBLANES : (examples + q + 1) * SUBLANES] = tiles_ref[pl.ds(first, SUBLANES)]
     extended[wide * SUBLANES :] = jnp.zeros((LANES * SUBLANES - wide * SUBLANES, LANES), jnp.float32)
     right = jnp.concatenate([extended[pl.ds(s, LANES, stride=SUBLANES)] for s in range(SUBLANES)], axis=1)
@@ -113,23 +115,22 @@
         scaled = pivot_row / system[k : k + 1, k : k + 1]
         system = jnp.where(row == k, scaled, system - system[:, k : k + 1] * scaled)
     solved[...] = system
-    first = lax.axis_index(axis) * per_dev
-    mine = solved[pl.ds(first, per_dev)]
-    scores_ref[...] = mine[:, examples : examples + nq]
+    first = place_of(lax.axis_index(AXES)) * per_dev
+    scores_ref[...] = solved[pl.ds(first, per_dev)][:, examples : examples + nq]
 
 
-def gram_scores(tiles, query_index, per_dev, axis):
-    examples = tiles.shape[0] // SUBLANES
+def gram_scores(tiles, query_index, per_dev, place_of):
     nq = query_index.shape[0]
     return pl.pallas_call(
-        functools.partial(solve_kernel, nq, per_dev, axis),
+        functools.partial(solve_kernel, nq, per_dev, place_of),
         out_shape=jax.ShapeDtypeStruct((per_dev, nq), jnp.float32),
         in_specs=[pl.BlockSpec(memory_space=pltpu.VMEM), pl.BlockSpec(memory_space=pltpu.SMEM)],
         out_specs=pl.BlockSpec(memory_space=pltpu.VMEM),
         scratch_shapes=[
             pltpu.VMEM((LANES * SUBLANES, LANES), jnp.float32),
-            pltpu.VMEM((examples, LANES), jnp.float32),
+            pltpu.VMEM((tiles.shape[0] // SUBLANES, LANES), jnp.float32),
         ],
+        compiler_params=pltpu.CompilerParams(vmem_limit_bytes=8 * 2**20),
     )(tiles, query_index)
 
 
@@ -148,26 +149,24 @@
 
 def local(activations, out_grads, project_in, project_out, lengths, query_index):
     per_dev = activations.shape[0]
+    outer, inner = (lax.axis_size(name) for name in AXES)
     tiles = sketch_rows(activations, out_grads, project_in, project_out, lengths)
-    every = lax.all_gather(tiles, "dp", axis=0, tiled=True)
-    examples = every.shape[0] // SUBLANES
-    if examples + query_index.shape[0] <= LANES:
-        return gram_scores(every, query_index, per_dev, "dp")
-    return large_scores(every, query_index, per_dev, "dp")
+    if outer * inner * per_dev + query_index.shape[0] <= LANES:
+        column = lax.all_gather(tiles, "outer", axis=0, tiled=True)
+        every = lax.all_gather(column, "inner", axis=0, tiled=True)
+        return gram_scores(every, query_index, per_dev, lambda p: p % inner * outer + p // inner)
+    return large_scores(lax.all_gather(tiles, AXES, axis=0, tiled=True), query_index, per_dev, AXES)
 
 
 def solution(mesh):
+    groups, size = mesh.shape["groups"], mesh.shape["dp"]
+    inner = 4
+    cut = jax.sharding.Mesh(mesh.devices.reshape(groups, size // inner, inner), ("groups",) + AXES)
+    every = ("groups",) + AXES
     return jax.shard_map(
         local,
-        mesh=mesh,
-        in_specs=(
-            P(("groups", "dp"), None, None),
-            P(("groups", "dp"), None, None),
-            P(),
-            P(),
-            P(("groups", "dp")),
-            P("groups"),
-        ),
-        out_specs=P(("groups", "dp"), None),
+        mesh=cut,
+        in_specs=(P(every, None, None), P(every, None, None), P(), P(), P(every), P("groups")),
+        out_specs=P(every, None),
         check_vma=False,
     )

time: 45.5 us -> 34.9 us (0.77)
  local copies, waits for them, and re-layouts: 7.11 us -> 0.01 us
  blocking collectives: 25.2 us -> 20.9 us
  Pallas kernels: 12.9 us -> 13.9 us
    unnamed x10 -> x2, local copies, waits for them, and re-layouts: 7.11 us -> 0.01 us
    all_gather x1 -> x2, blocking collectives: 25.2 us -> 20.9 us  [the longest x1 15.1 us: local(): column = lax.all_gather(tiles, 'outer', axis=0, tiled=True)]
    pallas_call x1, Pallas kernels: 5.02 us -> 6.28 us  [sketch_rows(): pl.pallas_call(functools.partial(sketch_kernel, chunks, seq_len), out_sha...]
where the time goes in v5:
time: 34.9 us; the launch traced here: 34.8 us
  blocking collectives  20.9 us (60%)
  Pallas kernels  13.9 us (40%)
    all_gather x1, blocking collectives, local(): column = lax.all_gather(tiles, 'outer', axis=0, tiled=True)  15.1 us
    pallas_call x1, Pallas kernels, gram_scores(): pl.pallas_call(functools.partial(solve_kernel, nq, per_dev, place_of), ou...  7.58 us
    pallas_call x1, Pallas kernels, sketch_rows(): pl.pallas_call(functools.partial(sketch_kernel, chunks, seq_len), out_sha...  6.28 us
    all_gather x1, blocking collectives, local(): every = lax.all_gather(column, 'inner', axis=0, tiled=True)  5.77 us

profile of v5, /device:TPU:0, one launch (start us, length us, event | category | flops | bytes accessed | tf_op | source)
XLA Modules:
  0.0 34.8 jit_solution(1570841738645385510)
XLA Ops:
  0.0 0.0 copy-start
  0.0 6.3 %shard_map.64 = f32[32,128]{1,0:T(8,128)} custom-call(bf16[256,8192]{1,0:T(8,128)(2,1)} %bitcast.4, bf16[256,8192]{1,0:T(8,128)(2,1)} %bitcast.5, bf16[32,8192]{1,0:T(8,128)(2,1)} %bitcast.6, bf16[32,8192]{1,0:T(8,128)(2,1)} %bitcast.7, s32[4]{0:T(128)} %lengths_ref.1), custom_call_target="tpu_custom_call" | custom-call | tf_op jit(solution)/shard_map/pallas_call | solution.py:71
  6.3 15.1 %all_gather.6 = f32[128,128]{1,0:T(8,128)S(1)} all-gather(f32[32,128]{1,0:T(8,128)} %shard_map.64), channel_id=1, replica_groups=mesh['groups'=2,'outer'=4,'inner'=4] {'outer'}, dimensions={0}, use_global_device_ids=true | all-gather | bytes 81920 | tf_op jit(solution)/shard_map/all_gather | solution.py:155
  21.4 5.8 %all_gather.7.tiles_ref = f32[512,128]{1,0:T(8,128)S(1)} all-gather(f32[128,128]{1,0:T(8,128)S(1)} %all_gather.6), channel_id=1, replica_groups=mesh['groups'=2,'outer'=4,'inner'=4] {'inner'}, dimensions={0}, use_global_device_ids=true | all-gather | bytes 327680 | tf_op jit(solution)/shard_map/all_gather | solution.py:156
  27.2 0.0 copy-done
  27.2 7.6 %shard_map.65 = f32[4,16]{1,0:T(4,128)} custom-call(f32[512,128]{1,0:T(8,128)S(1)} %all_gather.7.tiles_ref, s32[16]{0:T(128)S(1)} %copy-done), custom_call_target="tpu_custom_call" | custom-call | tf_op jit(solution)/shard_map/pallas_call | solution.py:124
Async XLA Ops:
  0.0 27.2 %copy-start = (s32[16]{0:T(128)S(1)}, s32[16]{0:T(128)}, u32[]{:S(2)}) copy-start(s32[16]{0:T(128)} %query_ref.1) | copy-start | bytes 196

commit v6 on v4

--- a/solution.py
+++ b/solution.py
@@ -30,26 +30,26 @@
         )
         for copy in copies[-1]:
             copy.start()
-    feat = jnp.zeros((rank_dim, rows), jnp.float32)
-    grad = jnp.zeros((rank_dim, rows), jnp.float32)
+    feat = jnp.zeros((rows, rank_dim), jnp.float32)
+    grad = jnp.zeros((rows, rank_dim), jnp.float32)
     for c in range(chunks):
         cols = slice(c * step, (c + 1) * step)
         for copy in copies[c]:
             copy.wait()
-        feat = feat + lax.dot_general(pin[:, cols], act[:, cols], NT, preferred_element_type=jnp.float32)
-        grad = grad + lax.dot_general(pout[:, cols], out[:, cols], NT, preferred_element_type=jnp.float32)
+        feat = feat + lax.dot_general(act[:, cols], pin[:, cols], NT, preferred_element_type=jnp.float32)
+        grad = grad + lax.dot_general(out[:, cols], pout[:, cols], NT, preferred_element_type=jnp.float32)
     count = rows // seq_len
     reps = LANES // rank_dim
-    position = lax.broadcasted_iota(jnp.int32, (rank_dim, rows), 1)
+    position = lax.broadcasted_iota(jnp.int32, (rows, rank_dim), 0)
     masked = []
     for e in range(count):
         first = e * seq_len
         live = (position >= first) & (position < first + lengths_ref[e])
         masked.append(jnp.where(live, grad, 0.0))
     outer = lax.dot_general(
-        jnp.concatenate(masked, axis=0),
-        jnp.concatenate([feat] * reps, axis=0),
-        NT,
+        jnp.concatenate(masked, axis=1),
+        jnp.concatenate([feat] * reps, axis=1),
+        (((0,), (0,)), ((), ())),
         precision=lax.Precision.HIGHEST,
         preferred_element_type=jnp.float32,
     )
@@ -88,6 +88,45 @@
     )
 
 
+def eliminate(system, count):
+    row = lax.broadcasted_iota(jnp.int32, (SUBLANES, system.shape[1]), 0)
+    shape = system.shape
+    for k in range(0, count, 4):
+        cols = [jnp.broadcast_to(system[:, k + j : k + j + 1], shape) for j in range(4)]
+        rows = [system[k + i : k + i + 1] for i in range(4)]
+        p = [[cols[j][k + i : k + i + 1] for j in range(4)] for i in range(4)]
+        scale = 1.0 / (p[0][0] * p[1][1] - p[0][1] * p[0][1])
+        a, b, c = p[1][1] * scale, -p[0][1] * scale, p[0][0] * scale
+        y = [
+            [a * p[0][2] + b * p[1][2], a * p[0][3] + b * p[1][3]],
+            [b * p[0][2] + c * p[1][2], b * p[0][3] + c * p[1][3]],
+        ]
+        s00 = p[2][2] - (p[0][2] * y[0][0] + p[1][2] * y[1][0])
+        s01 = p[2][3] - (p[0][2] * y[0][1] + p[1][2] * y[1][1])
+        s11 = p[3][3] - (p[0][3] * y[0][1] + p[1][3] * y[1][1])
+        scale = 1.0 / (s00 * s11 - s01 * s01)
+        d, e, f = s11 * scale, -s01 * scale, s00 * scale
+        z0 = a * rows[0] + b * rows[1]
+        z1 = b * rows[0] + c * rows[1]
+        t0 = rows[2] - (p[0][2] * z0 + p[1][2] * z1)
+        t1 = rows[3] - (p[0][3] * z0 + p[1][3] * z1)
+        w2 = d * t0 + e * t1
+        w3 = e * t0 + f * t1
+        w0 = z0 - (y[0][0] * w2 + y[0][1] * w3)
+        w1 = z1 - (y[1][0] * w2 + y[1][1] * w3)
+        done = [w0, w1, w2, w3]
+        parts = []
+        for r in range(0, count, SUBLANES):
+            own = slice(r, r + SUBLANES)
+            part = system[own] - (cols[0][own] * w0 + cols[1][own] * w1) - (cols[2][own] * w2 + cols[3][own] * w3)
+            if r <= k < r + SUBLANES:
+                for i in range(4):
+                    part = jnp.where(row == k - r + i, done[i], part)
+            parts.append(part)
+        system = jnp.concatenate(parts, axis=0)
+    return system
+
+
 def solve_kernel(nq, per_dev, inner, axis, *refs):
     tiles, (query_ref, scores_ref, extended) = refs[:-3], refs[-3:]
     block = tiles[0].shape[0]
@@ -115,10 +154,7 @@
     trace = jnp.sum(jnp.where(diagonal, system, 0.0))
     damping = damp_ratio * trace / fisher_dim
     system = jnp.where(diagonal, system + damping, system)
-    for k in range(examples):
-        pivot_row = system[k : k + 1]
-        scaled = pivot_row / system[k : k + 1, k : k + 1]
-        system = jnp.where(row == k, scaled, system - system[:, k : k + 1] * scaled)
+    system = eliminate(system, examples)
     scores_ref[...] = system[:per_dev, examples : examples + nq]
 
 

time: 30.6 us -> 27.3 us (0.89)
  Pallas kernels: 13.9 us -> 10.6 us
    pallas_call x1, Pallas kernels: 7.61 us -> 4.3 us  [gram_scores(): pl.pallas_call(functools.partial(solve_kernel, nq, per_dev, inner, axis),...]
where the time goes in v6:
time: 27.3 us; the launch traced here: 27.1 us
  Pallas kernels  10.6 us (39%)
  waiting for transfers between devices  8.14 us (30%)
  starting transfers between devices  7.62 us (28%)
  other arithmetic  0.72 us (3%)
    ppermute x6, waiting for transfers between devices, swap(): return lax.ppermute(block, axis, [(i, i ^ slot) for i in range(size)])  8.14 us
    ppermute x6, starting transfers between devices, swap(): return lax.ppermute(block, axis, [(i, i ^ slot) for i in range(size)])  7.62 us
    pallas_call x1, Pallas kernels, sketch_rows(): pl.pallas_call(functools.partial(sketch_kernel, chunks, seq_len), out_sha...  6.26 us
    pallas_call x1, Pallas kernels, gram_scores(): pl.pallas_call(functools.partial(solve_kernel, nq, per_dev, inner, axis),...  4.3 us
    concatenate x1, other arithmetic, gather_xor(): jnp.concatenate([tiles] + [swap(tiles, slot) for slot in range(inner, siz...  0.72 us
  transfers between devices with their start and end apart: 6, of which 4 were waited for; matrix products, arithmetic and copies ran while one was open for 0% of the time, Pallas kernels for 0%

profile of v6, /device:TPU:0, one launch (start us, length us, event | category | flops | bytes accessed | tf_op | source)
XLA Modules:
  0.0 27.1 jit_solution(2791394404433186722)
XLA Ops:
  0.0 0.0 copy-start
  0.0 6.3 %shard_map.64 = f32[32,128]{1,0:T(8,128)} custom-call(bf16[256,8192]{1,0:T(8,128)(2,1)} %bitcast.4, bf16[256,8192]{1,0:T(8,128)(2,1)} %bitcast.5, bf16[32,8192]{1,0:T(8,128)(2,1)} %bitcast.6, bf16[32,8192]{1,0:T(8,128)(2,1)} %bitcast.7, s32[4]{0:T(128)} %lengths_ref.1), custom_call_target="tpu_custom_call" | custom-call | tf_op jit(solution)/shard_map/pallas_call | solution.py:70
  6.3 5.1 %collective-permute-start.2 = (f32[32,128]{1,0:T(8,128)}, f32[32,128]{1,0:T(8,128)S(1)}, u32[]{:S(2)}, u32[]{:S(2)}) collective-permute-start(f32[32,128]{1,0:T(8,128)} %shard_map.64), channel_id=1, source_target_pairs={{0,12},{1,13},{2,14},{3,15},{4,8},{5,9},{6,10},{7,11},{8,4},{9,5},... | collective-permute-start | bytes 49160 | tf_op jit(solution)/shard_map/ppermute | solution.py:175
  11.4 0.0 collective-permute-start.1
  11.4 0.6 %collective-permute-start = (f32[32,128]{1,0:T(8,128)}, f32[32,128]{1,0:T(8,128)S(1)}, u32[]{:S(2)}, u32[]{:S(2)}) collective-permute-start(f32[32,128]{1,0:T(8,128)} %shard_map.64), channel_id=1, source_target_pairs={{0,4},{1,5},{2,6},{3,7},{4,0},{5,1},{6,2},{7,3},{8,12},{9,13},{10,... | collective-permute-start | bytes 49160 | tf_op jit(solution)/shard_map/ppermute | solution.py:175
  12.0 1.3 %collective-permute-done.2 = f32[32,128]{1,0:T(8,128)S(1)} collective-permute-done((f32[32,128]{1,0:T(8,128)}, f32[32,128]{1,0:T(8,128)S(1)}, u32[]{:S(2)}, u32[]{:S(2)}) %collective-permute-start.2) | collective-permute-done | bytes 16416 | tf_op jit(solution)/shard_map/ppermute | solution.py:175
  13.3 2.9 %collective-permute-done.1 = f32[32,128]{1,0:T(8,128)S(1)} collective-permute-done((f32[32,128]{1,0:T(8,128)}, f32[32,128]{1,0:T(8,128)S(1)}, u32[]{:S(2)}, u32[]{:S(2)}) %collective-permute-start.1) | collective-permute-done | bytes 16416 | tf_op jit(solution)/shard_map/ppermute | solution.py:175
  16.2 0.0 collective-permute-done
  16.2 0.7 %pad_maximum_fusion.refs_0_ = f32[128,128]{1,0:T(8,128)S(1)} fusion(f32[32,128]{1,0:T(8,128)S(1)} %collective-permute-done.2, f32[32,128]{1,0:T(8,128)S(1)} %collective-permute-done.1, f32[32,128]{1,0:T(8,128)S(1)} %collective-permute-done, f32[32,128]{1,0:T(8,128)} %shard_map.64), kind=kLoop, calls=%fused_computation | loop fusion | flops 49152 | bytes 131072 | tf_op jit(solution)/shard_map/concatenate | solution.py:177
  17.0 0.0 collective-permute-start.5
  17.0 1.5 %collective-permute-start.4 = (f32[128,128]{1,0:T(8,128)S(1)}, f32[128,128]{1,0:T(8,128)S(1)}, u32[]{:S(2)}, u32[]{:S(2)}) collective-permute-start(f32[128,128]{1,0:T(8,128)S(1)} %pad_maximum_fusion.refs_0_), channel_id=1, source_target_pairs={{0,2},{1,3},{2,0},{3,1},{4,6},{5,7},{6,4},{7,5},{8,10},{9,11},{10,... | collective-permute-start | bytes 196616 | tf_op jit(solution)/shard_map/ppermute | solution.py:175
  18.5 0.3 %collective-permute-start.3 = (f32[128,128]{1,0:T(8,128)S(1)}, f32[128,128]{1,0:T(8,128)S(1)}, u32[]{:S(2)}, u32[]{:S(2)}) collective-permute-start(f32[128,128]{1,0:T(8,128)S(1)} %pad_maximum_fusion.refs_0_), channel_id=1, source_target_pairs={{0,1},{1,0},{2,3},{3,2},{4,5},{5,4},{6,7},{7,6},{8,9},{9,8},{10,11... | collective-permute-start | bytes 196616 | tf_op jit(solution)/shard_map/ppermute | solution.py:175
  18.8 2.5 %collective-permute-done.5.refs_3_ = f32[128,128]{1,0:T(8,128)S(1)} collective-permute-done((f32[128,128]{1,0:T(8,128)S(1)}, f32[128,128]{1,0:T(8,128)S(1)}, u32[]{:S(2)}, u32[]{:S(2)}) %collective-permute-start.5) | collective-permute-done | bytes 65568 | tf_op jit(solution)/shard_map/ppermute | solution.py:175
  21.3 1.5 %collective-permute-done.4.refs_2_ = f32[128,128]{1,0:T(8,128)S(1)} collective-permute-done((f32[128,128]{1,0:T(8,128)S(1)}, f32[128,128]{1,0:T(8,128)S(1)}, u32[]{:S(2)}, u32[]{:S(2)}) %collective-permute-start.4) | collective-permute-done | bytes 65568 | tf_op jit(solution)/shard_map/ppermute | solution.py:175
  22.8 0.0 collective-permute-done.3.refs_1_
  22.8 0.0 copy-done
  22.8 4.3 %shard_map.65 = f32[4,16]{1,0:T(4,128)} custom-call(f32[128,128]{1,0:T(8,128)S(1)} %pad_maximum_fusion.refs_0_, f32[128,128]{1,0:T(8,128)S(1)} %collective-permute-done.3.refs_1_, f32[128,128]{1,0:T(8,128)S(1)} %collective-permute-done.4.refs_2_, f32[128,128]{1,0:T(8,128)S(1)} %collective-permute-done.5.refs_3_, s32[16]{0:T(128)S(1)} %copy-done), custom_call_target="tpu_custom_call" | custom-call | tf_op jit(solution)/shard_map/pallas_call | solution.py:163
Async XLA Ops:
  0.0 22.8 %copy-start = (s32[16]{0:T(128)S(1)}, s32[16]{0:T(128)}, u32[]{:S(2)}) copy-start(s32[16]{0:T(128)} %refs_4_.1) | copy-start | bytes 196
  6.3 7.0 %collective-permute-start.2 = (f32[32,128]{1,0:T(8,128)}, f32[32,128]{1,0:T(8,128)S(1)}, u32[]{:S(2)}, u32[]{:S(2)}) collective-permute-start(f32[32,128]{1,0:T(8,128)} %shard_map.64), channel_id=1, source_target_pairs={{0,12},{1,13},{2,14},{3,15},{4,8},{5,9},{6,10},{7,11},{8,4},{9,5},... | collective-permute-start | bytes 49160 | tf_op jit(solution)/shard_map/ppermute | solution.py:175
  11.4 4.8 %collective-permute-start.1 = (f32[32,128]{1,0:T(8,128)}, f32[32,128]{1,0:T(8,128)S(1)}, u32[]{:S(2)}, u32[]{:S(2)}) collective-permute-start(f32[32,128]{1,0:T(8,128)} %shard_map.64), channel_id=1, source_target_pairs={{0,8},{1,9},{2,10},{3,11},{4,12},{5,13},{6,14},{7,15},{8,0},{9,1},... | collective-permute-start | bytes 49160 | tf_op jit(solution)/shard_map/ppermute | solution.py:175
  11.4 4.8 %collective-permute-start = (f32[32,128]{1,0:T(8,128)}, f32[32,128]{1,0:T(8,128)S(1)}, u32[]{:S(2)}, u32[]{:S(2)}) collective-permute-start(f32[32,128]{1,0:T(8,128)} %shard_map.64), channel_id=1, source_target_pairs={{0,4},{1,5},{2,6},{3,7},{4,0},{5,1},{6,2},{7,3},{8,12},{9,13},{10,... | collective-permute-start | bytes 49160 | tf_op jit(solution)/shard_map/ppermute | solution.py:175
  17.0 4.3 %collective-permute-start.5 = (f32[128,128]{1,0:T(8,128)S(1)}, f32[128,128]{1,0:T(8,128)S(1)}, u32[]{:S(2)}, u32[]{:S(2)}) collective-permute-start(f32[128,128]{1,0:T(8,128)S(1)} %pad_maximum_fusion.refs_0_), channel_id=1, source_target_pairs={{0,3},{1,2},{2,1},{3,0},{4,7},{5,6},{6,5},{7,4},{8,11},{9,10},{10,... | collective-permute-start | bytes 196616 | tf_op jit(solution)/shard_map/ppermute | solution.py:175
  17.0 5.8 %collective-permute-start.4 = (f32[128,128]{1,0:T(8,128)S(1)}, f32[128,128]{1,0:T(8,128)S(1)}, u32[]{:S(2)}, u32[]{:S(2)}) collective-permute-start(f32[128,128]{1,0:T(8,128)S(1)} %pad_maximum_fusion.refs_0_), channel_id=1, source_target_pairs={{0,2},{1,3},{2,0},{3,1},{4,6},{5,7},{6,4},{7,5},{8,10},{9,11},{10,... | collective-permute-start | bytes 196616 | tf_op jit(solution)/shard_map/ppermute | solution.py:175
  18.5 4.3 %collective-permute-start.3 = (f32[128,128]{1,0:T(8,128)S(1)}, f32[128,128]{1,0:T(8,128)S(1)}, u32[]{:S(2)}, u32[]{:S(2)}) collective-permute-start(f32[128,128]{1,0:T(8,128)S(1)} %pad_maximum_fusion.refs_0_), channel_id=1, source_target_pairs={{0,1},{1,0},{2,3},{3,2},{4,5},{5,4},{6,7},{7,6},{8,9},{9,8},{10,11... | collective-permute-start | bytes 196616 | tf_op jit(solution)/shard_map/ppermute | solution.py:175

commit v7 on v6

--- a/solution.py
+++ b/solution.py
@@ -8,12 +8,13 @@
 from jax.sharding import PartitionSpec as P
 
 damp_ratio = 0.5
+AXES = ("outer", "inner")
 LANES = 128
 SUBLANES = 8
 NT = (((1,), (1,)), ((), ()))
 
 
-def sketch_kernel(chunks, seq_len, act_hbm, out_hbm, pin_hbm, pout_hbm, lengths_ref, sketch_ref, act, out, pin, pout, sems):
+def sketch_kernel(chunks, seq_len, copies_out, act_hbm, out_hbm, pin_hbm, pout_hbm, lengths_ref, sketch_ref, act, out, pin, pout, sems):
     rows, width = act.shape
     rank_dim = pin.shape[0]
     step = width // chunks
@@ -59,17 +60,19 @@
         for b in range(1, reps):
             first = e * rank_dim + b * SUBLANES
             entry = jnp.where(band == b, outer[first : first + SUBLANES], entry)
-        sketch_ref[e * SUBLANES : (e + 1) * SUBLANES] = entry
-
-
-def sketch_rows(activations, out_grads, project_in, project_out, lengths):
+        for n in range(copies_out):
+            first = (n * count + e) * SUBLANES
+            sketch_ref[first : first + SUBLANES] = entry
+
+
+def sketch_rows(activations, out_grads, project_in, project_out, lengths, copies_out):
     count, seq_len, width = activations.shape
     rank_dim = project_in.shape[1]
     rows = count * seq_len
     chunks = 8
     return pl.pallas_call(
-        functools.partial(sketch_kernel, chunks, seq_len),
-        out_shape=jax.ShapeDtypeStruct((count * SUBLANES, LANES), jnp.float32),
+        functools.partial(sketch_kernel, chunks, seq_len, copies_out),
+        out_shape=jax.ShapeDtypeStruct((copies_out * count * SUBLANES, LANES), jnp.float32),
         in_specs=[pl.BlockSpec(memory_space=pltpu.HBM)] * 4 + [pl.BlockSpec(memory_space=pltpu.SMEM)],
         out_specs=pl.BlockSpec(memory_space=pltpu.VMEM),
         scratch_shapes=[
@@ -79,6 +82,7 @@
             pltpu.VMEM((rank_dim, width), jnp.bfloat16),
             pltpu.SemaphoreType.DMA((4, chunks)),
         ],
+        compiler_params=pltpu.CompilerParams(vmem_limit_bytes=241 * 2**18),
     )(
         activations.reshape(rows, width),
         out_grads.reshape(rows, width),
@@ -127,20 +131,21 @@
     return system
 
 
-def solve_kernel(nq, per_dev, inner, axis, *refs):
-    tiles, (query_ref, scores_ref, extended) = refs[:-3], refs[-3:]
+def solve_kernel(nq, per_dev, *refs):
+    tiles, (query_ref, scores_ref, extended, solved) = refs[:-4], refs[-4:]
     block = tiles[0].shape[0]
-    examples = len(tiles) * block // SUBLANES
+    inner = len(tiles)
+    examples = inner * block // SUBLANES
     outer = examples // (inner * per_dev)
     wide = examples + nq
     fisher_dim = SUBLANES * LANES
-    me = lax.axis_index(axis)
+    mine_outer, mine_inner = (lax.axis_index(name) for name in AXES)
     for slot, tile in enumerate(tiles):
         extended[slot * block : (slot + 1) * block] = tile[...]
     for q in range(nq):
         number = query_ref[q]
-        slot = (number // per_dev) ^ me
-        place = ((slot % inner) * outer + slot // inner) * per_dev + number % per_dev
+        device = number // per_dev
+        place = ((device % inner ^ mine_inner) * outer + device // inner) * per_dev + number % per_dev
         first = pl.multiple_of(place * SUBLANES, SUBLANES)
         extended[(examples + q) * SUBLANES : (examples + q + 1) * SUBLANES] = extended[pl.ds(first, SUBLANES)]
     extended[wide * SUBLANES :] = jnp.zeros((LANES * SUBLANES - wide * SUBLANES, LANES), jnp.float32)
@@ -155,27 +160,24 @@
     damping = damp_ratio * trace / fisher_dim
     system = jnp.where(diagonal, system + damping, system)
     system = eliminate(system, examples)
-    scores_ref[...] = system[:per_dev, examples : examples + nq]
-
-
-def gram_scores(tiles, query_index, per_dev, inner, axis):
+    solved[...] = system
+    scores_ref[...] = solved[pl.ds(mine_outer * per_dev, per_dev)][:, examples : examples + nq]
+
+
+def gram_scores(tiles, query_index, per_dev):
     nq = query_index.shape[0]
+    examples = len(tiles) * tiles[0].shape[0] // SUBLANES
     return pl.pallas_call(
-        functools.partial(solve_kernel, nq, per_dev, inner, axis),
+        functools.partial(solve_kernel, nq, per_dev),
         out_shape=jax.ShapeDtypeStruct((per_dev, nq), jnp.float32),
         in_specs=[pl.BlockSpec(memory_space=pltpu.VMEM)] * len(tiles) + [pl.BlockSpec(memory_space=pltpu.SMEM)],
         out_specs=pl.BlockSpec(memory_space=pltpu.VMEM),
-        scratch_shapes=[pltpu.VMEM((LANES * SUBLANES, LANES), jnp.float32)],
+        scratch_shapes=[
+            pltpu.VMEM((LANES * SUBLANES, LANES), jnp.float32),
+            pltpu.VMEM((examples, LANES), jnp.float32),
+        ],
         compiler_params=pltpu.CompilerParams(vmem_limit_bytes=8 * 2**20),
     )(*tiles, query_index)
-
-
-def gather_xor(tiles, axis, size, inner):
-    def swap(block, slot):
-        return lax.ppermute(block, axis, [(i, i ^ slot) for i in range(size)])
-
-    column = jnp.concatenate([tiles] + [swap(tiles, slot) for slot in range(inner, size, inner)], axis=0)
-    return [column] + [swap(column, slot) for slot in range(1, inner)]
 
 
 def large_scores(tiles, query_index, per_dev, axis):
@@ -193,26 +195,27 @@
 
 def local(activations, out_grads, project_in, project_out, lengths, query_index):
     per_dev = activations.shape[0]
-    size = lax.axis_size("dp")
-    tiles = sketch_rows(activations, out_grads, project_in, project_out, lengths)
-    if size * per_dev + query_index.shape[0] <= LANES:
-        inner = 4
-        return gram_scores(gather_xor(tiles, "dp", size, inner), query_index, per_dev, inner, "dp")
-    return large_scores(lax.all_gather(tiles, "dp", axis=0, tiled=True), query_index, per_dev, "dp")
+    outer, inner = (lax.axis_size(name) for name in AXES)
+    small = outer * inner * per_dev + query_index.shape[0] <= LANES
+    tiles = sketch_rows(activations, out_grads, project_in, project_out, lengths, outer if small else 1)
+    if not small:
+        return large_scores(lax.all_gather(tiles, AXES, axis=0, tiled=True), query_index, per_dev, AXES)
+    column = lax.all_to_all(tiles, "outer", split_axis=0, concat_axis=0, tiled=True)
+    columns = [column] + [
+        lax.ppermute(column, "inner", [(i, i ^ slot) for i in range(inner)]) for slot in range(1, inner)
+    ]
+    return gram_scores(columns, query_index, per_dev)
 
 
 def solution(mesh):
+    groups, size = mesh.shape["groups"], mesh.shape["dp"]
+    inner = 4
+    cut = jax.sharding.Mesh(mesh.devices.reshape(groups, size // inner, inner), ("groups",) + AXES)
+    every = ("groups",) + AXES
     return jax.shard_map(
         local,
-        mesh=mesh,
-        in_specs=(
-            P(("groups", "dp"), None, None),
-            P(("groups", "dp"), None, None),
-            P(),
-            P(),
-            P(("groups", "dp")),
-            P("groups"),
-        ),
-        out_specs=P(("groups", "dp"), None),
+        mesh=cut,
+        in_specs=(P(every, None, None), P(every, None, None), P(), P(), P(every), P("groups")),
+        out_specs=P(every, None),
         check_vma=False,
     )

time: 27.3 us -> 28.8 us (1.055)
  blocking collectives: 0 us -> 12.1 us
  starting transfers between devices: 7.62 us -> 1.86 us
  waiting for transfers between devices: 8.14 us -> 3.94 us
  other arithmetic: 0.72 us -> 0 us
    all_to_all x0 -> x1, blocking collectives: none -> 12.1 us  [local(): lax.all_to_all(tiles, 'outer', split_axis=0, concat_axis=0, tiled=True)]
    ppermute x6 -> x3, starting transfers between devices: 7.62 us -> 1.86 us  [local(): lax.ppermute(column, 'inner', [(i, i ^ slot) for i in range(inner)])]
    ppermute x6 -> x3, waiting for transfers between devices: 8.14 us -> 3.94 us  [local(): lax.ppermute(column, 'inner', [(i, i ^ slot) for i in range(inner)])]
    concatenate x1 -> x0, other arithmetic: 0.72 us -> none  [gather_xor(): jnp.concatenate([tiles] + [swap(tiles, slot) for slot in range(inner, siz...]
  transfers between devices with their start and end apart: 6 -> 3, of which waited for: 4 -> 2; matrix products, arithmetic and copies ran while one was open for 0% -> 0% of each run, Pallas kernels for 0% -> 0%
where the time goes in v7:
time: 28.8 us; the launch traced here: 28.6 us
  blocking collectives  12.1 us (42%)
  Pallas kernels  10.7 us (37%)
  waiting for transfers between devices  3.94 us (14%)
  starting transfers between devices  1.86 us (6%)
    all_to_all x1, blocking collectives, local(): lax.all_to_all(tiles, 'outer', split_axis=0, concat_axis=0, tiled=True)  12.1 us
    pallas_call x1, Pallas kernels, sketch_rows(): pl.pallas_call(functools.partial(sketch_kernel, chunks, seq_len, copies_o...  6.27 us
    pallas_call x1, Pallas kernels, gram_scores(): pl.pallas_call(functools.partial(solve_kernel, nq, per_dev), out_shape=ja...  4.39 us
    ppermute x3, waiting for transfers between devices, local(): lax.ppermute(column, 'inner', [(i, i ^ slot) for i in range(inner)])  3.94 us
    ppermute x3, starting transfers between devices, local(): lax.ppermute(column, 'inner', [(i, i ^ slot) for i in range(inner)])  1.86 us
  transfers between devices with their start and end apart: 3, of which 2 were waited for; matrix products, arithmetic and copies ran while one was open for 0% of the time, Pallas kernels for 0%

profile of v7, /device:TPU:0, one launch (start us, length us, event | category | flops | bytes accessed | tf_op | source)
XLA Modules:
  0.0 28.6 jit_solution(8983251253191165319)
XLA Ops:
  0.0 0.0 copy-start
  0.0 6.3 %shard_map.64 = f32[128,128]{1,0:T(8,128)} custom-call(bf16[256,8192]{1,0:T(8,128)(2,1)} %bitcast.10, bf16[256,8192]{1,0:T(8,128)(2,1)} %bitcast.11, bf16[32,8192]{1,0:T(8,128)(2,1)} %bitcast.12, bf16[32,8192]{1,0:T(8,128)(2,1)} %bitcast.13, s32[4]{0:T(128)} %lengths_ref.1), custom_call_target="tpu_custom_call" | custom-call | tf_op jit(solution)/shard_map/pallas_call | solution.py:73
  6.3 12.1 %all_to_all.11 = f32[4,32,128]{2,1,0:T(8,128)S(1)} all-to-all(f32[4,32,128]{2,1,0:T(8,128)} %bitcast.14), channel_id=1, replica_groups=mesh['groups'=2,'outer'=4,'inner'=4] {'outer'}, dimensions={0} | all-to-all | bytes 131072 | tf_op jit(solution)/shard_map/all_to_all | solution.py:203
  18.4 0.0 collective-permute-start.2
  18.4 1.5 %collective-permute-start.1 = (f32[128,128]{1,0:T(8,128)S(1)}, f32[128,128]{1,0:T(8,128)S(1)}, u32[]{:S(2)}, u32[]{:S(2)}) collective-permute-start(f32[128,128]{1,0:T(8,128)S(1)} %bitcast.7), channel_id=1, source_target_pairs={{0,2},{1,3},{2,0},{3,1},{4,6},{5,7},{6,4},{7,5},{8,10},{9,11},{10,... | collective-permute-start | bytes 196616 | tf_op jit(solution)/shard_map/ppermute | solution.py:205
  19.9 0.3 %collective-permute-start = (f32[128,128]{1,0:T(8,128)S(1)}, f32[128,128]{1,0:T(8,128)S(1)}, u32[]{:S(2)}, u32[]{:S(2)}) collective-permute-start(f32[128,128]{1,0:T(8,128)S(1)} %bitcast.8), channel_id=1, source_target_pairs={{0,1},{1,0},{2,3},{3,2},{4,5},{5,4},{6,7},{7,6},{8,9},{9,8},{10,11... | collective-permute-start | bytes 196616 | tf_op jit(solution)/shard_map/ppermute | solution.py:205
  20.2 2.5 %collective-permute-done.2.refs_3_ = f32[128,128]{1,0:T(8,128)S(1)} collective-permute-done((f32[128,128]{1,0:T(8,128)S(1)}, f32[128,128]{1,0:T(8,128)S(1)}, u32[]{:S(2)}, u32[]{:S(2)}) %collective-permute-start.2) | collective-permute-done | bytes 65568 | tf_op jit(solution)/shard_map/ppermute | solution.py:205
  22.7 1.5 %collective-permute-done.1.refs_2_ = f32[128,128]{1,0:T(8,128)S(1)} collective-permute-done((f32[128,128]{1,0:T(8,128)S(1)}, f32[128,128]{1,0:T(8,128)S(1)}, u32[]{:S(2)}, u32[]{:S(2)}) %collective-permute-start.1) | collective-permute-done | bytes 65568 | tf_op jit(solution)/shard_map/ppermute | solution.py:205
  24.2 0.0 collective-permute-done.refs_1_
  24.2 0.0 copy-done
  24.2 4.4 %shard_map.65 = f32[4,16]{1,0:T(4,128)} custom-call(f32[128,128]{1,0:T(8,128)S(1)} %bitcast.9, f32[128,128]{1,0:T(8,128)S(1)} %collective-permute-done.refs_1_, f32[128,128]{1,0:T(8,128)S(1)} %collective-permute-done.1.refs_2_, f32[128,128]{1,0:T(8,128)S(1)} %collective-permute-done.2.refs_3_, s32[16]{0:T(128)S(1)} %copy-done), custom_call_target="tpu_custom_call" | custom-call | tf_op jit(solution)/shard_map/pallas_call | solution.py:170
Async XLA Ops:
  0.0 24.2 %copy-start = (s32[16]{0:T(128)S(1)}, s32[16]{0:T(128)}, u32[]{:S(2)}) copy-start(s32[16]{0:T(128)} %refs_4_.1) | copy-start | bytes 196
  18.4 4.3 %collective-permute-start.2 = (f32[128,128]{1,0:T(8,128)S(1)}, f32[128,128]{1,0:T(8,128)S(1)}, u32[]{:S(2)}, u32[]{:S(2)}) collective-permute-start(f32[128,128]{1,0:T(8,128)S(1)} %bitcast.6), channel_id=1, source_target_pairs={{0,3},{1,2},{2,1},{3,0},{4,7},{5,6},{6,5},{7,4},{8,11},{9,10},{10,... | collective-permute-start | bytes 196616 | tf_op jit(solution)/shard_map/ppermute | solution.py:205
  18.4 5.8 %collective-permute-start.1 = (f32[128,128]{1,0:T(8,128)S(1)}, f32[128,128]{1,0:T(8,128)S(1)}, u32[]{:S(2)}, u32[]{:S(2)}) collective-permute-start(f32[128,128]{1,0:T(8,128)S(1)} %bitcast.7), channel_id=1, source_target_pairs={{0,2},{1,3},{2,0},{3,1},{4,6},{5,7},{6,4},{7,5},{8,10},{9,11},{10,... | collective-permute-start | bytes 196616 | tf_op jit(solution)/shard_map/ppermute | solution.py:205
  19.9 4.3 %collective-permute-start = (f32[128,128]{1,0:T(8,128)S(1)}, f32[128,128]{1,0:T(8,128)S(1)}, u32[]{:S(2)}, u32[]{:S(2)}) collective-permute-start(f32[128,128]{1,0:T(8,128)S(1)} %bitcast.8), channel_id=1, source_target_pairs={{0,1},{1,0},{2,3},{3,2},{4,5},{5,4},{6,7},{7,6},{8,9},{9,8},{10,11... | collective-permute-start | bytes 196616 | tf_op jit(solution)/shard_map/ppermute | solution.py:205

commit v8 on v6

--- a/solution.py
+++ b/solution.py
@@ -13,10 +13,12 @@
 NT = (((1,), (1,)), ((), ()))
 
 
-def sketch_kernel(chunks, seq_len, act_hbm, out_hbm, pin_hbm, pout_hbm, lengths_ref, sketch_ref, act, out, pin, pout, sems):
+def sketch_kernel(chunks, seq_len, act_hbm, out_hbm, pin_hbm, pout_hbm, lengths_hbm, sketch_ref, act, out, pin, pout, lengths_ref, sems, lengths_sem):
     rows, width = act.shape
     rank_dim = pin.shape[0]
     step = width // chunks
+    lengths_copy = pltpu.make_async_copy(lengths_hbm, lengths_ref, lengths_sem)
+    lengths_copy.start()
     copies = []
     for c in range(chunks):
         cols = pl.ds(c * step, step)
@@ -40,6 +42,7 @@
         grad = grad + lax.dot_general(out[:, cols], pout[:, cols], NT, preferred_element_type=jnp.float32)
     count = rows // seq_len
     reps = LANES // rank_dim
+    lengths_copy.wait()
     position = lax.broadcasted_iota(jnp.int32, (rows, rank_dim), 0)
     masked = []
     for e in range(count):
@@ -70,21 +73,29 @@
     return pl.pallas_call(
         functools.partial(sketch_kernel, chunks, seq_len),
         out_shape=jax.ShapeDtypeStruct((count * SUBLANES, LANES), jnp.float32),
-        in_specs=[pl.BlockSpec(memory_space=pltpu.HBM)] * 4 + [pl.BlockSpec(memory_space=pltpu.SMEM)],
+        in_specs=[pl.BlockSpec(memory_space=pltpu.HBM)] * 5,
         out_specs=pl.BlockSpec(memory_space=pltpu.VMEM),
         scratch_shapes=[
             pltpu.VMEM((rows, width), jnp.bfloat16),
             pltpu.VMEM((rows, width), jnp.bfloat16),
             pltpu.VMEM((rank_dim, width), jnp.bfloat16),
             pltpu.VMEM((rank_dim, width), jnp.bfloat16),
+            pltpu.SMEM((count,), jnp.int32),
             pltpu.SemaphoreType.DMA((4, chunks)),
+            pltpu.SemaphoreType.DMA,
         ],
+        compiler_params=pltpu.CompilerParams(vmem_limit_bytes=16 * 2**20),
     )(
-        activations.reshape(rows, width),
-        out_grads.reshape(rows, width),
-        project_in.T,
-        project_out.T,
-        lengths,
+        *(
+            pltpu.with_memory_space_constraint(operand, pltpu.HBM)
+            for operand in (
+                activations.reshape(rows, width),
+                out_grads.reshape(rows, width),
+                project_in.T,
+                project_out.T,
+                lengths,
+            )
+        ),
     )
 
 
@@ -140,7 +151,7 @@
     for q in range(nq):
         number = query_ref[q]
         slot = (number // per_dev) ^ me
-        place = ((slot % inner) * outer + slot // inner) * per_dev + number % per_dev
+        place = (gray(slot % inner) * outer + gray(slot // inner)) * per_dev + number % per_dev
         first = pl.multiple_of(place * SUBLANES, SUBLANES)
         extended[(examples + q) * SUBLANES : (examples + q + 1) * SUBLANES] = extended[pl.ds(first, SUBLANES)]
     extended[wide * SUBLANES :] = jnp.zeros((LANES * SUBLANES - wide * SUBLANES, LANES), jnp.float32)
@@ -170,12 +181,16 @@
     )(*tiles, query_index)
 
 
+def gray(n):
+    return n ^ (n >> 1)
+
+
 def gather_xor(tiles, axis, size, inner):
-    def swap(block, slot):
-        return lax.ppermute(block, axis, [(i, i ^ slot) for i in range(size)])
-
-    column = jnp.concatenate([tiles] + [swap(tiles, slot) for slot in range(inner, size, inner)], axis=0)
-    return [column] + [swap(column, slot) for slot in range(1, inner)]
+    def swap_all(block, unit, count):
+        order = sorted(range(1, count), key=gray)
+        return [block] + [lax.ppermute(block, axis, [(i, i ^ n * unit) for i in range(size)]) for n in order]
+
+    return swap_all(jnp.concatenate(swap_all(tiles, inner, size // inner), axis=0), 1, inner)
 
 
 def large_scores(tiles, query_index, per_dev, axis):

time: 27.3 us -> 24.9 us (0.912)
  Pallas kernels: 10.6 us -> 9.31 us
  other arithmetic: 0.72 us -> 0.01 us
  waiting for transfers between devices: 8.14 us -> 7.49 us
    pallas_call x1, Pallas kernels: 6.26 us -> 4.99 us  [sketch_rows(): pl.pallas_call(functools.partial(sketch_kernel, chunks, seq_len), out_sha...]
    concatenate x1, other arithmetic: 0.72 us -> 0.01 us  [gather_xor(): jnp.concatenate(swap_all(tiles, inner, size // inner), axis=0)]
    ppermute x6, waiting for transfers between devices: 8.14 us -> 7.49 us  [swap_all(): lax.ppermute(block, axis, [(i, i ^ n * unit) for i in range(size)])]
where the time goes in v8:
time: 24.9 us; the launch traced here: 24.7 us
  Pallas kernels  9.31 us (37%)
  starting transfers between devices  7.89 us (32%)
  waiting for transfers between devices  7.49 us (30%)
    ppermute x6, starting transfers between devices, swap_all(): lax.ppermute(block, axis, [(i, i ^ n * unit) for i in range(size)])  7.89 us
    ppermute x6, waiting for transfers between devices, swap_all(): lax.ppermute(block, axis, [(i, i ^ n * unit) for i in range(size)])  7.49 us
    pallas_call x1, Pallas kernels, sketch_rows(): pl.pallas_call(functools.partial(sketch_kernel, chunks, seq_len), out_sha...  4.99 us
    pallas_call x1, Pallas kernels, gram_scores(): pl.pallas_call(functools.partial(solve_kernel, nq, per_dev, inner, axis),...  4.32 us
  transfers between devices with their start and end apart: 6, of which 4 were waited for; matrix products, arithmetic and copies ran while one was open for 0% of the time, Pallas kernels for 0%

profile of v8, /device:TPU:0, one launch (start us, length us, event | category | flops | bytes accessed | tf_op | source)
XLA Modules:
  0.0 24.7 jit_solution(3285803896262127717)
XLA Ops:
  0.0 0.0 copy-start
  0.0 5.0 %shard_map.64 = f32[32,128]{1,0:T(8,128)S(1)} custom-call(bf16[256,8192]{1,0:T(8,128)(2,1)} %bitcast.4, bf16[256,8192]{1,0:T(8,128)(2,1)} %bitcast.5, bf16[32,8192]{1,0:T(8,128)(2,1)} %bitcast.6, bf16[32,8192]{1,0:T(8,128)(2,1)} %bitcast.7, s32[4]{0:T(128)} %lengths_hbm.1), custom_call_target="tpu_custom_call" | custom-call | tf_op jit(solution)/shard_map/pallas_call | solution.py:73
  5.0 4.1 %collective-permute-start.2 = (f32[32,128]{1,0:T(8,128)S(1)}, f32[32,128]{1,0:T(8,128)S(1)}, u32[]{:S(2)}, u32[]{:S(2)}) collective-permute-start(f32[32,128]{1,0:T(8,128)S(1)} %shard_map.64), channel_id=1, source_target_pairs={{0,8},{1,9},{2,10},{3,11},{4,12},{5,13},{6,14},{7,15},{8,0},{9,1},... | collective-permute-start | bytes 49160 | tf_op jit(solution)/shard_map/ppermute | solution.py:191
  9.1 1.3 %collective-permute-start.1 = (f32[32,128]{1,0:T(8,128)S(1)}, f32[32,128]{1,0:T(8,128)S(1)}, u32[]{:S(2)}, u32[]{:S(2)}) collective-permute-start(f32[32,128]{1,0:T(8,128)S(1)} %shard_map.64), channel_id=1, source_target_pairs={{0,12},{1,13},{2,14},{3,15},{4,8},{5,9},{6,10},{7,11},{8,4},{9,5},... | collective-permute-start | bytes 49160 | tf_op jit(solution)/shard_map/ppermute | solution.py:191
  10.5 0.2 collective-permute-start
  10.7 0.1 collective-permute-done.2
  10.8 3.8 %collective-permute-done.1 = f32[32,128]{1,0:T(8,128)S(1)} collective-permute-done((f32[32,128]{1,0:T(8,128)S(1)}, f32[32,128]{1,0:T(8,128)S(1)}, u32[]{:S(2)}, u32[]{:S(2)}) %collective-permute-start.1) | collective-permute-done | bytes 16416 | tf_op jit(solution)/shard_map/ppermute | solution.py:191
  14.6 0.0 collective-permute-done
  14.7 1.6 %collective-permute-start.5 = (f32[128,128]{1,0:T(8,128)S(1)}, f32[128,128]{1,0:T(8,128)S(1)}, u32[]{:S(2)}, u32[]{:S(2)}) collective-permute-start(f32[128,128]{1,0:T(8,128)S(1)} %pad_maximum_fusion.refs_0_), channel_id=1, source_target_pairs={{0,2},{1,3},{2,0},{3,1},{4,6},{5,7},{6,4},{7,5},{8,10},{9,11},{10,... | collective-permute-start | bytes 196616 | tf_op jit(solution)/shard_map/ppermute | solution.py:191
  16.2 0.0 collective-permute-start.4
  16.2 0.7 %collective-permute-start.3 = (f32[128,128]{1,0:T(8,128)S(1)}, f32[128,128]{1,0:T(8,128)S(1)}, u32[]{:S(2)}, u32[]{:S(2)}) collective-permute-start(f32[128,128]{1,0:T(8,128)S(1)} %pad_maximum_fusion.refs_0_), channel_id=1, source_target_pairs={{0,1},{1,0},{2,3},{3,2},{4,5},{5,4},{6,7},{7,6},{8,9},{9,8},{10,11... | collective-permute-start | bytes 196616 | tf_op jit(solution)/shard_map/ppermute | solution.py:191
  16.9 2.1 %collective-permute-done.5.refs_3_ = f32[128,128]{1,0:T(8,128)S(1)} collective-permute-done((f32[128,128]{1,0:T(8,128)S(1)}, f32[128,128]{1,0:T(8,128)S(1)}, u32[]{:S(2)}, u32[]{:S(2)}) %collective-permute-start.5) | collective-permute-done | bytes 65568 | tf_op jit(solution)/shard_map/ppermute | solution.py:191
  19.0 1.4 %collective-permute-done.4.refs_2_ = f32[128,128]{1,0:T(8,128)S(1)} collective-permute-done((f32[128,128]{1,0:T(8,128)S(1)}, f32[128,128]{1,0:T(8,128)S(1)}, u32[]{:S(2)}, u32[]{:S(2)}) %collective-permute-start.4) | collective-permute-done | bytes 65568 | tf_op jit(solution)/shard_map/ppermute | solution.py:191
  20.4 0.0 collective-permute-done.3.refs_1_
  20.4 0.0 copy-done
  20.4 4.3 %shard_map.65 = f32[4,16]{1,0:T(4,128)} custom-call(f32[128,128]{1,0:T(8,128)S(1)} %pad_maximum_fusion.refs_0_, f32[128,128]{1,0:T(8,128)S(1)} %collective-permute-done.3.refs_1_, f32[128,128]{1,0:T(8,128)S(1)} %collective-permute-done.4.refs_2_, f32[128,128]{1,0:T(8,128)S(1)} %collective-permute-done.5.refs_3_, s32[16]{0:T(128)S(1)} %copy-done), custom_call_target="tpu_custom_call" | custom-call | tf_op jit(solution)/shard_map/pallas_call | solution.py:174
  (1 shorter events, 0.0 us)
Async XLA Ops:
  0.0 20.4 %copy-start = (s32[16]{0:T(128)S(1)}, s32[16]{0:T(128)}, u32[]{:S(2)}) copy-start(s32[16]{0:T(128)} %refs_4_.1) | copy-start | bytes 196
  5.0 5.8 %collective-permute-start.2 = (f32[32,128]{1,0:T(8,128)S(1)}, f32[32,128]{1,0:T(8,128)S(1)}, u32[]{:S(2)}, u32[]{:S(2)}) collective-permute-start(f32[32,128]{1,0:T(8,128)S(1)} %shard_map.64), channel_id=1, source_target_pairs={{0,8},{1,9},{2,10},{3,11},{4,12},{5,13},{6,14},{7,15},{8,0},{9,1},... | collective-permute-start | bytes 49160 | tf_op jit(solution)/shard_map/ppermute | solution.py:191
  9.1 5.5 %collective-permute-start.1 = (f32[32,128]{1,0:T(8,128)S(1)}, f32[32,128]{1,0:T(8,128)S(1)}, u32[]{:S(2)}, u32[]{:S(2)}) collective-permute-start(f32[32,128]{1,0:T(8,128)S(1)} %shard_map.64), channel_id=1, source_target_pairs={{0,12},{1,13},{2,14},{3,15},{4,8},{5,9},{6,10},{7,11},{8,4},{9,5},... | collective-permute-start | bytes 49160 | tf_op jit(solution)/shard_map/ppermute | solution.py:191
  10.5 4.2 %collective-permute-start = (f32[32,128]{1,0:T(8,128)S(1)}, f32[32,128]{1,0:T(8,128)S(1)}, u32[]{:S(2)}, u32[]{:S(2)}) collective-permute-start(f32[32,128]{1,0:T(8,128)S(1)} %shard_map.64), channel_id=1, source_target_pairs={{0,4},{1,5},{2,6},{3,7},{4,0},{5,1},{6,2},{7,3},{8,12},{9,13},{10,... | collective-permute-start | bytes 49160 | tf_op jit(solution)/shard_map/ppermute | solution.py:191
  14.7 4.3 %collective-permute-start.5 = (f32[128,128]{1,0:T(8,128)S(1)}, f32[128,128]{1,0:T(8,128)S(1)}, u32[]{:S(2)}, u32[]{:S(2)}) collective-permute-start(f32[128,128]{1,0:T(8,128)S(1)} %pad_maximum_fusion.refs_0_), channel_id=1, source_target_pairs={{0,2},{1,3},{2,0},{3,1},{4,6},{5,7},{6,4},{7,5},{8,10},{9,11},{10,... | collective-permute-start | bytes 196616 | tf_op jit(solution)/shard_map/ppermute | solution.py:191
  16.2 4.2 %collective-permute-start.4 = (f32[128,128]{1,0:T(8,128)S(1)}, f32[128,128]{1,0:T(8,128)S(1)}, u32[]{:S(2)}, u32[]{:S(2)}) collective-permute-start(f32[128,128]{1,0:T(8,128)S(1)} %pad_maximum_fusion.refs_0_), channel_id=1, source_target_pairs={{0,3},{1,2},{2,1},{3,0},{4,7},{5,6},{6,5},{7,4},{8,11},{9,10},{10,... | collective-permute-start | bytes 196616 | tf_op jit(solution)/shard_map/ppermute | solution.py:191
  16.2 4.2 %collective-permute-start.3 = (f32[128,128]{1,0:T(8,128)S(1)}, f32[128,128]{1,0:T(8,128)S(1)}, u32[]{:S(2)}, u32[]{:S(2)}) collective-permute-start(f32[128,128]{1,0:T(8,128)S(1)} %pad_maximum_fusion.refs_0_), channel_id=1, source_target_pairs={{0,1},{1,0},{2,3},{3,2},{4,5},{5,4},{6,7},{7,6},{8,9},{9,8},{10,11... | collective-permute-start | bytes 196616 | tf_op jit(solution)/shard_map/ppermute | solution.py:191

commit v9 on v8

--- a/solution.py
+++ b/solution.py
@@ -99,86 +99,120 @@
     )
 
 
-def eliminate(system, count):
-    row = lax.broadcasted_iota(jnp.int32, (SUBLANES, system.shape[1]), 0)
-    shape = system.shape
-    for k in range(0, count, 4):
-        cols = [jnp.broadcast_to(system[:, k + j : k + j + 1], shape) for j in range(4)]
-        rows = [system[k + i : k + i + 1] for i in range(4)]
-        p = [[cols[j][k + i : k + i + 1] for j in range(4)] for i in range(4)]
-        scale = 1.0 / (p[0][0] * p[1][1] - p[0][1] * p[0][1])
-        a, b, c = p[1][1] * scale, -p[0][1] * scale, p[0][0] * scale
-        y = [
-            [a * p[0][2] + b * p[1][2], a * p[0][3] + b * p[1][3]],
-            [b * p[0][2] + c * p[1][2], b * p[0][3] + c * p[1][3]],
-        ]
-        s00 = p[2][2] - (p[0][2] * y[0][0] + p[1][2] * y[1][0])
-        s01 = p[2][3] - (p[0][2] * y[0][1] + p[1][2] * y[1][1])
-        s11 = p[3][3] - (p[0][3] * y[0][1] + p[1][3] * y[1][1])
-        scale = 1.0 / (s00 * s11 - s01 * s01)
-        d, e, f = s11 * scale, -s01 * scale, s00 * scale
-        z0 = a * rows[0] + b * rows[1]
-        z1 = b * rows[0] + c * rows[1]
-        t0 = rows[2] - (p[0][2] * z0 + p[1][2] * z1)
-        t1 = rows[3] - (p[0][3] * z0 + p[1][3] * z1)
-        w2 = d * t0 + e * t1
-        w3 = e * t0 + f * t1
-        w0 = z0 - (y[0][0] * w2 + y[0][1] * w3)
-        w1 = z1 - (y[1][0] * w2 + y[1][1] * w3)
-        done = [w0, w1, w2, w3]
-        parts = []
-        for r in range(0, count, SUBLANES):
-            own = slice(r, r + SUBLANES)
-            part = system[own] - (cols[0][own] * w0 + cols[1][own] * w1) - (cols[2][own] * w2 + cols[3][own] * w3)
-            if r <= k < r + SUBLANES:
-                for i in range(4):
-                    part = jnp.where(row == k - r + i, done[i], part)
-            parts.append(part)
-        system = jnp.concatenate(parts, axis=0)
+def reciprocal(x):
+    guess = pl.reciprocal(x, approx=True)
+    guess = guess * (2.0 - x * guess)
+    return guess * (2.0 - x * guess)
+
+
+def pivot_solver(p):
+    scale = reciprocal(p[0][0] * p[1][1] - p[0][1] * p[0][1])
+    a, b, c = p[1][1] * scale, p[0][1] * scale, p[0][0] * scale
+    y = [
+        [a * p[0][2] - b * p[1][2], a * p[0][3] - b * p[1][3]],
+        [c * p[1][2] - b * p[0][2], c * p[1][3] - b * p[0][3]],
+    ]
+    s00 = p[2][2] - (p[0][2] * y[0][0] + p[1][2] * y[1][0])
+    s01 = p[2][3] - (p[0][2] * y[0][1] + p[1][2] * y[1][1])
+    s11 = p[3][3] - (p[0][3] * y[0][1] + p[1][3] * y[1][1])
+    scale = reciprocal(s00 * s11 - s01 * s01)
+    d, e, f = s11 * scale, s01 * scale, s00 * scale
+
+    def solve(r):
+        z0 = a * r[0] - b * r[1]
+        z1 = c * r[1] - b * r[0]
+        t0 = r[2] - (y[0][0] * r[0] + y[1][0] * r[1])
+        t1 = r[3] - (y[0][1] * r[0] + y[1][1] * r[1])
+        w2 = d * t0 - e * t1
+        w3 = f * t1 - e * t0
+        return z0 - (y[0][0] * w2 + y[0][1] * w3), z1 - (y[1][0] * w2 + y[1][1] * w3), w2, w3
+
+    return solve
+
+
+def eliminate(system):
+    step = 4
+    count = len(system) * SUBLANES
+    row = lax.broadcasted_iota(jnp.int32, (SUBLANES, LANES), 0)
+
+    def spread(column):
+        return [jnp.broadcast_to(tile[:, column : column + 1], tile.shape) for tile in system]
+
+    def row_of(tiles, number):
+        tile = tiles[number // SUBLANES]
+        return jnp.broadcast_to(tile[number % SUBLANES : number % SUBLANES + 1], tile.shape)
+
+    def update(tiles, columns, done, first):
+        updated = []
+        for n, tile in enumerate(tiles):
+            tile = tile - (columns[0][n] * done[0] + columns[1][n] * done[1]) - (columns[2][n] * done[2] + columns[3][n] * done[3])
+            if n == first // SUBLANES:
+                for i in range(step):
+                    tile = jnp.where(row == first % SUBLANES + i, done[i], tile)
+            updated.append(tile)
+        return updated
+
+    columns = [spread(j) for j in range(step)]
+    for first in range(0, count, step):
+        pivots = range(first, first + step)
+        solve = pivot_solver([[row_of(column, i) for column in columns] for i in pivots])
+        following = []
+        if first + step < count:
+            for j in range(first + step, first + 2 * step):
+                column = spread(j)
+                following.append(update(column, columns, solve([row_of(column, i) for i in pivots]), first))
+        system = update(system, columns, solve([row_of(system, i) for i in pivots]), first)
+        columns = following
     return system
 
 
-def solve_kernel(nq, per_dev, inner, axis, *refs):
-    tiles, (query_ref, scores_ref, extended) = refs[:-3], refs[-3:]
-    block = tiles[0].shape[0]
-    examples = len(tiles) * block // SUBLANES
+def solve_kernel(per_dev, inner, axis, *refs):
+    tiles, (query_ref, scores_ref, gram_ref) = refs[:-3], refs[-3:]
+    nq = query_ref.shape[1]
+    part = tiles[0].shape[0] // SUBLANES
+    examples = len(tiles) * part
     outer = examples // (inner * per_dev)
-    wide = examples + nq
     fisher_dim = SUBLANES * LANES
-    me = lax.axis_index(axis)
-    for slot, tile in enumerate(tiles):
-        extended[slot * block : (slot + 1) * block] = tile[...]
-    for q in range(nq):
-        number = query_ref[q]
-        slot = (number // per_dev) ^ me
-        place = (gray(slot % inner) * outer + gray(slot // inner)) * per_dev + number % per_dev
-        first = pl.multiple_of(place * SUBLANES, SUBLANES)
-        extended[(examples + q) * SUBLANES : (examples + q + 1) * SUBLANES] = extended[pl.ds(first, SUBLANES)]
-    extended[wide * SUBLANES :] = jnp.zeros((LANES * SUBLANES - wide * SUBLANES, LANES), jnp.float32)
-    right = jnp.concatenate([extended[pl.ds(s, LANES, stride=SUBLANES)] for s in range(SUBLANES)], axis=1)
-    system = lax.dot_general(
-        right[:examples], right, NT, precision=lax.Precision.HIGHEST, preferred_element_type=jnp.float32
-    )
-    row = lax.broadcasted_iota(jnp.int32, system.shape, 0)
-    col = lax.broadcasted_iota(jnp.int32, system.shape, 1)
-    diagonal = row == col
-    trace = jnp.sum(jnp.where(diagonal, system, 0.0))
-    damping = damp_ratio * trace / fisher_dim
-    system = jnp.where(diagonal, system + damping, system)
-    system = eliminate(system, examples)
-    scores_ref[...] = system[:per_dev, examples : examples + nq]
+    gram_ref[...] = jnp.zeros(gram_ref.shape, jnp.float32)
+    slot = (query_ref[...] // per_dev) ^ lax.axis_index(axis)
+    place = (gray(slot % inner) * outer + gray(slot // inner)) * per_dev + query_ref[...] % per_dev
+    rest = LANES - examples - nq
+    place = jnp.concatenate(
+        [jnp.zeros((1, examples), jnp.int32), place] + ([jnp.zeros((1, rest), jnp.int32)] if rest else []), axis=1
+    )
+    lane = lax.broadcasted_iota(jnp.int32, (SUBLANES, LANES), 1)
+    source = jnp.where(lane < examples, lane, jnp.broadcast_to(place, lane.shape))
+    sketches = jnp.concatenate(
+        [
+            jnp.concatenate([tile[pl.ds(s, part, stride=SUBLANES)] for tile in tiles], axis=0)
+            for s in range(SUBLANES)
+        ],
+        axis=1,
+    )
+    squares = jnp.sum(jnp.sum(sketches * sketches, axis=0, keepdims=True), axis=1, keepdims=True)
+    scale = jnp.broadcast_to(1.0 / squares, (SUBLANES, LANES))
+    gram_ref[:, :examples] = lax.dot_general(
+        sketches, sketches, NT, precision=lax.Precision.HIGHEST, preferred_element_type=jnp.float32
+    )
+    row = lax.broadcasted_iota(jnp.int32, (SUBLANES, LANES), 0)
+    system = []
+    for first in range(0, examples, SUBLANES):
+        tile = jnp.take_along_axis(gram_ref[first : first + SUBLANES], source, axis=1) * scale
+        system.append(jnp.where(lane == row + first, tile + damp_ratio / fisher_dim, tile))
+    scores_ref[...] = eliminate(system)[0][:per_dev, examples : examples + nq]
 
 
 def gram_scores(tiles, query_index, per_dev, inner, axis):
     nq = query_index.shape[0]
+    examples = len(tiles) * tiles[0].shape[0] // SUBLANES
     return pl.pallas_call(
-        functools.partial(solve_kernel, nq, per_dev, inner, axis),
+        functools.partial(solve_kernel, per_dev, inner, axis),
         out_shape=jax.ShapeDtypeStruct((per_dev, nq), jnp.float32),
-        in_specs=[pl.BlockSpec(memory_space=pltpu.VMEM)] * len(tiles) + [pl.BlockSpec(memory_space=pltpu.SMEM)],
+        in_specs=[pl.BlockSpec(memory_space=pltpu.VMEM)] * (len(tiles) + 1),
         out_specs=pl.BlockSpec(memory_space=pltpu.VMEM),
-        scratch_shapes=[pltpu.VMEM((LANES * SUBLANES, LANES), jnp.float32)],
+        scratch_shapes=[pltpu.VMEM((examples, LANES), jnp.float32)],
         compiler_params=pltpu.CompilerParams(vmem_limit_bytes=8 * 2**20),
-    )(*tiles, query_index)
+    )(*tiles, query_index.reshape(1, nq))
 
 
 def gray(n):
@@ -186,11 +220,13 @@
 
 
 def gather_xor(tiles, axis, size, inner):
-    def swap_all(block, unit, count):
-        order = sorted(range(1, count), key=gray)
-        return [block] + [lax.ppermute(block, axis, [(i, i ^ n * unit) for i in range(size)]) for n in order]
-
-    return swap_all(jnp.concatenate(swap_all(tiles, inner, size // inner), axis=0), 1, inner)
+    def swap(block, slot):
+        return lax.ppermute(block, axis, [(i, i ^ slot) for i in range(size)])
+
+    order = sorted(range(1, size // inner), key=gray)
+    column = jnp.concatenate([tiles] + [swap(tiles, n * inner) for n in order], axis=0)
+    across = swap(column, 2)
+    return [column, swap(column, 1), swap(across, 1), across]
 
 
 def large_scores(tiles, query_index, per_dev, axis):

time: 24.9 us -> 23.5 us (0.944)
  Pallas kernels: 9.31 us -> 8.11 us
  starting transfers between devices: 7.89 us -> 7.24 us
  waiting for transfers between devices: 7.49 us -> 7.98 us
    pallas_call x1, Pallas kernels: 4.32 us -> 3.12 us  [gram_scores(): pl.pallas_call(functools.partial(solve_kernel, per_dev, inner, axis), out...]
    ppermute x6, starting transfers between devices: 7.89 us -> 7.24 us  [swap(): return lax.ppermute(block, axis, [(i, i ^ slot) for i in range(size)])]
    ppermute x6, waiting for transfers between devices: 7.49 us -> 7.98 us  [swap(): return lax.ppermute(block, axis, [(i, i ^ slot) for i in range(size)])]
where the time goes in v9:
time: 23.5 us; the launch traced here: 23.4 us
  Pallas kernels  8.11 us (35%)
  waiting for transfers between devices  7.98 us (34%)
  starting transfers between devices  7.24 us (31%)
    ppermute x6, waiting for transfers between devices, swap(): return lax.ppermute(block, axis, [(i, i ^ slot) for i in range(size)])  7.98 us
    ppermute x6, starting transfers between devices, swap(): return lax.ppermute(block, axis, [(i, i ^ slot) for i in range(size)])  7.24 us
    pallas_call x1, Pallas kernels, sketch_rows(): pl.pallas_call(functools.partial(sketch_kernel, chunks, seq_len), out_sha...  4.99 us
    pallas_call x1, Pallas kernels, gram_scores(): pl.pallas_call(functools.partial(solve_kernel, per_dev, inner, axis), out...  3.12 us
  transfers between devices with their start and end apart: 6, of which 4 were waited for; matrix products, arithmetic and copies ran while one was open for 0% of the time, Pallas kernels for 0%

profile of v9, /device:TPU:0, one launch (start us, length us, event | category | flops | bytes accessed | tf_op | source)
XLA Modules:
  0.0 23.4 jit_solution(4456730743329777752)
XLA Ops:
  0.0 0.0 copy-start
  0.0 5.0 %shard_map.64 = f32[32,128]{1,0:T(8,128)S(1)} custom-call(bf16[256,8192]{1,0:T(8,128)(2,1)} %bitcast.6, bf16[256,8192]{1,0:T(8,128)(2,1)} %bitcast.7, bf16[32,8192]{1,0:T(8,128)(2,1)} %bitcast.8, bf16[32,8192]{1,0:T(8,128)(2,1)} %bitcast.9, s32[4]{0:T(128)} %lengths_hbm.1), custom_call_target="tpu_custom_call" | custom-call | tf_op jit(solution)/shard_map/pallas_call | solution.py:73
  5.0 4.1 %collective-permute-start.2 = (f32[32,128]{1,0:T(8,128)S(1)}, f32[32,128]{1,0:T(8,128)S(1)}, u32[]{:S(2)}, u32[]{:S(2)}) collective-permute-start(f32[32,128]{1,0:T(8,128)S(1)} %shard_map.64), channel_id=1, source_target_pairs={{0,8},{1,9},{2,10},{3,11},{4,12},{5,13},{6,14},{7,15},{8,0},{9,1},... | collective-permute-start | bytes 49160 | tf_op jit(solution)/shard_map/ppermute | solution.py:224
  9.1 1.3 %collective-permute-start.1 = (f32[32,128]{1,0:T(8,128)S(1)}, f32[32,128]{1,0:T(8,128)S(1)}, u32[]{:S(2)}, u32[]{:S(2)}) collective-permute-start(f32[32,128]{1,0:T(8,128)S(1)} %shard_map.64), channel_id=1, source_target_pairs={{0,12},{1,13},{2,14},{3,15},{4,8},{5,9},{6,10},{7,11},{8,4},{9,5},... | collective-permute-start | bytes 49160 | tf_op jit(solution)/shard_map/ppermute | solution.py:224
  10.5 0.2 collective-permute-start
  10.7 0.1 collective-permute-done.2
  10.8 3.8 %collective-permute-done.1 = f32[32,128]{1,0:T(8,128)S(1)} collective-permute-done((f32[32,128]{1,0:T(8,128)S(1)}, f32[32,128]{1,0:T(8,128)S(1)}, u32[]{:S(2)}, u32[]{:S(2)}) %collective-permute-start.1) | collective-permute-done | bytes 16416 | tf_op jit(solution)/shard_map/ppermute | solution.py:224
  14.6 0.0 collective-permute-done
  14.7 1.6 %collective-permute-start.4 = (f32[128,128]{1,0:T(8,128)S(1)}, f32[128,128]{1,0:T(8,128)S(1)}, u32[]{:S(2)}, u32[]{:S(2)}) collective-permute-start(f32[128,128]{1,0:T(8,128)S(1)} %pad_maximum_fusion.refs_0_), channel_id=1, source_target_pairs={{0,2},{1,3},{2,0},{3,1},{4,6},{5,7},{6,4},{7,5},{8,10},{9,11},{10,... | collective-permute-start | bytes 196616 | tf_op jit(solution)/shard_map/ppermute | solution.py:224
  16.2 0.0 collective-permute-start.3
  16.2 2.8 %collective-permute-done.4.refs_3_ = f32[128,128]{1,0:T(8,128)S(1)} collective-permute-done((f32[128,128]{1,0:T(8,128)S(1)}, f32[128,128]{1,0:T(8,128)S(1)}, u32[]{:S(2)}, u32[]{:S(2)}) %collective-permute-start.4) | collective-permute-done | bytes 65568 | tf_op jit(solution)/shard_map/ppermute | solution.py:224
  19.0 0.0 collective-permute-start.5
  19.0 0.0 collective-permute-done.3.refs_1_
  19.0 1.2 %collective-permute-done.5.refs_2_ = f32[128,128]{1,0:T(8,128)S(1)} collective-permute-done((f32[128,128]{1,0:T(8,128)S(1)}, f32[128,128]{1,0:T(8,128)S(1)}, u32[]{:S(2)}, u32[]{:S(2)}) %collective-permute-start.5) | collective-permute-done | bytes 65568 | tf_op jit(solution)/shard_map/ppermute | solution.py:224
  20.2 0.0 copy-done
  20.2 3.1 %shard_map.65 = f32[4,16]{1,0:T(4,128)} custom-call(f32[128,128]{1,0:T(8,128)S(1)} %pad_maximum_fusion.refs_0_, f32[128,128]{1,0:T(8,128)S(1)} %collective-permute-done.3.refs_1_, f32[128,128]{1,0:T(8,128)S(1)} %collective-permute-done.5.refs_2_, f32[128,128]{1,0:T(8,128)S(1)} %collective-permute-done.4.refs_3_, s32[1,16]{1,0:T(1,128)S(1)} %bitcast.5), custom_call_target="tpu_custom_call" | custom-call | tf_op jit(solution)/shard_map/pallas_call | solution.py:208
  (1 shorter events, 0.0 us)
Async XLA Ops:
  0.0 20.2 %copy-start = (s32[16]{0:T(128)S(1)}, s32[16]{0:T(128)}, u32[]{:S(2)}) copy-start(s32[16]{0:T(128)} %param.11) | copy-start | bytes 196
  5.0 5.8 %collective-permute-start.2 = (f32[32,128]{1,0:T(8,128)S(1)}, f32[32,128]{1,0:T(8,128)S(1)}, u32[]{:S(2)}, u32[]{:S(2)}) collective-permute-start(f32[32,128]{1,0:T(8,128)S(1)} %shard_map.64), channel_id=1, source_target_pairs={{0,8},{1,9},{2,10},{3,11},{4,12},{5,13},{6,14},{7,15},{8,0},{9,1},... | collective-permute-start | bytes 49160 | tf_op jit(solution)/shard_map/ppermute | solution.py:224
  9.1 5.5 %collective-permute-start.1 = (f32[32,128]{1,0:T(8,128)S(1)}, f32[32,128]{1,0:T(8,128)S(1)}, u32[]{:S(2)}, u32[]{:S(2)}) collective-permute-start(f32[32,128]{1,0:T(8,128)S(1)} %shard_map.64), channel_id=1, source_target_pairs={{0,12},{1,13},{2,14},{3,15},{4,8},{5,9},{6,10},{7,11},{8,4},{9,5},... | collective-permute-start | bytes 49160 | tf_op jit(solution)/shard_map/ppermute | solution.py:224
  10.5 4.2 %collective-permute-start = (f32[32,128]{1,0:T(8,128)S(1)}, f32[32,128]{1,0:T(8,128)S(1)}, u32[]{:S(2)}, u32[]{:S(2)}) collective-permute-start(f32[32,128]{1,0:T(8,128)S(1)} %shard_map.64), channel_id=1, source_target_pairs={{0,4},{1,5},{2,6},{3,7},{4,0},{5,1},{6,2},{7,3},{8,12},{9,13},{10,... | collective-permute-start | bytes 49160 | tf_op jit(solution)/shard_map/ppermute | solution.py:224
  14.7 4.3 %collective-permute-start.4 = (f32[128,128]{1,0:T(8,128)S(1)}, f32[128,128]{1,0:T(8,128)S(1)}, u32[]{:S(2)}, u32[]{:S(2)}) collective-permute-start(f32[128,128]{1,0:T(8,128)S(1)} %pad_maximum_fusion.refs_0_), channel_id=1, source_target_pairs={{0,2},{1,3},{2,0},{3,1},{4,6},{5,7},{6,4},{7,5},{8,10},{9,11},{10,... | collective-permute-start | bytes 196616 | tf_op jit(solution)/shard_map/ppermute | solution.py:224
  16.2 2.8 %collective-permute-start.3 = (f32[128,128]{1,0:T(8,128)S(1)}, f32[128,128]{1,0:T(8,128)S(1)}, u32[]{:S(2)}, u32[]{:S(2)}) collective-permute-start(f32[128,128]{1,0:T(8,128)S(1)} %pad_maximum_fusion.refs_0_), channel_id=1, source_target_pairs={{0,1},{1,0},{2,3},{3,2},{4,5},{5,4},{6,7},{7,6},{8,9},{9,8},{10,11... | collective-permute-start | bytes 196616 | tf_op jit(solution)/shard_map/ppermute | solution.py:224
  19.0 1.3 %collective-permute-start.5 = (f32[128,128]{1,0:T(8,128)S(1)}, f32[128,128]{1,0:T(8,128)S(1)}, u32[]{:S(2)}, u32[]{:S(2)}) collective-permute-start(f32[128,128]{1,0:T(8,128)S(1)} %collective-permute-done.4.refs_3_), channel_id=1, source_target_pairs={{0,1},{1,0},{2,3},{3,2},{4,5},{5,4},{6,7},{7,6},{8,9},{9,8},{10,11... | collective-permute-start | bytes 196616 | tf_op jit(solution)/shard_map/ppermute | solution.py:224

commit v10 on v9

--- a/solution.py
+++ b/solution.py
@@ -13,42 +13,85 @@
 NT = (((1,), (1,)), ((), ()))
 
 
-def sketch_kernel(chunks, seq_len, act_hbm, out_hbm, pin_hbm, pout_hbm, lengths_hbm, sketch_ref, act, out, pin, pout, lengths_ref, sems, lengths_sem):
-    rows, width = act.shape
+def sketch_kernel(chunks, floor, act_hbm, out_hbm, pin_hbm, pout_hbm, lengths_hbm, sketch_ref, act, out, pin, pout, lengths_ref, sems, lengths_sem):
+    count, seq_len, width = act.shape
     rank_dim = pin.shape[0]
+    rows = count * seq_len
     step = width // chunks
     lengths_copy = pltpu.make_async_copy(lengths_hbm, lengths_ref, lengths_sem)
     lengths_copy.start()
-    copies = []
+
+    def tail(c, e, n):
+        src, dst = ((act_hbm, act), (out_hbm, out))[n]
+        part = (e, pl.ds(floor, seq_len - floor), pl.ds(c * step, step))
+        return pltpu.make_async_copy(src.at[part], dst.at[part], sems.at[c, 4 + 2 * e + n])
+
+    heads = []
     for c in range(chunks):
         cols = pl.ds(c * step, step)
-        copies.append(
+        head = (slice(None), pl.ds(0, floor), cols)
+        heads.append(
             [
-                pltpu.make_async_copy(src.at[:, cols], dst.at[:, cols], sems.at[n, c])
-                for n, (src, dst) in enumerate(
-                    ((pin_hbm, pin), (act_hbm, act), (pout_hbm, pout), (out_hbm, out))
+                pltpu.make_async_copy(src.at[part], dst.at[part], sems.at[c, n])
+                for n, (src, dst, part) in enumerate(
+                    (
+                        (pin_hbm, pin, (slice(None), cols)),
+                        (act_hbm, act, head),
+                        (pout_hbm, pout, (slice(None), cols)),
+                        (out_hbm, out, head),
+                    )
                 )
             ]
         )
-        for copy in copies[-1]:
+
+    def start_heads(c):
+        for copy in heads[c]:
             copy.start()
+
+    def start_tails(c):
+        for e in range(count):
+
+            @pl.when(lengths_ref[e] > floor)
+            def _():
+                tail(c, e, 0).start()
+                tail(c, e, 1).start()
+
+    for c in range(2):
+        start_heads(c)
+    lengths_copy.wait()
+    for c in range(chunks):
+        if c >= 2:
+            start_heads(c)
+        start_tails(c)
     feat = jnp.zeros((rows, rank_dim), jnp.float32)
     grad = jnp.zeros((rows, rank_dim), jnp.float32)
     for c in range(chunks):
         cols = slice(c * step, (c + 1) * step)
-        for copy in copies[c]:
+        for copy in heads[c]:
             copy.wait()
-        feat = feat + lax.dot_general(act[:, cols], pin[:, cols], NT, preferred_element_type=jnp.float32)
-        grad = grad + lax.dot_general(out[:, cols], pout[:, cols], NT, preferred_element_type=jnp.float32)
-    count = rows // seq_len
+        for e in range(count):
+
+            @pl.when(lengths_ref[e] > floor)
+            def _():
+                tail(c, e, 0).wait()
+                tail(c, e, 1).wait()
+
+        feat = feat + lax.dot_general(
+            act[:, :, cols].reshape(rows, step), pin[:, cols], NT, preferred_element_type=jnp.float32
+        )
+        grad = grad + lax.dot_general(
+            out[:, :, cols].reshape(rows, step), pout[:, cols], NT, preferred_element_type=jnp.float32
+        )
     reps = LANES // rank_dim
-    lengths_copy.wait()
     position = lax.broadcasted_iota(jnp.int32, (rows, rank_dim), 0)
     masked = []
+    live_any = jnp.zeros((rows, rank_dim), jnp.bool_)
     for e in range(count):
         first = e * seq_len
         live = (position >= first) & (position < first + lengths_ref[e])
         masked.append(jnp.where(live, grad, 0.0))
+        live_any = live_any | live
+    feat = jnp.where(live_any, feat, 0.0)
     outer = lax.dot_general(
         jnp.concatenate(masked, axis=1),
         jnp.concatenate([feat] * reps, axis=1),
@@ -68,34 +111,28 @@
 def sketch_rows(activations, out_grads, project_in, project_out, lengths):
     count, seq_len, width = activations.shape
     rank_dim = project_in.shape[1]
-    rows = count * seq_len
     chunks = 8
+    floor = 16
     return pl.pallas_call(
-        functools.partial(sketch_kernel, chunks, seq_len),
+        functools.partial(sketch_kernel, chunks, floor),
         out_shape=jax.ShapeDtypeStruct((count * SUBLANES, LANES), jnp.float32),
         in_specs=[pl.BlockSpec(memory_space=pltpu.HBM)] * 5,
         out_specs=pl.BlockSpec(memory_space=pltpu.VMEM),
         scratch_shapes=[
-            pltpu.VMEM((rows, width), jnp.bfloat16),
-            pltpu.VMEM((rows, width), jnp.bfloat16),
+            pltpu.VMEM((count, seq_len, width), jnp.bfloat16),
+            pltpu.VMEM((count, seq_len, width), jnp.bfloat16),
             pltpu.VMEM((rank_dim, width), jnp.bfloat16),
             pltpu.VMEM((rank_dim, width), jnp.bfloat16),
             pltpu.SMEM((count,), jnp.int32),
-            pltpu.SemaphoreType.DMA((4, chunks)),
+            pltpu.SemaphoreType.DMA((chunks, 4 + 2 * count)),
             pltpu.SemaphoreType.DMA,
         ],
         compiler_params=pltpu.CompilerParams(vmem_limit_bytes=16 * 2**20),
     )(
         *(
             pltpu.with_memory_space_constraint(operand, pltpu.HBM)
-            for operand in (
-                activations.reshape(rows, width),
-                out_grads.reshape(rows, width),
-                project_in.T,
-                project_out.T,
-                lengths,
-            )
-        ),
+            for operand in (activations, out_grads, project_in.T, project_out.T, lengths)
+        )
     )
 
 
@@ -130,10 +167,8 @@
     return solve
 
 
-def eliminate(system):
+def solve_first(system):
     step = 4
-    count = len(system) * SUBLANES
-    row = lax.broadcasted_iota(jnp.int32, (SUBLANES, LANES), 0)
 
     def spread(column):
         return [jnp.broadcast_to(tile[:, column : column + 1], tile.shape) for tile in system]
@@ -142,28 +177,28 @@
         tile = tiles[number // SUBLANES]
         return jnp.broadcast_to(tile[number % SUBLANES : number % SUBLANES + 1], tile.shape)
 
-    def update(tiles, columns, done, first):
-        updated = []
-        for n, tile in enumerate(tiles):
-            tile = tile - (columns[0][n] * done[0] + columns[1][n] * done[1]) - (columns[2][n] * done[2] + columns[3][n] * done[3])
-            if n == first // SUBLANES:
-                for i in range(step):
-                    tile = jnp.where(row == first % SUBLANES + i, done[i], tile)
-            updated.append(tile)
-        return updated
-
-    columns = [spread(j) for j in range(step)]
-    for first in range(0, count, step):
+    def update(tiles, columns, done):
+        return [
+            tile - (c0 * done[0] + c1 * done[1]) - (c2 * done[2] + c3 * done[3])
+            for tile, c0, c1, c2, c3 in zip(tiles, *columns)
+        ]
+
+    count = len(system) * SUBLANES
+    columns = [spread(j) for j in range(count - step, count)]
+    for first in range(count - step, 0, -step):
         pivots = range(first, first + step)
+        left = pl.cdiv(first, SUBLANES)
         solve = pivot_solver([[row_of(column, i) for column in columns] for i in pivots])
         following = []
-        if first + step < count:
-            for j in range(first + step, first + 2 * step):
-                column = spread(j)
-                following.append(update(column, columns, solve([row_of(column, i) for i in pivots]), first))
-        system = update(system, columns, solve([row_of(system, i) for i in pivots]), first)
+        for j in range(first - step, first):
+            column = spread(j)
+            done = solve([row_of(column, i) for i in pivots])
+            following.append(update(column[:left], [c[:left] for c in columns], done))
+        done = solve([row_of(system, i) for i in pivots])
+        system = update(system[:left], [c[:left] for c in columns], done)
         columns = following
-    return system
+    solve = pivot_solver([[row_of(column, i) for column in columns] for i in range(step)])
+    return solve([row_of(system, i) for i in range(step)])
 
 
 def solve_kernel(per_dev, inner, axis, *refs):
@@ -199,7 +234,11 @@
     for first in range(0, examples, SUBLANES):
         tile = jnp.take_along_axis(gram_ref[first : first + SUBLANES], source, axis=1) * scale
         system.append(jnp.where(lane == row + first, tile + damp_ratio / fisher_dim, tile))
-    scores_ref[...] = eliminate(system)[0][:per_dev, examples : examples + nq]
+    solved = solve_first(system)
+    scores = solved[0]
+    for i in range(1, len(solved)):
+        scores = jnp.where(row == i, solved[i], scores)
+    scores_ref[...] = scores[:per_dev, examples : examples + nq]
 
 
 def gram_scores(tiles, query_index, per_dev, inner, axis):
@@ -220,13 +259,11 @@
 
 
 def gather_xor(tiles, axis, size, inner):
-    def swap(block, slot):
-        return lax.ppermute(block, axis, [(i, i ^ slot) for i in range(size)])
-
-    order = sorted(range(1, size // inner), key=gray)
-    column = jnp.concatenate([tiles] + [swap(tiles, n * inner) for n in order], axis=0)
-    across = swap(column, 2)
-    return [column, swap(column, 1), swap(across, 1), across]
+    def swap_all(block, unit, count):
+        order = sorted(range(1, count), key=gray)
+        return [block] + [lax.ppermute(block, axis, [(i, i ^ n * unit) for i in range(size)]) for n in order]
+
+    return swap_all(jnp.concatenate(swap_all(tiles, inner, size // inner), axis=0), 1, inner)
 
 
 def large_scores(tiles, query_index, per_dev, axis):

time: 23.5 us -> 24.6 us (1.047)
  Pallas kernels: 8.11 us -> 9.08 us
  starting transfers between devices: 7.24 us -> 7.89 us
  waiting for transfers between devices: 7.98 us -> 7.49 us
    pallas_call x1, Pallas kernels: 4.99 us -> 6 us  [sketch_rows(): pl.pallas_call(functools.partial(sketch_kernel, chunks, floor), out_shape...]
    ppermute x6, starting transfers between devices: 7.24 us -> 7.89 us  [swap_all(): lax.ppermute(block, axis, [(i, i ^ n * unit) for i in range(size)])]
    ppermute x6, waiting for transfers between devices: 7.98 us -> 7.49 us  [swap_all(): lax.ppermute(block, axis, [(i, i ^ n * unit) for i in range(size)])]
where the time goes in v10:
time: 24.6 us; the launch traced here: 24.5 us
  Pallas kernels  9.08 us (37%)
  starting transfers between devices  7.89 us (32%)
  waiting for transfers between devices  7.49 us (30%)
    ppermute x6, starting transfers between devices, swap_all(): lax.ppermute(block, axis, [(i, i ^ n * unit) for i in range(size)])  7.89 us
    ppermute x6, waiting for transfers between devices, swap_all(): lax.ppermute(block, axis, [(i, i ^ n * unit) for i in range(size)])  7.49 us
    pallas_call x1, Pallas kernels, sketch_rows(): pl.pallas_call(functools.partial(sketch_kernel, chunks, floor), out_shape...  6 us
    pallas_call x1, Pallas kernels, gram_scores(): pl.pallas_call(functools.partial(solve_kernel, per_dev, inner, axis), out...  3.08 us
  transfers between devices with their start and end apart: 6, of which 4 were waited for; matrix products, arithmetic and copies ran while one was open for 0% of the time, Pallas kernels for 0%

profile of v10, /device:TPU:0, one launch (start us, length us, event | category | flops | bytes accessed | tf_op | source)
XLA Modules:
  0.0 24.5 jit_solution(6390039048609942173)
XLA Ops:
  0.0 0.0 copy-start
  0.0 6.0 %shard_map.64 = f32[32,128]{1,0:T(8,128)S(1)} custom-call(bf16[4,64,8192]{2,1,0:T(8,128)(2,1)} %act_hbm.1, bf16[4,64,8192]{2,1,0:T(8,128)(2,1)} %out_hbm.1, bf16[32,8192]{1,0:T(8,128)(2,1)} %bitcast.4, bf16[32,8192]{1,0:T(8,128)(2,1)} %bitcast.5, s32[4]{0:T(128)} %lengths_hbm.1), custom_call_target="tpu_custom_call" | custom-call | tf_op jit(solution)/shard_map/pallas_call | solution.py:116
  6.0 4.1 %collective-permute-start.2 = (f32[32,128]{1,0:T(8,128)S(1)}, f32[32,128]{1,0:T(8,128)S(1)}, u32[]{:S(2)}, u32[]{:S(2)}) collective-permute-start(f32[32,128]{1,0:T(8,128)S(1)} %shard_map.64), channel_id=1, source_target_pairs={{0,8},{1,9},{2,10},{3,11},{4,12},{5,13},{6,14},{7,15},{8,0},{9,1},... | collective-permute-start | bytes 49160 | tf_op jit(solution)/shard_map/ppermute | solution.py:264
  10.1 1.2 %collective-permute-start.1 = (f32[32,128]{1,0:T(8,128)S(1)}, f32[32,128]{1,0:T(8,128)S(1)}, u32[]{:S(2)}, u32[]{:S(2)}) collective-permute-start(f32[32,128]{1,0:T(8,128)S(1)} %shard_map.64), channel_id=1, source_target_pairs={{0,12},{1,13},{2,14},{3,15},{4,8},{5,9},{6,10},{7,11},{8,4},{9,5},... | collective-permute-start | bytes 49160 | tf_op jit(solution)/shard_map/ppermute | solution.py:264
  11.3 0.4 %collective-permute-start = (f32[32,128]{1,0:T(8,128)S(1)}, f32[32,128]{1,0:T(8,128)S(1)}, u32[]{:S(2)}, u32[]{:S(2)}) collective-permute-start(f32[32,128]{1,0:T(8,128)S(1)} %shard_map.64), channel_id=1, source_target_pairs={{0,4},{1,5},{2,6},{3,7},{4,0},{5,1},{6,2},{7,3},{8,12},{9,13},{10,... | collective-permute-start | bytes 49160 | tf_op jit(solution)/shard_map/ppermute | solution.py:264
  11.7 0.1 collective-permute-done.2
  11.8 3.8 %collective-permute-done.1 = f32[32,128]{1,0:T(8,128)S(1)} collective-permute-done((f32[32,128]{1,0:T(8,128)S(1)}, f32[32,128]{1,0:T(8,128)S(1)}, u32[]{:S(2)}, u32[]{:S(2)}) %collective-permute-start.1) | collective-permute-done | bytes 16416 | tf_op jit(solution)/shard_map/ppermute | solution.py:264
  15.7 0.0 collective-permute-done
  15.7 1.4 %collective-permute-start.5 = (f32[128,128]{1,0:T(8,128)S(1)}, f32[128,128]{1,0:T(8,128)S(1)}, u32[]{:S(2)}, u32[]{:S(2)}) collective-permute-start(f32[128,128]{1,0:T(8,128)S(1)} %pad_maximum_fusion.refs_0_), channel_id=1, source_target_pairs={{0,2},{1,3},{2,0},{3,1},{4,6},{5,7},{6,4},{7,5},{8,10},{9,11},{10,... | collective-permute-start | bytes 196616 | tf_op jit(solution)/shard_map/ppermute | solution.py:264
  17.1 0.0 collective-permute-start.4
  17.1 0.8 %collective-permute-start.3 = (f32[128,128]{1,0:T(8,128)S(1)}, f32[128,128]{1,0:T(8,128)S(1)}, u32[]{:S(2)}, u32[]{:S(2)}) collective-permute-start(f32[128,128]{1,0:T(8,128)S(1)} %pad_maximum_fusion.refs_0_), channel_id=1, source_target_pairs={{0,1},{1,0},{2,3},{3,2},{4,5},{5,4},{6,7},{7,6},{8,9},{9,8},{10,11... | collective-permute-start | bytes 196616 | tf_op jit(solution)/shard_map/ppermute | solution.py:264
  17.9 2.1 %collective-permute-done.5.refs_3_ = f32[128,128]{1,0:T(8,128)S(1)} collective-permute-done((f32[128,128]{1,0:T(8,128)S(1)}, f32[128,128]{1,0:T(8,128)S(1)}, u32[]{:S(2)}, u32[]{:S(2)}) %collective-permute-start.5) | collective-permute-done | bytes 65568 | tf_op jit(solution)/shard_map/ppermute | solution.py:264
  20.0 1.4 %collective-permute-done.4.refs_2_ = f32[128,128]{1,0:T(8,128)S(1)} collective-permute-done((f32[128,128]{1,0:T(8,128)S(1)}, f32[128,128]{1,0:T(8,128)S(1)}, u32[]{:S(2)}, u32[]{:S(2)}) %collective-permute-start.4) | collective-permute-done | bytes 65568 | tf_op jit(solution)/shard_map/ppermute | solution.py:264
  21.4 0.0 collective-permute-done.3.refs_1_
  21.4 0.0 copy-done
  21.4 3.1 %shard_map.65 = f32[4,16]{1,0:T(4,128)} custom-call(f32[128,128]{1,0:T(8,128)S(1)} %pad_maximum_fusion.refs_0_, f32[128,128]{1,0:T(8,128)S(1)} %collective-permute-done.3.refs_1_, f32[128,128]{1,0:T(8,128)S(1)} %collective-permute-done.4.refs_2_, f32[128,128]{1,0:T(8,128)S(1)} %collective-permute-done.5.refs_3_, s32[1,16]{1,0:T(1,128)S(1)} %bitcast.3), custom_call_target="tpu_custom_call" | custom-call | tf_op jit(solution)/shard_map/pallas_call | solution.py:247
  (1 shorter events, 0.0 us)
Async XLA Ops:
  0.0 21.4 %copy-start = (s32[16]{0:T(128)S(1)}, s32[16]{0:T(128)}, u32[]{:S(2)}) copy-start(s32[16]{0:T(128)} %param.11) | copy-start | bytes 196
  6.0 5.8 %collective-permute-start.2 = (f32[32,128]{1,0:T(8,128)S(1)}, f32[32,128]{1,0:T(8,128)S(1)}, u32[]{:S(2)}, u32[]{:S(2)}) collective-permute-start(f32[32,128]{1,0:T(8,128)S(1)} %shard_map.64), channel_id=1, source_target_pairs={{0,8},{1,9},{2,10},{3,11},{4,12},{5,13},{6,14},{7,15},{8,0},{9,1},... | collective-permute-start | bytes 49160 | tf_op jit(solution)/shard_map/ppermute | solution.py:264
  10.1 5.5 %collective-permute-start.1 = (f32[32,128]{1,0:T(8,128)S(1)}, f32[32,128]{1,0:T(8,128)S(1)}, u32[]{:S(2)}, u32[]{:S(2)}) collective-permute-start(f32[32,128]{1,0:T(8,128)S(1)} %shard_map.64), channel_id=1, source_target_pairs={{0,12},{1,13},{2,14},{3,15},{4,8},{5,9},{6,10},{7,11},{8,4},{9,5},... | collective-permute-start | bytes 49160 | tf_op jit(solution)/shard_map/ppermute | solution.py:264
  11.3 4.3 %collective-permute-start = (f32[32,128]{1,0:T(8,128)S(1)}, f32[32,128]{1,0:T(8,128)S(1)}, u32[]{:S(2)}, u32[]{:S(2)}) collective-permute-start(f32[32,128]{1,0:T(8,128)S(1)} %shard_map.64), channel_id=1, source_target_pairs={{0,4},{1,5},{2,6},{3,7},{4,0},{5,1},{6,2},{7,3},{8,12},{9,13},{10,... | collective-permute-start | bytes 49160 | tf_op jit(solution)/shard_map/ppermute | solution.py:264
  15.7 4.3 %collective-permute-start.5 = (f32[128,128]{1,0:T(8,128)S(1)}, f32[128,128]{1,0:T(8,128)S(1)}, u32[]{:S(2)}, u32[]{:S(2)}) collective-permute-start(f32[128,128]{1,0:T(8,128)S(1)} %pad_maximum_fusion.refs_0_), channel_id=1, source_target_pairs={{0,2},{1,3},{2,0},{3,1},{4,6},{5,7},{6,4},{7,5},{8,10},{9,11},{10,... | collective-permute-start | bytes 196616 | tf_op jit(solution)/shard_map/ppermute | solution.py:264
  17.1 4.3 %collective-permute-start.4 = (f32[128,128]{1,0:T(8,128)S(1)}, f32[128,128]{1,0:T(8,128)S(1)}, u32[]{:S(2)}, u32[]{:S(2)}) collective-permute-start(f32[128,128]{1,0:T(8,128)S(1)} %pad_maximum_fusion.refs_0_), channel_id=1, source_target_pairs={{0,3},{1,2},{2,1},{3,0},{4,7},{5,6},{6,5},{7,4},{8,11},{9,10},{10,... | collective-permute-start | bytes 196616 | tf_op jit(solution)/shard_map/ppermute | solution.py:264
  17.1 4.3 %collective-permute-start.3 = (f32[128,128]{1,0:T(8,128)S(1)}, f32[128,128]{1,0:T(8,128)S(1)}, u32[]{:S(2)}, u32[]{:S(2)}) collective-permute-start(f32[128,128]{1,0:T(8,128)S(1)} %pad_maximum_fusion.refs_0_), channel_id=1, source_target_pairs={{0,1},{1,0},{2,3},{3,2},{4,5},{5,4},{6,7},{7,6},{8,9},{9,8},{10,11... | collective-permute-start | bytes 196616 | tf_op jit(solution)/shard_map/ppermute | solution.py:264

commit v11 on v10

--- a/solution.py
+++ b/solution.py
@@ -13,22 +13,23 @@
 NT = (((1,), (1,)), ((), ()))
 
 
-def sketch_kernel(chunks, floor, act_hbm, out_hbm, pin_hbm, pout_hbm, lengths_hbm, sketch_ref, act, out, pin, pout, lengths_ref, sems, lengths_sem):
+def sketch_kernel(bounds, floor, act_hbm, out_hbm, pin_hbm, pout_hbm, lengths_hbm, sketch_ref, act, out, pin, pout, lengths_ref, sems, lengths_sem):
     count, seq_len, width = act.shape
     rank_dim = pin.shape[0]
     rows = count * seq_len
-    step = width // chunks
+    chunks = len(bounds) - 1
+    columns = [pl.ds(a, b - a) for a, b in zip(bounds, bounds[1:])]
     lengths_copy = pltpu.make_async_copy(lengths_hbm, lengths_ref, lengths_sem)
     lengths_copy.start()
 
     def tail(c, e, n):
         src, dst = ((act_hbm, act), (out_hbm, out))[n]
-        part = (e, pl.ds(floor, seq_len - floor), pl.ds(c * step, step))
+        part = (e, pl.ds(floor, seq_len - floor), columns[c])
         return pltpu.make_async_copy(src.at[part], dst.at[part], sems.at[c, 4 + 2 * e + n])
 
     heads = []
     for c in range(chunks):
-        cols = pl.ds(c * step, step)
+        cols = columns[c]
         head = (slice(None), pl.ds(0, floor), cols)
         heads.append(
             [
@@ -44,11 +45,11 @@
             ]
         )
 
-    def start_heads(c):
+    for c in range(chunks):
         for copy in heads[c]:
             copy.start()
-
-    def start_tails(c):
+    lengths_copy.wait()
+    for c in range(chunks):
         for e in range(count):
 
             @pl.when(lengths_ref[e] > floor)
@@ -56,17 +57,11 @@
                 tail(c, e, 0).start()
                 tail(c, e, 1).start()
 
-    for c in range(2):
-        start_heads(c)
-    lengths_copy.wait()
-    for c in range(chunks):
-        if c >= 2:
-            start_heads(c)
-        start_tails(c)
     feat = jnp.zeros((rows, rank_dim), jnp.float32)
     grad = jnp.zeros((rows, rank_dim), jnp.float32)
     for c in range(chunks):
-        cols = slice(c * step, (c + 1) * step)
+        cols = slice(bounds[c], bounds[c + 1])
+        step = bounds[c + 1] - bounds[c]
         for copy in heads[c]:
             copy.wait()
         for e in range(count):
@@ -111,10 +106,12 @@
 def sketch_rows(activations, out_grads, project_in, project_out, lengths):
     count, seq_len, width = activations.shape
     rank_dim = project_in.shape[1]
-    chunks = 8
+    unit = width // 16
+    bounds = (0, 5 * unit, 10 * unit, 14 * unit, width)
+    chunks = len(bounds) - 1
     floor = 16
     return pl.pallas_call(
-        functools.partial(sketch_kernel, chunks, floor),
+        functools.partial(sketch_kernel, bounds, floor),
         out_shape=jax.ShapeDtypeStruct((count * SUBLANES, LANES), jnp.float32),
         in_specs=[pl.BlockSpec(memory_space=pltpu.HBM)] * 5,
         out_specs=pl.BlockSpec(memory_space=pltpu.VMEM),
@@ -136,37 +133,6 @@
     )
 
 
-def reciprocal(x):
-    guess = pl.reciprocal(x, approx=True)
-    guess = guess * (2.0 - x * guess)
-    return guess * (2.0 - x * guess)
-
-
-def pivot_solver(p):
-    scale = reciprocal(p[0][0] * p[1][1] - p[0][1] * p[0][1])
-    a, b, c = p[1][1] * scale, p[0][1] * scale, p[0][0] * scale
-    y = [
-        [a * p[0][2] - b * p[1][2], a * p[0][3] - b * p[1][3]],
-        [c * p[1][2] - b * p[0][2], c * p[1][3] - b * p[0][3]],
-    ]
-    s00 = p[2][2] - (p[0][2] * y[0][0] + p[1][2] * y[1][0])
-    s01 = p[2][3] - (p[0][2] * y[0][1] + p[1][2] * y[1][1])
-    s11 = p[3][3] - (p[0][3] * y[0][1] + p[1][3] * y[1][1])
-    scale = reciprocal(s00 * s11 - s01 * s01)
-    d, e, f = s11 * scale, s01 * scale, s00 * scale
-
-    def solve(r):
-        z0 = a * r[0] - b * r[1]
-        z1 = c * r[1] - b * r[0]
-        t0 = r[2] - (y[0][0] * r[0] + y[1][0] * r[1])
-        t1 = r[3] - (y[0][1] * r[0] + y[1][1] * r[1])
-        w2 = d * t0 - e * t1
-        w3 = f * t1 - e * t0
-        return z0 - (y[0][0] * w2 + y[0][1] * w3), z1 - (y[1][0] * w2 + y[1][1] * w3), w2, w3
-
-    return solve
-
-
 def solve_first(system):
     step = 4
 
@@ -177,28 +143,52 @@
         tile = tiles[number // SUBLANES]
         return jnp.broadcast_to(tile[number % SUBLANES : number % SUBLANES + 1], tile.shape)
 
-    def update(tiles, columns, done):
-        return [
-            tile - (c0 * done[0] + c1 * done[1]) - (c2 * done[2] + c3 * done[3])
-            for tile, c0, c1, c2, c3 in zip(tiles, *columns)
-        ]
+    def factor(columns, first):
+        p = {(i, j): row_of(columns[j], first + i) for j in range(step) for i in range(j + 1)}
+        lower, inverse = {}, []
+        for k in range(step):
+            inverse.append(pl.reciprocal(p[k, k]))
+            for i in range(k + 1, step):
+                lower[i, k] = p[k, i] * inverse[k]
+            for i in range(k + 1, step):
+                for j in range(i, step):
+                    p[i, j] = p[i, j] - lower[i, k] * p[k, j]
+        return lower, inverse
+
+    def forward(lower, parts):
+        parts = list(parts)
+        for k in range(step):
+            for i in range(k + 1, step):
+                parts[i] = [part - lower[i, k] * other for part, other in zip(parts[i], parts[k])]
+        return parts
+
+    def update(tiles, columns, lower, inverse, rows):
+        rows = forward(lower, [[r] for r in rows])
+        for column, row, scale in zip(columns, rows, inverse):
+            done = row[0] * scale
+            tiles = [tile - c * done for tile, c in zip(tiles, column)]
+        return tiles
 
     count = len(system) * SUBLANES
     columns = [spread(j) for j in range(count - step, count)]
     for first in range(count - step, 0, -step):
         pivots = range(first, first + step)
         left = pl.cdiv(first, SUBLANES)
-        solve = pivot_solver([[row_of(column, i) for column in columns] for i in pivots])
+        lower, inverse = factor(columns, first)
+        columns = forward(lower, [c[:left] for c in columns])
         following = []
         for j in range(first - step, first):
             column = spread(j)
-            done = solve([row_of(column, i) for i in pivots])
-            following.append(update(column[:left], [c[:left] for c in columns], done))
-        done = solve([row_of(system, i) for i in pivots])
-        system = update(system[:left], [c[:left] for c in columns], done)
+            following.append(update(column[:left], columns, lower, inverse, [row_of(column, i) for i in pivots]))
+        system = update(system[:left], columns, lower, inverse, [row_of(system, i) for i in pivots])
         columns = following
-    solve = pivot_solver([[row_of(column, i) for column in columns] for i in range(step)])
-    return solve([row_of(system, i) for i in range(step)])
+    lower, inverse = factor(columns, 0)
+    rows = forward(lower, [[row_of(system, i)] for i in range(step)])
+    solved = [row[0] * scale for row, scale in zip(rows, inverse)]
+    for k in reversed(range(step)):
+        for i in range(k):
+            solved[i] = solved[i] - lower[k, i] * solved[k]
+    return solved
 
 
 def solve_kernel(per_dev, inner, axis, *refs):

time: 24.6 us -> 24.5 us (level)
  no operation moved by 1% of the time
where the time goes in v11:
time: 24.5 us; the launch traced here: 24.4 us
  Pallas kernels  9.1 us (37%)
  starting transfers between devices  7.88 us (32%)
  waiting for transfers between devices  7.38 us (30%)
    ppermute x6, starting transfers between devices, swap_all(): lax.ppermute(block, axis, [(i, i ^ n * unit) for i in range(size)])  7.88 us
    ppermute x6, waiting for transfers between devices, swap_all(): lax.ppermute(block, axis, [(i, i ^ n * unit) for i in range(size)])  7.38 us
    pallas_call x1, Pallas kernels, sketch_rows(): pl.pallas_call(functools.partial(sketch_kernel, bounds, floor), out_shape...  6.24 us
    pallas_call x1, Pallas kernels, gram_scores(): pl.pallas_call(functools.partial(solve_kernel, per_dev, inner, axis), out...  2.87 us
  transfers between devices with their start and end apart: 6, of which 4 were waited for; matrix products, arithmetic and copies ran while one was open for 0% of the time, Pallas kernels for 0%

profile of v11, /device:TPU:0, one launch (start us, length us, event | category | flops | bytes accessed | tf_op | source)
XLA Modules:
  0.0 24.4 jit_solution(14396212909174527252)
XLA Ops:
  0.0 0.0 copy-start
  0.0 6.2 %shard_map.64 = f32[32,128]{1,0:T(8,128)S(1)} custom-call(bf16[4,64,8192]{2,1,0:T(8,128)(2,1)} %act_hbm.1, bf16[4,64,8192]{2,1,0:T(8,128)(2,1)} %out_hbm.1, bf16[32,8192]{1,0:T(8,128)(2,1)} %bitcast.4, bf16[32,8192]{1,0:T(8,128)(2,1)} %bitcast.5, s32[4]{0:T(128)} %lengths_hbm.1), custom_call_target="tpu_custom_call" | custom-call | tf_op jit(solution)/shard_map/pallas_call | solution.py:113
  6.2 4.1 %collective-permute-start.2 = (f32[32,128]{1,0:T(8,128)S(1)}, f32[32,128]{1,0:T(8,128)S(1)}, u32[]{:S(2)}, u32[]{:S(2)}) collective-permute-start(f32[32,128]{1,0:T(8,128)S(1)} %shard_map.64), channel_id=1, source_target_pairs={{0,8},{1,9},{2,10},{3,11},{4,12},{5,13},{6,14},{7,15},{8,0},{9,1},... | collective-permute-start | bytes 49160 | tf_op jit(solution)/shard_map/ppermute | solution.py:254
  10.3 1.1 %collective-permute-start.1 = (f32[32,128]{1,0:T(8,128)S(1)}, f32[32,128]{1,0:T(8,128)S(1)}, u32[]{:S(2)}, u32[]{:S(2)}) collective-permute-start(f32[32,128]{1,0:T(8,128)S(1)} %shard_map.64), channel_id=1, source_target_pairs={{0,12},{1,13},{2,14},{3,15},{4,8},{5,9},{6,10},{7,11},{8,4},{9,5},... | collective-permute-start | bytes 49160 | tf_op jit(solution)/shard_map/ppermute | solution.py:254
  11.4 0.5 %collective-permute-start = (f32[32,128]{1,0:T(8,128)S(1)}, f32[32,128]{1,0:T(8,128)S(1)}, u32[]{:S(2)}, u32[]{:S(2)}) collective-permute-start(f32[32,128]{1,0:T(8,128)S(1)} %shard_map.64), channel_id=1, source_target_pairs={{0,4},{1,5},{2,6},{3,7},{4,0},{5,1},{6,2},{7,3},{8,12},{9,13},{10,... | collective-permute-start | bytes 49160 | tf_op jit(solution)/shard_map/ppermute | solution.py:254
  11.9 0.1 collective-permute-done.2
  12.1 3.8 %collective-permute-done.1 = f32[32,128]{1,0:T(8,128)S(1)} collective-permute-done((f32[32,128]{1,0:T(8,128)S(1)}, f32[32,128]{1,0:T(8,128)S(1)}, u32[]{:S(2)}, u32[]{:S(2)}) %collective-permute-start.1) | collective-permute-done | bytes 16416 | tf_op jit(solution)/shard_map/ppermute | solution.py:254
  15.9 0.0 collective-permute-done
  15.9 1.3 %collective-permute-start.5 = (f32[128,128]{1,0:T(8,128)S(1)}, f32[128,128]{1,0:T(8,128)S(1)}, u32[]{:S(2)}, u32[]{:S(2)}) collective-permute-start(f32[128,128]{1,0:T(8,128)S(1)} %pad_maximum_fusion.refs_0_), channel_id=1, source_target_pairs={{0,2},{1,3},{2,0},{3,1},{4,6},{5,7},{6,4},{7,5},{8,10},{9,11},{10,... | collective-permute-start | bytes 196616 | tf_op jit(solution)/shard_map/ppermute | solution.py:254
  17.2 0.0 collective-permute-start.4
  17.2 0.9 %collective-permute-start.3 = (f32[128,128]{1,0:T(8,128)S(1)}, f32[128,128]{1,0:T(8,128)S(1)}, u32[]{:S(2)}, u32[]{:S(2)}) collective-permute-start(f32[128,128]{1,0:T(8,128)S(1)} %pad_maximum_fusion.refs_0_), channel_id=1, source_target_pairs={{0,1},{1,0},{2,3},{3,2},{4,5},{5,4},{6,7},{7,6},{8,9},{9,8},{10,11... | collective-permute-start | bytes 196616 | tf_op jit(solution)/shard_map/ppermute | solution.py:254
  18.1 2.2 %collective-permute-done.5.refs_3_ = f32[128,128]{1,0:T(8,128)S(1)} collective-permute-done((f32[128,128]{1,0:T(8,128)S(1)}, f32[128,128]{1,0:T(8,128)S(1)}, u32[]{:S(2)}, u32[]{:S(2)}) %collective-permute-start.5) | collective-permute-done | bytes 65568 | tf_op jit(solution)/shard_map/ppermute | solution.py:254
  20.3 1.2 %collective-permute-done.4.refs_2_ = f32[128,128]{1,0:T(8,128)S(1)} collective-permute-done((f32[128,128]{1,0:T(8,128)S(1)}, f32[128,128]{1,0:T(8,128)S(1)}, u32[]{:S(2)}, u32[]{:S(2)}) %collective-permute-start.4) | collective-permute-done | bytes 65568 | tf_op jit(solution)/shard_map/ppermute | solution.py:254
  21.5 0.0 collective-permute-done.3.refs_1_
  21.5 0.0 copy-done
  21.5 2.9 %shard_map.65 = f32[4,16]{1,0:T(4,128)} custom-call(f32[128,128]{1,0:T(8,128)S(1)} %pad_maximum_fusion.refs_0_, f32[128,128]{1,0:T(8,128)S(1)} %collective-permute-done.3.refs_1_, f32[128,128]{1,0:T(8,128)S(1)} %collective-permute-done.4.refs_2_, f32[128,128]{1,0:T(8,128)S(1)} %collective-permute-done.5.refs_3_, s32[1,16]{1,0:T(1,128)S(1)} %bitcast.3), custom_call_target="tpu_custom_call" | custom-call | tf_op jit(solution)/shard_map/pallas_call | solution.py:237
  (1 shorter events, 0.0 us)
Async XLA Ops:
  0.0 21.5 %copy-start = (s32[16]{0:T(128)S(1)}, s32[16]{0:T(128)}, u32[]{:S(2)}) copy-start(s32[16]{0:T(128)} %param.11) | copy-start | bytes 196
  6.2 5.8 %collective-permute-start.2 = (f32[32,128]{1,0:T(8,128)S(1)}, f32[32,128]{1,0:T(8,128)S(1)}, u32[]{:S(2)}, u32[]{:S(2)}) collective-permute-start(f32[32,128]{1,0:T(8,128)S(1)} %shard_map.64), channel_id=1, source_target_pairs={{0,8},{1,9},{2,10},{3,11},{4,12},{5,13},{6,14},{7,15},{8,0},{9,1},... | collective-permute-start | bytes 49160 | tf_op jit(solution)/shard_map/ppermute | solution.py:254
  10.3 5.5 %collective-permute-start.1 = (f32[32,128]{1,0:T(8,128)S(1)}, f32[32,128]{1,0:T(8,128)S(1)}, u32[]{:S(2)}, u32[]{:S(2)}) collective-permute-start(f32[32,128]{1,0:T(8,128)S(1)} %shard_map.64), channel_id=1, source_target_pairs={{0,12},{1,13},{2,14},{3,15},{4,8},{5,9},{6,10},{7,11},{8,4},{9,5},... | collective-permute-start | bytes 49160 | tf_op jit(solution)/shard_map/ppermute | solution.py:254
  11.4 4.4 %collective-permute-start = (f32[32,128]{1,0:T(8,128)S(1)}, f32[32,128]{1,0:T(8,128)S(1)}, u32[]{:S(2)}, u32[]{:S(2)}) collective-permute-start(f32[32,128]{1,0:T(8,128)S(1)} %shard_map.64), channel_id=1, source_target_pairs={{0,4},{1,5},{2,6},{3,7},{4,0},{5,1},{6,2},{7,3},{8,12},{9,13},{10,... | collective-permute-start | bytes 49160 | tf_op jit(solution)/shard_map/ppermute | solution.py:254
  15.9 4.4 %collective-permute-start.5 = (f32[128,128]{1,0:T(8,128)S(1)}, f32[128,128]{1,0:T(8,128)S(1)}, u32[]{:S(2)}, u32[]{:S(2)}) collective-permute-start(f32[128,128]{1,0:T(8,128)S(1)} %pad_maximum_fusion.refs_0_), channel_id=1, source_target_pairs={{0,2},{1,3},{2,0},{3,1},{4,6},{5,7},{6,4},{7,5},{8,10},{9,11},{10,... | collective-permute-start | bytes 196616 | tf_op jit(solution)/shard_map/ppermute | solution.py:254
  17.2 4.3 %collective-permute-start.4 = (f32[128,128]{1,0:T(8,128)S(1)}, f32[128,128]{1,0:T(8,128)S(1)}, u32[]{:S(2)}, u32[]{:S(2)}) collective-permute-start(f32[128,128]{1,0:T(8,128)S(1)} %pad_maximum_fusion.refs_0_), channel_id=1, source_target_pairs={{0,3},{1,2},{2,1},{3,0},{4,7},{5,6},{6,5},{7,4},{8,11},{9,10},{10,... | collective-permute-start | bytes 196616 | tf_op jit(solution)/shard_map/ppermute | solution.py:254
  17.2 4.3 %collective-permute-start.3 = (f32[128,128]{1,0:T(8,128)S(1)}, f32[128,128]{1,0:T(8,128)S(1)}, u32[]{:S(2)}, u32[]{:S(2)}) collective-permute-start(f32[128,128]{1,0:T(8,128)S(1)} %pad_maximum_fusion.refs_0_), channel_id=1, source_target_pairs={{0,1},{1,0},{2,3},{3,2},{4,5},{5,4},{6,7},{7,6},{8,9},{9,8},{10,11... | collective-permute-start | bytes 196616 | tf_op jit(solution)/shard_map/ppermute | solution.py:254

commit v12 on v11

--- a/solution.py
+++ b/solution.py
@@ -13,80 +13,42 @@
 NT = (((1,), (1,)), ((), ()))
 
 
-def sketch_kernel(bounds, floor, act_hbm, out_hbm, pin_hbm, pout_hbm, lengths_hbm, sketch_ref, act, out, pin, pout, lengths_ref, sems, lengths_sem):
-    count, seq_len, width = act.shape
+def sketch_kernel(bounds, seq_len, act_hbm, out_hbm, pin_hbm, pout_hbm, lengths_hbm, sketch_ref, act, out, pin, pout, lengths_ref, sems, lengths_sem):
+    rows, width = act.shape
     rank_dim = pin.shape[0]
-    rows = count * seq_len
     chunks = len(bounds) - 1
-    columns = [pl.ds(a, b - a) for a, b in zip(bounds, bounds[1:])]
     lengths_copy = pltpu.make_async_copy(lengths_hbm, lengths_ref, lengths_sem)
     lengths_copy.start()
-
-    def tail(c, e, n):
-        src, dst = ((act_hbm, act), (out_hbm, out))[n]
-        part = (e, pl.ds(floor, seq_len - floor), columns[c])
-        return pltpu.make_async_copy(src.at[part], dst.at[part], sems.at[c, 4 + 2 * e + n])
-
-    heads = []
+    copies = []
     for c in range(chunks):
-        cols = columns[c]
-        head = (slice(None), pl.ds(0, floor), cols)
-        heads.append(
+        cols = pl.ds(bounds[c], bounds[c + 1] - bounds[c])
+        copies.append(
             [
-                pltpu.make_async_copy(src.at[part], dst.at[part], sems.at[c, n])
-                for n, (src, dst, part) in enumerate(
-                    (
-                        (pin_hbm, pin, (slice(None), cols)),
-                        (act_hbm, act, head),
-                        (pout_hbm, pout, (slice(None), cols)),
-                        (out_hbm, out, head),
-                    )
+                pltpu.make_async_copy(src.at[:, cols], dst.at[:, cols], sems.at[n, c])
+                for n, (src, dst) in enumerate(
+                    ((pin_hbm, pin), (act_hbm, act), (pout_hbm, pout), (out_hbm, out))
                 )
             ]
         )
-
-    for c in range(chunks):
-        for copy in heads[c]:
+        for copy in copies[-1]:
             copy.start()
-    lengths_copy.wait()
-    for c in range(chunks):
-        for e in range(count):
-
-            @pl.when(lengths_ref[e] > floor)
-            def _():
-                tail(c, e, 0).start()
-                tail(c, e, 1).start()
-
     feat = jnp.zeros((rows, rank_dim), jnp.float32)
     grad = jnp.zeros((rows, rank_dim), jnp.float32)
     for c in range(chunks):
         cols = slice(bounds[c], bounds[c + 1])
-        step = bounds[c + 1] - bounds[c]
-        for copy in heads[c]:
+        for copy in copies[c]:
             copy.wait()
-        for e in range(count):
-
-            @pl.when(lengths_ref[e] > floor)
-            def _():
-                tail(c, e, 0).wait()
-                tail(c, e, 1).wait()
-
-        feat = feat + lax.dot_general(
-            act[:, :, cols].reshape(rows, step), pin[:, cols], NT, preferred_element_type=jnp.float32
-        )
-        grad = grad + lax.dot_general(
-            out[:, :, cols].reshape(rows, step), pout[:, cols], NT, preferred_element_type=jnp.float32
-        )
+        feat = feat + lax.dot_general(act[:, cols], pin[:, cols], NT, preferred_element_type=jnp.float32)
+        grad = grad + lax.dot_general(out[:, cols], pout[:, cols], NT, preferred_element_type=jnp.float32)
+    count = rows // seq_len
     reps = LANES // rank_dim
+    lengths_copy.wait()
     position = lax.broadcasted_iota(jnp.int32, (rows, rank_dim), 0)
     masked = []
-    live_any = jnp.zeros((rows, rank_dim), jnp.bool_)
     for e in range(count):
         first = e * seq_len
         live = (position >= first) & (position < first + lengths_ref[e])
         masked.append(jnp.where(live, grad, 0.0))
-        live_any = live_any | live
-    feat = jnp.where(live_any, feat, 0.0)
     outer = lax.dot_general(
         jnp.concatenate(masked, axis=1),
         jnp.concatenate([feat] * reps, axis=1),
@@ -106,30 +68,36 @@
 def sketch_rows(activations, out_grads, project_in, project_out, lengths):
     count, seq_len, width = activations.shape
     rank_dim = project_in.shape[1]
-    unit = width // 16
-    bounds = (0, 5 * unit, 10 * unit, 14 * unit, width)
+    rows = count * seq_len
+    unit = width // 32
+    bounds = [n * unit for n in (0, 5, 10, 15, 20, 25, 29, 31, 32)]
     chunks = len(bounds) - 1
-    floor = 16
     return pl.pallas_call(
-        functools.partial(sketch_kernel, bounds, floor),
+        functools.partial(sketch_kernel, bounds, seq_len),
         out_shape=jax.ShapeDtypeStruct((count * SUBLANES, LANES), jnp.float32),
         in_specs=[pl.BlockSpec(memory_space=pltpu.HBM)] * 5,
         out_specs=pl.BlockSpec(memory_space=pltpu.VMEM),
         scratch_shapes=[
-            pltpu.VMEM((count, seq_len, width), jnp.bfloat16),
-            pltpu.VMEM((count, seq_len, width), jnp.bfloat16),
+            pltpu.VMEM((rows, width), jnp.bfloat16),
+            pltpu.VMEM((rows, width), jnp.bfloat16),
             pltpu.VMEM((rank_dim, width), jnp.bfloat16),
             pltpu.VMEM((rank_dim, width), jnp.bfloat16),
             pltpu.SMEM((count,), jnp.int32),
-            pltpu.SemaphoreType.DMA((chunks, 4 + 2 * count)),
+            pltpu.SemaphoreType.DMA((4, chunks)),
             pltpu.SemaphoreType.DMA,
         ],
         compiler_params=pltpu.CompilerParams(vmem_limit_bytes=16 * 2**20),
     )(
         *(
             pltpu.with_memory_space_constraint(operand, pltpu.HBM)
-            for operand in (activations, out_grads, project_in.T, project_out.T, lengths)
-        )
+            for operand in (
+                activations.reshape(rows, width),
+                out_grads.reshape(rows, width),
+                project_in.T,
+                project_out.T,
+                lengths,
+            )
+        ),
     )
 
 

time: 24.5 us -> 23.5 us (0.959)
  Pallas kernels: 9.1 us -> 7.99 us
    pallas_call x1, Pallas kernels: 6.24 us -> 5.13 us  [sketch_rows(): pl.pallas_call(functools.partial(sketch_kernel, bounds, seq_len), out_sha...]
where the time goes in v12:
time: 23.5 us; the launch traced here: 23.4 us
  Pallas kernels  7.99 us (34%)
  starting transfers between devices  7.89 us (34%)
  waiting for transfers between devices  7.48 us (32%)
    ppermute x6, starting transfers between devices, swap_all(): lax.ppermute(block, axis, [(i, i ^ n * unit) for i in range(size)])  7.89 us
    ppermute x6, waiting for transfers between devices, swap_all(): lax.ppermute(block, axis, [(i, i ^ n * unit) for i in range(size)])  7.48 us
    pallas_call x1, Pallas kernels, sketch_rows(): pl.pallas_call(functools.partial(sketch_kernel, bounds, seq_len), out_sha...  5.13 us
    pallas_call x1, Pallas kernels, gram_scores(): pl.pallas_call(functools.partial(solve_kernel, per_dev, inner, axis), out...  2.86 us
  transfers between devices with their start and end apart: 6, of which 4 were waited for; matrix products, arithmetic and copies ran while one was open for 0% of the time, Pallas kernels for 0%

profile of v12, /device:TPU:0, one launch (start us, length us, event | category | flops | bytes accessed | tf_op | source)
XLA Modules:
  0.0 23.4 jit_solution(1390471886855412471)
XLA Ops:
  0.0 0.0 copy-start
  0.0 5.1 %shard_map.64 = f32[32,128]{1,0:T(8,128)S(1)} custom-call(bf16[256,8192]{1,0:T(8,128)(2,1)} %bitcast.6, bf16[256,8192]{1,0:T(8,128)(2,1)} %bitcast.7, bf16[32,8192]{1,0:T(8,128)(2,1)} %bitcast.8, bf16[32,8192]{1,0:T(8,128)(2,1)} %bitcast.9, s32[4]{0:T(128)} %lengths_hbm.1), custom_call_target="tpu_custom_call" | custom-call | tf_op jit(solution)/shard_map/pallas_call | solution.py:75
  5.1 4.1 %collective-permute-start.2 = (f32[32,128]{1,0:T(8,128)S(1)}, f32[32,128]{1,0:T(8,128)S(1)}, u32[]{:S(2)}, u32[]{:S(2)}) collective-permute-start(f32[32,128]{1,0:T(8,128)S(1)} %shard_map.64), channel_id=1, source_target_pairs={{0,8},{1,9},{2,10},{3,11},{4,12},{5,13},{6,14},{7,15},{8,0},{9,1},... | collective-permute-start | bytes 49160 | tf_op jit(solution)/shard_map/ppermute | solution.py:222
  9.2 1.3 %collective-permute-start.1 = (f32[32,128]{1,0:T(8,128)S(1)}, f32[32,128]{1,0:T(8,128)S(1)}, u32[]{:S(2)}, u32[]{:S(2)}) collective-permute-start(f32[32,128]{1,0:T(8,128)S(1)} %shard_map.64), channel_id=1, source_target_pairs={{0,12},{1,13},{2,14},{3,15},{4,8},{5,9},{6,10},{7,11},{8,4},{9,5},... | collective-permute-start | bytes 49160 | tf_op jit(solution)/shard_map/ppermute | solution.py:222
  10.6 0.2 %collective-permute-start = (f32[32,128]{1,0:T(8,128)S(1)}, f32[32,128]{1,0:T(8,128)S(1)}, u32[]{:S(2)}, u32[]{:S(2)}) collective-permute-start(f32[32,128]{1,0:T(8,128)S(1)} %shard_map.64), channel_id=1, source_target_pairs={{0,4},{1,5},{2,6},{3,7},{4,0},{5,1},{6,2},{7,3},{8,12},{9,13},{10,... | collective-permute-start | bytes 49160 | tf_op jit(solution)/shard_map/ppermute | solution.py:222
  10.8 0.1 collective-permute-done.2
  11.0 3.8 %collective-permute-done.1 = f32[32,128]{1,0:T(8,128)S(1)} collective-permute-done((f32[32,128]{1,0:T(8,128)S(1)}, f32[32,128]{1,0:T(8,128)S(1)}, u32[]{:S(2)}, u32[]{:S(2)}) %collective-permute-start.1) | collective-permute-done | bytes 16416 | tf_op jit(solution)/shard_map/ppermute | solution.py:222
  14.8 0.0 collective-permute-done
  14.8 1.6 %collective-permute-start.5 = (f32[128,128]{1,0:T(8,128)S(1)}, f32[128,128]{1,0:T(8,128)S(1)}, u32[]{:S(2)}, u32[]{:S(2)}) collective-permute-start(f32[128,128]{1,0:T(8,128)S(1)} %pad_maximum_fusion.refs_0_), channel_id=1, source_target_pairs={{0,2},{1,3},{2,0},{3,1},{4,6},{5,7},{6,4},{7,5},{8,10},{9,11},{10,... | collective-permute-start | bytes 196616 | tf_op jit(solution)/shard_map/ppermute | solution.py:222
  16.3 0.0 collective-permute-start.4
  16.4 0.6 %collective-permute-start.3 = (f32[128,128]{1,0:T(8,128)S(1)}, f32[128,128]{1,0:T(8,128)S(1)}, u32[]{:S(2)}, u32[]{:S(2)}) collective-permute-start(f32[128,128]{1,0:T(8,128)S(1)} %pad_maximum_fusion.refs_0_), channel_id=1, source_target_pairs={{0,1},{1,0},{2,3},{3,2},{4,5},{5,4},{6,7},{7,6},{8,9},{9,8},{10,11... | collective-permute-start | bytes 196616 | tf_op jit(solution)/shard_map/ppermute | solution.py:222
  17.0 2.1 %collective-permute-done.5.refs_3_ = f32[128,128]{1,0:T(8,128)S(1)} collective-permute-done((f32[128,128]{1,0:T(8,128)S(1)}, f32[128,128]{1,0:T(8,128)S(1)}, u32[]{:S(2)}, u32[]{:S(2)}) %collective-permute-start.5) | collective-permute-done | bytes 65568 | tf_op jit(solution)/shard_map/ppermute | solution.py:222
  19.1 1.4 %collective-permute-done.4.refs_2_ = f32[128,128]{1,0:T(8,128)S(1)} collective-permute-done((f32[128,128]{1,0:T(8,128)S(1)}, f32[128,128]{1,0:T(8,128)S(1)}, u32[]{:S(2)}, u32[]{:S(2)}) %collective-permute-start.4) | collective-permute-done | bytes 65568 | tf_op jit(solution)/shard_map/ppermute | solution.py:222
  20.5 0.0 collective-permute-done.3.refs_1_
  20.5 0.0 copy-done
  20.5 2.9 %shard_map.65 = f32[4,16]{1,0:T(4,128)} custom-call(f32[128,128]{1,0:T(8,128)S(1)} %pad_maximum_fusion.refs_0_, f32[128,128]{1,0:T(8,128)S(1)} %collective-permute-done.3.refs_1_, f32[128,128]{1,0:T(8,128)S(1)} %collective-permute-done.4.refs_2_, f32[128,128]{1,0:T(8,128)S(1)} %collective-permute-done.5.refs_3_, s32[1,16]{1,0:T(1,128)S(1)} %bitcast.5), custom_call_target="tpu_custom_call" | custom-call | tf_op jit(solution)/shard_map/pallas_call | solution.py:205
  (1 shorter events, 0.0 us)
Async XLA Ops:
  0.0 20.5 %copy-start = (s32[16]{0:T(128)S(1)}, s32[16]{0:T(128)}, u32[]{:S(2)}) copy-start(s32[16]{0:T(128)} %param.11) | copy-start | bytes 196
  5.1 5.8 %collective-permute-start.2 = (f32[32,128]{1,0:T(8,128)S(1)}, f32[32,128]{1,0:T(8,128)S(1)}, u32[]{:S(2)}, u32[]{:S(2)}) collective-permute-start(f32[32,128]{1,0:T(8,128)S(1)} %shard_map.64), channel_id=1, source_target_pairs={{0,8},{1,9},{2,10},{3,11},{4,12},{5,13},{6,14},{7,15},{8,0},{9,1},... | collective-permute-start | bytes 49160 | tf_op jit(solution)/shard_map/ppermute | solution.py:222
  9.2 5.5 %collective-permute-start.1 = (f32[32,128]{1,0:T(8,128)S(1)}, f32[32,128]{1,0:T(8,128)S(1)}, u32[]{:S(2)}, u32[]{:S(2)}) collective-permute-start(f32[32,128]{1,0:T(8,128)S(1)} %shard_map.64), channel_id=1, source_target_pairs={{0,12},{1,13},{2,14},{3,15},{4,8},{5,9},{6,10},{7,11},{8,4},{9,5},... | collective-permute-start | bytes 49160 | tf_op jit(solution)/shard_map/ppermute | solution.py:222
  10.6 4.2 %collective-permute-start = (f32[32,128]{1,0:T(8,128)S(1)}, f32[32,128]{1,0:T(8,128)S(1)}, u32[]{:S(2)}, u32[]{:S(2)}) collective-permute-start(f32[32,128]{1,0:T(8,128)S(1)} %shard_map.64), channel_id=1, source_target_pairs={{0,4},{1,5},{2,6},{3,7},{4,0},{5,1},{6,2},{7,3},{8,12},{9,13},{10,... | collective-permute-start | bytes 49160 | tf_op jit(solution)/shard_map/ppermute | solution.py:222
  14.8 4.3 %collective-permute-start.5 = (f32[128,128]{1,0:T(8,128)S(1)}, f32[128,128]{1,0:T(8,128)S(1)}, u32[]{:S(2)}, u32[]{:S(2)}) collective-permute-start(f32[128,128]{1,0:T(8,128)S(1)} %pad_maximum_fusion.refs_0_), channel_id=1, source_target_pairs={{0,2},{1,3},{2,0},{3,1},{4,6},{5,7},{6,4},{7,5},{8,10},{9,11},{10,... | collective-permute-start | bytes 196616 | tf_op jit(solution)/shard_map/ppermute | solution.py:222
  16.3 4.2 %collective-permute-start.4 = (f32[128,128]{1,0:T(8,128)S(1)}, f32[128,128]{1,0:T(8,128)S(1)}, u32[]{:S(2)}, u32[]{:S(2)}) collective-permute-start(f32[128,128]{1,0:T(8,128)S(1)} %pad_maximum_fusion.refs_0_), channel_id=1, source_target_pairs={{0,3},{1,2},{2,1},{3,0},{4,7},{5,6},{6,5},{7,4},{8,11},{9,10},{10,... | collective-permute-start | bytes 196616 | tf_op jit(solution)/shard_map/ppermute | solution.py:222
  16.4 4.2 %collective-permute-start.3 = (f32[128,128]{1,0:T(8,128)S(1)}, f32[128,128]{1,0:T(8,128)S(1)}, u32[]{:S(2)}, u32[]{:S(2)}) collective-permute-start(f32[128,128]{1,0:T(8,128)S(1)} %pad_maximum_fusion.refs_0_), channel_id=1, source_target_pairs={{0,1},{1,0},{2,3},{3,2},{4,5},{5,4},{6,7},{7,6},{8,9},{9,8},{10,11... | collective-permute-start | bytes 196616 | tf_op jit(solution)/shard_map/ppermute | solution.py:222

commit v13 on v12

--- a/solution.py
+++ b/solution.py
@@ -69,9 +69,8 @@
     count, seq_len, width = activations.shape
     rank_dim = project_in.shape[1]
     rows = count * seq_len
-    unit = width // 32
-    bounds = [n * unit for n in (0, 5, 10, 15, 20, 25, 29, 31, 32)]
-    chunks = len(bounds) - 1
+    chunks = 8
+    bounds = [n * (width // chunks) for n in range(chunks + 1)]
     return pl.pallas_call(
         functools.partial(sketch_kernel, bounds, seq_len),
         out_shape=jax.ShapeDtypeStruct((count * SUBLANES, LANES), jnp.float32),
@@ -159,6 +158,10 @@
     return solved
 
 
+def gray(n):
+    return n ^ (n >> 1)
+
+
 def solve_kernel(per_dev, inner, axis, *refs):
     tiles, (query_ref, scores_ref, gram_ref) = refs[:-3], refs[-3:]
     nq = query_ref.shape[1]
@@ -168,7 +171,7 @@
     fisher_dim = SUBLANES * LANES
     gram_ref[...] = jnp.zeros(gram_ref.shape, jnp.float32)
     slot = (query_ref[...] // per_dev) ^ lax.axis_index(axis)
-    place = (gray(slot % inner) * outer + gray(slot // inner)) * per_dev + query_ref[...] % per_dev
+    place = (gray(slot % inner) * outer + (outer - slot // inner) % outer) * per_dev + query_ref[...] % per_dev
     rest = LANES - examples - nq
     place = jnp.concatenate(
         [jnp.zeros((1, examples), jnp.int32), place] + ([jnp.zeros((1, rest), jnp.int32)] if rest else []), axis=1
@@ -212,16 +215,20 @@
     )(*tiles, query_index.reshape(1, nq))
 
 
-def gray(n):
-    return n ^ (n >> 1)
-
-
 def gather_xor(tiles, axis, size, inner):
-    def swap_all(block, unit, count):
-        order = sorted(range(1, count), key=gray)
-        return [block] + [lax.ppermute(block, axis, [(i, i ^ n * unit) for i in range(size)]) for n in order]
-
-    return swap_all(jnp.concatenate(swap_all(tiles, inner, size // inner), axis=0), 1, inner)
+    def swap(block, slot, senders=range(size)):
+        return lax.ppermute(block, axis, [(i, i ^ slot) for i in senders])
+
+    outer = size // inner
+    late = size - inner
+    last = swap(tiles, late, range(late))
+    near = [swap(tiles, n * inner) for n in range(outer - 2, 0, -1)]
+    parts = [(0, tiles), (1, last)] + list(enumerate(near, 2)) + [(1, swap(tiles, late, range(late, size)))]
+    rows = tiles.shape[0]
+    column = functools.reduce(
+        jnp.add, [jnp.pad(part, ((n * rows, (outer - 1 - n) * rows), (0, 0))) for n, part in parts]
+    )
+    return [column] + [swap(column, n) for n in sorted(range(1, inner), key=gray)]
 
 
 def large_scores(tiles, query_index, per_dev, axis):

time: 23.5 us -> 24.3 us (1.034)
  the two profiles are of different devices: /device:TPU:0 before, /device:TPU:13 now
where the time goes in v13:
time: 24.3 us; the launch traced here: 24.1 us
  starting transfers between devices  10.4 us (43%)
  Pallas kernels  7.85 us (32%)
  waiting for transfers between devices  5.78 us (24%)
    ppermute x7, starting transfers between devices, swap(): return lax.ppermute(block, axis, [(i, i ^ slot) for i in senders])  10.4 us
    ppermute x7, waiting for transfers between devices, swap(): return lax.ppermute(block, axis, [(i, i ^ slot) for i in senders])  5.78 us
    pallas_call x1, Pallas kernels, sketch_rows(): pl.pallas_call(functools.partial(sketch_kernel, bounds, seq_len), out_sha...  4.99 us
    pallas_call x1, Pallas kernels, gram_scores(): pl.pallas_call(functools.partial(solve_kernel, per_dev, inner, axis), out...  2.86 us
  transfers between devices with their start and end apart: 7, of which 2 were waited for; matrix products, arithmetic and copies ran while one was open for 0% of the time, Pallas kernels for 0%

profile of v13, /device:TPU:13, one launch (start us, length us, event | category | flops | bytes accessed | tf_op | source)
XLA Modules:
  0.0 24.1 jit_solution(14784281051596476951)
XLA Ops:
  0.0 0.0 copy-start
  0.0 5.0 %shard_map.64 = f32[32,128]{1,0:T(8,128)S(1)} custom-call(bf16[256,8192]{1,0:T(8,128)(2,1)} %bitcast.6, bf16[256,8192]{1,0:T(8,128)(2,1)} %bitcast.7, bf16[32,8192]{1,0:T(8,128)(2,1)} %bitcast.8, bf16[32,8192]{1,0:T(8,128)(2,1)} %bitcast.9, s32[4]{0:T(128)} %lengths_hbm.1), custom_call_target="tpu_custom_call" | custom-call | tf_op jit(solution)/shard_map/pallas_call | solution.py:74
  5.0 0.7 %collective-permute-start.3 = (f32[32,128]{1,0:T(8,128)S(1)}, f32[32,128]{1,0:T(8,128)S(1)}, u32[]{:S(2)}, u32[]{:S(2)}) collective-permute-start(f32[32,128]{1,0:T(8,128)S(1)} %shard_map.64), channel_id=1, source_target_pairs={{12,0},{13,1},{14,2},{15,3},{28,16},{29,17},{30,18},{31,19}} | collective-permute-start | bytes 49160 | tf_op jit(solution)/shard_map/ppermute | solution.py:220
  5.7 0.9 %collective-permute-start.2 = (f32[32,128]{1,0:T(8,128)S(1)}, f32[32,128]{1,0:T(8,128)S(1)}, u32[]{:S(2)}, u32[]{:S(2)}) collective-permute-start(f32[32,128]{1,0:T(8,128)S(1)} %shard_map.64), channel_id=1, source_target_pairs={{0,4},{1,5},{2,6},{3,7},{4,0},{5,1},{6,2},{7,3},{8,12},{9,13},{10,... | collective-permute-start | bytes 49160 | tf_op jit(solution)/shard_map/ppermute | solution.py:220
  6.5 2.8 %collective-permute-start.1 = (f32[32,128]{1,0:T(8,128)S(1)}, f32[32,128]{1,0:T(8,128)S(1)}, u32[]{:S(2)}, u32[]{:S(2)}) collective-permute-start(f32[32,128]{1,0:T(8,128)S(1)} %shard_map.64), channel_id=1, source_target_pairs={{0,8},{1,9},{2,10},{3,11},{4,12},{5,13},{6,14},{7,15},{8,0},{9,1},... | collective-permute-start | bytes 49160 | tf_op jit(solution)/shard_map/ppermute | solution.py:220
  9.3 2.1 %collective-permute-start = (f32[32,128]{1,0:T(8,128)S(1)}, f32[32,128]{1,0:T(8,128)S(1)}, u32[]{:S(2)}, u32[]{:S(2)}) collective-permute-start(f32[32,128]{1,0:T(8,128)S(1)} %shard_map.64), channel_id=1, source_target_pairs={{0,12},{1,13},{2,14},{3,15},{4,8},{5,9},{6,10},{7,11},{8,4},{9,5},... | collective-permute-start | bytes 49160 | tf_op jit(solution)/shard_map/ppermute | solution.py:220
  11.4 0.0 collective-permute-done.3
  11.4 0.0 collective-permute-done.2
  11.4 0.0 collective-permute-done.1
  11.5 2.3 %collective-permute-done = f32[32,128]{1,0:T(8,128)S(1)} collective-permute-done((f32[32,128]{1,0:T(8,128)S(1)}, f32[32,128]{1,0:T(8,128)S(1)}, u32[]{:S(2)}, u32[]{:S(2)}) %collective-permute-start) | collective-permute-done | bytes 16416 | tf_op jit(solution)/shard_map/ppermute | solution.py:220
  13.8 1.2 %collective-permute-start.6 = (f32[128,128]{1,0:T(8,128)S(1)}, f32[128,128]{1,0:T(8,128)S(1)}, u32[]{:S(2)}, u32[]{:S(2)}) collective-permute-start(f32[128,128]{1,0:T(8,128)S(1)} %pad_add_fusion.refs_0_), channel_id=1, source_target_pairs={{0,2},{1,3},{2,0},{3,1},{4,6},{5,7},{6,4},{7,5},{8,10},{9,11},{10,... | collective-permute-start | bytes 196616 | tf_op jit(solution)/shard_map/ppermute | solution.py:220
  15.0 2.8 %collective-permute-start.5 = (f32[128,128]{1,0:T(8,128)S(1)}, f32[128,128]{1,0:T(8,128)S(1)}, u32[]{:S(2)}, u32[]{:S(2)}) collective-permute-start(f32[128,128]{1,0:T(8,128)S(1)} %pad_add_fusion.refs_0_), channel_id=1, source_target_pairs={{0,3},{1,2},{2,1},{3,0},{4,7},{5,6},{6,5},{7,4},{8,11},{9,10},{10,... | collective-permute-start | bytes 196616 | tf_op jit(solution)/shard_map/ppermute | solution.py:220
  17.8 0.0 collective-permute-start.4
  17.8 0.0 collective-permute-done.6.refs_3_
  17.8 3.4 %collective-permute-done.5.refs_2_ = f32[128,128]{1,0:T(8,128)S(1)} collective-permute-done((f32[128,128]{1,0:T(8,128)S(1)}, f32[128,128]{1,0:T(8,128)S(1)}, u32[]{:S(2)}, u32[]{:S(2)}) %collective-permute-start.5) | collective-permute-done | bytes 65568 | tf_op jit(solution)/shard_map/ppermute | solution.py:220
  21.2 0.0 collective-permute-done.4.refs_1_
  21.3 0.0 copy-done
  21.3 2.9 %shard_map.65 = f32[4,16]{1,0:T(4,128)} custom-call(f32[128,128]{1,0:T(8,128)S(1)} %pad_add_fusion.refs_0_, f32[128,128]{1,0:T(8,128)S(1)} %collective-permute-done.4.refs_1_, f32[128,128]{1,0:T(8,128)S(1)} %collective-permute-done.5.refs_2_, f32[128,128]{1,0:T(8,128)S(1)} %collective-permute-done.6.refs_3_, s32[1,16]{1,0:T(1,128)S(1)} %bitcast.5), custom_call_target="tpu_custom_call" | custom-call | tf_op jit(solution)/shard_map/pallas_call | solution.py:208
  (1 shorter events, 0.0 us)
Async XLA Ops:
  0.0 21.3 %copy-start = (s32[16]{0:T(128)S(1)}, s32[16]{0:T(128)}, u32[]{:S(2)}) copy-start(s32[16]{0:T(128)} %param.11) | copy-start | bytes 196
  5.0 6.4 %collective-permute-start.3 = (f32[32,128]{1,0:T(8,128)S(1)}, f32[32,128]{1,0:T(8,128)S(1)}, u32[]{:S(2)}, u32[]{:S(2)}) collective-permute-start(f32[32,128]{1,0:T(8,128)S(1)} %shard_map.64), channel_id=1, source_target_pairs={{12,0},{13,1},{14,2},{15,3},{28,16},{29,17},{30,18},{31,19}} | collective-permute-start | bytes 49160 | tf_op jit(solution)/shard_map/ppermute | solution.py:220
  5.7 5.8 %collective-permute-start.2 = (f32[32,128]{1,0:T(8,128)S(1)}, f32[32,128]{1,0:T(8,128)S(1)}, u32[]{:S(2)}, u32[]{:S(2)}) collective-permute-start(f32[32,128]{1,0:T(8,128)S(1)} %shard_map.64), channel_id=1, source_target_pairs={{0,4},{1,5},{2,6},{3,7},{4,0},{5,1},{6,2},{7,3},{8,12},{9,13},{10,... | collective-permute-start | bytes 49160 | tf_op jit(solution)/shard_map/ppermute | solution.py:220
  6.5 4.9 %collective-permute-start.1 = (f32[32,128]{1,0:T(8,128)S(1)}, f32[32,128]{1,0:T(8,128)S(1)}, u32[]{:S(2)}, u32[]{:S(2)}) collective-permute-start(f32[32,128]{1,0:T(8,128)S(1)} %shard_map.64), channel_id=1, source_target_pairs={{0,8},{1,9},{2,10},{3,11},{4,12},{5,13},{6,14},{7,15},{8,0},{9,1},... | collective-permute-start | bytes 49160 | tf_op jit(solution)/shard_map/ppermute | solution.py:220
  9.3 4.5 %collective-permute-start = (f32[32,128]{1,0:T(8,128)S(1)}, f32[32,128]{1,0:T(8,128)S(1)}, u32[]{:S(2)}, u32[]{:S(2)}) collective-permute-start(f32[32,128]{1,0:T(8,128)S(1)} %shard_map.64), channel_id=1, source_target_pairs={{0,12},{1,13},{2,14},{3,15},{4,8},{5,9},{6,10},{7,11},{8,4},{9,5},... | collective-permute-start | bytes 49160 | tf_op jit(solution)/shard_map/ppermute | solution.py:220
  13.8 4.0 %collective-permute-start.6 = (f32[128,128]{1,0:T(8,128)S(1)}, f32[128,128]{1,0:T(8,128)S(1)}, u32[]{:S(2)}, u32[]{:S(2)}) collective-permute-start(f32[128,128]{1,0:T(8,128)S(1)} %pad_add_fusion.refs_0_), channel_id=1, source_target_pairs={{0,2},{1,3},{2,0},{3,1},{4,6},{5,7},{6,4},{7,5},{8,10},{9,11},{10,... | collective-permute-start | bytes 196616 | tf_op jit(solution)/shard_map/ppermute | solution.py:220
  15.0 6.3 %collective-permute-start.5 = (f32[128,128]{1,0:T(8,128)S(1)}, f32[128,128]{1,0:T(8,128)S(1)}, u32[]{:S(2)}, u32[]{:S(2)}) collective-permute-start(f32[128,128]{1,0:T(8,128)S(1)} %pad_add_fusion.refs_0_), channel_id=1, source_target_pairs={{0,3},{1,2},{2,1},{3,0},{4,7},{5,6},{6,5},{7,4},{8,11},{9,10},{10,... | collective-permute-start | bytes 196616 | tf_op jit(solution)/shard_map/ppermute | solution.py:220
  17.8 3.4 %collective-permute-start.4 = (f32[128,128]{1,0:T(8,128)S(1)}, f32[128,128]{1,0:T(8,128)S(1)}, u32[]{:S(2)}, u32[]{:S(2)}) collective-permute-start(f32[128,128]{1,0:T(8,128)S(1)} %pad_add_fusion.refs_0_), channel_id=1, source_target_pairs={{0,1},{1,0},{2,3},{3,2},{4,5},{5,4},{6,7},{7,6},{8,9},{9,8},{10,11... | collective-permute-start | bytes 196616 | tf_op jit(solution)/shard_map/ppermute | solution.py:220

commit v14 on v12

--- a/solution.py
+++ b/solution.py
@@ -33,26 +33,26 @@
         for copy in copies[-1]:
             copy.start()
     feat = jnp.zeros((rows, rank_dim), jnp.float32)
-    grad = jnp.zeros((rows, rank_dim), jnp.float32)
+    grad = jnp.zeros((rank_dim, rows), jnp.float32)
     for c in range(chunks):
         cols = slice(bounds[c], bounds[c + 1])
         for copy in copies[c]:
             copy.wait()
         feat = feat + lax.dot_general(act[:, cols], pin[:, cols], NT, preferred_element_type=jnp.float32)
-        grad = grad + lax.dot_general(out[:, cols], pout[:, cols], NT, preferred_element_type=jnp.float32)
+        grad = grad + lax.dot_general(pout[:, cols], out[:, cols], NT, preferred_element_type=jnp.float32)
     count = rows // seq_len
     reps = LANES // rank_dim
     lengths_copy.wait()
-    position = lax.broadcasted_iota(jnp.int32, (rows, rank_dim), 0)
+    position = lax.broadcasted_iota(jnp.int32, (rank_dim, rows), 1)
     masked = []
     for e in range(count):
         first = e * seq_len
         live = (position >= first) & (position < first + lengths_ref[e])
         masked.append(jnp.where(live, grad, 0.0))
     outer = lax.dot_general(
-        jnp.concatenate(masked, axis=1),
+        jnp.concatenate(masked, axis=0),
         jnp.concatenate([feat] * reps, axis=1),
-        (((0,), (0,)), ((), ())),
+        (((1,), (0,)), ((), ())),
         precision=lax.Precision.HIGHEST,
         preferred_element_type=jnp.float32,
     )
@@ -70,7 +70,7 @@
     rank_dim = project_in.shape[1]
     rows = count * seq_len
     unit = width // 32
-    bounds = [n * unit for n in (0, 5, 10, 15, 20, 25, 29, 31, 32)]
+    bounds = [n * unit for n in (0, 1, 4, 8, 12, 16, 20, 24, 28, 32)]
     chunks = len(bounds) - 1
     return pl.pallas_call(
         functools.partial(sketch_kernel, bounds, seq_len),

time: 23.5 us -> 23.4 us (level)
  no operation moved by 1% of the time
where the time goes in v14:
time: 23.4 us; the launch traced here: 23.2 us
  starting transfers between devices  7.89 us (34%)
  Pallas kernels  7.83 us (33%)
  waiting for transfers between devices  7.49 us (32%)
    ppermute x6, starting transfers between devices, swap_all(): lax.ppermute(block, axis, [(i, i ^ n * unit) for i in range(size)])  7.89 us
    ppermute x6, waiting for transfers between devices, swap_all(): lax.ppermute(block, axis, [(i, i ^ n * unit) for i in range(size)])  7.49 us
    pallas_call x1, Pallas kernels, sketch_rows(): pl.pallas_call(functools.partial(sketch_kernel, bounds, seq_len), out_sha...  4.96 us
    pallas_call x1, Pallas kernels, gram_scores(): pl.pallas_call(functools.partial(solve_kernel, per_dev, inner, axis), out...  2.87 us
  transfers between devices with their start and end apart: 6, of which 4 were waited for; matrix products, arithmetic and copies ran while one was open for 0% of the time, Pallas kernels for 0%

profile of v14, /device:TPU:0, one launch (start us, length us, event | category | flops | bytes accessed | tf_op | source)
XLA Modules:
  0.0 23.2 jit_solution(3400727889789439390)
XLA Ops:
  0.0 0.0 copy-start
  0.0 5.0 %shard_map.64 = f32[32,128]{1,0:T(8,128)S(1)} custom-call(bf16[256,8192]{1,0:T(8,128)(2,1)} %bitcast.6, bf16[256,8192]{1,0:T(8,128)(2,1)} %bitcast.7, bf16[32,8192]{1,0:T(8,128)(2,1)} %bitcast.8, bf16[32,8192]{1,0:T(8,128)(2,1)} %bitcast.9, s32[4]{0:T(128)} %lengths_hbm.1), custom_call_target="tpu_custom_call" | custom-call | tf_op jit(solution)/shard_map/pallas_call | solution.py:75
  5.0 4.1 %collective-permute-start.2 = (f32[32,128]{1,0:T(8,128)S(1)}, f32[32,128]{1,0:T(8,128)S(1)}, u32[]{:S(2)}, u32[]{:S(2)}) collective-permute-start(f32[32,128]{1,0:T(8,128)S(1)} %shard_map.64), channel_id=1, source_target_pairs={{0,8},{1,9},{2,10},{3,11},{4,12},{5,13},{6,14},{7,15},{8,0},{9,1},... | collective-permute-start | bytes 49160 | tf_op jit(solution)/shard_map/ppermute | solution.py:222
  9.1 1.3 %collective-permute-start.1 = (f32[32,128]{1,0:T(8,128)S(1)}, f32[32,128]{1,0:T(8,128)S(1)}, u32[]{:S(2)}, u32[]{:S(2)}) collective-permute-start(f32[32,128]{1,0:T(8,128)S(1)} %shard_map.64), channel_id=1, source_target_pairs={{0,12},{1,13},{2,14},{3,15},{4,8},{5,9},{6,10},{7,11},{8,4},{9,5},... | collective-permute-start | bytes 49160 | tf_op jit(solution)/shard_map/ppermute | solution.py:222
  10.4 0.2 collective-permute-start
  10.7 0.1 collective-permute-done.2
  10.8 3.8 %collective-permute-done.1 = f32[32,128]{1,0:T(8,128)S(1)} collective-permute-done((f32[32,128]{1,0:T(8,128)S(1)}, f32[32,128]{1,0:T(8,128)S(1)}, u32[]{:S(2)}, u32[]{:S(2)}) %collective-permute-start.1) | collective-permute-done | bytes 16416 | tf_op jit(solution)/shard_map/ppermute | solution.py:222
  14.6 0.0 collective-permute-done
  14.6 1.6 %collective-permute-start.5 = (f32[128,128]{1,0:T(8,128)S(1)}, f32[128,128]{1,0:T(8,128)S(1)}, u32[]{:S(2)}, u32[]{:S(2)}) collective-permute-start(f32[128,128]{1,0:T(8,128)S(1)} %pad_maximum_fusion.refs_0_), channel_id=1, source_target_pairs={{0,2},{1,3},{2,0},{3,1},{4,6},{5,7},{6,4},{7,5},{8,10},{9,11},{10,... | collective-permute-start | bytes 196616 | tf_op jit(solution)/shard_map/ppermute | solution.py:222
  16.2 0.0 collective-permute-start.4
  16.2 0.6 %collective-permute-start.3 = (f32[128,128]{1,0:T(8,128)S(1)}, f32[128,128]{1,0:T(8,128)S(1)}, u32[]{:S(2)}, u32[]{:S(2)}) collective-permute-start(f32[128,128]{1,0:T(8,128)S(1)} %pad_maximum_fusion.refs_0_), channel_id=1, source_target_pairs={{0,1},{1,0},{2,3},{3,2},{4,5},{5,4},{6,7},{7,6},{8,9},{9,8},{10,11... | collective-permute-start | bytes 196616 | tf_op jit(solution)/shard_map/ppermute | solution.py:222
  16.8 2.1 %collective-permute-done.5.refs_3_ = f32[128,128]{1,0:T(8,128)S(1)} collective-permute-done((f32[128,128]{1,0:T(8,128)S(1)}, f32[128,128]{1,0:T(8,128)S(1)}, u32[]{:S(2)}, u32[]{:S(2)}) %collective-permute-start.5) | collective-permute-done | bytes 65568 | tf_op jit(solution)/shard_map/ppermute | solution.py:222
  19.0 1.4 %collective-permute-done.4.refs_2_ = f32[128,128]{1,0:T(8,128)S(1)} collective-permute-done((f32[128,128]{1,0:T(8,128)S(1)}, f32[128,128]{1,0:T(8,128)S(1)}, u32[]{:S(2)}, u32[]{:S(2)}) %collective-permute-start.4) | collective-permute-done | bytes 65568 | tf_op jit(solution)/shard_map/ppermute | solution.py:222
  20.4 0.0 collective-permute-done.3.refs_1_
  20.4 0.0 copy-done
  20.4 2.9 %shard_map.65 = f32[4,16]{1,0:T(4,128)} custom-call(f32[128,128]{1,0:T(8,128)S(1)} %pad_maximum_fusion.refs_0_, f32[128,128]{1,0:T(8,128)S(1)} %collective-permute-done.3.refs_1_, f32[128,128]{1,0:T(8,128)S(1)} %collective-permute-done.4.refs_2_, f32[128,128]{1,0:T(8,128)S(1)} %collective-permute-done.5.refs_3_, s32[1,16]{1,0:T(1,128)S(1)} %bitcast.5), custom_call_target="tpu_custom_call" | custom-call | tf_op jit(solution)/shard_map/pallas_call | solution.py:205
  (1 shorter events, 0.0 us)
Async XLA Ops:
  0.0 20.4 %copy-start = (s32[16]{0:T(128)S(1)}, s32[16]{0:T(128)}, u32[]{:S(2)}) copy-start(s32[16]{0:T(128)} %param.11) | copy-start | bytes 196
  5.0 5.8 %collective-permute-start.2 = (f32[32,128]{1,0:T(8,128)S(1)}, f32[32,128]{1,0:T(8,128)S(1)}, u32[]{:S(2)}, u32[]{:S(2)}) collective-permute-start(f32[32,128]{1,0:T(8,128)S(1)} %shard_map.64), channel_id=1, source_target_pairs={{0,8},{1,9},{2,10},{3,11},{4,12},{5,13},{6,14},{7,15},{8,0},{9,1},... | collective-permute-start | bytes 49160 | tf_op jit(solution)/shard_map/ppermute | solution.py:222
  9.1 5.5 %collective-permute-start.1 = (f32[32,128]{1,0:T(8,128)S(1)}, f32[32,128]{1,0:T(8,128)S(1)}, u32[]{:S(2)}, u32[]{:S(2)}) collective-permute-start(f32[32,128]{1,0:T(8,128)S(1)} %shard_map.64), channel_id=1, source_target_pairs={{0,12},{1,13},{2,14},{3,15},{4,8},{5,9},{6,10},{7,11},{8,4},{9,5},... | collective-permute-start | bytes 49160 | tf_op jit(solution)/shard_map/ppermute | solution.py:222
  10.4 4.2 %collective-permute-start = (f32[32,128]{1,0:T(8,128)S(1)}, f32[32,128]{1,0:T(8,128)S(1)}, u32[]{:S(2)}, u32[]{:S(2)}) collective-permute-start(f32[32,128]{1,0:T(8,128)S(1)} %shard_map.64), channel_id=1, source_target_pairs={{0,4},{1,5},{2,6},{3,7},{4,0},{5,1},{6,2},{7,3},{8,12},{9,13},{10,... | collective-permute-start | bytes 49160 | tf_op jit(solution)/shard_map/ppermute | solution.py:222
  14.6 4.3 %collective-permute-start.5 = (f32[128,128]{1,0:T(8,128)S(1)}, f32[128,128]{1,0:T(8,128)S(1)}, u32[]{:S(2)}, u32[]{:S(2)}) collective-permute-start(f32[128,128]{1,0:T(8,128)S(1)} %pad_maximum_fusion.refs_0_), channel_id=1, source_target_pairs={{0,2},{1,3},{2,0},{3,1},{4,6},{5,7},{6,4},{7,5},{8,10},{9,11},{10,... | collective-permute-start | bytes 196616 | tf_op jit(solution)/shard_map/ppermute | solution.py:222
  16.2 4.2 %collective-permute-start.4 = (f32[128,128]{1,0:T(8,128)S(1)}, f32[128,128]{1,0:T(8,128)S(1)}, u32[]{:S(2)}, u32[]{:S(2)}) collective-permute-start(f32[128,128]{1,0:T(8,128)S(1)} %pad_maximum_fusion.refs_0_), channel_id=1, source_target_pairs={{0,3},{1,2},{2,1},{3,0},{4,7},{5,6},{6,5},{7,4},{8,11},{9,10},{10,... | collective-permute-start | bytes 196616 | tf_op jit(solution)/shard_map/ppermute | solution.py:222
  16.2 4.2 %collective-permute-start.3 = (f32[128,128]{1,0:T(8,128)S(1)}, f32[128,128]{1,0:T(8,128)S(1)}, u32[]{:S(2)}, u32[]{:S(2)}) collective-permute-start(f32[128,128]{1,0:T(8,128)S(1)} %pad_maximum_fusion.refs_0_), channel_id=1, source_target_pairs={{0,1},{1,0},{2,3},{3,2},{4,5},{5,4},{6,7},{7,6},{8,9},{9,8},{10,11... | collective-permute-start | bytes 196616 | tf_op jit(solution)/shard_map/ppermute | solution.py:222

commit v15 on v14

--- a/solution.py
+++ b/solution.py
@@ -40,28 +40,30 @@
             copy.wait()
         feat = feat + lax.dot_general(act[:, cols], pin[:, cols], NT, preferred_element_type=jnp.float32)
         grad = grad + lax.dot_general(pout[:, cols], out[:, cols], NT, preferred_element_type=jnp.float32)
+    lengths_copy.wait()
     count = rows // seq_len
     reps = LANES // rank_dim
-    lengths_copy.wait()
-    position = lax.broadcasted_iota(jnp.int32, (rank_dim, rows), 1)
-    masked = []
+    position = lax.broadcasted_iota(jnp.int32, (rows, LANES), 0)
+    band = lax.broadcasted_iota(jnp.int32, (rows, LANES), 1) // rank_dim
+    live = jnp.zeros((rows, LANES), jnp.bool_)
     for e in range(count):
         first = e * seq_len
-        live = (position >= first) & (position < first + lengths_ref[e])
-        masked.append(jnp.where(live, grad, 0.0))
+        live = live | ((band == e) & (position >= first) & (position < first + lengths_ref[e]))
     outer = lax.dot_general(
-        jnp.concatenate(masked, axis=0),
-        jnp.concatenate([feat] * reps, axis=1),
+        grad,
+        jnp.where(live, jnp.concatenate([feat] * reps, axis=1), 0.0),
         (((1,), (0,)), ((), ())),
         precision=lax.Precision.HIGHEST,
         preferred_element_type=jnp.float32,
     )
-    band = lax.broadcasted_iota(jnp.int32, (SUBLANES, LANES), 1) // rank_dim
+    band = band[:SUBLANES]
     for e in range(count):
-        entry = outer[e * rank_dim : e * rank_dim + SUBLANES]
-        for b in range(1, reps):
-            first = e * rank_dim + b * SUBLANES
-            entry = jnp.where(band == b, outer[first : first + SUBLANES], entry)
+        entry = None
+        for b in range(reps):
+            part = outer[b * SUBLANES : (b + 1) * SUBLANES]
+            if b != e:
+                part = pltpu.roll(part, (b - e) * rank_dim % LANES, 1)
+            entry = part if entry is None else jnp.where(band == b, part, entry)
         sketch_ref[e * SUBLANES : (e + 1) * SUBLANES] = entry
 
 
@@ -70,7 +72,7 @@
     rank_dim = project_in.shape[1]
     rows = count * seq_len
     unit = width // 32
-    bounds = [n * unit for n in (0, 1, 4, 8, 12, 16, 20, 24, 28, 32)]
+    bounds = [n * unit for n in (0, 2, 6, 10, 14, 18, 22, 26, 30, 32)]
     chunks = len(bounds) - 1
     return pl.pallas_call(
         functools.partial(sketch_kernel, bounds, seq_len),
@@ -159,6 +161,22 @@
     return solved
 
 
+def gram(x):
+    high = x.astype(jnp.bfloat16)
+    rest = x - high.astype(jnp.float32)
+    middle = rest.astype(jnp.bfloat16)
+    low = (rest - middle.astype(jnp.float32)).astype(jnp.bfloat16)
+    parts = [high, middle, low]
+    count = x.shape[0]
+    terms = []
+    for n, held in enumerate(parts):
+        streamed = jnp.concatenate(parts[: len(parts) - n], axis=0)
+        product = lax.dot_general(streamed, held, NT, preferred_element_type=jnp.float32)
+        terms.append([product[k : k + count] for k in range(0, product.shape[0], count)])
+    (hh, mh, lh), (hm, mm), (hl,) = terms
+    return hh + ((mh + hm) + (lh + hl + mm))
+
+
 def solve_kernel(per_dev, inner, axis, *refs):
     tiles, (query_ref, scores_ref, gram_ref) = refs[:-3], refs[-3:]
     nq = query_ref.shape[1]
@@ -184,9 +202,7 @@
     )
     squares = jnp.sum(jnp.sum(sketches * sketches, axis=0, keepdims=True), axis=1, keepdims=True)
     scale = jnp.broadcast_to(1.0 / squares, (SUBLANES, LANES))
-    gram_ref[:, :examples] = lax.dot_general(
-        sketches, sketches, NT, precision=lax.Precision.HIGHEST, preferred_element_type=jnp.float32
-    )
+    gram_ref[:, :examples] = gram(sketches)
     row = lax.broadcasted_iota(jnp.int32, (SUBLANES, LANES), 0)
     system = []
     for first in range(0, examples, SUBLANES):

time: 23.4 us -> 23.3 us (level)
  no operation moved by 1% of the time
where the time goes in v15:
time: 23.3 us; the launch traced here: 23.1 us
  starting transfers between devices  7.89 us (34%)
  Pallas kernels  7.71 us (33%)
  waiting for transfers between devices  7.49 us (32%)
    ppermute x6, starting transfers between devices, swap_all(): lax.ppermute(block, axis, [(i, i ^ n * unit) for i in range(size)])  7.89 us
    ppermute x6, waiting for transfers between devices, swap_all(): lax.ppermute(block, axis, [(i, i ^ n * unit) for i in range(size)])  7.49 us
    pallas_call x1, Pallas kernels, sketch_rows(): pl.pallas_call(functools.partial(sketch_kernel, bounds, seq_len), out_sha...  4.87 us
    pallas_call x1, Pallas kernels, gram_scores(): pl.pallas_call(functools.partial(solve_kernel, per_dev, inner, axis), out...  2.84 us
  transfers between devices with their start and end apart: 6, of which 4 were waited for; matrix products, arithmetic and copies ran while one was open for 0% of the time, Pallas kernels for 0%

profile of v15, /device:TPU:0, one launch (start us, length us, event | category | flops | bytes accessed | tf_op | source)
XLA Modules:
  0.0 23.1 jit_solution(7113499515771576827)
XLA Ops:
  0.0 0.0 copy-start
  0.0 4.9 %shard_map.64 = f32[32,128]{1,0:T(8,128)S(1)} custom-call(bf16[256,8192]{1,0:T(8,128)(2,1)} %bitcast.6, bf16[256,8192]{1,0:T(8,128)(2,1)} %bitcast.7, bf16[32,8192]{1,0:T(8,128)(2,1)} %bitcast.8, bf16[32,8192]{1,0:T(8,128)(2,1)} %bitcast.9, s32[4]{0:T(128)} %lengths_hbm.1), custom_call_target="tpu_custom_call" | custom-call | tf_op jit(solution)/shard_map/pallas_call | solution.py:77
  4.9 4.1 %collective-permute-start.2 = (f32[32,128]{1,0:T(8,128)S(1)}, f32[32,128]{1,0:T(8,128)S(1)}, u32[]{:S(2)}, u32[]{:S(2)}) collective-permute-start(f32[32,128]{1,0:T(8,128)S(1)} %shard_map.64), channel_id=1, source_target_pairs={{0,8},{1,9},{2,10},{3,11},{4,12},{5,13},{6,14},{7,15},{8,0},{9,1},... | collective-permute-start | bytes 49160 | tf_op jit(solution)/shard_map/ppermute | solution.py:238
  9.0 1.3 %collective-permute-start.1 = (f32[32,128]{1,0:T(8,128)S(1)}, f32[32,128]{1,0:T(8,128)S(1)}, u32[]{:S(2)}, u32[]{:S(2)}) collective-permute-start(f32[32,128]{1,0:T(8,128)S(1)} %shard_map.64), channel_id=1, source_target_pairs={{0,12},{1,13},{2,14},{3,15},{4,8},{5,9},{6,10},{7,11},{8,4},{9,5},... | collective-permute-start | bytes 49160 | tf_op jit(solution)/shard_map/ppermute | solution.py:238
  10.3 0.2 collective-permute-start
  10.6 0.1 collective-permute-done.2
  10.7 3.8 %collective-permute-done.1 = f32[32,128]{1,0:T(8,128)S(1)} collective-permute-done((f32[32,128]{1,0:T(8,128)S(1)}, f32[32,128]{1,0:T(8,128)S(1)}, u32[]{:S(2)}, u32[]{:S(2)}) %collective-permute-start.1) | collective-permute-done | bytes 16416 | tf_op jit(solution)/shard_map/ppermute | solution.py:238
  14.5 0.0 collective-permute-done
  14.5 1.6 %collective-permute-start.5 = (f32[128,128]{1,0:T(8,128)S(1)}, f32[128,128]{1,0:T(8,128)S(1)}, u32[]{:S(2)}, u32[]{:S(2)}) collective-permute-start(f32[128,128]{1,0:T(8,128)S(1)} %pad_maximum_fusion.refs_0_), channel_id=1, source_target_pairs={{0,2},{1,3},{2,0},{3,1},{4,6},{5,7},{6,4},{7,5},{8,10},{9,11},{10,... | collective-permute-start | bytes 196616 | tf_op jit(solution)/shard_map/ppermute | solution.py:238
  16.1 0.0 collective-permute-start.4
  16.1 0.6 %collective-permute-start.3 = (f32[128,128]{1,0:T(8,128)S(1)}, f32[128,128]{1,0:T(8,128)S(1)}, u32[]{:S(2)}, u32[]{:S(2)}) collective-permute-start(f32[128,128]{1,0:T(8,128)S(1)} %pad_maximum_fusion.refs_0_), channel_id=1, source_target_pairs={{0,1},{1,0},{2,3},{3,2},{4,5},{5,4},{6,7},{7,6},{8,9},{9,8},{10,11... | collective-permute-start | bytes 196616 | tf_op jit(solution)/shard_map/ppermute | solution.py:238
  16.7 2.1 %collective-permute-done.5.refs_3_ = f32[128,128]{1,0:T(8,128)S(1)} collective-permute-done((f32[128,128]{1,0:T(8,128)S(1)}, f32[128,128]{1,0:T(8,128)S(1)}, u32[]{:S(2)}, u32[]{:S(2)}) %collective-permute-start.5) | collective-permute-done | bytes 65568 | tf_op jit(solution)/shard_map/ppermute | solution.py:238
  18.9 1.4 %collective-permute-done.4.refs_2_ = f32[128,128]{1,0:T(8,128)S(1)} collective-permute-done((f32[128,128]{1,0:T(8,128)S(1)}, f32[128,128]{1,0:T(8,128)S(1)}, u32[]{:S(2)}, u32[]{:S(2)}) %collective-permute-start.4) | collective-permute-done | bytes 65568 | tf_op jit(solution)/shard_map/ppermute | solution.py:238
  20.3 0.0 collective-permute-done.3.refs_1_
  20.3 0.0 copy-done
  20.3 2.8 %shard_map.65 = f32[4,16]{1,0:T(4,128)} custom-call(f32[128,128]{1,0:T(8,128)S(1)} %pad_maximum_fusion.refs_0_, f32[128,128]{1,0:T(8,128)S(1)} %collective-permute-done.3.refs_1_, f32[128,128]{1,0:T(8,128)S(1)} %collective-permute-done.4.refs_2_, f32[128,128]{1,0:T(8,128)S(1)} %collective-permute-done.5.refs_3_, s32[1,16]{1,0:T(1,128)S(1)} %bitcast.5), custom_call_target="tpu_custom_call" | custom-call | tf_op jit(solution)/shard_map/pallas_call | solution.py:221
  (1 shorter events, 0.0 us)
Async XLA Ops:
  0.0 20.3 %copy-start = (s32[16]{0:T(128)S(1)}, s32[16]{0:T(128)}, u32[]{:S(2)}) copy-start(s32[16]{0:T(128)} %param.11) | copy-start | bytes 196
  4.9 5.8 %collective-permute-start.2 = (f32[32,128]{1,0:T(8,128)S(1)}, f32[32,128]{1,0:T(8,128)S(1)}, u32[]{:S(2)}, u32[]{:S(2)}) collective-permute-start(f32[32,128]{1,0:T(8,128)S(1)} %shard_map.64), channel_id=1, source_target_pairs={{0,8},{1,9},{2,10},{3,11},{4,12},{5,13},{6,14},{7,15},{8,0},{9,1},... | collective-permute-start | bytes 49160 | tf_op jit(solution)/shard_map/ppermute | solution.py:238
  9.0 5.5 %collective-permute-start.1 = (f32[32,128]{1,0:T(8,128)S(1)}, f32[32,128]{1,0:T(8,128)S(1)}, u32[]{:S(2)}, u32[]{:S(2)}) collective-permute-start(f32[32,128]{1,0:T(8,128)S(1)} %shard_map.64), channel_id=1, source_target_pairs={{0,12},{1,13},{2,14},{3,15},{4,8},{5,9},{6,10},{7,11},{8,4},{9,5},... | collective-permute-start | bytes 49160 | tf_op jit(solution)/shard_map/ppermute | solution.py:238
  10.3 4.2 %collective-permute-start = (f32[32,128]{1,0:T(8,128)S(1)}, f32[32,128]{1,0:T(8,128)S(1)}, u32[]{:S(2)}, u32[]{:S(2)}) collective-permute-start(f32[32,128]{1,0:T(8,128)S(1)} %shard_map.64), channel_id=1, source_target_pairs={{0,4},{1,5},{2,6},{3,7},{4,0},{5,1},{6,2},{7,3},{8,12},{9,13},{10,... | collective-permute-start | bytes 49160 | tf_op jit(solution)/shard_map/ppermute | solution.py:238
  14.5 4.3 %collective-permute-start.5 = (f32[128,128]{1,0:T(8,128)S(1)}, f32[128,128]{1,0:T(8,128)S(1)}, u32[]{:S(2)}, u32[]{:S(2)}) collective-permute-start(f32[128,128]{1,0:T(8,128)S(1)} %pad_maximum_fusion.refs_0_), channel_id=1, source_target_pairs={{0,2},{1,3},{2,0},{3,1},{4,6},{5,7},{6,4},{7,5},{8,10},{9,11},{10,... | collective-permute-start | bytes 196616 | tf_op jit(solution)/shard_map/ppermute | solution.py:238
  16.1 4.2 %collective-permute-start.4 = (f32[128,128]{1,0:T(8,128)S(1)}, f32[128,128]{1,0:T(8,128)S(1)}, u32[]{:S(2)}, u32[]{:S(2)}) collective-permute-start(f32[128,128]{1,0:T(8,128)S(1)} %pad_maximum_fusion.refs_0_), channel_id=1, source_target_pairs={{0,3},{1,2},{2,1},{3,0},{4,7},{5,6},{6,5},{7,4},{8,11},{9,10},{10,... | collective-permute-start | bytes 196616 | tf_op jit(solution)/shard_map/ppermute | solution.py:238
  16.1 4.2 %collective-permute-start.3 = (f32[128,128]{1,0:T(8,128)S(1)}, f32[128,128]{1,0:T(8,128)S(1)}, u32[]{:S(2)}, u32[]{:S(2)}) collective-permute-start(f32[128,128]{1,0:T(8,128)S(1)} %pad_maximum_fusion.refs_0_), channel_id=1, source_target_pairs={{0,1},{1,0},{2,3},{3,2},{4,5},{5,4},{6,7},{7,6},{8,9},{9,8},{10,11... | collective-permute-start | bytes 196616 | tf_op jit(solution)/shard_map/ppermute | solution.py:238

commit v16 on v15

--- a/solution.py
+++ b/solution.py
@@ -19,29 +19,39 @@
     chunks = len(bounds) - 1
     lengths_copy = pltpu.make_async_copy(lengths_hbm, lengths_ref, lengths_sem)
     lengths_copy.start()
-    copies = []
-    for c in range(chunks):
+    count = rows // seq_len
+
+    def copies(c, lengths):
         cols = pl.ds(bounds[c], bounds[c + 1] - bounds[c])
-        copies.append(
-            [
-                pltpu.make_async_copy(src.at[:, cols], dst.at[:, cols], sems.at[n, c])
-                for n, (src, dst) in enumerate(
-                    ((pin_hbm, pin), (act_hbm, act), (pout_hbm, pout), (out_hbm, out))
-                )
-            ]
-        )
-        for copy in copies[-1]:
-            copy.start()
+        parts = [(pin_hbm, pin, slice(None)), (pout_hbm, pout, slice(None))]
+        for src, dst in ((act_hbm, act), (out_hbm, out)):
+            if lengths is None:
+                parts.append((src, dst, slice(None)))
+            else:
+                parts += [(src, dst, pl.ds(e * seq_len, lengths[e])) for e in range(count)]
+        return [
+            pltpu.make_async_copy(src.at[part, cols], dst.at[part, cols], sems.at[n, c])
+            for n, (src, dst, part) in enumerate(parts)
+        ]
+
+    full = 3
+    started = [copies(c, None) for c in range(full)]
+    for copy in sum(started, []):
+        copy.start()
+    lengths_copy.wait()
+    lengths = [pl.multiple_of((lengths_ref[e] + 15) // 16 * 16, 16) for e in range(count)]
+    started += [copies(c, lengths) for c in range(full, chunks)]
     feat = jnp.zeros((rows, rank_dim), jnp.float32)
     grad = jnp.zeros((rank_dim, rows), jnp.float32)
     for c in range(chunks):
         cols = slice(bounds[c], bounds[c + 1])
-        for copy in copies[c]:
+        if full + c < chunks:
+            for copy in started[full + c]:
+                copy.start()
+        for copy in started[c]:
             copy.wait()
         feat = feat + lax.dot_general(act[:, cols], pin[:, cols], NT, preferred_element_type=jnp.float32)
         grad = grad + lax.dot_general(pout[:, cols], out[:, cols], NT, preferred_element_type=jnp.float32)
-    lengths_copy.wait()
-    count = rows // seq_len
     reps = LANES // rank_dim
     position = lax.broadcasted_iota(jnp.int32, (rows, LANES), 0)
     band = lax.broadcasted_iota(jnp.int32, (rows, LANES), 1) // rank_dim
@@ -49,8 +59,12 @@
     for e in range(count):
         first = e * seq_len
         live = live | ((band == e) & (position >= first) & (position < first + lengths_ref[e]))
+    position = lax.broadcasted_iota(jnp.int32, grad.shape, 1)
+    read = position < 0
+    for e in range(count):
+        read = read | ((position >= e * seq_len) & (position < e * seq_len + lengths_ref[e]))
     outer = lax.dot_general(
-        grad,
+        jnp.where(read, grad, 0.0),
         jnp.where(live, jnp.concatenate([feat] * reps, axis=1), 0.0),
         (((1,), (0,)), ((), ())),
         precision=lax.Precision.HIGHEST,
@@ -72,7 +86,7 @@
     rank_dim = project_in.shape[1]
     rows = count * seq_len
     unit = width // 32
-    bounds = [n * unit for n in (0, 2, 6, 10, 14, 18, 22, 26, 30, 32)]
+    bounds = [n * unit for n in range(0, 33, 4)]
     chunks = len(bounds) - 1
     return pl.pallas_call(
         functools.partial(sketch_kernel, bounds, seq_len),
@@ -85,7 +99,7 @@
             pltpu.VMEM((rank_dim, width), jnp.bfloat16),
             pltpu.VMEM((rank_dim, width), jnp.bfloat16),
             pltpu.SMEM((count,), jnp.int32),
-            pltpu.SemaphoreType.DMA((4, chunks)),
+            pltpu.SemaphoreType.DMA((2 + 2 * count, chunks)),
             pltpu.SemaphoreType.DMA,
         ],
         compiler_params=pltpu.CompilerParams(vmem_limit_bytes=16 * 2**20),
@@ -186,7 +200,8 @@
     fisher_dim = SUBLANES * LANES
     gram_ref[...] = jnp.zeros(gram_ref.shape, jnp.float32)
     slot = (query_ref[...] // per_dev) ^ lax.axis_index(axis)
-    place = (gray(slot % inner) * outer + gray(slot // inner)) * per_dev + query_ref[...] % per_dev
+    n = slot // inner
+    place = (gray((slot ^ partner(n, inner)) % inner) * outer + gray(n)) * per_dev + query_ref[...] % per_dev
     rest = LANES - examples - nq
     place = jnp.concatenate(
         [jnp.zeros((1, examples), jnp.int32), place] + ([jnp.zeros((1, rest), jnp.int32)] if rest else []), axis=1
@@ -232,12 +247,17 @@
     return n ^ (n >> 1)
 
 
+def partner(n, inner):
+    return n * inner ^ gray(n) & 1
+
+
 def gather_xor(tiles, axis, size, inner):
-    def swap_all(block, unit, count):
-        order = sorted(range(1, count), key=gray)
-        return [block] + [lax.ppermute(block, axis, [(i, i ^ n * unit) for i in range(size)]) for n in order]
-
-    return swap_all(jnp.concatenate(swap_all(tiles, inner, size // inner), axis=0), 1, inner)
+    def swap(block, slot):
+        return lax.ppermute(block, axis, [(i, i ^ slot) for i in range(size)])
+
+    rows = sorted(range(1, size // inner), key=gray)
+    column = jnp.concatenate([tiles] + [swap(tiles, partner(n, inner)) for n in rows], axis=0)
+    return [column] + [swap(column, n) for n in sorted(range(1, inner), key=gray)]
 
 
 def large_scores(tiles, query_index, per_dev, axis):

time: 23.3 us -> 23.4 us (level)
  Pallas kernels: 7.71 us -> 8.28 us
  starting transfers between devices: 7.89 us -> 7.57 us
    pallas_call x1, Pallas kernels: 4.87 us -> 5.44 us  [sketch_rows(): pl.pallas_call(functools.partial(sketch_kernel, bounds, seq_len), out_sha...]
    ppermute x6, starting transfers between devices: 7.89 us -> 7.57 us  [swap(): return lax.ppermute(block, axis, [(i, i ^ slot) for i in range(size)])]
  transfers between devices with their start and end apart: 6 -> 6, of which waited for: 4 -> 3; matrix products, arithmetic and copies ran while one was open for 0% -> 0% of each run, Pallas kernels for 0% -> 0%
where the time goes in v16:
time: 23.4 us; the launch traced here: 23.2 us
  Pallas kernels  8.28 us (35%)
  starting transfers between devices  7.57 us (32%)
  waiting for transfers between devices  7.36 us (31%)
    ppermute x6, starting transfers between devices, swap(): return lax.ppermute(block, axis, [(i, i ^ slot) for i in range(size)])  7.57 us
    ppermute x6, waiting for transfers between devices, swap(): return lax.ppermute(block, axis, [(i, i ^ slot) for i in range(size)])  7.36 us
    pallas_call x1, Pallas kernels, sketch_rows(): pl.pallas_call(functools.partial(sketch_kernel, bounds, seq_len), out_sha...  5.44 us
    pallas_call x1, Pallas kernels, gram_scores(): pl.pallas_call(functools.partial(solve_kernel, per_dev, inner, axis), out...  2.84 us
  transfers between devices with their start and end apart: 6, of which 3 were waited for; matrix products, arithmetic and copies ran while one was open for 0% of the time, Pallas kernels for 0%

profile of v16, /device:TPU:0, one launch (start us, length us, event | category | flops | bytes accessed | tf_op | source)
XLA Modules:
  0.0 23.2 jit_solution(7665125008058650951)
XLA Ops:
  0.0 0.0 copy-start
  0.0 5.4 %shard_map.64 = f32[32,128]{1,0:T(8,128)S(1)} custom-call(bf16[256,8192]{1,0:T(8,128)(2,1)} %bitcast.6, bf16[256,8192]{1,0:T(8,128)(2,1)} %bitcast.7, bf16[32,8192]{1,0:T(8,128)(2,1)} %bitcast.8, bf16[32,8192]{1,0:T(8,128)(2,1)} %bitcast.9, s32[4]{0:T(128)} %lengths_hbm.1), custom_call_target="tpu_custom_call" | custom-call | tf_op jit(solution)/shard_map/pallas_call | solution.py:91
  5.5 3.5 %collective-permute-start.2 = (f32[32,128]{1,0:T(8,128)S(1)}, f32[32,128]{1,0:T(8,128)S(1)}, u32[]{:S(2)}, u32[]{:S(2)}) collective-permute-start(f32[32,128]{1,0:T(8,128)S(1)} %shard_map.64), channel_id=1, source_target_pairs={{0,9},{1,8},{2,11},{3,10},{4,13},{5,12},{6,15},{7,14},{8,1},{9,0},... | collective-permute-start | bytes 49160 | tf_op jit(solution)/shard_map/ppermute | solution.py:256
  9.0 1.7 %collective-permute-start.1 = (f32[32,128]{1,0:T(8,128)S(1)}, f32[32,128]{1,0:T(8,128)S(1)}, u32[]{:S(2)}, u32[]{:S(2)}) collective-permute-start(f32[32,128]{1,0:T(8,128)S(1)} %shard_map.64), channel_id=1, source_target_pairs={{0,12},{1,13},{2,14},{3,15},{4,8},{5,9},{6,10},{7,11},{8,4},{9,5},... | collective-permute-start | bytes 49160 | tf_op jit(solution)/shard_map/ppermute | solution.py:256
  10.6 0.2 collective-permute-start
  10.8 0.0 collective-permute-done.2
  10.8 3.8 %collective-permute-done.1 = f32[32,128]{1,0:T(8,128)S(1)} collective-permute-done((f32[32,128]{1,0:T(8,128)S(1)}, f32[32,128]{1,0:T(8,128)S(1)}, u32[]{:S(2)}, u32[]{:S(2)}) %collective-permute-start.1) | collective-permute-done | bytes 16416 | tf_op jit(solution)/shard_map/ppermute | solution.py:256
  14.6 0.0 collective-permute-done
  14.7 1.5 %collective-permute-start.5 = (f32[128,128]{1,0:T(8,128)S(1)}, f32[128,128]{1,0:T(8,128)S(1)}, u32[]{:S(2)}, u32[]{:S(2)}) collective-permute-start(f32[128,128]{1,0:T(8,128)S(1)} %pad_maximum_fusion.refs_0_), channel_id=1, source_target_pairs={{0,2},{1,3},{2,0},{3,1},{4,6},{5,7},{6,4},{7,5},{8,10},{9,11},{10,... | collective-permute-start | bytes 196616 | tf_op jit(solution)/shard_map/ppermute | solution.py:256
  16.2 0.0 collective-permute-start.4
  16.2 0.7 %collective-permute-start.3 = (f32[128,128]{1,0:T(8,128)S(1)}, f32[128,128]{1,0:T(8,128)S(1)}, u32[]{:S(2)}, u32[]{:S(2)}) collective-permute-start(f32[128,128]{1,0:T(8,128)S(1)} %pad_maximum_fusion.refs_0_), channel_id=1, source_target_pairs={{0,1},{1,0},{2,3},{3,2},{4,5},{5,4},{6,7},{7,6},{8,9},{9,8},{10,11... | collective-permute-start | bytes 196616 | tf_op jit(solution)/shard_map/ppermute | solution.py:256
  16.9 2.1 %collective-permute-done.5.refs_3_ = f32[128,128]{1,0:T(8,128)S(1)} collective-permute-done((f32[128,128]{1,0:T(8,128)S(1)}, f32[128,128]{1,0:T(8,128)S(1)}, u32[]{:S(2)}, u32[]{:S(2)}) %collective-permute-start.5) | collective-permute-done | bytes 65568 | tf_op jit(solution)/shard_map/ppermute | solution.py:256
  19.0 1.4 %collective-permute-done.4.refs_2_ = f32[128,128]{1,0:T(8,128)S(1)} collective-permute-done((f32[128,128]{1,0:T(8,128)S(1)}, f32[128,128]{1,0:T(8,128)S(1)}, u32[]{:S(2)}, u32[]{:S(2)}) %collective-permute-start.4) | collective-permute-done | bytes 65568 | tf_op jit(solution)/shard_map/ppermute | solution.py:256
  20.4 0.0 collective-permute-done.3.refs_1_
  20.4 0.0 copy-done
  20.4 2.8 %shard_map.65 = f32[4,16]{1,0:T(4,128)} custom-call(f32[128,128]{1,0:T(8,128)S(1)} %pad_maximum_fusion.refs_0_, f32[128,128]{1,0:T(8,128)S(1)} %collective-permute-done.3.refs_1_, f32[128,128]{1,0:T(8,128)S(1)} %collective-permute-done.4.refs_2_, f32[128,128]{1,0:T(8,128)S(1)} %collective-permute-done.5.refs_3_, s32[1,16]{1,0:T(1,128)S(1)} %bitcast.5), custom_call_target="tpu_custom_call" | custom-call | tf_op jit(solution)/shard_map/pallas_call | solution.py:236
  (1 shorter events, 0.0 us)
Async XLA Ops:
  0.0 20.4 %copy-start = (s32[16]{0:T(128)S(1)}, s32[16]{0:T(128)}, u32[]{:S(2)}) copy-start(s32[16]{0:T(128)} %param.11) | copy-start | bytes 196
  5.5 5.4 %collective-permute-start.2 = (f32[32,128]{1,0:T(8,128)S(1)}, f32[32,128]{1,0:T(8,128)S(1)}, u32[]{:S(2)}, u32[]{:S(2)}) collective-permute-start(f32[32,128]{1,0:T(8,128)S(1)} %shard_map.64), channel_id=1, source_target_pairs={{0,9},{1,8},{2,11},{3,10},{4,13},{5,12},{6,15},{7,14},{8,1},{9,0},... | collective-permute-start | bytes 49160 | tf_op jit(solution)/shard_map/ppermute | solution.py:256
  9.0 5.7 %collective-permute-start.1 = (f32[32,128]{1,0:T(8,128)S(1)}, f32[32,128]{1,0:T(8,128)S(1)}, u32[]{:S(2)}, u32[]{:S(2)}) collective-permute-start(f32[32,128]{1,0:T(8,128)S(1)} %shard_map.64), channel_id=1, source_target_pairs={{0,12},{1,13},{2,14},{3,15},{4,8},{5,9},{6,10},{7,11},{8,4},{9,5},... | collective-permute-start | bytes 49160 | tf_op jit(solution)/shard_map/ppermute | solution.py:256
  10.6 4.0 %collective-permute-start = (f32[32,128]{1,0:T(8,128)S(1)}, f32[32,128]{1,0:T(8,128)S(1)}, u32[]{:S(2)}, u32[]{:S(2)}) collective-permute-start(f32[32,128]{1,0:T(8,128)S(1)} %shard_map.64), channel_id=1, source_target_pairs={{0,5},{1,4},{2,7},{3,6},{4,1},{5,0},{6,3},{7,2},{8,13},{9,12},{10,... | collective-permute-start | bytes 49160 | tf_op jit(solution)/shard_map/ppermute | solution.py:256
  14.7 4.3 %collective-permute-start.5 = (f32[128,128]{1,0:T(8,128)S(1)}, f32[128,128]{1,0:T(8,128)S(1)}, u32[]{:S(2)}, u32[]{:S(2)}) collective-permute-start(f32[128,128]{1,0:T(8,128)S(1)} %pad_maximum_fusion.refs_0_), channel_id=1, source_target_pairs={{0,2},{1,3},{2,0},{3,1},{4,6},{5,7},{6,4},{7,5},{8,10},{9,11},{10,... | collective-permute-start | bytes 196616 | tf_op jit(solution)/shard_map/ppermute | solution.py:256
  16.2 4.2 %collective-permute-start.4 = (f32[128,128]{1,0:T(8,128)S(1)}, f32[128,128]{1,0:T(8,128)S(1)}, u32[]{:S(2)}, u32[]{:S(2)}) collective-permute-start(f32[128,128]{1,0:T(8,128)S(1)} %pad_maximum_fusion.refs_0_), channel_id=1, source_target_pairs={{0,3},{1,2},{2,1},{3,0},{4,7},{5,6},{6,5},{7,4},{8,11},{9,10},{10,... | collective-permute-start | bytes 196616 | tf_op jit(solution)/shard_map/ppermute | solution.py:256
  16.2 4.2 %collective-permute-start.3 = (f32[128,128]{1,0:T(8,128)S(1)}, f32[128,128]{1,0:T(8,128)S(1)}, u32[]{:S(2)}, u32[]{:S(2)}) collective-permute-start(f32[128,128]{1,0:T(8,128)S(1)} %pad_maximum_fusion.refs_0_), channel_id=1, source_target_pairs={{0,1},{1,0},{2,3},{3,2},{4,5},{5,4},{6,7},{7,6},{8,9},{9,8},{10,11... | collective-permute-start | bytes 196616 | tf_op jit(solution)/shard_map/ppermute | solution.py:256

commit v17 on v16

--- a/solution.py
+++ b/solution.py
@@ -13,107 +13,68 @@
 NT = (((1,), (1,)), ((), ()))
 
 
-def sketch_kernel(bounds, seq_len, act_hbm, out_hbm, pin_hbm, pout_hbm, lengths_hbm, sketch_ref, act, out, pin, pout, lengths_ref, sems, lengths_sem):
-    rows, width = act.shape
+def sketch_kernel(act_hbm, out_hbm, pin_hbm, pout_hbm, lengths_hbm, sketch_ref, act, out, pin, pout, lengths_ref, sems, p_sems):
+    count, seq_len, width = act.shape
     rank_dim = pin.shape[0]
-    chunks = len(bounds) - 1
-    lengths_copy = pltpu.make_async_copy(lengths_hbm, lengths_ref, lengths_sem)
-    lengths_copy.start()
-    count = rows // seq_len
-
-    def copies(c, lengths):
-        cols = pl.ds(bounds[c], bounds[c + 1] - bounds[c])
-        parts = [(pin_hbm, pin, slice(None)), (pout_hbm, pout, slice(None))]
-        for src, dst in ((act_hbm, act), (out_hbm, out)):
-            if lengths is None:
-                parts.append((src, dst, slice(None)))
-            else:
-                parts += [(src, dst, pl.ds(e * seq_len, lengths[e])) for e in range(count)]
-        return [
-            pltpu.make_async_copy(src.at[part, cols], dst.at[part, cols], sems.at[n, c])
-            for n, (src, dst, part) in enumerate(parts)
-        ]
-
-    full = 3
-    started = [copies(c, None) for c in range(full)]
-    for copy in sum(started, []):
-        copy.start()
-    lengths_copy.wait()
-    lengths = [pl.multiple_of((lengths_ref[e] + 15) // 16 * 16, 16) for e in range(count)]
-    started += [copies(c, lengths) for c in range(full, chunks)]
-    feat = jnp.zeros((rows, rank_dim), jnp.float32)
-    grad = jnp.zeros((rank_dim, rows), jnp.float32)
-    for c in range(chunks):
-        cols = slice(bounds[c], bounds[c + 1])
-        if full + c < chunks:
-            for copy in started[full + c]:
-                copy.start()
-        for copy in started[c]:
-            copy.wait()
-        feat = feat + lax.dot_general(act[:, cols], pin[:, cols], NT, preferred_element_type=jnp.float32)
-        grad = grad + lax.dot_general(pout[:, cols], out[:, cols], NT, preferred_element_type=jnp.float32)
     reps = LANES // rank_dim
-    position = lax.broadcasted_iota(jnp.int32, (rows, LANES), 0)
-    band = lax.broadcasted_iota(jnp.int32, (rows, LANES), 1) // rank_dim
-    live = jnp.zeros((rows, LANES), jnp.bool_)
+    pairs = ((pin_hbm, pin, p_sems.at[0]), (pout_hbm, pout, p_sems.at[1]), (lengths_hbm, lengths_ref, p_sems.at[2]))
+    copy_in, copy_out, copy_lengths = (pltpu.make_async_copy(*pair) for pair in pairs)
+    acts = [pltpu.make_async_copy(act_hbm.at[e], act.at[e], sems.at[0, e]) for e in range(count)]
+    outs = [pltpu.make_async_copy(out_hbm.at[e], out.at[e], sems.at[1, e]) for e in range(count)]
+    copy_lengths.start()
+    copy_in.start()
+    acts[0].start()
+    copy_out.start()
+    outs[0].start()
+    for e in range(1, count):
+        acts[e].start()
+        outs[e].start()
+    copy_in.wait()
+    copy_out.wait()
+    copy_lengths.wait()
+    position = lax.broadcasted_iota(jnp.int32, (rank_dim, seq_len), 1)
+    band = lax.broadcasted_iota(jnp.int32, (SUBLANES, LANES), 1) // rank_dim
     for e in range(count):
-        first = e * seq_len
-        live = live | ((band == e) & (position >= first) & (position < first + lengths_ref[e]))
-    position = lax.broadcasted_iota(jnp.int32, grad.shape, 1)
-    read = position < 0
-    for e in range(count):
-        read = read | ((position >= e * seq_len) & (position < e * seq_len + lengths_ref[e]))
-    outer = lax.dot_general(
-        jnp.where(read, grad, 0.0),
-        jnp.where(live, jnp.concatenate([feat] * reps, axis=1), 0.0),
-        (((1,), (0,)), ((), ())),
-        precision=lax.Precision.HIGHEST,
-        preferred_element_type=jnp.float32,
-    )
-    band = band[:SUBLANES]
-    for e in range(count):
-        entry = None
-        for b in range(reps):
-            part = outer[b * SUBLANES : (b + 1) * SUBLANES]
-            if b != e:
-                part = pltpu.roll(part, (b - e) * rank_dim % LANES, 1)
-            entry = part if entry is None else jnp.where(band == b, part, entry)
+        acts[e].wait()
+        feat = lax.dot_general(act[e], pin[...], NT, preferred_element_type=jnp.float32)
+        outs[e].wait()
+        grad = lax.dot_general(pout[...], out[e], NT, preferred_element_type=jnp.float32)
+        outer = lax.dot_general(
+            jnp.where(position < lengths_ref[e], grad, 0.0),
+            jnp.concatenate([feat] * reps, axis=1),
+            (((1,), (0,)), ((), ())),
+            precision=lax.Precision.HIGHEST,
+            preferred_element_type=jnp.float32,
+        )
+        entry = outer[:SUBLANES]
+        for b in range(1, reps):
+            entry = jnp.where(band == b, outer[b * SUBLANES : (b + 1) * SUBLANES], entry)
         sketch_ref[e * SUBLANES : (e + 1) * SUBLANES] = entry
 
 
 def sketch_rows(activations, out_grads, project_in, project_out, lengths):
     count, seq_len, width = activations.shape
     rank_dim = project_in.shape[1]
-    rows = count * seq_len
-    unit = width // 32
-    bounds = [n * unit for n in range(0, 33, 4)]
-    chunks = len(bounds) - 1
     return pl.pallas_call(
-        functools.partial(sketch_kernel, bounds, seq_len),
+        sketch_kernel,
         out_shape=jax.ShapeDtypeStruct((count * SUBLANES, LANES), jnp.float32),
         in_specs=[pl.BlockSpec(memory_space=pltpu.HBM)] * 5,
         out_specs=pl.BlockSpec(memory_space=pltpu.VMEM),
         scratch_shapes=[
-            pltpu.VMEM((rows, width), jnp.bfloat16),
-            pltpu.VMEM((rows, width), jnp.bfloat16),
+            pltpu.VMEM((count, seq_len, width), jnp.bfloat16),
+            pltpu.VMEM((count, seq_len, width), jnp.bfloat16),
             pltpu.VMEM((rank_dim, width), jnp.bfloat16),
             pltpu.VMEM((rank_dim, width), jnp.bfloat16),
             pltpu.SMEM((count,), jnp.int32),
-            pltpu.SemaphoreType.DMA((2 + 2 * count, chunks)),
-            pltpu.SemaphoreType.DMA,
+            pltpu.SemaphoreType.DMA((2, count)),
+            pltpu.SemaphoreType.DMA((3,)),
         ],
         compiler_params=pltpu.CompilerParams(vmem_limit_bytes=16 * 2**20),
     )(
         *(
             pltpu.with_memory_space_constraint(operand, pltpu.HBM)
-            for operand in (
-                activations.reshape(rows, width),
-                out_grads.reshape(rows, width),
-                project_in.T,
-                project_out.T,
-                lengths,
-            )
-        ),
+            for operand in (activations, out_grads, project_in.T, project_out.T, lengths)
+        )
     )
 
 

time: 23.4 us -> 27.3 us (1.17)
  Pallas kernels: 8.28 us -> 12.3 us
    pallas_call x1, Pallas kernels: 5.44 us -> 9.43 us  [sketch_rows(): pl.pallas_call(sketch_kernel, out_shape=jax.ShapeDtypeStruct((count * SUB...]
where the time goes in v17:
time: 27.3 us; the launch traced here: 27.2 us
  Pallas kernels  12.3 us (45%)
  starting transfers between devices  7.61 us (28%)
  waiting for transfers between devices  7.25 us (27%)
    pallas_call x1, Pallas kernels, sketch_rows(): pl.pallas_call(sketch_kernel, out_shape=jax.ShapeDtypeStruct((count * SUB...  9.43 us
    ppermute x6, starting transfers between devices, swap(): return lax.ppermute(block, axis, [(i, i ^ slot) for i in range(size)])  7.61 us
    ppermute x6, waiting for transfers between devices, swap(): return lax.ppermute(block, axis, [(i, i ^ slot) for i in range(size)])  7.25 us
    pallas_call x1, Pallas kernels, gram_scores(): pl.pallas_call(functools.partial(solve_kernel, per_dev, inner, axis), out...  2.84 us
  transfers between devices with their start and end apart: 6, of which 3 were waited for; matrix products, arithmetic and copies ran while one was open for 0% of the time, Pallas kernels for 0%

profile of v17, /device:TPU:0, one launch (start us, length us, event | category | flops | bytes accessed | tf_op | source)
XLA Modules:
  0.0 27.2 jit_solution(18326457450742413742)
XLA Ops:
  0.0 0.0 copy-start
  0.0 9.4 %shard_map.64 = f32[32,128]{1,0:T(8,128)S(1)} custom-call(bf16[4,64,8192]{2,1,0:T(8,128)(2,1)} %act_hbm.1, bf16[4,64,8192]{2,1,0:T(8,128)(2,1)} %out_hbm.1, bf16[32,8192]{1,0:T(8,128)(2,1)} %bitcast.4, bf16[32,8192]{1,0:T(8,128)(2,1)} %bitcast.5, s32[4]{0:T(128)} %lengths_hbm.1), custom_call_target="tpu_custom_call" | custom-call | tf_op jit(solution)/shard_map/pallas_call | solution.py:58
  9.4 3.5 %collective-permute-start.2 = (f32[32,128]{1,0:T(8,128)S(1)}, f32[32,128]{1,0:T(8,128)S(1)}, u32[]{:S(2)}, u32[]{:S(2)}) collective-permute-start(f32[32,128]{1,0:T(8,128)S(1)} %shard_map.64), channel_id=1, source_target_pairs={{0,9},{1,8},{2,11},{3,10},{4,13},{5,12},{6,15},{7,14},{8,1},{9,0},... | collective-permute-start | bytes 49160 | tf_op jit(solution)/shard_map/ppermute | solution.py:217
  13.0 1.7 %collective-permute-start.1 = (f32[32,128]{1,0:T(8,128)S(1)}, f32[32,128]{1,0:T(8,128)S(1)}, u32[]{:S(2)}, u32[]{:S(2)}) collective-permute-start(f32[32,128]{1,0:T(8,128)S(1)} %shard_map.64), channel_id=1, source_target_pairs={{0,12},{1,13},{2,14},{3,15},{4,8},{5,9},{6,10},{7,11},{8,4},{9,5},... | collective-permute-start | bytes 49160 | tf_op jit(solution)/shard_map/ppermute | solution.py:217
  14.7 0.2 collective-permute-start
  14.8 0.0 collective-permute-done.2
  14.8 3.7 %collective-permute-done.1 = f32[32,128]{1,0:T(8,128)S(1)} collective-permute-done((f32[32,128]{1,0:T(8,128)S(1)}, f32[32,128]{1,0:T(8,128)S(1)}, u32[]{:S(2)}, u32[]{:S(2)}) %collective-permute-start.1) | collective-permute-done | bytes 16416 | tf_op jit(solution)/shard_map/ppermute | solution.py:217
  18.6 0.0 collective-permute-done
  18.6 1.6 %collective-permute-start.5 = (f32[128,128]{1,0:T(8,128)S(1)}, f32[128,128]{1,0:T(8,128)S(1)}, u32[]{:S(2)}, u32[]{:S(2)}) collective-permute-start(f32[128,128]{1,0:T(8,128)S(1)} %pad_maximum_fusion.refs_0_), channel_id=1, source_target_pairs={{0,2},{1,3},{2,0},{3,1},{4,6},{5,7},{6,4},{7,5},{8,10},{9,11},{10,... | collective-permute-start | bytes 196616 | tf_op jit(solution)/shard_map/ppermute | solution.py:217
  20.2 0.0 collective-permute-start.4
  20.2 0.6 %collective-permute-start.3 = (f32[128,128]{1,0:T(8,128)S(1)}, f32[128,128]{1,0:T(8,128)S(1)}, u32[]{:S(2)}, u32[]{:S(2)}) collective-permute-start(f32[128,128]{1,0:T(8,128)S(1)} %pad_maximum_fusion.refs_0_), channel_id=1, source_target_pairs={{0,1},{1,0},{2,3},{3,2},{4,5},{5,4},{6,7},{7,6},{8,9},{9,8},{10,11... | collective-permute-start | bytes 196616 | tf_op jit(solution)/shard_map/ppermute | solution.py:217
  20.8 2.1 %collective-permute-done.5.refs_3_ = f32[128,128]{1,0:T(8,128)S(1)} collective-permute-done((f32[128,128]{1,0:T(8,128)S(1)}, f32[128,128]{1,0:T(8,128)S(1)}, u32[]{:S(2)}, u32[]{:S(2)}) %collective-permute-start.5) | collective-permute-done | bytes 65568 | tf_op jit(solution)/shard_map/ppermute | solution.py:217
  22.9 1.4 %collective-permute-done.4.refs_2_ = f32[128,128]{1,0:T(8,128)S(1)} collective-permute-done((f32[128,128]{1,0:T(8,128)S(1)}, f32[128,128]{1,0:T(8,128)S(1)}, u32[]{:S(2)}, u32[]{:S(2)}) %collective-permute-start.4) | collective-permute-done | bytes 65568 | tf_op jit(solution)/shard_map/ppermute | solution.py:217
  24.3 0.0 collective-permute-done.3.refs_1_
  24.3 0.0 copy-done
  24.3 2.8 %shard_map.65 = f32[4,16]{1,0:T(4,128)} custom-call(f32[128,128]{1,0:T(8,128)S(1)} %pad_maximum_fusion.refs_0_, f32[128,128]{1,0:T(8,128)S(1)} %collective-permute-done.3.refs_1_, f32[128,128]{1,0:T(8,128)S(1)} %collective-permute-done.4.refs_2_, f32[128,128]{1,0:T(8,128)S(1)} %collective-permute-done.5.refs_3_, s32[1,16]{1,0:T(1,128)S(1)} %bitcast.3), custom_call_target="tpu_custom_call" | custom-call | tf_op jit(solution)/shard_map/pallas_call | solution.py:197
  (1 shorter events, 0.0 us)
Async XLA Ops:
  0.0 24.3 %copy-start = (s32[16]{0:T(128)S(1)}, s32[16]{0:T(128)}, u32[]{:S(2)}) copy-start(s32[16]{0:T(128)} %param.11) | copy-start | bytes 196
  9.4 5.4 %collective-permute-start.2 = (f32[32,128]{1,0:T(8,128)S(1)}, f32[32,128]{1,0:T(8,128)S(1)}, u32[]{:S(2)}, u32[]{:S(2)}) collective-permute-start(f32[32,128]{1,0:T(8,128)S(1)} %shard_map.64), channel_id=1, source_target_pairs={{0,9},{1,8},{2,11},{3,10},{4,13},{5,12},{6,15},{7,14},{8,1},{9,0},... | collective-permute-start | bytes 49160 | tf_op jit(solution)/shard_map/ppermute | solution.py:217
  13.0 5.6 %collective-permute-start.1 = (f32[32,128]{1,0:T(8,128)S(1)}, f32[32,128]{1,0:T(8,128)S(1)}, u32[]{:S(2)}, u32[]{:S(2)}) collective-permute-start(f32[32,128]{1,0:T(8,128)S(1)} %shard_map.64), channel_id=1, source_target_pairs={{0,12},{1,13},{2,14},{3,15},{4,8},{5,9},{6,10},{7,11},{8,4},{9,5},... | collective-permute-start | bytes 49160 | tf_op jit(solution)/shard_map/ppermute | solution.py:217
  14.7 3.9 %collective-permute-start = (f32[32,128]{1,0:T(8,128)S(1)}, f32[32,128]{1,0:T(8,128)S(1)}, u32[]{:S(2)}, u32[]{:S(2)}) collective-permute-start(f32[32,128]{1,0:T(8,128)S(1)} %shard_map.64), channel_id=1, source_target_pairs={{0,5},{1,4},{2,7},{3,6},{4,1},{5,0},{6,3},{7,2},{8,13},{9,12},{10,... | collective-permute-start | bytes 49160 | tf_op jit(solution)/shard_map/ppermute | solution.py:217
  18.6 4.3 %collective-permute-start.5 = (f32[128,128]{1,0:T(8,128)S(1)}, f32[128,128]{1,0:T(8,128)S(1)}, u32[]{:S(2)}, u32[]{:S(2)}) collective-permute-start(f32[128,128]{1,0:T(8,128)S(1)} %pad_maximum_fusion.refs_0_), channel_id=1, source_target_pairs={{0,2},{1,3},{2,0},{3,1},{4,6},{5,7},{6,4},{7,5},{8,10},{9,11},{10,... | collective-permute-start | bytes 196616 | tf_op jit(solution)/shard_map/ppermute | solution.py:217
  20.2 4.1 %collective-permute-start.4 = (f32[128,128]{1,0:T(8,128)S(1)}, f32[128,128]{1,0:T(8,128)S(1)}, u32[]{:S(2)}, u32[]{:S(2)}) collective-permute-start(f32[128,128]{1,0:T(8,128)S(1)} %pad_maximum_fusion.refs_0_), channel_id=1, source_target_pairs={{0,3},{1,2},{2,1},{3,0},{4,7},{5,6},{6,5},{7,4},{8,11},{9,10},{10,... | collective-permute-start | bytes 196616 | tf_op jit(solution)/shard_map/ppermute | solution.py:217
  20.2 4.1 %collective-permute-start.3 = (f32[128,128]{1,0:T(8,128)S(1)}, f32[128,128]{1,0:T(8,128)S(1)}, u32[]{:S(2)}, u32[]{:S(2)}) collective-permute-start(f32[128,128]{1,0:T(8,128)S(1)} %pad_maximum_fusion.refs_0_), channel_id=1, source_target_pairs={{0,1},{1,0},{2,3},{3,2},{4,5},{5,4},{6,7},{7,6},{8,9},{9,8},{10,11... | collective-permute-start | bytes 196616 | tf_op jit(solution)/shard_map/ppermute | solution.py:217

commit v18 on v15

--- a/solution.py
+++ b/solution.py
@@ -13,50 +13,53 @@
 NT = (((1,), (1,)), ((), ()))
 
 
-def sketch_kernel(bounds, seq_len, act_hbm, out_hbm, pin_hbm, pout_hbm, lengths_hbm, sketch_ref, act, out, pin, pout, lengths_ref, sems, lengths_sem):
-    rows, width = act.shape
-    rank_dim = pin.shape[0]
+def sketch_kernel(bounds, seq_len, act_hbm, out_hbm, pin_hbm, pout_hbm, lengths_hbm, sketch_ref, rows_ref, proj, lengths_ref, sems, lengths_sem):
+    rows = rows_ref.shape[0] // 2
+    rank_dim = proj.shape[0] // 2
     chunks = len(bounds) - 1
     lengths_copy = pltpu.make_async_copy(lengths_hbm, lengths_ref, lengths_sem)
     lengths_copy.start()
     copies = []
     for c in range(chunks):
         cols = pl.ds(bounds[c], bounds[c + 1] - bounds[c])
+        parts = (
+            (pin_hbm, proj, 0, rank_dim),
+            (pout_hbm, proj, rank_dim, rank_dim),
+            (act_hbm, rows_ref, 0, rows),
+            (out_hbm, rows_ref, rows, rows),
+        )
         copies.append(
             [
-                pltpu.make_async_copy(src.at[:, cols], dst.at[:, cols], sems.at[n, c])
-                for n, (src, dst) in enumerate(
-                    ((pin_hbm, pin), (act_hbm, act), (pout_hbm, pout), (out_hbm, out))
-                )
+                pltpu.make_async_copy(src.at[:, cols], dst.at[pl.ds(first, size), cols], sems.at[n, c])
+                for n, (src, dst, first, size) in enumerate(parts)
             ]
         )
         for copy in copies[-1]:
             copy.start()
-    feat = jnp.zeros((rows, rank_dim), jnp.float32)
-    grad = jnp.zeros((rank_dim, rows), jnp.float32)
+    both = jnp.zeros((2 * rank_dim, 2 * rows), jnp.float32)
     for c in range(chunks):
         cols = slice(bounds[c], bounds[c + 1])
         for copy in copies[c]:
             copy.wait()
-        feat = feat + lax.dot_general(act[:, cols], pin[:, cols], NT, preferred_element_type=jnp.float32)
-        grad = grad + lax.dot_general(pout[:, cols], out[:, cols], NT, preferred_element_type=jnp.float32)
+        both = both + lax.dot_general(proj[:, cols], rows_ref[:, cols], NT, preferred_element_type=jnp.float32)
+    feat, grad = both[:rank_dim, :rows], both[rank_dim:, rows:]
     lengths_copy.wait()
     count = rows // seq_len
     reps = LANES // rank_dim
-    position = lax.broadcasted_iota(jnp.int32, (rows, LANES), 0)
-    band = lax.broadcasted_iota(jnp.int32, (rows, LANES), 1) // rank_dim
-    live = jnp.zeros((rows, LANES), jnp.bool_)
+    position = lax.broadcasted_iota(jnp.int32, (rank_dim, rows), 1)
+    masked = []
     for e in range(count):
         first = e * seq_len
-        live = live | ((band == e) & (position >= first) & (position < first + lengths_ref[e]))
+        live = (position >= first) & (position < first + lengths_ref[e])
+        masked.append(jnp.where(live, feat, 0.0))
     outer = lax.dot_general(
         grad,
-        jnp.where(live, jnp.concatenate([feat] * reps, axis=1), 0.0),
-        (((1,), (0,)), ((), ())),
+        jnp.concatenate(masked, axis=0),
+        NT,
         precision=lax.Precision.HIGHEST,
         preferred_element_type=jnp.float32,
     )
-    band = band[:SUBLANES]
+    band = lax.broadcasted_iota(jnp.int32, (SUBLANES, LANES), 1) // rank_dim
     for e in range(count):
         entry = None
         for b in range(reps):
@@ -71,19 +74,16 @@
     count, seq_len, width = activations.shape
     rank_dim = project_in.shape[1]
     rows = count * seq_len
-    unit = width // 32
-    bounds = [n * unit for n in (0, 2, 6, 10, 14, 18, 22, 26, 30, 32)]
-    chunks = len(bounds) - 1
+    chunks = 8
+    bounds = [n * (width // chunks) for n in range(chunks + 1)]
     return pl.pallas_call(
         functools.partial(sketch_kernel, bounds, seq_len),
         out_shape=jax.ShapeDtypeStruct((count * SUBLANES, LANES), jnp.float32),
         in_specs=[pl.BlockSpec(memory_space=pltpu.HBM)] * 5,
         out_specs=pl.BlockSpec(memory_space=pltpu.VMEM),
         scratch_shapes=[
-            pltpu.VMEM((rows, width), jnp.bfloat16),
-            pltpu.VMEM((rows, width), jnp.bfloat16),
-            pltpu.VMEM((rank_dim, width), jnp.bfloat16),
-            pltpu.VMEM((rank_dim, width), jnp.bfloat16),
+            pltpu.VMEM((2 * rows, width), jnp.bfloat16),
+            pltpu.VMEM((2 * rank_dim, width), jnp.bfloat16),
             pltpu.SMEM((count,), jnp.int32),
             pltpu.SemaphoreType.DMA((4, chunks)),
             pltpu.SemaphoreType.DMA,
@@ -99,7 +99,7 @@
                 project_out.T,
                 lengths,
             )
-        ),
+        )
     )
 
 
@@ -186,7 +186,8 @@
     fisher_dim = SUBLANES * LANES
     gram_ref[...] = jnp.zeros(gram_ref.shape, jnp.float32)
     slot = (query_ref[...] // per_dev) ^ lax.axis_index(axis)
-    place = (gray(slot % inner) * outer + gray(slot // inner)) * per_dev + query_ref[...] % per_dev
+    n = slot // inner
+    place = (gray((slot ^ partner(n, inner)) % inner) * outer + gray(n)) * per_dev + query_ref[...] % per_dev
     rest = LANES - examples - nq
     place = jnp.concatenate(
         [jnp.zeros((1, examples), jnp.int32), place] + ([jnp.zeros((1, rest), jnp.int32)] if rest else []), axis=1
@@ -232,12 +233,17 @@
     return n ^ (n >> 1)
 
 
+def partner(n, inner):
+    return n * inner ^ gray(n) & 1
+
+
 def gather_xor(tiles, axis, size, inner):
-    def swap_all(block, unit, count):
-        order = sorted(range(1, count), key=gray)
-        return [block] + [lax.ppermute(block, axis, [(i, i ^ n * unit) for i in range(size)]) for n in order]
-
-    return swap_all(jnp.concatenate(swap_all(tiles, inner, size // inner), axis=0), 1, inner)
+    def swap(block, slot):
+        return lax.ppermute(block, axis, [(i, i ^ slot) for i in range(size)])
+
+    rows = sorted(range(1, size // inner), key=gray)
+    column = jnp.concatenate([tiles] + [swap(tiles, partner(n, inner)) for n in rows], axis=0)
+    return [column] + [swap(column, n) for n in sorted(range(1, inner), key=gray)]
 
 
 def large_scores(tiles, query_index, per_dev, axis):

time: 23.3 us -> 23.6 us (1.013)
  Pallas kernels: 7.71 us -> 8.55 us
  starting transfers between devices: 7.89 us -> 7.61 us
    pallas_call x1, Pallas kernels: 4.87 us -> 5.71 us  [sketch_rows(): pl.pallas_call(functools.partial(sketch_kernel, bounds, seq_len), out_sha...]
    ppermute x6, starting transfers between devices: 7.89 us -> 7.61 us  [swap(): return lax.ppermute(block, axis, [(i, i ^ slot) for i in range(size)])]
  transfers between devices with their start and end apart: 6 -> 6, of which waited for: 4 -> 3; matrix products, arithmetic and copies ran while one was open for 0% -> 0% of each run, Pallas kernels for 0% -> 0%
where the time goes in v18:
time: 23.6 us; the launch traced here: 23.5 us
  Pallas kernels  8.55 us (36%)
  starting transfers between devices  7.61 us (32%)
  waiting for transfers between devices  7.28 us (31%)
    ppermute x6, starting transfers between devices, swap(): return lax.ppermute(block, axis, [(i, i ^ slot) for i in range(size)])  7.61 us
    ppermute x6, waiting for transfers between devices, swap(): return lax.ppermute(block, axis, [(i, i ^ slot) for i in range(size)])  7.28 us
    pallas_call x1, Pallas kernels, sketch_rows(): pl.pallas_call(functools.partial(sketch_kernel, bounds, seq_len), out_sha...  5.71 us
    pallas_call x1, Pallas kernels, gram_scores(): pl.pallas_call(functools.partial(solve_kernel, per_dev, inner, axis), out...  2.84 us
  transfers between devices with their start and end apart: 6, of which 3 were waited for; matrix products, arithmetic and copies ran while one was open for 0% of the time, Pallas kernels for 0%

profile of v18, /device:TPU:0, one launch (start us, length us, event | category | flops | bytes accessed | tf_op | source)
XLA Modules:
  0.0 23.5 jit_solution(4020379207389380047)
XLA Ops:
  0.0 0.0 copy-start
  0.0 5.7 %shard_map.64 = f32[32,128]{1,0:T(8,128)S(1)} custom-call(bf16[256,8192]{1,0:T(8,128)(2,1)} %bitcast.6, bf16[256,8192]{1,0:T(8,128)(2,1)} %bitcast.7, bf16[32,8192]{1,0:T(8,128)(2,1)} %bitcast.8, bf16[32,8192]{1,0:T(8,128)(2,1)} %bitcast.9, s32[4]{0:T(128)} %lengths_hbm.1), custom_call_target="tpu_custom_call" | custom-call | tf_op jit(solution)/shard_map/pallas_call | solution.py:79
  5.7 3.5 %collective-permute-start.2 = (f32[32,128]{1,0:T(8,128)S(1)}, f32[32,128]{1,0:T(8,128)S(1)}, u32[]{:S(2)}, u32[]{:S(2)}) collective-permute-start(f32[32,128]{1,0:T(8,128)S(1)} %shard_map.64), channel_id=1, source_target_pairs={{0,9},{1,8},{2,11},{3,10},{4,13},{5,12},{6,15},{7,14},{8,1},{9,0},... | collective-permute-start | bytes 49160 | tf_op jit(solution)/shard_map/ppermute | solution.py:242
  9.3 1.7 %collective-permute-start.1 = (f32[32,128]{1,0:T(8,128)S(1)}, f32[32,128]{1,0:T(8,128)S(1)}, u32[]{:S(2)}, u32[]{:S(2)}) collective-permute-start(f32[32,128]{1,0:T(8,128)S(1)} %shard_map.64), channel_id=1, source_target_pairs={{0,12},{1,13},{2,14},{3,15},{4,8},{5,9},{6,10},{7,11},{8,4},{9,5},... | collective-permute-start | bytes 49160 | tf_op jit(solution)/shard_map/ppermute | solution.py:242
  10.9 0.2 collective-permute-start
  11.1 0.0 collective-permute-done.2
  11.1 3.7 %collective-permute-done.1 = f32[32,128]{1,0:T(8,128)S(1)} collective-permute-done((f32[32,128]{1,0:T(8,128)S(1)}, f32[32,128]{1,0:T(8,128)S(1)}, u32[]{:S(2)}, u32[]{:S(2)}) %collective-permute-start.1) | collective-permute-done | bytes 16416 | tf_op jit(solution)/shard_map/ppermute | solution.py:242
  14.9 0.0 collective-permute-done
  14.9 1.5 %collective-permute-start.5 = (f32[128,128]{1,0:T(8,128)S(1)}, f32[128,128]{1,0:T(8,128)S(1)}, u32[]{:S(2)}, u32[]{:S(2)}) collective-permute-start(f32[128,128]{1,0:T(8,128)S(1)} %pad_maximum_fusion.refs_0_), channel_id=1, source_target_pairs={{0,2},{1,3},{2,0},{3,1},{4,6},{5,7},{6,4},{7,5},{8,10},{9,11},{10,... | collective-permute-start | bytes 196616 | tf_op jit(solution)/shard_map/ppermute | solution.py:242
  16.4 0.0 collective-permute-start.4
  16.4 0.7 %collective-permute-start.3 = (f32[128,128]{1,0:T(8,128)S(1)}, f32[128,128]{1,0:T(8,128)S(1)}, u32[]{:S(2)}, u32[]{:S(2)}) collective-permute-start(f32[128,128]{1,0:T(8,128)S(1)} %pad_maximum_fusion.refs_0_), channel_id=1, source_target_pairs={{0,1},{1,0},{2,3},{3,2},{4,5},{5,4},{6,7},{7,6},{8,9},{9,8},{10,11... | collective-permute-start | bytes 196616 | tf_op jit(solution)/shard_map/ppermute | solution.py:242
  17.1 2.1 %collective-permute-done.5.refs_3_ = f32[128,128]{1,0:T(8,128)S(1)} collective-permute-done((f32[128,128]{1,0:T(8,128)S(1)}, f32[128,128]{1,0:T(8,128)S(1)}, u32[]{:S(2)}, u32[]{:S(2)}) %collective-permute-start.5) | collective-permute-done | bytes 65568 | tf_op jit(solution)/shard_map/ppermute | solution.py:242
  19.2 1.4 %collective-permute-done.4.refs_2_ = f32[128,128]{1,0:T(8,128)S(1)} collective-permute-done((f32[128,128]{1,0:T(8,128)S(1)}, f32[128,128]{1,0:T(8,128)S(1)}, u32[]{:S(2)}, u32[]{:S(2)}) %collective-permute-start.4) | collective-permute-done | bytes 65568 | tf_op jit(solution)/shard_map/ppermute | solution.py:242
  20.6 0.0 collective-permute-done.3.refs_1_
  20.6 0.0 copy-done
  20.6 2.8 %shard_map.65 = f32[4,16]{1,0:T(4,128)} custom-call(f32[128,128]{1,0:T(8,128)S(1)} %pad_maximum_fusion.refs_0_, f32[128,128]{1,0:T(8,128)S(1)} %collective-permute-done.3.refs_1_, f32[128,128]{1,0:T(8,128)S(1)} %collective-permute-done.4.refs_2_, f32[128,128]{1,0:T(8,128)S(1)} %collective-permute-done.5.refs_3_, s32[1,16]{1,0:T(1,128)S(1)} %bitcast.5), custom_call_target="tpu_custom_call" | custom-call | tf_op jit(solution)/shard_map/pallas_call | solution.py:222
  (1 shorter events, 0.0 us)
Async XLA Ops:
  0.0 20.6 %copy-start = (s32[16]{0:T(128)S(1)}, s32[16]{0:T(128)}, u32[]{:S(2)}) copy-start(s32[16]{0:T(128)} %param.11) | copy-start | bytes 196
  5.7 5.4 %collective-permute-start.2 = (f32[32,128]{1,0:T(8,128)S(1)}, f32[32,128]{1,0:T(8,128)S(1)}, u32[]{:S(2)}, u32[]{:S(2)}) collective-permute-start(f32[32,128]{1,0:T(8,128)S(1)} %shard_map.64), channel_id=1, source_target_pairs={{0,9},{1,8},{2,11},{3,10},{4,13},{5,12},{6,15},{7,14},{8,1},{9,0},... | collective-permute-start | bytes 49160 | tf_op jit(solution)/shard_map/ppermute | solution.py:242
  9.3 5.6 %collective-permute-start.1 = (f32[32,128]{1,0:T(8,128)S(1)}, f32[32,128]{1,0:T(8,128)S(1)}, u32[]{:S(2)}, u32[]{:S(2)}) collective-permute-start(f32[32,128]{1,0:T(8,128)S(1)} %shard_map.64), channel_id=1, source_target_pairs={{0,12},{1,13},{2,14},{3,15},{4,8},{5,9},{6,10},{7,11},{8,4},{9,5},... | collective-permute-start | bytes 49160 | tf_op jit(solution)/shard_map/ppermute | solution.py:242
  10.9 3.9 %collective-permute-start = (f32[32,128]{1,0:T(8,128)S(1)}, f32[32,128]{1,0:T(8,128)S(1)}, u32[]{:S(2)}, u32[]{:S(2)}) collective-permute-start(f32[32,128]{1,0:T(8,128)S(1)} %shard_map.64), channel_id=1, source_target_pairs={{0,5},{1,4},{2,7},{3,6},{4,1},{5,0},{6,3},{7,2},{8,13},{9,12},{10,... | collective-permute-start | bytes 49160 | tf_op jit(solution)/shard_map/ppermute | solution.py:242
  14.9 4.3 %collective-permute-start.5 = (f32[128,128]{1,0:T(8,128)S(1)}, f32[128,128]{1,0:T(8,128)S(1)}, u32[]{:S(2)}, u32[]{:S(2)}) collective-permute-start(f32[128,128]{1,0:T(8,128)S(1)} %pad_maximum_fusion.refs_0_), channel_id=1, source_target_pairs={{0,2},{1,3},{2,0},{3,1},{4,6},{5,7},{6,4},{7,5},{8,10},{9,11},{10,... | collective-permute-start | bytes 196616 | tf_op jit(solution)/shard_map/ppermute | solution.py:242
  16.4 4.2 %collective-permute-start.4 = (f32[128,128]{1,0:T(8,128)S(1)}, f32[128,128]{1,0:T(8,128)S(1)}, u32[]{:S(2)}, u32[]{:S(2)}) collective-permute-start(f32[128,128]{1,0:T(8,128)S(1)} %pad_maximum_fusion.refs_0_), channel_id=1, source_target_pairs={{0,3},{1,2},{2,1},{3,0},{4,7},{5,6},{6,5},{7,4},{8,11},{9,10},{10,... | collective-permute-start | bytes 196616 | tf_op jit(solution)/shard_map/ppermute | solution.py:242
  16.4 4.2 %collective-permute-start.3 = (f32[128,128]{1,0:T(8,128)S(1)}, f32[128,128]{1,0:T(8,128)S(1)}, u32[]{:S(2)}, u32[]{:S(2)}) collective-permute-start(f32[128,128]{1,0:T(8,128)S(1)} %pad_maximum_fusion.refs_0_), channel_id=1, source_target_pairs={{0,1},{1,0},{2,3},{3,2},{4,5},{5,4},{6,7},{7,6},{8,9},{9,8},{10,11... | collective-permute-start | bytes 196616 | tf_op jit(solution)/shard_map/ppermute | solution.py:242

commit v19 on v15

--- a/solution.py
+++ b/solution.py
@@ -115,14 +115,17 @@
 
     def factor(columns, first):
         p = {(i, j): row_of(columns[j], first + i) for j in range(step) for i in range(j + 1)}
-        lower, inverse = {}, []
-        for k in range(step):
-            inverse.append(pl.reciprocal(p[k, k]))
-            for i in range(k + 1, step):
-                lower[i, k] = p[k, i] * inverse[k]
-            for i in range(k + 1, step):
-                for j in range(i, step):
-                    p[i, j] = p[i, j] - lower[i, k] * p[k, j]
+        lower, inverse = {}, [None] * step
+        for k in range(0, step, 2):
+            a, b, c = p[k, k], p[k, k + 1], p[k + 1, k + 1]
+            inverse[k] = pl.reciprocal(a)
+            inverse[k + 1] = a * pl.reciprocal(a * c - b * b)
+            for m in (k, k + 1):
+                for i in range(m + 1, step):
+                    lower[i, m] = p[m, i] * inverse[m]
+                for i in range(m + 1, step):
+                    for j in range(i, step):
+                        p[i, j] = p[i, j] - lower[i, m] * p[m, j]
         return lower, inverse
 
     def forward(lower, parts):
@@ -186,7 +189,8 @@
     fisher_dim = SUBLANES * LANES
     gram_ref[...] = jnp.zeros(gram_ref.shape, jnp.float32)
     slot = (query_ref[...] // per_dev) ^ lax.axis_index(axis)
-    place = (gray(slot % inner) * outer + gray(slot // inner)) * per_dev + query_ref[...] % per_dev
+    n = slot // inner
+    place = (gray((slot ^ partner(n, inner)) % inner) * outer + gray(n)) * per_dev + query_ref[...] % per_dev
     rest = LANES - examples - nq
     place = jnp.concatenate(
         [jnp.zeros((1, examples), jnp.int32), place] + ([jnp.zeros((1, rest), jnp.int32)] if rest else []), axis=1
@@ -232,12 +236,17 @@
     return n ^ (n >> 1)
 
 
+def partner(n, inner):
+    return n * inner ^ gray(n) & 1
+
+
 def gather_xor(tiles, axis, size, inner):
-    def swap_all(block, unit, count):
-        order = sorted(range(1, count), key=gray)
-        return [block] + [lax.ppermute(block, axis, [(i, i ^ n * unit) for i in range(size)]) for n in order]
-
-    return swap_all(jnp.concatenate(swap_all(tiles, inner, size // inner), axis=0), 1, inner)
+    def swap(block, slot):
+        return lax.ppermute(block, axis, [(i, i ^ slot) for i in range(size)])
+
+    rows = sorted(range(1, size // inner), key=gray)
+    column = jnp.concatenate([tiles] + [swap(tiles, partner(n, inner)) for n in rows], axis=0)
+    return [column] + [swap(column, n) for n in sorted(range(1, inner), key=gray)]
 
 
 def large_scores(tiles, query_index, per_dev, axis):

time: 23.3 us -> 22.7 us (0.974)
  starting transfers between devices: 7.89 us -> 7.61 us
    ppermute x6, starting transfers between devices: 7.89 us -> 7.61 us  [swap(): return lax.ppermute(block, axis, [(i, i ^ slot) for i in range(size)])]
  transfers between devices with their start and end apart: 6 -> 6, of which waited for: 4 -> 3; matrix products, arithmetic and copies ran while one was open for 0% -> 0% of each run, Pallas kernels for 0% -> 0%
where the time goes in v19:
time: 22.7 us; the launch traced here: 22.5 us
  Pallas kernels  7.61 us (34%)
  starting transfers between devices  7.61 us (34%)
  waiting for transfers between devices  7.28 us (32%)
    ppermute x6, starting transfers between devices, swap(): return lax.ppermute(block, axis, [(i, i ^ slot) for i in range(size)])  7.61 us
    ppermute x6, waiting for transfers between devices, swap(): return lax.ppermute(block, axis, [(i, i ^ slot) for i in range(size)])  7.28 us
    pallas_call x1, Pallas kernels, sketch_rows(): pl.pallas_call(functools.partial(sketch_kernel, bounds, seq_len), out_sha...  4.87 us
    pallas_call x1, Pallas kernels, gram_scores(): pl.pallas_call(functools.partial(solve_kernel, per_dev, inner, axis), out...  2.74 us
  transfers between devices with their start and end apart: 6, of which 3 were waited for; matrix products, arithmetic and copies ran while one was open for 0% of the time, Pallas kernels for 0%

profile of v19, /device:TPU:0, one launch (start us, length us, event | category | flops | bytes accessed | tf_op | source)
XLA Modules:
  0.0 22.5 jit_solution(2128816389907121266)
XLA Ops:
  0.0 0.0 copy-start
  0.0 4.9 %shard_map.64 = f32[32,128]{1,0:T(8,128)S(1)} custom-call(bf16[256,8192]{1,0:T(8,128)(2,1)} %bitcast.6, bf16[256,8192]{1,0:T(8,128)(2,1)} %bitcast.7, bf16[32,8192]{1,0:T(8,128)(2,1)} %bitcast.8, bf16[32,8192]{1,0:T(8,128)(2,1)} %bitcast.9, s32[4]{0:T(128)} %lengths_hbm.1), custom_call_target="tpu_custom_call" | custom-call | tf_op jit(solution)/shard_map/pallas_call | solution.py:77
  4.9 3.5 %collective-permute-start.2 = (f32[32,128]{1,0:T(8,128)S(1)}, f32[32,128]{1,0:T(8,128)S(1)}, u32[]{:S(2)}, u32[]{:S(2)}) collective-permute-start(f32[32,128]{1,0:T(8,128)S(1)} %shard_map.64), channel_id=1, source_target_pairs={{0,9},{1,8},{2,11},{3,10},{4,13},{5,12},{6,15},{7,14},{8,1},{9,0},... | collective-permute-start | bytes 49160 | tf_op jit(solution)/shard_map/ppermute | solution.py:245
  8.4 1.7 %collective-permute-start.1 = (f32[32,128]{1,0:T(8,128)S(1)}, f32[32,128]{1,0:T(8,128)S(1)}, u32[]{:S(2)}, u32[]{:S(2)}) collective-permute-start(f32[32,128]{1,0:T(8,128)S(1)} %shard_map.64), channel_id=1, source_target_pairs={{0,12},{1,13},{2,14},{3,15},{4,8},{5,9},{6,10},{7,11},{8,4},{9,5},... | collective-permute-start | bytes 49160 | tf_op jit(solution)/shard_map/ppermute | solution.py:245
  10.1 0.2 collective-permute-start
  10.3 0.0 collective-permute-done.2
  10.3 3.7 %collective-permute-done.1 = f32[32,128]{1,0:T(8,128)S(1)} collective-permute-done((f32[32,128]{1,0:T(8,128)S(1)}, f32[32,128]{1,0:T(8,128)S(1)}, u32[]{:S(2)}, u32[]{:S(2)}) %collective-permute-start.1) | collective-permute-done | bytes 16416 | tf_op jit(solution)/shard_map/ppermute | solution.py:245
  14.0 0.0 collective-permute-done
  14.0 1.6 %collective-permute-start.5 = (f32[128,128]{1,0:T(8,128)S(1)}, f32[128,128]{1,0:T(8,128)S(1)}, u32[]{:S(2)}, u32[]{:S(2)}) collective-permute-start(f32[128,128]{1,0:T(8,128)S(1)} %pad_maximum_fusion.refs_0_), channel_id=1, source_target_pairs={{0,2},{1,3},{2,0},{3,1},{4,6},{5,7},{6,4},{7,5},{8,10},{9,11},{10,... | collective-permute-start | bytes 196616 | tf_op jit(solution)/shard_map/ppermute | solution.py:245
  15.6 0.0 collective-permute-start.4
  15.6 0.6 %collective-permute-start.3 = (f32[128,128]{1,0:T(8,128)S(1)}, f32[128,128]{1,0:T(8,128)S(1)}, u32[]{:S(2)}, u32[]{:S(2)}) collective-permute-start(f32[128,128]{1,0:T(8,128)S(1)} %pad_maximum_fusion.refs_0_), channel_id=1, source_target_pairs={{0,1},{1,0},{2,3},{3,2},{4,5},{5,4},{6,7},{7,6},{8,9},{9,8},{10,11... | collective-permute-start | bytes 196616 | tf_op jit(solution)/shard_map/ppermute | solution.py:245
  16.2 2.1 %collective-permute-done.5.refs_3_ = f32[128,128]{1,0:T(8,128)S(1)} collective-permute-done((f32[128,128]{1,0:T(8,128)S(1)}, f32[128,128]{1,0:T(8,128)S(1)}, u32[]{:S(2)}, u32[]{:S(2)}) %collective-permute-start.5) | collective-permute-done | bytes 65568 | tf_op jit(solution)/shard_map/ppermute | solution.py:245
  18.4 1.4 %collective-permute-done.4.refs_2_ = f32[128,128]{1,0:T(8,128)S(1)} collective-permute-done((f32[128,128]{1,0:T(8,128)S(1)}, f32[128,128]{1,0:T(8,128)S(1)}, u32[]{:S(2)}, u32[]{:S(2)}) %collective-permute-start.4) | collective-permute-done | bytes 65568 | tf_op jit(solution)/shard_map/ppermute | solution.py:245
  19.8 0.0 collective-permute-done.3.refs_1_
  19.8 0.0 copy-done
  19.8 2.7 %shard_map.65 = f32[4,16]{1,0:T(4,128)} custom-call(f32[128,128]{1,0:T(8,128)S(1)} %pad_maximum_fusion.refs_0_, f32[128,128]{1,0:T(8,128)S(1)} %collective-permute-done.3.refs_1_, f32[128,128]{1,0:T(8,128)S(1)} %collective-permute-done.4.refs_2_, f32[128,128]{1,0:T(8,128)S(1)} %collective-permute-done.5.refs_3_, s32[1,16]{1,0:T(1,128)S(1)} %bitcast.5), custom_call_target="tpu_custom_call" | custom-call | tf_op jit(solution)/shard_map/pallas_call | solution.py:225
  (1 shorter events, 0.0 us)
Async XLA Ops:
  0.0 19.8 %copy-start = (s32[16]{0:T(128)S(1)}, s32[16]{0:T(128)}, u32[]{:S(2)}) copy-start(s32[16]{0:T(128)} %param.11) | copy-start | bytes 196
  4.9 5.4 %collective-permute-start.2 = (f32[32,128]{1,0:T(8,128)S(1)}, f32[32,128]{1,0:T(8,128)S(1)}, u32[]{:S(2)}, u32[]{:S(2)}) collective-permute-start(f32[32,128]{1,0:T(8,128)S(1)} %shard_map.64), channel_id=1, source_target_pairs={{0,9},{1,8},{2,11},{3,10},{4,13},{5,12},{6,15},{7,14},{8,1},{9,0},... | collective-permute-start | bytes 49160 | tf_op jit(solution)/shard_map/ppermute | solution.py:245
  8.4 5.6 %collective-permute-start.1 = (f32[32,128]{1,0:T(8,128)S(1)}, f32[32,128]{1,0:T(8,128)S(1)}, u32[]{:S(2)}, u32[]{:S(2)}) collective-permute-start(f32[32,128]{1,0:T(8,128)S(1)} %shard_map.64), channel_id=1, source_target_pairs={{0,12},{1,13},{2,14},{3,15},{4,8},{5,9},{6,10},{7,11},{8,4},{9,5},... | collective-permute-start | bytes 49160 | tf_op jit(solution)/shard_map/ppermute | solution.py:245
  10.1 3.9 %collective-permute-start = (f32[32,128]{1,0:T(8,128)S(1)}, f32[32,128]{1,0:T(8,128)S(1)}, u32[]{:S(2)}, u32[]{:S(2)}) collective-permute-start(f32[32,128]{1,0:T(8,128)S(1)} %shard_map.64), channel_id=1, source_target_pairs={{0,5},{1,4},{2,7},{3,6},{4,1},{5,0},{6,3},{7,2},{8,13},{9,12},{10,... | collective-permute-start | bytes 49160 | tf_op jit(solution)/shard_map/ppermute | solution.py:245
  14.0 4.3 %collective-permute-start.5 = (f32[128,128]{1,0:T(8,128)S(1)}, f32[128,128]{1,0:T(8,128)S(1)}, u32[]{:S(2)}, u32[]{:S(2)}) collective-permute-start(f32[128,128]{1,0:T(8,128)S(1)} %pad_maximum_fusion.refs_0_), channel_id=1, source_target_pairs={{0,2},{1,3},{2,0},{3,1},{4,6},{5,7},{6,4},{7,5},{8,10},{9,11},{10,... | collective-permute-start | bytes 196616 | tf_op jit(solution)/shard_map/ppermute | solution.py:245
  15.6 4.2 %collective-permute-start.4 = (f32[128,128]{1,0:T(8,128)S(1)}, f32[128,128]{1,0:T(8,128)S(1)}, u32[]{:S(2)}, u32[]{:S(2)}) collective-permute-start(f32[128,128]{1,0:T(8,128)S(1)} %pad_maximum_fusion.refs_0_), channel_id=1, source_target_pairs={{0,3},{1,2},{2,1},{3,0},{4,7},{5,6},{6,5},{7,4},{8,11},{9,10},{10,... | collective-permute-start | bytes 196616 | tf_op jit(solution)/shard_map/ppermute | solution.py:245
  15.6 4.2 %collective-permute-start.3 = (f32[128,128]{1,0:T(8,128)S(1)}, f32[128,128]{1,0:T(8,128)S(1)}, u32[]{:S(2)}, u32[]{:S(2)}) collective-permute-start(f32[128,128]{1,0:T(8,128)S(1)} %pad_maximum_fusion.refs_0_), channel_id=1, source_target_pairs={{0,1},{1,0},{2,3},{3,2},{4,5},{5,4},{6,7},{7,6},{8,9},{9,8},{10,11... | collective-permute-start | bytes 196616 | tf_op jit(solution)/shard_map/ppermute | solution.py:245

commit v20 on v19

--- a/solution.py
+++ b/solution.py
@@ -8,6 +8,12 @@
 from jax.sharding import PartitionSpec as P
 
 damp_ratio = 0.5
+ROUTES = (
+    ((1, 0), (3, 1), (2, 0), (0, 0)),
+    ((2, 1), (1, 0), (0, 0), (3, 0)),
+    ((3, 1), (0, 0), (1, 0), (2, 0)),
+    ((0, 0), (2, 0), (3, 1), (1, 0)),
+)
 LANES = 128
 SUBLANES = 8
 NT = (((1,), (1,)), ((), ()))
@@ -183,23 +189,26 @@
 def solve_kernel(per_dev, inner, axis, *refs):
     tiles, (query_ref, scores_ref, gram_ref) = refs[:-3], refs[-3:]
     nq = query_ref.shape[1]
-    part = tiles[0].shape[0] // SUBLANES
-    examples = len(tiles) * part
-    outer = examples // (inner * per_dev)
+    held = tiles[0].shape[0] // SUBLANES
+    examples = len(tiles) * held
     fisher_dim = SUBLANES * LANES
     gram_ref[...] = jnp.zeros(gram_ref.shape, jnp.float32)
-    slot = (query_ref[...] // per_dev) ^ lax.axis_index(axis)
-    n = slot // inner
-    place = (gray((slot ^ partner(n, inner)) % inner) * outer + gray(n)) * per_dev + query_ref[...] % per_dev
+    mine = lax.axis_index(axis)
+    device = query_ref[...] // per_dev
+    part = part_of(device // inner, mine // inner)
+    place = gray((device ^ mine ^ (part & 1)) % inner) * len(ROUTES) + (part >> 1)
+    place = place * per_dev + query_ref[...] % per_dev
     rest = LANES - examples - nq
     place = jnp.concatenate(
         [jnp.zeros((1, examples), jnp.int32), place] + ([jnp.zeros((1, rest), jnp.int32)] if rest else []), axis=1
     )
     lane = lax.broadcasted_iota(jnp.int32, (SUBLANES, LANES), 1)
-    source = jnp.where(lane < examples, lane, jnp.broadcast_to(place, lane.shape))
+    own = part_of(mine // inner, mine // inner) >> 1
+    source = jnp.where(lane < len(ROUTES) * per_dev, lane ^ (own * per_dev), lane)
+    source = jnp.where(lane < examples, source, jnp.broadcast_to(place, lane.shape))
     sketches = jnp.concatenate(
         [
-            jnp.concatenate([tile[pl.ds(s, part, stride=SUBLANES)] for tile in tiles], axis=0)
+            jnp.concatenate([tile[pl.ds(s, held, stride=SUBLANES)] for tile in tiles], axis=0)
             for s in range(SUBLANES)
         ],
         axis=1,
@@ -210,7 +219,12 @@
     row = lax.broadcasted_iota(jnp.int32, (SUBLANES, LANES), 0)
     system = []
     for first in range(0, examples, SUBLANES):
-        tile = jnp.take_along_axis(gram_ref[first : first + SUBLANES], source, axis=1) * scale
+        if first < len(ROUTES) * per_dev:
+            tile = gram_ref[pl.ds(pl.multiple_of(first ^ (own // 2 * SUBLANES), SUBLANES), SUBLANES)]
+            tile = jnp.where(own % 2 == 1, pltpu.roll(tile, per_dev, 0), tile)
+        else:
+            tile = gram_ref[first : first + SUBLANES]
+        tile = jnp.take_along_axis(tile, source, axis=1) * scale
         system.append(jnp.where(lane == row + first, tile + damp_ratio / fisher_dim, tile))
     solved = solve_first(system)
     scores = solved[0]
@@ -236,17 +250,23 @@
     return n ^ (n >> 1)
 
 
-def partner(n, inner):
-    return n * inner ^ gray(n) & 1
-
-
-def gather_xor(tiles, axis, size, inner):
-    def swap(block, slot):
-        return lax.ppermute(block, axis, [(i, i ^ slot) for i in range(size)])
-
-    rows = sorted(range(1, size // inner), key=gray)
-    column = jnp.concatenate([tiles] + [swap(tiles, partner(n, inner)) for n in rows], axis=0)
-    return [column] + [swap(column, n) for n in sorted(range(1, inner), key=gray)]
+def gather_rows(tiles, axis, size, inner):
+    rows = range(size // inner)
+    parts = []
+    for routes in ROUTES:
+        pairs = [(z * inner + k, routes[z][0] * inner + (k ^ routes[z][1])) for z in rows for k in range(inner)]
+        parts.append(lax.ppermute(tiles, axis, pairs))
+    column = jnp.concatenate(parts[::-1], axis=0)
+    order = sorted(range(1, inner), key=gray)
+    return [column] + [lax.ppermute(column, axis, [(i, i ^ n) for i in range(size)]) for n in order]
+
+
+def part_of(row, mine):
+    found = jnp.zeros_like(row)
+    for n, routes in enumerate(ROUTES):
+        for z, (target, flip) in enumerate(routes):
+            found = jnp.where((row == z) & (mine == target), (len(ROUTES) - 1 - n) * 2 + flip, found)
+    return found
 
 
 def large_scores(tiles, query_index, per_dev, axis):
@@ -266,9 +286,9 @@
     per_dev = activations.shape[0]
     size = lax.axis_size("dp")
     tiles = sketch_rows(activations, out_grads, project_in, project_out, lengths)
-    if size * per_dev + query_index.shape[0] <= LANES:
-        inner = 4
-        return gram_scores(gather_xor(tiles, "dp", size, inner), query_index, per_dev, inner, "dp")
+    inner = 4
+    if size == len(ROUTES) * inner and size * per_dev + query_index.shape[0] <= LANES:
+        return gram_scores(gather_rows(tiles, "dp", size, inner), query_index, per_dev, inner, "dp")
     return large_scores(lax.all_gather(tiles, "dp", axis=0, tiled=True), query_index, per_dev, "dp")
 
 

time: 22.7 us -> 28.5 us (1.26)
  starting transfers between devices: 7.61 us -> 12.6 us
  waiting for transfers between devices: 7.28 us -> 8.04 us
    ppermute x6 -> x7, starting transfers between devices: 7.61 us -> 12.6 us  [the longest x4 10.4 us: gather_rows(): parts.append(lax.ppermute(tiles, axis, pairs))]
    ppermute x6 -> x7, waiting for transfers between devices: 7.28 us -> 8.04 us  [the longest x4 4.51 us: gather_rows(): parts.append(lax.ppermute(tiles, axis, pairs))]
  transfers between devices with their start and end apart: 6 -> 7, of which waited for: 3 -> 4; matrix products, arithmetic and copies ran while one was open for 0% -> 0% of each run, Pallas kernels for 0% -> 0%
where the time goes in v20:
time: 28.5 us; the launch traced here: 28.3 us
  starting transfers between devices  12.6 us (44%)
  waiting for transfers between devices  8.04 us (28%)
  Pallas kernels  7.58 us (27%)
    ppermute x4, starting transfers between devices, gather_rows(): parts.append(lax.ppermute(tiles, axis, pairs))  10.4 us
    pallas_call x1, Pallas kernels, sketch_rows(): pl.pallas_call(functools.partial(sketch_kernel, bounds, seq_len), out_sha...  4.87 us
    ppermute x4, waiting for transfers between devices, gather_rows(): parts.append(lax.ppermute(tiles, axis, pairs))  4.51 us
    ppermute x3, waiting for transfers between devices, gather_rows(): lax.ppermute(column, axis, [(i, i ^ n) for i in range(size)])  3.53 us
    pallas_call x1, Pallas kernels, gram_scores(): pl.pallas_call(functools.partial(solve_kernel, per_dev, inner, axis), out...  2.71 us
    ppermute x3, starting transfers between devices, gather_rows(): lax.ppermute(column, axis, [(i, i ^ n) for i in range(size)])  2.21 us
  transfers between devices with their start and end apart: 7, of which 4 were waited for; matrix products, arithmetic and copies ran while one was open for 0% of the time, Pallas kernels for 0%

profile of v20, /device:TPU:0, one launch (start us, length us, event | category | flops | bytes accessed | tf_op | source)
XLA Modules:
  0.0 28.3 jit_solution(11212476380162529473)
XLA Ops:
  0.0 0.0 copy-start
  0.0 4.9 %shard_map.64 = f32[32,128]{1,0:T(8,128)S(1)} custom-call(bf16[256,8192]{1,0:T(8,128)(2,1)} %bitcast.6, bf16[256,8192]{1,0:T(8,128)(2,1)} %bitcast.7, bf16[32,8192]{1,0:T(8,128)(2,1)} %bitcast.8, bf16[32,8192]{1,0:T(8,128)(2,1)} %bitcast.9, s32[4]{0:T(128)} %lengths_hbm.1), custom_call_target="tpu_custom_call" | custom-call | tf_op jit(solution)/shard_map/pallas_call | solution.py:83
  4.9 0.7 %collective-permute-start = (f32[32,128]{1,0:T(8,128)S(1)}, f32[32,128]{1,0:T(8,128)S(1)}, u32[]{:S(2)}, u32[]{:S(2)}) collective-permute-start(f32[32,128]{1,0:T(8,128)S(1)} %shard_map.64), channel_id=1, source_target_pairs={{0,0},{1,1},{2,2},{3,3},{4,8},{5,9},{6,10},{7,11},{8,13},{9,12},{1... | collective-permute-start | bytes 49160 | tf_op jit(solution)/shard_map/ppermute | solution.py:258
  5.5 7.8 %collective-permute-start.3 = (f32[32,128]{1,0:T(8,128)S(1)}, f32[32,128]{1,0:T(8,128)S(1)}, u32[]{:S(2)}, u32[]{:S(2)}) collective-permute-start(f32[32,128]{1,0:T(8,128)S(1)} %shard_map.64), channel_id=1, source_target_pairs={{0,4},{1,5},{2,6},{3,7},{4,13},{5,12},{6,15},{7,14},{8,8},{9,9},{1... | collective-permute-start | bytes 49160 | tf_op jit(solution)/shard_map/ppermute | solution.py:258
  13.3 1.9 %collective-permute-start.2 = (f32[32,128]{1,0:T(8,128)S(1)}, f32[32,128]{1,0:T(8,128)S(1)}, u32[]{:S(2)}, u32[]{:S(2)}) collective-permute-start(f32[32,128]{1,0:T(8,128)S(1)} %shard_map.64), channel_id=1, source_target_pairs={{0,9},{1,8},{2,11},{3,10},{4,4},{5,5},{6,6},{7,7},{8,0},{9,1},{10,... | collective-permute-start | bytes 49160 | tf_op jit(solution)/shard_map/ppermute | solution.py:258
  15.2 0.1 collective-permute-start.1
  15.3 0.0 collective-permute-done
  15.3 3.7 %collective-permute-done.1 = f32[32,128]{1,0:T(8,128)S(1)} collective-permute-done((f32[32,128]{1,0:T(8,128)S(1)}, f32[32,128]{1,0:T(8,128)S(1)}, u32[]{:S(2)}, u32[]{:S(2)}) %collective-permute-start.1) | collective-permute-done | bytes 16416 | tf_op jit(solution)/shard_map/ppermute | solution.py:258
  19.0 0.8 %collective-permute-done.2 = f32[32,128]{1,0:T(8,128)S(1)} collective-permute-done((f32[32,128]{1,0:T(8,128)S(1)}, f32[32,128]{1,0:T(8,128)S(1)}, u32[]{:S(2)}, u32[]{:S(2)}) %collective-permute-start.2) | collective-permute-done | bytes 16416 | tf_op jit(solution)/shard_map/ppermute | solution.py:258
  19.8 0.0 collective-permute-done.3
  19.9 1.6 %collective-permute-start.6 = (f32[128,128]{1,0:T(8,128)S(1)}, f32[128,128]{1,0:T(8,128)S(1)}, u32[]{:S(2)}, u32[]{:S(2)}) collective-permute-start(f32[128,128]{1,0:T(8,128)S(1)} %constant_dynamic-update-slice_fusion.refs_0_), channel_id=1, source_target_pairs={{0,2},{1,3},{2,0},{3,1},{4,6},{5,7},{6,4},{7,5},{8,10},{9,11},{10,... | collective-permute-start | bytes 196616 | tf_op jit(solution)/shard_map/ppermute | solution.py:261
  21.4 0.0 collective-permute-start.5
  21.4 0.6 %collective-permute-start.4 = (f32[128,128]{1,0:T(8,128)S(1)}, f32[128,128]{1,0:T(8,128)S(1)}, u32[]{:S(2)}, u32[]{:S(2)}) collective-permute-start(f32[128,128]{1,0:T(8,128)S(1)} %constant_dynamic-update-slice_fusion.refs_0_), channel_id=1, source_target_pairs={{0,1},{1,0},{2,3},{3,2},{4,5},{5,4},{6,7},{7,6},{8,9},{9,8},{10,11... | collective-permute-start | bytes 196616 | tf_op jit(solution)/shard_map/ppermute | solution.py:261
  22.1 2.1 %collective-permute-done.6.refs_3_ = f32[128,128]{1,0:T(8,128)S(1)} collective-permute-done((f32[128,128]{1,0:T(8,128)S(1)}, f32[128,128]{1,0:T(8,128)S(1)}, u32[]{:S(2)}, u32[]{:S(2)}) %collective-permute-start.6) | collective-permute-done | bytes 65568 | tf_op jit(solution)/shard_map/ppermute | solution.py:261
  24.2 1.4 %collective-permute-done.5.refs_2_ = f32[128,128]{1,0:T(8,128)S(1)} collective-permute-done((f32[128,128]{1,0:T(8,128)S(1)}, f32[128,128]{1,0:T(8,128)S(1)}, u32[]{:S(2)}, u32[]{:S(2)}) %collective-permute-start.5) | collective-permute-done | bytes 65568 | tf_op jit(solution)/shard_map/ppermute | solution.py:261
  25.6 0.0 collective-permute-done.4.refs_1_
  25.6 0.0 copy-done
  25.6 2.7 %shard_map.65 = f32[4,16]{1,0:T(4,128)} custom-call(f32[128,128]{1,0:T(8,128)S(1)} %constant_dynamic-update-slice_fusion.refs_0_, f32[128,128]{1,0:T(8,128)S(1)} %collective-permute-done.4.refs_1_, f32[128,128]{1,0:T(8,128)S(1)} %collective-permute-done.5.refs_2_, f32[128,128]{1,0:T(8,128)S(1)} %collective-permute-done.6.refs_3_, s32[1,16]{1,0:T(1,128)S(1)} %bitcast.5), custom_call_target="tpu_custom_call" | custom-call | tf_op jit(solution)/shard_map/pallas_call | solution.py:239
  (4 shorter events, 0.0 us)
Async XLA Ops:
  0.0 25.6 %copy-start = (s32[16]{0:T(128)S(1)}, s32[16]{0:T(128)}, u32[]{:S(2)}) copy-start(s32[16]{0:T(128)} %param.11) | copy-start | bytes 196
  4.9 10.4 %collective-permute-start = (f32[32,128]{1,0:T(8,128)S(1)}, f32[32,128]{1,0:T(8,128)S(1)}, u32[]{:S(2)}, u32[]{:S(2)}) collective-permute-start(f32[32,128]{1,0:T(8,128)S(1)} %shard_map.64), channel_id=1, source_target_pairs={{0,0},{1,1},{2,2},{3,3},{4,8},{5,9},{6,10},{7,11},{8,13},{9,12},{1... | collective-permute-start | bytes 49160 | tf_op jit(solution)/shard_map/ppermute | solution.py:258
  5.5 14.3 %collective-permute-start.3 = (f32[32,128]{1,0:T(8,128)S(1)}, f32[32,128]{1,0:T(8,128)S(1)}, u32[]{:S(2)}, u32[]{:S(2)}) collective-permute-start(f32[32,128]{1,0:T(8,128)S(1)} %shard_map.64), channel_id=1, source_target_pairs={{0,4},{1,5},{2,6},{3,7},{4,13},{5,12},{6,15},{7,14},{8,8},{9,9},{1... | collective-permute-start | bytes 49160 | tf_op jit(solution)/shard_map/ppermute | solution.py:258
  13.3 6.5 %collective-permute-start.2 = (f32[32,128]{1,0:T(8,128)S(1)}, f32[32,128]{1,0:T(8,128)S(1)}, u32[]{:S(2)}, u32[]{:S(2)}) collective-permute-start(f32[32,128]{1,0:T(8,128)S(1)} %shard_map.64), channel_id=1, source_target_pairs={{0,9},{1,8},{2,11},{3,10},{4,4},{5,5},{6,6},{7,7},{8,0},{9,1},{10,... | collective-permute-start | bytes 49160 | tf_op jit(solution)/shard_map/ppermute | solution.py:258
  15.2 3.8 %collective-permute-start.1 = (f32[32,128]{1,0:T(8,128)S(1)}, f32[32,128]{1,0:T(8,128)S(1)}, u32[]{:S(2)}, u32[]{:S(2)}) collective-permute-start(f32[32,128]{1,0:T(8,128)S(1)} %shard_map.64), channel_id=1, source_target_pairs={{0,13},{1,12},{2,15},{3,14},{4,0},{5,1},{6,2},{7,3},{8,4},{9,5},{1... | collective-permute-start | bytes 49160 | tf_op jit(solution)/shard_map/ppermute | solution.py:258
  19.9 4.3 %collective-permute-start.6 = (f32[128,128]{1,0:T(8,128)S(1)}, f32[128,128]{1,0:T(8,128)S(1)}, u32[]{:S(2)}, u32[]{:S(2)}) collective-permute-start(f32[128,128]{1,0:T(8,128)S(1)} %constant_dynamic-update-slice_fusion.refs_0_), channel_id=1, source_target_pairs={{0,2},{1,3},{2,0},{3,1},{4,6},{5,7},{6,4},{7,5},{8,10},{9,11},{10,... | collective-permute-start | bytes 196616 | tf_op jit(solution)/shard_map/ppermute | solution.py:261
  21.4 4.2 %collective-permute-start.5 = (f32[128,128]{1,0:T(8,128)S(1)}, f32[128,128]{1,0:T(8,128)S(1)}, u32[]{:S(2)}, u32[]{:S(2)}) collective-permute-start(f32[128,128]{1,0:T(8,128)S(1)} %constant_dynamic-update-slice_fusion.refs_0_), channel_id=1, source_target_pairs={{0,3},{1,2},{2,1},{3,0},{4,7},{5,6},{6,5},{7,4},{8,11},{9,10},{10,... | collective-permute-start | bytes 196616 | tf_op jit(solution)/shard_map/ppermute | solution.py:261
  21.4 4.2 %collective-permute-start.4 = (f32[128,128]{1,0:T(8,128)S(1)}, f32[128,128]{1,0:T(8,128)S(1)}, u32[]{:S(2)}, u32[]{:S(2)}) collective-permute-start(f32[128,128]{1,0:T(8,128)S(1)} %constant_dynamic-update-slice_fusion.refs_0_), channel_id=1, source_target_pairs={{0,1},{1,0},{2,3},{3,2},{4,5},{5,4},{6,7},{7,6},{8,9},{9,8},{10,11... | collective-permute-start | bytes 196616 | tf_op jit(solution)/shard_map/ppermute | solution.py:261

commit v21 on v20

--- a/solution.py
+++ b/solution.py
@@ -256,7 +256,12 @@
     for routes in ROUTES:
         pairs = [(z * inner + k, routes[z][0] * inner + (k ^ routes[z][1])) for z in rows for k in range(inner)]
         parts.append(lax.ppermute(tiles, axis, pairs))
-    column = jnp.concatenate(parts[::-1], axis=0)
+    block = tiles.shape[0]
+    last = len(parts) - 1
+    column = functools.reduce(
+        jnp.add,
+        [jnp.pad(parts[last - n], ((n * block, (last - n) * block), (0, 0))) for n in range(len(parts))],
+    )
     order = sorted(range(1, inner), key=gray)
     return [column] + [lax.ppermute(column, axis, [(i, i ^ n) for i in range(size)]) for n in order]
 

time: 28.5 us -> 26 us (0.912)
  the two profiles are of different devices: /device:TPU:0 before, /device:TPU:9 now
where the time goes in v21:
time: 26 us; the launch traced here: 25.8 us
  starting transfers between devices  12.6 us (48%)
  Pallas kernels  7.58 us (29%)
  waiting for transfers between devices  5.58 us (21%)
    ppermute x4, starting transfers between devices, gather_rows(): parts.append(lax.ppermute(tiles, axis, pairs))  8.86 us
    pallas_call x1, Pallas kernels, sketch_rows(): pl.pallas_call(functools.partial(sketch_kernel, bounds, seq_len), out_sha...  4.87 us
    ppermute x3, starting transfers between devices, gather_rows(): lax.ppermute(column, axis, [(i, i ^ n) for i in range(size)])  3.7 us
    ppermute x3, waiting for transfers between devices, gather_rows(): lax.ppermute(column, axis, [(i, i ^ n) for i in range(size)])  3.44 us
    pallas_call x1, Pallas kernels, gram_scores(): pl.pallas_call(functools.partial(solve_kernel, per_dev, inner, axis), out...  2.71 us
    ppermute x4, waiting for transfers between devices, gather_rows(): parts.append(lax.ppermute(tiles, axis, pairs))  2.15 us
  transfers between devices with their start and end apart: 7, of which 2 were waited for; matrix products, arithmetic and copies ran while one was open for 0% of the time, Pallas kernels for 0%

profile of v21, /device:TPU:9, one launch (start us, length us, event | category | flops | bytes accessed | tf_op | source)
XLA Modules:
  0.0 25.8 jit_solution(11748774260597419796)
XLA Ops:
  0.0 0.0 copy-start
  0.0 4.9 %shard_map.64 = f32[32,128]{1,0:T(8,128)S(1)} custom-call(bf16[256,8192]{1,0:T(8,128)(2,1)} %bitcast.6, bf16[256,8192]{1,0:T(8,128)(2,1)} %bitcast.7, bf16[32,8192]{1,0:T(8,128)(2,1)} %bitcast.8, bf16[32,8192]{1,0:T(8,128)(2,1)} %bitcast.9, s32[4]{0:T(128)} %lengths_hbm.1), custom_call_target="tpu_custom_call" | custom-call | tf_op jit(solution)/shard_map/pallas_call | solution.py:83
  4.9 4.8 %collective-permute-start.3 = (f32[32,128]{1,0:T(8,128)S(1)}, f32[32,128]{1,0:T(8,128)S(1)}, u32[]{:S(2)}, u32[]{:S(2)}) collective-permute-start(f32[32,128]{1,0:T(8,128)S(1)} %shard_map.64), channel_id=1, source_target_pairs={{0,4},{1,5},{2,6},{3,7},{4,13},{5,12},{6,15},{7,14},{8,8},{9,9},{1... | collective-permute-start | bytes 49160 | tf_op jit(solution)/shard_map/ppermute | solution.py:258
  9.7 0.7 %collective-permute-start.2 = (f32[32,128]{1,0:T(8,128)S(1)}, f32[32,128]{1,0:T(8,128)S(1)}, u32[]{:S(2)}, u32[]{:S(2)}) collective-permute-start(f32[32,128]{1,0:T(8,128)S(1)} %shard_map.64), channel_id=1, source_target_pairs={{0,9},{1,8},{2,11},{3,10},{4,4},{5,5},{6,6},{7,7},{8,0},{9,1},{10,... | collective-permute-start | bytes 49160 | tf_op jit(solution)/shard_map/ppermute | solution.py:258
  10.3 0.2 collective-permute-start.1
  10.6 3.2 %collective-permute-start = (f32[32,128]{1,0:T(8,128)S(1)}, f32[32,128]{1,0:T(8,128)S(1)}, u32[]{:S(2)}, u32[]{:S(2)}) collective-permute-start(f32[32,128]{1,0:T(8,128)S(1)} %shard_map.64), channel_id=1, source_target_pairs={{0,0},{1,1},{2,2},{3,3},{4,8},{5,9},{6,10},{7,11},{8,13},{9,12},{1... | collective-permute-start | bytes 49160 | tf_op jit(solution)/shard_map/ppermute | solution.py:258
  13.8 0.0 collective-permute-done.3
  13.8 0.0 collective-permute-done.2
  13.8 0.0 collective-permute-done.1
  13.8 2.1 %collective-permute-done = f32[32,128]{1,0:T(8,128)S(1)} collective-permute-done((f32[32,128]{1,0:T(8,128)S(1)}, f32[32,128]{1,0:T(8,128)S(1)}, u32[]{:S(2)}, u32[]{:S(2)}) %collective-permute-start) | collective-permute-done | bytes 16416 | tf_op jit(solution)/shard_map/ppermute | solution.py:258
  15.9 1.2 %collective-permute-start.6 = (f32[128,128]{1,0:T(8,128)S(1)}, f32[128,128]{1,0:T(8,128)S(1)}, u32[]{:S(2)}, u32[]{:S(2)}) collective-permute-start(f32[128,128]{1,0:T(8,128)S(1)} %pad_add_fusion.refs_0_), channel_id=1, source_target_pairs={{0,2},{1,3},{2,0},{3,1},{4,6},{5,7},{6,4},{7,5},{8,10},{9,11},{10,... | collective-permute-start | bytes 196616 | tf_op jit(solution)/shard_map/ppermute | solution.py:266
  17.2 2.5 %collective-permute-start.5 = (f32[128,128]{1,0:T(8,128)S(1)}, f32[128,128]{1,0:T(8,128)S(1)}, u32[]{:S(2)}, u32[]{:S(2)}) collective-permute-start(f32[128,128]{1,0:T(8,128)S(1)} %pad_add_fusion.refs_0_), channel_id=1, source_target_pairs={{0,3},{1,2},{2,1},{3,0},{4,7},{5,6},{6,5},{7,4},{8,11},{9,10},{10,... | collective-permute-start | bytes 196616 | tf_op jit(solution)/shard_map/ppermute | solution.py:266
  19.6 0.0 collective-permute-start.4
  19.6 0.0 collective-permute-done.6.refs_3_
  19.6 3.4 %collective-permute-done.5.refs_2_ = f32[128,128]{1,0:T(8,128)S(1)} collective-permute-done((f32[128,128]{1,0:T(8,128)S(1)}, f32[128,128]{1,0:T(8,128)S(1)}, u32[]{:S(2)}, u32[]{:S(2)}) %collective-permute-start.5) | collective-permute-done | bytes 65568 | tf_op jit(solution)/shard_map/ppermute | solution.py:266
  23.1 0.0 collective-permute-done.4.refs_1_
  23.1 0.0 copy-done
  23.1 2.7 %shard_map.65 = f32[4,16]{1,0:T(4,128)} custom-call(f32[128,128]{1,0:T(8,128)S(1)} %pad_add_fusion.refs_0_, f32[128,128]{1,0:T(8,128)S(1)} %collective-permute-done.4.refs_1_, f32[128,128]{1,0:T(8,128)S(1)} %collective-permute-done.5.refs_2_, f32[128,128]{1,0:T(8,128)S(1)} %collective-permute-done.6.refs_3_, s32[1,16]{1,0:T(1,128)S(1)} %bitcast.5), custom_call_target="tpu_custom_call" | custom-call | tf_op jit(solution)/shard_map/pallas_call | solution.py:239
  (1 shorter events, 0.0 us)
Async XLA Ops:
  0.0 23.1 %copy-start = (s32[16]{0:T(128)S(1)}, s32[16]{0:T(128)}, u32[]{:S(2)}) copy-start(s32[16]{0:T(128)} %param.11) | copy-start | bytes 196
  4.9 8.9 %collective-permute-start.3 = (f32[32,128]{1,0:T(8,128)S(1)}, f32[32,128]{1,0:T(8,128)S(1)}, u32[]{:S(2)}, u32[]{:S(2)}) collective-permute-start(f32[32,128]{1,0:T(8,128)S(1)} %shard_map.64), channel_id=1, source_target_pairs={{0,4},{1,5},{2,6},{3,7},{4,13},{5,12},{6,15},{7,14},{8,8},{9,9},{1... | collective-permute-start | bytes 49160 | tf_op jit(solution)/shard_map/ppermute | solution.py:258
  9.7 4.1 %collective-permute-start.2 = (f32[32,128]{1,0:T(8,128)S(1)}, f32[32,128]{1,0:T(8,128)S(1)}, u32[]{:S(2)}, u32[]{:S(2)}) collective-permute-start(f32[32,128]{1,0:T(8,128)S(1)} %shard_map.64), channel_id=1, source_target_pairs={{0,9},{1,8},{2,11},{3,10},{4,4},{5,5},{6,6},{7,7},{8,0},{9,1},{10,... | collective-permute-start | bytes 49160 | tf_op jit(solution)/shard_map/ppermute | solution.py:258
  10.3 3.5 %collective-permute-start.1 = (f32[32,128]{1,0:T(8,128)S(1)}, f32[32,128]{1,0:T(8,128)S(1)}, u32[]{:S(2)}, u32[]{:S(2)}) collective-permute-start(f32[32,128]{1,0:T(8,128)S(1)} %shard_map.64), channel_id=1, source_target_pairs={{0,13},{1,12},{2,15},{3,14},{4,0},{5,1},{6,2},{7,3},{8,4},{9,5},{1... | collective-permute-start | bytes 49160 | tf_op jit(solution)/shard_map/ppermute | solution.py:258
  10.6 5.4 %collective-permute-start = (f32[32,128]{1,0:T(8,128)S(1)}, f32[32,128]{1,0:T(8,128)S(1)}, u32[]{:S(2)}, u32[]{:S(2)}) collective-permute-start(f32[32,128]{1,0:T(8,128)S(1)} %shard_map.64), channel_id=1, source_target_pairs={{0,0},{1,1},{2,2},{3,3},{4,8},{5,9},{6,10},{7,11},{8,13},{9,12},{1... | collective-permute-start | bytes 49160 | tf_op jit(solution)/shard_map/ppermute | solution.py:258
  15.9 3.7 %collective-permute-start.6 = (f32[128,128]{1,0:T(8,128)S(1)}, f32[128,128]{1,0:T(8,128)S(1)}, u32[]{:S(2)}, u32[]{:S(2)}) collective-permute-start(f32[128,128]{1,0:T(8,128)S(1)} %pad_add_fusion.refs_0_), channel_id=1, source_target_pairs={{0,2},{1,3},{2,0},{3,1},{4,6},{5,7},{6,4},{7,5},{8,10},{9,11},{10,... | collective-permute-start | bytes 196616 | tf_op jit(solution)/shard_map/ppermute | solution.py:266
  17.2 5.9 %collective-permute-start.5 = (f32[128,128]{1,0:T(8,128)S(1)}, f32[128,128]{1,0:T(8,128)S(1)}, u32[]{:S(2)}, u32[]{:S(2)}) collective-permute-start(f32[128,128]{1,0:T(8,128)S(1)} %pad_add_fusion.refs_0_), channel_id=1, source_target_pairs={{0,3},{1,2},{2,1},{3,0},{4,7},{5,6},{6,5},{7,4},{8,11},{9,10},{10,... | collective-permute-start | bytes 196616 | tf_op jit(solution)/shard_map/ppermute | solution.py:266
  19.6 3.4 %collective-permute-start.4 = (f32[128,128]{1,0:T(8,128)S(1)}, f32[128,128]{1,0:T(8,128)S(1)}, u32[]{:S(2)}, u32[]{:S(2)}) collective-permute-start(f32[128,128]{1,0:T(8,128)S(1)} %pad_add_fusion.refs_0_), channel_id=1, source_target_pairs={{0,1},{1,0},{2,3},{3,2},{4,5},{5,4},{6,7},{7,6},{8,9},{9,8},{10,11... | collective-permute-start | bytes 196616 | tf_op jit(solution)/shard_map/ppermute | solution.py:266

commit v22 on v19

--- a/solution.py
+++ b/solution.py
@@ -148,11 +148,9 @@
         pivots = range(first, first + step)
         left = pl.cdiv(first, SUBLANES)
         lower, inverse = factor(columns, first)
+        across = {j: [row_of(column, j) for column in columns] for j in range(first - step, first)}
         columns = forward(lower, [c[:left] for c in columns])
-        following = []
-        for j in range(first - step, first):
-            column = spread(j)
-            following.append(update(column[:left], columns, lower, inverse, [row_of(column, i) for i in pivots]))
+        following = [update(spread(j)[:left], columns, lower, inverse, across[j]) for j in across]
         system = update(system[:left], columns, lower, inverse, [row_of(system, i) for i in pivots])
         columns = following
     lower, inverse = factor(columns, 0)

time: 22.7 us -> 22.1 us (0.974)
  Pallas kernels: 7.61 us -> 7.02 us
    pallas_call x1, Pallas kernels: 2.74 us -> 2.15 us  [gram_scores(): pl.pallas_call(functools.partial(solve_kernel, per_dev, inner, axis), out...]
where the time goes in v22:
time: 22.1 us; the launch traced here: 21.9 us
  starting transfers between devices  7.61 us (34%)
  waiting for transfers between devices  7.28 us (33%)
  Pallas kernels  7.02 us (32%)
    ppermute x6, starting transfers between devices, swap(): return lax.ppermute(block, axis, [(i, i ^ slot) for i in range(size)])  7.61 us
    ppermute x6, waiting for transfers between devices, swap(): return lax.ppermute(block, axis, [(i, i ^ slot) for i in range(size)])  7.28 us
    pallas_call x1, Pallas kernels, sketch_rows(): pl.pallas_call(functools.partial(sketch_kernel, bounds, seq_len), out_sha...  4.87 us
    pallas_call x1, Pallas kernels, gram_scores(): pl.pallas_call(functools.partial(solve_kernel, per_dev, inner, axis), out...  2.15 us
  transfers between devices with their start and end apart: 6, of which 3 were waited for; matrix products, arithmetic and copies ran while one was open for 0% of the time, Pallas kernels for 0%

profile of v22, /device:TPU:0, one launch (start us, length us, event | category | flops | bytes accessed | tf_op | source)
XLA Modules:
  0.0 21.9 jit_solution(15536868854309441980)
XLA Ops:
  0.0 0.0 copy-start
  0.0 4.9 %shard_map.64 = f32[32,128]{1,0:T(8,128)S(1)} custom-call(bf16[256,8192]{1,0:T(8,128)(2,1)} %bitcast.6, bf16[256,8192]{1,0:T(8,128)(2,1)} %bitcast.7, bf16[32,8192]{1,0:T(8,128)(2,1)} %bitcast.8, bf16[32,8192]{1,0:T(8,128)(2,1)} %bitcast.9, s32[4]{0:T(128)} %lengths_hbm.1), custom_call_target="tpu_custom_call" | custom-call | tf_op jit(solution)/shard_map/pallas_call | solution.py:77
  4.9 3.5 %collective-permute-start.2 = (f32[32,128]{1,0:T(8,128)S(1)}, f32[32,128]{1,0:T(8,128)S(1)}, u32[]{:S(2)}, u32[]{:S(2)}) collective-permute-start(f32[32,128]{1,0:T(8,128)S(1)} %shard_map.64), channel_id=1, source_target_pairs={{0,9},{1,8},{2,11},{3,10},{4,13},{5,12},{6,15},{7,14},{8,1},{9,0},... | collective-permute-start | bytes 49160 | tf_op jit(solution)/shard_map/ppermute | solution.py:243
  8.4 1.7 %collective-permute-start.1 = (f32[32,128]{1,0:T(8,128)S(1)}, f32[32,128]{1,0:T(8,128)S(1)}, u32[]{:S(2)}, u32[]{:S(2)}) collective-permute-start(f32[32,128]{1,0:T(8,128)S(1)} %shard_map.64), channel_id=1, source_target_pairs={{0,12},{1,13},{2,14},{3,15},{4,8},{5,9},{6,10},{7,11},{8,4},{9,5},... | collective-permute-start | bytes 49160 | tf_op jit(solution)/shard_map/ppermute | solution.py:243
  10.1 0.2 collective-permute-start
  10.3 0.0 collective-permute-done.2
  10.3 3.7 %collective-permute-done.1 = f32[32,128]{1,0:T(8,128)S(1)} collective-permute-done((f32[32,128]{1,0:T(8,128)S(1)}, f32[32,128]{1,0:T(8,128)S(1)}, u32[]{:S(2)}, u32[]{:S(2)}) %collective-permute-start.1) | collective-permute-done | bytes 16416 | tf_op jit(solution)/shard_map/ppermute | solution.py:243
  14.0 0.0 collective-permute-done
  14.0 1.6 %collective-permute-start.5 = (f32[128,128]{1,0:T(8,128)S(1)}, f32[128,128]{1,0:T(8,128)S(1)}, u32[]{:S(2)}, u32[]{:S(2)}) collective-permute-start(f32[128,128]{1,0:T(8,128)S(1)} %pad_maximum_fusion.refs_0_), channel_id=1, source_target_pairs={{0,2},{1,3},{2,0},{3,1},{4,6},{5,7},{6,4},{7,5},{8,10},{9,11},{10,... | collective-permute-start | bytes 196616 | tf_op jit(solution)/shard_map/ppermute | solution.py:243
  15.6 0.0 collective-permute-start.4
  15.6 0.6 %collective-permute-start.3 = (f32[128,128]{1,0:T(8,128)S(1)}, f32[128,128]{1,0:T(8,128)S(1)}, u32[]{:S(2)}, u32[]{:S(2)}) collective-permute-start(f32[128,128]{1,0:T(8,128)S(1)} %pad_maximum_fusion.refs_0_), channel_id=1, source_target_pairs={{0,1},{1,0},{2,3},{3,2},{4,5},{5,4},{6,7},{7,6},{8,9},{9,8},{10,11... | collective-permute-start | bytes 196616 | tf_op jit(solution)/shard_map/ppermute | solution.py:243
  16.2 2.1 %collective-permute-done.5.refs_3_ = f32[128,128]{1,0:T(8,128)S(1)} collective-permute-done((f32[128,128]{1,0:T(8,128)S(1)}, f32[128,128]{1,0:T(8,128)S(1)}, u32[]{:S(2)}, u32[]{:S(2)}) %collective-permute-start.5) | collective-permute-done | bytes 65568 | tf_op jit(solution)/shard_map/ppermute | solution.py:243
  18.4 1.4 %collective-permute-done.4.refs_2_ = f32[128,128]{1,0:T(8,128)S(1)} collective-permute-done((f32[128,128]{1,0:T(8,128)S(1)}, f32[128,128]{1,0:T(8,128)S(1)}, u32[]{:S(2)}, u32[]{:S(2)}) %collective-permute-start.4) | collective-permute-done | bytes 65568 | tf_op jit(solution)/shard_map/ppermute | solution.py:243
  19.8 0.0 collective-permute-done.3.refs_1_
  19.8 0.0 copy-done
  19.8 2.2 %shard_map.65 = f32[4,16]{1,0:T(4,128)} custom-call(f32[128,128]{1,0:T(8,128)S(1)} %pad_maximum_fusion.refs_0_, f32[128,128]{1,0:T(8,128)S(1)} %collective-permute-done.3.refs_1_, f32[128,128]{1,0:T(8,128)S(1)} %collective-permute-done.4.refs_2_, f32[128,128]{1,0:T(8,128)S(1)} %collective-permute-done.5.refs_3_, s32[1,16]{1,0:T(1,128)S(1)} %bitcast.5), custom_call_target="tpu_custom_call" | custom-call | tf_op jit(solution)/shard_map/pallas_call | solution.py:223
  (1 shorter events, 0.0 us)
Async XLA Ops:
  0.0 19.8 %copy-start = (s32[16]{0:T(128)S(1)}, s32[16]{0:T(128)}, u32[]{:S(2)}) copy-start(s32[16]{0:T(128)} %param.11) | copy-start | bytes 196
  4.9 5.4 %collective-permute-start.2 = (f32[32,128]{1,0:T(8,128)S(1)}, f32[32,128]{1,0:T(8,128)S(1)}, u32[]{:S(2)}, u32[]{:S(2)}) collective-permute-start(f32[32,128]{1,0:T(8,128)S(1)} %shard_map.64), channel_id=1, source_target_pairs={{0,9},{1,8},{2,11},{3,10},{4,13},{5,12},{6,15},{7,14},{8,1},{9,0},... | collective-permute-start | bytes 49160 | tf_op jit(solution)/shard_map/ppermute | solution.py:243
  8.4 5.6 %collective-permute-start.1 = (f32[32,128]{1,0:T(8,128)S(1)}, f32[32,128]{1,0:T(8,128)S(1)}, u32[]{:S(2)}, u32[]{:S(2)}) collective-permute-start(f32[32,128]{1,0:T(8,128)S(1)} %shard_map.64), channel_id=1, source_target_pairs={{0,12},{1,13},{2,14},{3,15},{4,8},{5,9},{6,10},{7,11},{8,4},{9,5},... | collective-permute-start | bytes 49160 | tf_op jit(solution)/shard_map/ppermute | solution.py:243
  10.1 3.9 %collective-permute-start = (f32[32,128]{1,0:T(8,128)S(1)}, f32[32,128]{1,0:T(8,128)S(1)}, u32[]{:S(2)}, u32[]{:S(2)}) collective-permute-start(f32[32,128]{1,0:T(8,128)S(1)} %shard_map.64), channel_id=1, source_target_pairs={{0,5},{1,4},{2,7},{3,6},{4,1},{5,0},{6,3},{7,2},{8,13},{9,12},{10,... | collective-permute-start | bytes 49160 | tf_op jit(solution)/shard_map/ppermute | solution.py:243
  14.0 4.3 %collective-permute-start.5 = (f32[128,128]{1,0:T(8,128)S(1)}, f32[128,128]{1,0:T(8,128)S(1)}, u32[]{:S(2)}, u32[]{:S(2)}) collective-permute-start(f32[128,128]{1,0:T(8,128)S(1)} %pad_maximum_fusion.refs_0_), channel_id=1, source_target_pairs={{0,2},{1,3},{2,0},{3,1},{4,6},{5,7},{6,4},{7,5},{8,10},{9,11},{10,... | collective-permute-start | bytes 196616 | tf_op jit(solution)/shard_map/ppermute | solution.py:243
  15.6 4.2 %collective-permute-start.4 = (f32[128,128]{1,0:T(8,128)S(1)}, f32[128,128]{1,0:T(8,128)S(1)}, u32[]{:S(2)}, u32[]{:S(2)}) collective-permute-start(f32[128,128]{1,0:T(8,128)S(1)} %pad_maximum_fusion.refs_0_), channel_id=1, source_target_pairs={{0,3},{1,2},{2,1},{3,0},{4,7},{5,6},{6,5},{7,4},{8,11},{9,10},{10,... | collective-permute-start | bytes 196616 | tf_op jit(solution)/shard_map/ppermute | solution.py:243
  15.6 4.2 %collective-permute-start.3 = (f32[128,128]{1,0:T(8,128)S(1)}, f32[128,128]{1,0:T(8,128)S(1)}, u32[]{:S(2)}, u32[]{:S(2)}) collective-permute-start(f32[128,128]{1,0:T(8,128)S(1)} %pad_maximum_fusion.refs_0_), channel_id=1, source_target_pairs={{0,1},{1,0},{2,3},{3,2},{4,5},{5,4},{6,7},{7,6},{8,9},{9,8},{10,11... | collective-permute-start | bytes 196616 | tf_op jit(solution)/shard_map/ppermute | solution.py:243

commit v23 on v22

--- a/solution.py
+++ b/solution.py
@@ -103,15 +103,23 @@
     )
 
 
-def solve_first(system):
+def solve_first(system, scratch):
     step = 4
 
     def spread(column):
         return [jnp.broadcast_to(tile[:, column : column + 1], tile.shape) for tile in system]
 
+    stored = {}
+
     def row_of(tiles, number):
         tile = tiles[number // SUBLANES]
-        return jnp.broadcast_to(tile[number % SUBLANES : number % SUBLANES + 1], tile.shape)
+        if id(tile) not in stored:
+            slot = len(stored)
+            scratch[slot] = tile
+            stored[id(tile)] = slot, tile
+        slot, _ = stored[id(tile)]
+        row = scratch[slot, number % SUBLANES : number % SUBLANES + 1]
+        return jnp.broadcast_to(row, tile.shape)
 
     def factor(columns, first):
         p = {(i, j): row_of(columns[j], first + i) for j in range(step) for i in range(j + 1)}
@@ -179,7 +187,7 @@
 
 
 def solve_kernel(per_dev, inner, axis, *refs):
-    tiles, (query_ref, scores_ref, gram_ref) = refs[:-3], refs[-3:]
+    tiles, (query_ref, scores_ref, gram_ref, scratch) = refs[:-4], refs[-4:]
     nq = query_ref.shape[1]
     part = tiles[0].shape[0] // SUBLANES
     examples = len(tiles) * part
@@ -210,7 +218,7 @@
     for first in range(0, examples, SUBLANES):
         tile = jnp.take_along_axis(gram_ref[first : first + SUBLANES], source, axis=1) * scale
         system.append(jnp.where(lane == row + first, tile + damp_ratio / fisher_dim, tile))
-    solved = solve_first(system)
+    solved = solve_first(system, scratch)
     scores = solved[0]
     for i in range(1, len(solved)):
         scores = jnp.where(row == i, solved[i], scores)
@@ -225,7 +233,10 @@
         out_shape=jax.ShapeDtypeStruct((per_dev, nq), jnp.float32),
         in_specs=[pl.BlockSpec(memory_space=pltpu.VMEM)] * (len(tiles) + 1),
         out_specs=pl.BlockSpec(memory_space=pltpu.VMEM),
-        scratch_shapes=[pltpu.VMEM((examples, LANES), jnp.float32)],
+        scratch_shapes=[
+            pltpu.VMEM((examples, LANES), jnp.float32),
+            pltpu.VMEM((3 * examples, SUBLANES, LANES), jnp.float32),
+        ],
         compiler_params=pltpu.CompilerParams(vmem_limit_bytes=8 * 2**20),
     )(*tiles, query_index.reshape(1, nq))
 

time: 22.1 us -> 22.1 us (level)
  no operation moved by 1% of the time
where the time goes in v23:
time: 22.1 us; the launch traced here: 21.9 us
  starting transfers between devices  7.61 us (34%)
  waiting for transfers between devices  7.28 us (33%)
  Pallas kernels  7.02 us (32%)
    ppermute x6, starting transfers between devices, swap(): return lax.ppermute(block, axis, [(i, i ^ slot) for i in range(size)])  7.61 us
    ppermute x6, waiting for transfers between devices, swap(): return lax.ppermute(block, axis, [(i, i ^ slot) for i in range(size)])  7.28 us
    pallas_call x1, Pallas kernels, sketch_rows(): pl.pallas_call(functools.partial(sketch_kernel, bounds, seq_len), out_sha...  4.87 us
    pallas_call x1, Pallas kernels, gram_scores(): pl.pallas_call(functools.partial(solve_kernel, per_dev, inner, axis), out...  2.15 us
  transfers between devices with their start and end apart: 6, of which 3 were waited for; matrix products, arithmetic and copies ran while one was open for 0% of the time, Pallas kernels for 0%

profile of v23, /device:TPU:0, one launch (start us, length us, event | category | flops | bytes accessed | tf_op | source)
XLA Modules:
  0.0 21.9 jit_solution(17473983766406290085)
XLA Ops:
  0.0 0.0 copy-start
  0.0 4.9 %shard_map.64 = f32[32,128]{1,0:T(8,128)S(1)} custom-call(bf16[256,8192]{1,0:T(8,128)(2,1)} %bitcast.6, bf16[256,8192]{1,0:T(8,128)(2,1)} %bitcast.7, bf16[32,8192]{1,0:T(8,128)(2,1)} %bitcast.8, bf16[32,8192]{1,0:T(8,128)(2,1)} %bitcast.9, s32[4]{0:T(128)} %lengths_hbm.1), custom_call_target="tpu_custom_call" | custom-call | tf_op jit(solution)/shard_map/pallas_call | solution.py:77
  4.9 3.5 %collective-permute-start.2 = (f32[32,128]{1,0:T(8,128)S(1)}, f32[32,128]{1,0:T(8,128)S(1)}, u32[]{:S(2)}, u32[]{:S(2)}) collective-permute-start(f32[32,128]{1,0:T(8,128)S(1)} %shard_map.64), channel_id=1, source_target_pairs={{0,9},{1,8},{2,11},{3,10},{4,13},{5,12},{6,15},{7,14},{8,1},{9,0},... | collective-permute-start | bytes 49160 | tf_op jit(solution)/shard_map/ppermute | solution.py:254
  8.4 1.7 %collective-permute-start.1 = (f32[32,128]{1,0:T(8,128)S(1)}, f32[32,128]{1,0:T(8,128)S(1)}, u32[]{:S(2)}, u32[]{:S(2)}) collective-permute-start(f32[32,128]{1,0:T(8,128)S(1)} %shard_map.64), channel_id=1, source_target_pairs={{0,12},{1,13},{2,14},{3,15},{4,8},{5,9},{6,10},{7,11},{8,4},{9,5},... | collective-permute-start | bytes 49160 | tf_op jit(solution)/shard_map/ppermute | solution.py:254
  10.1 0.2 collective-permute-start
  10.3 0.0 collective-permute-done.2
  10.3 3.7 %collective-permute-done.1 = f32[32,128]{1,0:T(8,128)S(1)} collective-permute-done((f32[32,128]{1,0:T(8,128)S(1)}, f32[32,128]{1,0:T(8,128)S(1)}, u32[]{:S(2)}, u32[]{:S(2)}) %collective-permute-start.1) | collective-permute-done | bytes 16416 | tf_op jit(solution)/shard_map/ppermute | solution.py:254
  14.0 0.0 collective-permute-done
  14.0 1.6 %collective-permute-start.5 = (f32[128,128]{1,0:T(8,128)S(1)}, f32[128,128]{1,0:T(8,128)S(1)}, u32[]{:S(2)}, u32[]{:S(2)}) collective-permute-start(f32[128,128]{1,0:T(8,128)S(1)} %pad_maximum_fusion.refs_0_), channel_id=1, source_target_pairs={{0,2},{1,3},{2,0},{3,1},{4,6},{5,7},{6,4},{7,5},{8,10},{9,11},{10,... | collective-permute-start | bytes 196616 | tf_op jit(solution)/shard_map/ppermute | solution.py:254
  15.6 0.0 collective-permute-start.4
  15.6 0.6 %collective-permute-start.3 = (f32[128,128]{1,0:T(8,128)S(1)}, f32[128,128]{1,0:T(8,128)S(1)}, u32[]{:S(2)}, u32[]{:S(2)}) collective-permute-start(f32[128,128]{1,0:T(8,128)S(1)} %pad_maximum_fusion.refs_0_), channel_id=1, source_target_pairs={{0,1},{1,0},{2,3},{3,2},{4,5},{5,4},{6,7},{7,6},{8,9},{9,8},{10,11... | collective-permute-start | bytes 196616 | tf_op jit(solution)/shard_map/ppermute | solution.py:254
  16.2 2.1 %collective-permute-done.5.refs_3_ = f32[128,128]{1,0:T(8,128)S(1)} collective-permute-done((f32[128,128]{1,0:T(8,128)S(1)}, f32[128,128]{1,0:T(8,128)S(1)}, u32[]{:S(2)}, u32[]{:S(2)}) %collective-permute-start.5) | collective-permute-done | bytes 65568 | tf_op jit(solution)/shard_map/ppermute | solution.py:254
  18.4 1.4 %collective-permute-done.4.refs_2_ = f32[128,128]{1,0:T(8,128)S(1)} collective-permute-done((f32[128,128]{1,0:T(8,128)S(1)}, f32[128,128]{1,0:T(8,128)S(1)}, u32[]{:S(2)}, u32[]{:S(2)}) %collective-permute-start.4) | collective-permute-done | bytes 65568 | tf_op jit(solution)/shard_map/ppermute | solution.py:254
  19.8 0.0 collective-permute-done.3.refs_1_
  19.8 0.0 copy-done
  19.8 2.1 %shard_map.65 = f32[4,16]{1,0:T(4,128)} custom-call(f32[128,128]{1,0:T(8,128)S(1)} %pad_maximum_fusion.refs_0_, f32[128,128]{1,0:T(8,128)S(1)} %collective-permute-done.3.refs_1_, f32[128,128]{1,0:T(8,128)S(1)} %collective-permute-done.4.refs_2_, f32[128,128]{1,0:T(8,128)S(1)} %collective-permute-done.5.refs_3_, s32[1,16]{1,0:T(1,128)S(1)} %bitcast.5), custom_call_target="tpu_custom_call" | custom-call | tf_op jit(solution)/shard_map/pallas_call | solution.py:231
  (1 shorter events, 0.0 us)
Async XLA Ops:
  0.0 19.8 %copy-start = (s32[16]{0:T(128)S(1)}, s32[16]{0:T(128)}, u32[]{:S(2)}) copy-start(s32[16]{0:T(128)} %param.11) | copy-start | bytes 196
  4.9 5.4 %collective-permute-start.2 = (f32[32,128]{1,0:T(8,128)S(1)}, f32[32,128]{1,0:T(8,128)S(1)}, u32[]{:S(2)}, u32[]{:S(2)}) collective-permute-start(f32[32,128]{1,0:T(8,128)S(1)} %shard_map.64), channel_id=1, source_target_pairs={{0,9},{1,8},{2,11},{3,10},{4,13},{5,12},{6,15},{7,14},{8,1},{9,0},... | collective-permute-start | bytes 49160 | tf_op jit(solution)/shard_map/ppermute | solution.py:254
  8.4 5.6 %collective-permute-start.1 = (f32[32,128]{1,0:T(8,128)S(1)}, f32[32,128]{1,0:T(8,128)S(1)}, u32[]{:S(2)}, u32[]{:S(2)}) collective-permute-start(f32[32,128]{1,0:T(8,128)S(1)} %shard_map.64), channel_id=1, source_target_pairs={{0,12},{1,13},{2,14},{3,15},{4,8},{5,9},{6,10},{7,11},{8,4},{9,5},... | collective-permute-start | bytes 49160 | tf_op jit(solution)/shard_map/ppermute | solution.py:254
  10.1 3.9 %collective-permute-start = (f32[32,128]{1,0:T(8,128)S(1)}, f32[32,128]{1,0:T(8,128)S(1)}, u32[]{:S(2)}, u32[]{:S(2)}) collective-permute-start(f32[32,128]{1,0:T(8,128)S(1)} %shard_map.64), channel_id=1, source_target_pairs={{0,5},{1,4},{2,7},{3,6},{4,1},{5,0},{6,3},{7,2},{8,13},{9,12},{10,... | collective-permute-start | bytes 49160 | tf_op jit(solution)/shard_map/ppermute | solution.py:254
  14.0 4.3 %collective-permute-start.5 = (f32[128,128]{1,0:T(8,128)S(1)}, f32[128,128]{1,0:T(8,128)S(1)}, u32[]{:S(2)}, u32[]{:S(2)}) collective-permute-start(f32[128,128]{1,0:T(8,128)S(1)} %pad_maximum_fusion.refs_0_), channel_id=1, source_target_pairs={{0,2},{1,3},{2,0},{3,1},{4,6},{5,7},{6,4},{7,5},{8,10},{9,11},{10,... | collective-permute-start | bytes 196616 | tf_op jit(solution)/shard_map/ppermute | solution.py:254
  15.6 4.2 %collective-permute-start.4 = (f32[128,128]{1,0:T(8,128)S(1)}, f32[128,128]{1,0:T(8,128)S(1)}, u32[]{:S(2)}, u32[]{:S(2)}) collective-permute-start(f32[128,128]{1,0:T(8,128)S(1)} %pad_maximum_fusion.refs_0_), channel_id=1, source_target_pairs={{0,3},{1,2},{2,1},{3,0},{4,7},{5,6},{6,5},{7,4},{8,11},{9,10},{10,... | collective-permute-start | bytes 196616 | tf_op jit(solution)/shard_map/ppermute | solution.py:254
  15.6 4.2 %collective-permute-start.3 = (f32[128,128]{1,0:T(8,128)S(1)}, f32[128,128]{1,0:T(8,128)S(1)}, u32[]{:S(2)}, u32[]{:S(2)}) collective-permute-start(f32[128,128]{1,0:T(8,128)S(1)} %pad_maximum_fusion.refs_0_), channel_id=1, source_target_pairs={{0,1},{1,0},{2,3},{3,2},{4,5},{5,4},{6,7},{7,6},{8,9},{9,8},{10,11... | collective-permute-start | bytes 196616 | tf_op jit(solution)/shard_map/ppermute | solution.py:254

commit v24 on v23

--- a/solution.py
+++ b/solution.py
@@ -170,53 +170,83 @@
     return solved
 
 
-def gram(x):
+def split(x):
     high = x.astype(jnp.bfloat16)
     rest = x - high.astype(jnp.float32)
     middle = rest.astype(jnp.bfloat16)
-    low = (rest - middle.astype(jnp.float32)).astype(jnp.bfloat16)
-    parts = [high, middle, low]
-    count = x.shape[0]
+    return [high, middle, (rest - middle.astype(jnp.float32)).astype(jnp.bfloat16)]
+
+
+def products(left, right):
+    count = left[0].shape[0]
     terms = []
-    for n, held in enumerate(parts):
-        streamed = jnp.concatenate(parts[: len(parts) - n], axis=0)
+    for n, held in enumerate(right):
+        streamed = jnp.concatenate(left[: len(left) - n], axis=0)
         product = lax.dot_general(streamed, held, NT, preferred_element_type=jnp.float32)
         terms.append([product[k : k + count] for k in range(0, product.shape[0], count)])
     (hh, mh, lh), (hm, mm), (hl,) = terms
     return hh + ((mh + hm) + (lh + hl + mm))
 
 
-def solve_kernel(per_dev, inner, axis, *refs):
-    tiles, (query_ref, scores_ref, gram_ref, scratch) = refs[:-4], refs[-4:]
+def sketch_matrix(tile):
+    count = tile.shape[0] // SUBLANES
+    return jnp.concatenate([tile[pl.ds(s, count, stride=SUBLANES)] for s in range(SUBLANES)], axis=1)
+
+
+def square_sums(x):
+    sums = jnp.sum(x * x, axis=0, keepdims=True)
+    return functools.reduce(jnp.add, [sums[:, k : k + LANES] for k in range(0, x.shape[1], LANES)])
+
+
+def early_kernel(own_ref, across_ref, gram_ref, squares_ref, high_ref, middle_ref, low_ref):
+    own, across = sketch_matrix(own_ref), sketch_matrix(across_ref)
+    late = jnp.zeros_like(own)
+    sketches = jnp.concatenate([own, late, late, across], axis=0)
+    parts = split(sketches)
+    for ref, part in zip((high_ref, middle_ref, low_ref), parts):
+        ref[...] = part
+    squares_ref[...] = square_sums(sketches)
+    gram_ref[...] = jnp.zeros(gram_ref.shape, jnp.float32)
+    gram_ref[:, : sketches.shape[0]] = products(parts, parts)
+
+
+def solve_kernel(per_dev, inner, axis, late_ref, last_ref, gram_ref, squares_ref, high_ref, middle_ref, low_ref, query_ref, scores_ref, late_rows, scratch):
     nq = query_ref.shape[1]
-    part = tiles[0].shape[0] // SUBLANES
-    examples = len(tiles) * part
+    held_rows = late_ref.shape[0] // SUBLANES
+    examples = gram_ref.shape[0]
+    late = slice(held_rows, examples - held_rows)
     outer = examples // (inner * per_dev)
     fisher_dim = SUBLANES * LANES
-    gram_ref[...] = jnp.zeros(gram_ref.shape, jnp.float32)
+    late_rows[...] = jnp.zeros(late_rows.shape, jnp.float32)
     slot = (query_ref[...] // per_dev) ^ lax.axis_index(axis)
     n = slot // inner
-    place = (gray((slot ^ partner(n, inner)) % inner) * outer + gray(n)) * per_dev + query_ref[...] % per_dev
+    place = block_of((slot ^ partner(n, inner)) % inner) * outer + (outer - gray(n)) % outer
+    place = place * per_dev + query_ref[...] % per_dev
     rest = LANES - examples - nq
     place = jnp.concatenate(
         [jnp.zeros((1, examples), jnp.int32), place] + ([jnp.zeros((1, rest), jnp.int32)] if rest else []), axis=1
     )
     lane = lax.broadcasted_iota(jnp.int32, (SUBLANES, LANES), 1)
     source = jnp.where(lane < examples, lane, jnp.broadcast_to(place, lane.shape))
-    sketches = jnp.concatenate(
-        [
-            jnp.concatenate([tile[pl.ds(s, part, stride=SUBLANES)] for tile in tiles], axis=0)
-            for s in range(SUBLANES)
-        ],
-        axis=1,
-    )
-    squares = jnp.sum(jnp.sum(sketches * sketches, axis=0, keepdims=True), axis=1, keepdims=True)
+    sketches = jnp.concatenate([sketch_matrix(late_ref), sketch_matrix(last_ref)], axis=0)
+    parts = split(sketches)
+    held = [
+        jnp.concatenate([ref[: late.start], part, ref[late.stop :]], axis=0)
+        for ref, part in zip((high_ref, middle_ref, low_ref), parts)
+    ]
+    squares = jnp.sum(squares_ref[...] + square_sums(sketches), axis=1, keepdims=True)
     scale = jnp.broadcast_to(1.0 / squares, (SUBLANES, LANES))
-    gram_ref[:, :examples] = gram(sketches)
+    late_rows[late, :examples] = products(parts, held)
+    turned = jnp.transpose(late_rows[...])
     row = lax.broadcasted_iota(jnp.int32, (SUBLANES, LANES), 0)
     system = []
     for first in range(0, examples, SUBLANES):
-        tile = jnp.take_along_axis(gram_ref[first : first + SUBLANES], source, axis=1) * scale
+        own = slice(first, first + SUBLANES)
+        if late.start <= first < late.stop:
+            tile = late_rows[own]
+        else:
+            tile = gram_ref[own] + turned[own]
+        tile = jnp.take_along_axis(tile, source, axis=1) * scale
         system.append(jnp.where(lane == row + first, tile + damp_ratio / fisher_dim, tile))
     solved = solve_first(system, scratch)
     scores = solved[0]
@@ -225,20 +255,37 @@
     scores_ref[...] = scores[:per_dev, examples : examples + nq]
 
 
-def gram_scores(tiles, query_index, per_dev, inner, axis):
+def gram_scores(columns, query_index, per_dev, inner, axis):
+    own, late, last, across = columns
     nq = query_index.shape[0]
-    examples = len(tiles) * tiles[0].shape[0] // SUBLANES
+    examples = len(columns) * own.shape[0] // SUBLANES
+    width = SUBLANES * LANES
+    vmem = pl.BlockSpec(memory_space=pltpu.VMEM)
+    early = pl.pallas_call(
+        early_kernel,
+        out_shape=[
+            jax.ShapeDtypeStruct((examples, LANES), jnp.float32),
+            jax.ShapeDtypeStruct((1, LANES), jnp.float32),
+        ]
+        + [jax.ShapeDtypeStruct((examples, width), jnp.bfloat16)] * 3,
+        in_specs=[vmem] * 2,
+        out_specs=[vmem] * 5,
+        compiler_params=pltpu.CompilerParams(vmem_limit_bytes=8 * 2**20),
+        cost_estimate=pl.CostEstimate(
+            flops=12 * examples * examples * width, bytes_accessed=10 * examples * width, transcendentals=0
+        ),
+    )(own, across)
     return pl.pallas_call(
         functools.partial(solve_kernel, per_dev, inner, axis),
         out_shape=jax.ShapeDtypeStruct((per_dev, nq), jnp.float32),
-        in_specs=[pl.BlockSpec(memory_space=pltpu.VMEM)] * (len(tiles) + 1),
-        out_specs=pl.BlockSpec(memory_space=pltpu.VMEM),
+        in_specs=[vmem] * 8,
+        out_specs=vmem,
         scratch_shapes=[
-            pltpu.VMEM((examples, LANES), jnp.float32),
+            pltpu.VMEM((LANES, LANES), jnp.float32),
             pltpu.VMEM((3 * examples, SUBLANES, LANES), jnp.float32),
         ],
         compiler_params=pltpu.CompilerParams(vmem_limit_bytes=8 * 2**20),
-    )(*tiles, query_index.reshape(1, nq))
+    )(late, last, *early, query_index.reshape(1, nq))
 
 
 def gray(n):
@@ -247,15 +294,19 @@
 
 def partner(n, inner):
     return n * inner ^ gray(n) & 1
+
+
+def block_of(n):
+    return jnp.where(n == 0, 0, n % 3 + 1)
 
 
 def gather_xor(tiles, axis, size, inner):
     def swap(block, slot):
         return lax.ppermute(block, axis, [(i, i ^ slot) for i in range(size)])
 
-    rows = sorted(range(1, size // inner), key=gray)
+    rows = sorted(range(1, size // inner), key=gray, reverse=True)
     column = jnp.concatenate([tiles] + [swap(tiles, partner(n, inner)) for n in rows], axis=0)
-    return [column] + [swap(column, n) for n in sorted(range(1, inner), key=gray)]
+    return [column, swap(column, 3), swap(column, 1), swap(column, 2)]
 
 
 def large_scores(tiles, query_index, per_dev, axis):

time: 22.1 us -> 22.1 us (level)
  waiting for transfers between devices: 7.28 us -> 6.91 us
  Pallas kernels: 7.02 us -> 7.38 us
    ppermute x6, waiting for transfers between devices: 7.28 us -> 6.91 us  [swap(): return lax.ppermute(block, axis, [(i, i ^ slot) for i in range(size)])]
    pallas_call x0 -> x1, Pallas kernels: none -> 0.36 us  [gram_scores(): pl.pallas_call(early_kernel, out_shape=[jax.ShapeDtypeStruct((examples, L...]
  transfers between devices with their start and end apart: 6 -> 6, of which waited for: 3 -> 3; matrix products, arithmetic and copies ran while one was open for 0% -> 0% of each run, Pallas kernels for 0% -> 2%
where the time goes in v24:
time: 22.1 us; the launch traced here: 21.9 us
  starting transfers between devices  7.61 us (34%)
  Pallas kernels  7.38 us (33%)
  waiting for transfers between devices  6.91 us (31%)
    ppermute x6, starting transfers between devices, swap(): return lax.ppermute(block, axis, [(i, i ^ slot) for i in range(size)])  7.61 us
    ppermute x6, waiting for transfers between devices, swap(): return lax.ppermute(block, axis, [(i, i ^ slot) for i in range(size)])  6.91 us
    pallas_call x1, Pallas kernels, sketch_rows(): pl.pallas_call(functools.partial(sketch_kernel, bounds, seq_len), out_sha...  4.87 us
    pallas_call x1, Pallas kernels, gram_scores(): pl.pallas_call(functools.partial(solve_kernel, per_dev, inner, axis), out...  2.15 us
  transfers between devices with their start and end apart: 6, of which 3 were waited for; matrix products, arithmetic and copies ran while one was open for 0% of the time, Pallas kernels for 2%

profile of v24, /device:TPU:0, one launch (start us, length us, event | category | flops | bytes accessed | tf_op | source)
XLA Modules:
  0.0 21.9 jit_solution(4972613898273234874)
XLA Ops:
  0.0 0.0 copy-start
  0.0 4.9 %shard_map.64 = f32[32,128]{1,0:T(8,128)S(1)} custom-call(bf16[256,8192]{1,0:T(8,128)(2,1)} %bitcast.6, bf16[256,8192]{1,0:T(8,128)(2,1)} %bitcast.7, bf16[32,8192]{1,0:T(8,128)(2,1)} %bitcast.8, bf16[32,8192]{1,0:T(8,128)(2,1)} %bitcast.9, s32[4]{0:T(128)} %lengths_hbm.1), custom_call_target="tpu_custom_call" | custom-call | tf_op jit(solution)/shard_map/pallas_call | solution.py:77
  4.9 3.5 %collective-permute-start = (f32[32,128]{1,0:T(8,128)S(1)}, f32[32,128]{1,0:T(8,128)S(1)}, u32[]{:S(2)}, u32[]{:S(2)}) collective-permute-start(f32[32,128]{1,0:T(8,128)S(1)} %shard_map.64), channel_id=1, source_target_pairs={{0,9},{1,8},{2,11},{3,10},{4,13},{5,12},{6,15},{7,14},{8,1},{9,0},... | collective-permute-start | bytes 49160 | tf_op jit(solution)/shard_map/ppermute | solution.py:305
  8.4 1.7 %collective-permute-start.1 = (f32[32,128]{1,0:T(8,128)S(1)}, f32[32,128]{1,0:T(8,128)S(1)}, u32[]{:S(2)}, u32[]{:S(2)}) collective-permute-start(f32[32,128]{1,0:T(8,128)S(1)} %shard_map.64), channel_id=1, source_target_pairs={{0,12},{1,13},{2,14},{3,15},{4,8},{5,9},{6,10},{7,11},{8,4},{9,5},... | collective-permute-start | bytes 49160 | tf_op jit(solution)/shard_map/ppermute | solution.py:305
  10.1 0.2 collective-permute-start.2
  10.3 0.0 collective-permute-done
  10.3 3.7 %collective-permute-done.1 = f32[32,128]{1,0:T(8,128)S(1)} collective-permute-done((f32[32,128]{1,0:T(8,128)S(1)}, f32[32,128]{1,0:T(8,128)S(1)}, u32[]{:S(2)}, u32[]{:S(2)}) %collective-permute-start.1) | collective-permute-done | bytes 16416 | tf_op jit(solution)/shard_map/ppermute | solution.py:305
  14.0 0.0 collective-permute-done.2
  14.0 1.6 %collective-permute-start.5 = (f32[128,128]{1,0:T(8,128)S(1)}, f32[128,128]{1,0:T(8,128)S(1)}, u32[]{:S(2)}, u32[]{:S(2)}) collective-permute-start(f32[128,128]{1,0:T(8,128)S(1)} %pad_maximum_fusion.own_ref), channel_id=1, source_target_pairs={{0,2},{1,3},{2,0},{3,1},{4,6},{5,7},{6,4},{7,5},{8,10},{9,11},{10,... | collective-permute-start | bytes 196616 | tf_op jit(solution)/shard_map/ppermute | solution.py:305
  15.6 0.0 collective-permute-start.3
  15.6 0.6 %collective-permute-start.4 = (f32[128,128]{1,0:T(8,128)S(1)}, f32[128,128]{1,0:T(8,128)S(1)}, u32[]{:S(2)}, u32[]{:S(2)}) collective-permute-start(f32[128,128]{1,0:T(8,128)S(1)} %pad_maximum_fusion.own_ref), channel_id=1, source_target_pairs={{0,1},{1,0},{2,3},{3,2},{4,5},{5,4},{6,7},{7,6},{8,9},{9,8},{10,11... | collective-permute-start | bytes 196616 | tf_op jit(solution)/shard_map/ppermute | solution.py:305
  16.2 2.1 %collective-permute-done.5.across_ref = f32[128,128]{1,0:T(8,128)S(1)} collective-permute-done((f32[128,128]{1,0:T(8,128)S(1)}, f32[128,128]{1,0:T(8,128)S(1)}, u32[]{:S(2)}, u32[]{:S(2)}) %collective-permute-start.5) | collective-permute-done | bytes 65568 | tf_op jit(solution)/shard_map/ppermute | solution.py:305
  18.4 0.4 %shard_map.65 = (f32[64,128]{1,0:T(8,128)S(1)}, f32[1,128]{1,0:T(1,128)S(1)}, bf16[64,1024]{1,0:T(8,128)(2,1)S(1)}, bf16[64,1024]{1,0:T(8,128)(2,1)S(1)}, bf16[64,1024]{1,0:T(8,128)(2,1)S(1)}) custom-call(f32[128,128]{1,0:T(8,128)S(1)} %pad_maximum_fusion.own_ref, f32[128,128]{1,0:T(8,128)S(1)} %collective-permute-done.5.across_ref), custom_call_target="tpu_custom_call" | custom-call | flops 50331648 | bytes 655360 | tf_op jit(solution)/shard_map/pallas_call | solution.py:264
  18.7 1.0 %collective-permute-done.3.late_ref = f32[128,128]{1,0:T(8,128)S(1)} collective-permute-done((f32[128,128]{1,0:T(8,128)S(1)}, f32[128,128]{1,0:T(8,128)S(1)}, u32[]{:S(2)}, u32[]{:S(2)}) %collective-permute-start.3) | collective-permute-done | bytes 65568 | tf_op jit(solution)/shard_map/ppermute | solution.py:305
  19.8 0.0 collective-permute-done.4.last_ref
  19.8 0.0 copy-done
  19.8 2.2 %shard_map.66 = f32[4,16]{1,0:T(4,128)} custom-call(f32[128,128]{1,0:T(8,128)S(1)} %collective-permute-done.3.late_ref, f32[128,128]{1,0:T(8,128)S(1)} %collective-permute-done.4.last_ref, f32[64,128]{1,0:T(8,128)S(1)} %get-tuple-element.10.gram_ref, f32[1,128]{1,0:T(1,128)S(1)} %get-tuple-element.11.squares_ref, ...), custom_call_target="tpu_custom_call" | custom-call | tf_op jit(solution)/shard_map/pallas_call | solution.py:278
  (1 shorter events, 0.0 us)
Async XLA Ops:
  0.0 19.8 %copy-start = (s32[16]{0:T(128)S(1)}, s32[16]{0:T(128)}, u32[]{:S(2)}) copy-start(s32[16]{0:T(128)} %param.11) | copy-start | bytes 196
  4.9 5.4 %collective-permute-start = (f32[32,128]{1,0:T(8,128)S(1)}, f32[32,128]{1,0:T(8,128)S(1)}, u32[]{:S(2)}, u32[]{:S(2)}) collective-permute-start(f32[32,128]{1,0:T(8,128)S(1)} %shard_map.64), channel_id=1, source_target_pairs={{0,9},{1,8},{2,11},{3,10},{4,13},{5,12},{6,15},{7,14},{8,1},{9,0},... | collective-permute-start | bytes 49160 | tf_op jit(solution)/shard_map/ppermute | solution.py:305
  8.4 5.6 %collective-permute-start.1 = (f32[32,128]{1,0:T(8,128)S(1)}, f32[32,128]{1,0:T(8,128)S(1)}, u32[]{:S(2)}, u32[]{:S(2)}) collective-permute-start(f32[32,128]{1,0:T(8,128)S(1)} %shard_map.64), channel_id=1, source_target_pairs={{0,12},{1,13},{2,14},{3,15},{4,8},{5,9},{6,10},{7,11},{8,4},{9,5},... | collective-permute-start | bytes 49160 | tf_op jit(solution)/shard_map/ppermute | solution.py:305
  10.1 3.9 %collective-permute-start.2 = (f32[32,128]{1,0:T(8,128)S(1)}, f32[32,128]{1,0:T(8,128)S(1)}, u32[]{:S(2)}, u32[]{:S(2)}) collective-permute-start(f32[32,128]{1,0:T(8,128)S(1)} %shard_map.64), channel_id=1, source_target_pairs={{0,5},{1,4},{2,7},{3,6},{4,1},{5,0},{6,3},{7,2},{8,13},{9,12},{10,... | collective-permute-start | bytes 49160 | tf_op jit(solution)/shard_map/ppermute | solution.py:305
  14.0 4.3 %collective-permute-start.5 = (f32[128,128]{1,0:T(8,128)S(1)}, f32[128,128]{1,0:T(8,128)S(1)}, u32[]{:S(2)}, u32[]{:S(2)}) collective-permute-start(f32[128,128]{1,0:T(8,128)S(1)} %pad_maximum_fusion.own_ref), channel_id=1, source_target_pairs={{0,2},{1,3},{2,0},{3,1},{4,6},{5,7},{6,4},{7,5},{8,10},{9,11},{10,... | collective-permute-start | bytes 196616 | tf_op jit(solution)/shard_map/ppermute | solution.py:305
  15.6 4.2 %collective-permute-start.3 = (f32[128,128]{1,0:T(8,128)S(1)}, f32[128,128]{1,0:T(8,128)S(1)}, u32[]{:S(2)}, u32[]{:S(2)}) collective-permute-start(f32[128,128]{1,0:T(8,128)S(1)} %pad_maximum_fusion.own_ref), channel_id=1, source_target_pairs={{0,3},{1,2},{2,1},{3,0},{4,7},{5,6},{6,5},{7,4},{8,11},{9,10},{10,... | collective-permute-start | bytes 196616 | tf_op jit(solution)/shard_map/ppermute | solution.py:305
  15.6 4.2 %collective-permute-start.4 = (f32[128,128]{1,0:T(8,128)S(1)}, f32[128,128]{1,0:T(8,128)S(1)}, u32[]{:S(2)}, u32[]{:S(2)}) collective-permute-start(f32[128,128]{1,0:T(8,128)S(1)} %pad_maximum_fusion.own_ref), channel_id=1, source_target_pairs={{0,1},{1,0},{2,3},{3,2},{4,5},{5,4},{6,7},{7,6},{8,9},{9,8},{10,11... | collective-permute-start | bytes 196616 | tf_op jit(solution)/shard_map/ppermute | solution.py:305

commit v25 on v23

--- a/solution.py
+++ b/solution.py
@@ -103,8 +103,8 @@
     )
 
 
-def solve_first(system, scratch):
-    step = 4
+def solve_first(system, scratch, wanted):
+    step = 2
 
     def spread(column):
         return [jnp.broadcast_to(tile[:, column : column + 1], tile.shape) for tile in system]
@@ -122,24 +122,25 @@
         return jnp.broadcast_to(row, tile.shape)
 
     def factor(columns, first):
-        p = {(i, j): row_of(columns[j], first + i) for j in range(step) for i in range(j + 1)}
-        lower, inverse = {}, [None] * step
-        for k in range(0, step, 2):
+        size = len(columns)
+        p = {(i, j): row_of(columns[j], first + i) for j in range(size) for i in range(j + 1)}
+        lower, inverse = {}, [None] * size
+        for k in range(0, size, 2):
             a, b, c = p[k, k], p[k, k + 1], p[k + 1, k + 1]
             inverse[k] = pl.reciprocal(a)
             inverse[k + 1] = a * pl.reciprocal(a * c - b * b)
             for m in (k, k + 1):
-                for i in range(m + 1, step):
+                for i in range(m + 1, size):
                     lower[i, m] = p[m, i] * inverse[m]
-                for i in range(m + 1, step):
-                    for j in range(i, step):
+                for i in range(m + 1, size):
+                    for j in range(i, size):
                         p[i, j] = p[i, j] - lower[i, m] * p[m, j]
         return lower, inverse
 
     def forward(lower, parts):
         parts = list(parts)
-        for k in range(step):
-            for i in range(k + 1, step):
+        for k in range(len(parts)):
+            for i in range(k + 1, len(parts)):
                 parts[i] = [part - lower[i, k] * other for part, other in zip(parts[i], parts[k])]
         return parts
 
@@ -150,21 +151,23 @@
             tiles = [tile - c * done for tile, c in zip(tiles, column)]
         return tiles
 
-    count = len(system) * SUBLANES
-    columns = [spread(j) for j in range(count - step, count)]
-    for first in range(count - step, 0, -step):
-        pivots = range(first, first + step)
+    first = len(system) * SUBLANES - step
+    columns = [spread(j) for j in range(first, first + step)]
+    while first >= wanted:
         left = pl.cdiv(first, SUBLANES)
+        following = range(first - step, first) if first > wanted else range(wanted)
         lower, inverse = factor(columns, first)
-        across = {j: [row_of(column, j) for column in columns] for j in range(first - step, first)}
+        across = {j: [row_of(column, j) for column in columns] for j in following}
+        size = len(columns)
         columns = forward(lower, [c[:left] for c in columns])
-        following = [update(spread(j)[:left], columns, lower, inverse, across[j]) for j in across]
-        system = update(system[:left], columns, lower, inverse, [row_of(system, i) for i in pivots])
-        columns = following
+        updated = [update(spread(j)[:left], columns, lower, inverse, across[j]) for j in following]
+        system = update(system[:left], columns, lower, inverse, [row_of(system, first + i) for i in range(size)])
+        columns = updated
+        first -= len(following)
     lower, inverse = factor(columns, 0)
-    rows = forward(lower, [[row_of(system, i)] for i in range(step)])
+    rows = forward(lower, [[row_of(system, i)] for i in range(wanted)])
     solved = [row[0] * scale for row, scale in zip(rows, inverse)]
-    for k in reversed(range(step)):
+    for k in reversed(range(wanted)):
         for i in range(k):
             solved[i] = solved[i] - lower[k, i] * solved[k]
     return solved
@@ -218,7 +221,7 @@
     for first in range(0, examples, SUBLANES):
         tile = jnp.take_along_axis(gram_ref[first : first + SUBLANES], source, axis=1) * scale
         system.append(jnp.where(lane == row + first, tile + damp_ratio / fisher_dim, tile))
-    solved = solve_first(system, scratch)
+    solved = solve_first(system, scratch, per_dev)
     scores = solved[0]
     for i in range(1, len(solved)):
         scores = jnp.where(row == i, solved[i], scores)
@@ -235,7 +238,7 @@
         out_specs=pl.BlockSpec(memory_space=pltpu.VMEM),
         scratch_shapes=[
             pltpu.VMEM((examples, LANES), jnp.float32),
-            pltpu.VMEM((3 * examples, SUBLANES, LANES), jnp.float32),
+            pltpu.VMEM((4 * examples, SUBLANES, LANES), jnp.float32),
         ],
         compiler_params=pltpu.CompilerParams(vmem_limit_bytes=8 * 2**20),
     )(*tiles, query_index.reshape(1, nq))

time: 22.1 us -> 22.6 us (1.023)
  Pallas kernels: 7.02 us -> 7.53 us
    pallas_call x1, Pallas kernels: 2.15 us -> 2.66 us  [gram_scores(): pl.pallas_call(functools.partial(solve_kernel, per_dev, inner, axis), out...]
where the time goes in v25:
time: 22.6 us; the launch traced here: 22.4 us
  starting transfers between devices  7.61 us (34%)
  Pallas kernels  7.53 us (33%)
  waiting for transfers between devices  7.28 us (32%)
    ppermute x6, starting transfers between devices, swap(): return lax.ppermute(block, axis, [(i, i ^ slot) for i in range(size)])  7.61 us
    ppermute x6, waiting for transfers between devices, swap(): return lax.ppermute(block, axis, [(i, i ^ slot) for i in range(size)])  7.28 us
    pallas_call x1, Pallas kernels, sketch_rows(): pl.pallas_call(functools.partial(sketch_kernel, bounds, seq_len), out_sha...  4.87 us
    pallas_call x1, Pallas kernels, gram_scores(): pl.pallas_call(functools.partial(solve_kernel, per_dev, inner, axis), out...  2.66 us
  transfers between devices with their start and end apart: 6, of which 3 were waited for; matrix products, arithmetic and copies ran while one was open for 0% of the time, Pallas kernels for 0%

profile of v25, /device:TPU:0, one launch (start us, length us, event | category | flops | bytes accessed | tf_op | source)
XLA Modules:
  0.0 22.4 jit_solution(16036226709623252981)
XLA Ops:
  0.0 0.0 copy-start
  0.0 4.9 %shard_map.64 = f32[32,128]{1,0:T(8,128)S(1)} custom-call(bf16[256,8192]{1,0:T(8,128)(2,1)} %bitcast.6, bf16[256,8192]{1,0:T(8,128)(2,1)} %bitcast.7, bf16[32,8192]{1,0:T(8,128)(2,1)} %bitcast.8, bf16[32,8192]{1,0:T(8,128)(2,1)} %bitcast.9, s32[4]{0:T(128)} %lengths_hbm.1), custom_call_target="tpu_custom_call" | custom-call | tf_op jit(solution)/shard_map/pallas_call | solution.py:77
  4.9 3.5 %collective-permute-start.2 = (f32[32,128]{1,0:T(8,128)S(1)}, f32[32,128]{1,0:T(8,128)S(1)}, u32[]{:S(2)}, u32[]{:S(2)}) collective-permute-start(f32[32,128]{1,0:T(8,128)S(1)} %shard_map.64), channel_id=1, source_target_pairs={{0,9},{1,8},{2,11},{3,10},{4,13},{5,12},{6,15},{7,14},{8,1},{9,0},... | collective-permute-start | bytes 49160 | tf_op jit(solution)/shard_map/ppermute | solution.py:257
  8.4 1.7 %collective-permute-start.1 = (f32[32,128]{1,0:T(8,128)S(1)}, f32[32,128]{1,0:T(8,128)S(1)}, u32[]{:S(2)}, u32[]{:S(2)}) collective-permute-start(f32[32,128]{1,0:T(8,128)S(1)} %shard_map.64), channel_id=1, source_target_pairs={{0,12},{1,13},{2,14},{3,15},{4,8},{5,9},{6,10},{7,11},{8,4},{9,5},... | collective-permute-start | bytes 49160 | tf_op jit(solution)/shard_map/ppermute | solution.py:257
  10.1 0.2 collective-permute-start
  10.3 0.0 collective-permute-done.2
  10.3 3.7 %collective-permute-done.1 = f32[32,128]{1,0:T(8,128)S(1)} collective-permute-done((f32[32,128]{1,0:T(8,128)S(1)}, f32[32,128]{1,0:T(8,128)S(1)}, u32[]{:S(2)}, u32[]{:S(2)}) %collective-permute-start.1) | collective-permute-done | bytes 16416 | tf_op jit(solution)/shard_map/ppermute | solution.py:257
  14.0 0.0 collective-permute-done
  14.0 1.6 %collective-permute-start.5 = (f32[128,128]{1,0:T(8,128)S(1)}, f32[128,128]{1,0:T(8,128)S(1)}, u32[]{:S(2)}, u32[]{:S(2)}) collective-permute-start(f32[128,128]{1,0:T(8,128)S(1)} %pad_maximum_fusion.refs_0_), channel_id=1, source_target_pairs={{0,2},{1,3},{2,0},{3,1},{4,6},{5,7},{6,4},{7,5},{8,10},{9,11},{10,... | collective-permute-start | bytes 196616 | tf_op jit(solution)/shard_map/ppermute | solution.py:257
  15.6 0.0 collective-permute-start.4
  15.6 0.6 %collective-permute-start.3 = (f32[128,128]{1,0:T(8,128)S(1)}, f32[128,128]{1,0:T(8,128)S(1)}, u32[]{:S(2)}, u32[]{:S(2)}) collective-permute-start(f32[128,128]{1,0:T(8,128)S(1)} %pad_maximum_fusion.refs_0_), channel_id=1, source_target_pairs={{0,1},{1,0},{2,3},{3,2},{4,5},{5,4},{6,7},{7,6},{8,9},{9,8},{10,11... | collective-permute-start | bytes 196616 | tf_op jit(solution)/shard_map/ppermute | solution.py:257
  16.2 2.1 %collective-permute-done.5.refs_3_ = f32[128,128]{1,0:T(8,128)S(1)} collective-permute-done((f32[128,128]{1,0:T(8,128)S(1)}, f32[128,128]{1,0:T(8,128)S(1)}, u32[]{:S(2)}, u32[]{:S(2)}) %collective-permute-start.5) | collective-permute-done | bytes 65568 | tf_op jit(solution)/shard_map/ppermute | solution.py:257
  18.4 1.4 %collective-permute-done.4.refs_2_ = f32[128,128]{1,0:T(8,128)S(1)} collective-permute-done((f32[128,128]{1,0:T(8,128)S(1)}, f32[128,128]{1,0:T(8,128)S(1)}, u32[]{:S(2)}, u32[]{:S(2)}) %collective-permute-start.4) | collective-permute-done | bytes 65568 | tf_op jit(solution)/shard_map/ppermute | solution.py:257
  19.8 0.0 collective-permute-done.3.refs_1_
  19.8 0.0 copy-done
  19.8 2.7 %shard_map.65 = f32[4,16]{1,0:T(4,128)} custom-call(f32[128,128]{1,0:T(8,128)S(1)} %pad_maximum_fusion.refs_0_, f32[128,128]{1,0:T(8,128)S(1)} %collective-permute-done.3.refs_1_, f32[128,128]{1,0:T(8,128)S(1)} %collective-permute-done.4.refs_2_, f32[128,128]{1,0:T(8,128)S(1)} %collective-permute-done.5.refs_3_, s32[1,16]{1,0:T(1,128)S(1)} %bitcast.5), custom_call_target="tpu_custom_call" | custom-call | tf_op jit(solution)/shard_map/pallas_call | solution.py:234
  (1 shorter events, 0.0 us)
Async XLA Ops:
  0.0 19.8 %copy-start = (s32[16]{0:T(128)S(1)}, s32[16]{0:T(128)}, u32[]{:S(2)}) copy-start(s32[16]{0:T(128)} %param.11) | copy-start | bytes 196
  4.9 5.4 %collective-permute-start.2 = (f32[32,128]{1,0:T(8,128)S(1)}, f32[32,128]{1,0:T(8,128)S(1)}, u32[]{:S(2)}, u32[]{:S(2)}) collective-permute-start(f32[32,128]{1,0:T(8,128)S(1)} %shard_map.64), channel_id=1, source_target_pairs={{0,9},{1,8},{2,11},{3,10},{4,13},{5,12},{6,15},{7,14},{8,1},{9,0},... | collective-permute-start | bytes 49160 | tf_op jit(solution)/shard_map/ppermute | solution.py:257
  8.4 5.6 %collective-permute-start.1 = (f32[32,128]{1,0:T(8,128)S(1)}, f32[32,128]{1,0:T(8,128)S(1)}, u32[]{:S(2)}, u32[]{:S(2)}) collective-permute-start(f32[32,128]{1,0:T(8,128)S(1)} %shard_map.64), channel_id=1, source_target_pairs={{0,12},{1,13},{2,14},{3,15},{4,8},{5,9},{6,10},{7,11},{8,4},{9,5},... | collective-permute-start | bytes 49160 | tf_op jit(solution)/shard_map/ppermute | solution.py:257
  10.1 3.9 %collective-permute-start = (f32[32,128]{1,0:T(8,128)S(1)}, f32[32,128]{1,0:T(8,128)S(1)}, u32[]{:S(2)}, u32[]{:S(2)}) collective-permute-start(f32[32,128]{1,0:T(8,128)S(1)} %shard_map.64), channel_id=1, source_target_pairs={{0,5},{1,4},{2,7},{3,6},{4,1},{5,0},{6,3},{7,2},{8,13},{9,12},{10,... | collective-permute-start | bytes 49160 | tf_op jit(solution)/shard_map/ppermute | solution.py:257
  14.0 4.3 %collective-permute-start.5 = (f32[128,128]{1,0:T(8,128)S(1)}, f32[128,128]{1,0:T(8,128)S(1)}, u32[]{:S(2)}, u32[]{:S(2)}) collective-permute-start(f32[128,128]{1,0:T(8,128)S(1)} %pad_maximum_fusion.refs_0_), channel_id=1, source_target_pairs={{0,2},{1,3},{2,0},{3,1},{4,6},{5,7},{6,4},{7,5},{8,10},{9,11},{10,... | collective-permute-start | bytes 196616 | tf_op jit(solution)/shard_map/ppermute | solution.py:257
  15.6 4.2 %collective-permute-start.4 = (f32[128,128]{1,0:T(8,128)S(1)}, f32[128,128]{1,0:T(8,128)S(1)}, u32[]{:S(2)}, u32[]{:S(2)}) collective-permute-start(f32[128,128]{1,0:T(8,128)S(1)} %pad_maximum_fusion.refs_0_), channel_id=1, source_target_pairs={{0,3},{1,2},{2,1},{3,0},{4,7},{5,6},{6,5},{7,4},{8,11},{9,10},{10,... | collective-permute-start | bytes 196616 | tf_op jit(solution)/shard_map/ppermute | solution.py:257
  15.6 4.2 %collective-permute-start.3 = (f32[128,128]{1,0:T(8,128)S(1)}, f32[128,128]{1,0:T(8,128)S(1)}, u32[]{:S(2)}, u32[]{:S(2)}) collective-permute-start(f32[128,128]{1,0:T(8,128)S(1)} %pad_maximum_fusion.refs_0_), channel_id=1, source_target_pairs={{0,1},{1,0},{2,3},{3,2},{4,5},{5,4},{6,7},{7,6},{8,9},{9,8},{10,11... | collective-permute-start | bytes 196616 | tf_op jit(solution)/shard_map/ppermute | solution.py:257

commit v26 on v23

--- a/solution.py
+++ b/solution.py
@@ -32,31 +32,31 @@
         )
         for copy in copies[-1]:
             copy.start()
-    feat = jnp.zeros((rows, rank_dim), jnp.float32)
+    feat = jnp.zeros((rank_dim, rows), jnp.float32)
     grad = jnp.zeros((rank_dim, rows), jnp.float32)
     for c in range(chunks):
         cols = slice(bounds[c], bounds[c + 1])
         for copy in copies[c]:
             copy.wait()
-        feat = feat + lax.dot_general(act[:, cols], pin[:, cols], NT, preferred_element_type=jnp.float32)
+        feat = feat + lax.dot_general(pin[:, cols], act[:, cols], NT, preferred_element_type=jnp.float32)
         grad = grad + lax.dot_general(pout[:, cols], out[:, cols], NT, preferred_element_type=jnp.float32)
     lengths_copy.wait()
     count = rows // seq_len
     reps = LANES // rank_dim
-    position = lax.broadcasted_iota(jnp.int32, (rows, LANES), 0)
-    band = lax.broadcasted_iota(jnp.int32, (rows, LANES), 1) // rank_dim
-    live = jnp.zeros((rows, LANES), jnp.bool_)
+    position = lax.broadcasted_iota(jnp.int32, (rank_dim, rows), 1)
+    masked = []
     for e in range(count):
         first = e * seq_len
-        live = live | ((band == e) & (position >= first) & (position < first + lengths_ref[e]))
+        live = (position >= first) & (position < first + lengths_ref[e])
+        masked.append(jnp.where(live, feat, 0.0))
     outer = lax.dot_general(
         grad,
-        jnp.where(live, jnp.concatenate([feat] * reps, axis=1), 0.0),
-        (((1,), (0,)), ((), ())),
+        jnp.concatenate(masked, axis=0),
+        NT,
         precision=lax.Precision.HIGHEST,
         preferred_element_type=jnp.float32,
     )
-    band = band[:SUBLANES]
+    band = lax.broadcasted_iota(jnp.int32, (SUBLANES, LANES), 1) // rank_dim
     for e in range(count):
         entry = None
         for b in range(reps):
@@ -72,7 +72,7 @@
     rank_dim = project_in.shape[1]
     rows = count * seq_len
     unit = width // 32
-    bounds = [n * unit for n in (0, 2, 6, 10, 14, 18, 22, 26, 30, 32)]
+    bounds = [n * unit for n in (0, 1, 3, 6, 10, 14, 18, 22, 26, 30, 32)]
     chunks = len(bounds) - 1
     return pl.pallas_call(
         functools.partial(sketch_kernel, bounds, seq_len),
@@ -103,11 +103,11 @@
     )
 
 
-def solve_first(system, scratch):
+def solve_first(system, plain, scratch):
     step = 4
 
     def spread(column):
-        return [jnp.broadcast_to(tile[:, column : column + 1], tile.shape) for tile in system]
+        return [jnp.broadcast_to(tile[:, column : column + 1], tile.shape) for tile in plain]
 
     stored = {}
 
@@ -159,7 +159,7 @@
         across = {j: [row_of(column, j) for column in columns] for j in range(first - step, first)}
         columns = forward(lower, [c[:left] for c in columns])
         following = [update(spread(j)[:left], columns, lower, inverse, across[j]) for j in across]
-        system = update(system[:left], columns, lower, inverse, [row_of(system, i) for i in pivots])
+        system = plain = update(system[:left], columns, lower, inverse, [row_of(system, i) for i in pivots])
         columns = following
     lower, inverse = factor(columns, 0)
     rows = forward(lower, [[row_of(system, i)] for i in range(step)])
@@ -214,11 +214,12 @@
     scale = jnp.broadcast_to(1.0 / squares, (SUBLANES, LANES))
     gram_ref[:, :examples] = gram(sketches)
     row = lax.broadcasted_iota(jnp.int32, (SUBLANES, LANES), 0)
-    system = []
+    system, plain = [], []
     for first in range(0, examples, SUBLANES):
-        tile = jnp.take_along_axis(gram_ref[first : first + SUBLANES], source, axis=1) * scale
-        system.append(jnp.where(lane == row + first, tile + damp_ratio / fisher_dim, tile))
-    solved = solve_first(system, scratch)
+        tile = gram_ref[first : first + SUBLANES] * scale
+        plain.append(jnp.where(lane == row + first, tile + damp_ratio / fisher_dim, tile))
+        system.append(jnp.where(lane < examples, plain[-1], jnp.take_along_axis(tile, source, axis=1)))
+    solved = solve_first(system, plain, scratch)
     scores = solved[0]
     for i in range(1, len(solved)):
         scores = jnp.where(row == i, solved[i], scores)

time: 22.1 us -> 22.1 us (level)
  no operation moved by 1% of the time
where the time goes in v26:
time: 22.1 us; the launch traced here: 22 us
  starting transfers between devices  7.61 us (34%)
  waiting for transfers between devices  7.28 us (33%)
  Pallas kernels  7.07 us (32%)
    ppermute x6, starting transfers between devices, swap(): return lax.ppermute(block, axis, [(i, i ^ slot) for i in range(size)])  7.61 us
    ppermute x6, waiting for transfers between devices, swap(): return lax.ppermute(block, axis, [(i, i ^ slot) for i in range(size)])  7.28 us
    pallas_call x1, Pallas kernels, sketch_rows(): pl.pallas_call(functools.partial(sketch_kernel, bounds, seq_len), out_sha...  4.98 us
    pallas_call x1, Pallas kernels, gram_scores(): pl.pallas_call(functools.partial(solve_kernel, per_dev, inner, axis), out...  2.09 us
  transfers between devices with their start and end apart: 6, of which 3 were waited for; matrix products, arithmetic and copies ran while one was open for 0% of the time, Pallas kernels for 0%

profile of v26, /device:TPU:0, one launch (start us, length us, event | category | flops | bytes accessed | tf_op | source)
XLA Modules:
  0.0 22.0 jit_solution(15196001369159381968)
XLA Ops:
  0.0 0.0 copy-start
  0.0 5.0 %shard_map.64 = f32[32,128]{1,0:T(8,128)S(1)} custom-call(bf16[256,8192]{1,0:T(8,128)(2,1)} %bitcast.6, bf16[256,8192]{1,0:T(8,128)(2,1)} %bitcast.7, bf16[32,8192]{1,0:T(8,128)(2,1)} %bitcast.8, bf16[32,8192]{1,0:T(8,128)(2,1)} %bitcast.9, s32[4]{0:T(128)} %lengths_hbm.1), custom_call_target="tpu_custom_call" | custom-call | tf_op jit(solution)/shard_map/pallas_call | solution.py:77
  5.0 3.5 %collective-permute-start.2 = (f32[32,128]{1,0:T(8,128)S(1)}, f32[32,128]{1,0:T(8,128)S(1)}, u32[]{:S(2)}, u32[]{:S(2)}) collective-permute-start(f32[32,128]{1,0:T(8,128)S(1)} %shard_map.64), channel_id=1, source_target_pairs={{0,9},{1,8},{2,11},{3,10},{4,13},{5,12},{6,15},{7,14},{8,1},{9,0},... | collective-permute-start | bytes 49160 | tf_op jit(solution)/shard_map/ppermute | solution.py:255
  8.5 1.7 %collective-permute-start.1 = (f32[32,128]{1,0:T(8,128)S(1)}, f32[32,128]{1,0:T(8,128)S(1)}, u32[]{:S(2)}, u32[]{:S(2)}) collective-permute-start(f32[32,128]{1,0:T(8,128)S(1)} %shard_map.64), channel_id=1, source_target_pairs={{0,12},{1,13},{2,14},{3,15},{4,8},{5,9},{6,10},{7,11},{8,4},{9,5},... | collective-permute-start | bytes 49160 | tf_op jit(solution)/shard_map/ppermute | solution.py:255
  10.2 0.2 collective-permute-start
  10.4 0.0 collective-permute-done.2
  10.4 3.7 %collective-permute-done.1 = f32[32,128]{1,0:T(8,128)S(1)} collective-permute-done((f32[32,128]{1,0:T(8,128)S(1)}, f32[32,128]{1,0:T(8,128)S(1)}, u32[]{:S(2)}, u32[]{:S(2)}) %collective-permute-start.1) | collective-permute-done | bytes 16416 | tf_op jit(solution)/shard_map/ppermute | solution.py:255
  14.1 0.0 collective-permute-done
  14.2 1.5 %collective-permute-start.5 = (f32[128,128]{1,0:T(8,128)S(1)}, f32[128,128]{1,0:T(8,128)S(1)}, u32[]{:S(2)}, u32[]{:S(2)}) collective-permute-start(f32[128,128]{1,0:T(8,128)S(1)} %pad_maximum_fusion.refs_0_), channel_id=1, source_target_pairs={{0,2},{1,3},{2,0},{3,1},{4,6},{5,7},{6,4},{7,5},{8,10},{9,11},{10,... | collective-permute-start | bytes 196616 | tf_op jit(solution)/shard_map/ppermute | solution.py:255
  15.7 0.0 collective-permute-start.4
  15.7 0.7 %collective-permute-start.3 = (f32[128,128]{1,0:T(8,128)S(1)}, f32[128,128]{1,0:T(8,128)S(1)}, u32[]{:S(2)}, u32[]{:S(2)}) collective-permute-start(f32[128,128]{1,0:T(8,128)S(1)} %pad_maximum_fusion.refs_0_), channel_id=1, source_target_pairs={{0,1},{1,0},{2,3},{3,2},{4,5},{5,4},{6,7},{7,6},{8,9},{9,8},{10,11... | collective-permute-start | bytes 196616 | tf_op jit(solution)/shard_map/ppermute | solution.py:255
  16.4 2.1 %collective-permute-done.5.refs_3_ = f32[128,128]{1,0:T(8,128)S(1)} collective-permute-done((f32[128,128]{1,0:T(8,128)S(1)}, f32[128,128]{1,0:T(8,128)S(1)}, u32[]{:S(2)}, u32[]{:S(2)}) %collective-permute-start.5) | collective-permute-done | bytes 65568 | tf_op jit(solution)/shard_map/ppermute | solution.py:255
  18.5 1.4 %collective-permute-done.4.refs_2_ = f32[128,128]{1,0:T(8,128)S(1)} collective-permute-done((f32[128,128]{1,0:T(8,128)S(1)}, f32[128,128]{1,0:T(8,128)S(1)}, u32[]{:S(2)}, u32[]{:S(2)}) %collective-permute-start.4) | collective-permute-done | bytes 65568 | tf_op jit(solution)/shard_map/ppermute | solution.py:255
  19.9 0.0 collective-permute-done.3.refs_1_
  19.9 0.0 copy-done
  19.9 2.1 %shard_map.65 = f32[4,16]{1,0:T(4,128)} custom-call(f32[128,128]{1,0:T(8,128)S(1)} %pad_maximum_fusion.refs_0_, f32[128,128]{1,0:T(8,128)S(1)} %collective-permute-done.3.refs_1_, f32[128,128]{1,0:T(8,128)S(1)} %collective-permute-done.4.refs_2_, f32[128,128]{1,0:T(8,128)S(1)} %collective-permute-done.5.refs_3_, s32[1,16]{1,0:T(1,128)S(1)} %bitcast.5), custom_call_target="tpu_custom_call" | custom-call | tf_op jit(solution)/shard_map/pallas_call | solution.py:232
  (1 shorter events, 0.0 us)
Async XLA Ops:
  0.0 19.9 %copy-start = (s32[16]{0:T(128)S(1)}, s32[16]{0:T(128)}, u32[]{:S(2)}) copy-start(s32[16]{0:T(128)} %param.11) | copy-start | bytes 196
  5.0 5.4 %collective-permute-start.2 = (f32[32,128]{1,0:T(8,128)S(1)}, f32[32,128]{1,0:T(8,128)S(1)}, u32[]{:S(2)}, u32[]{:S(2)}) collective-permute-start(f32[32,128]{1,0:T(8,128)S(1)} %shard_map.64), channel_id=1, source_target_pairs={{0,9},{1,8},{2,11},{3,10},{4,13},{5,12},{6,15},{7,14},{8,1},{9,0},... | collective-permute-start | bytes 49160 | tf_op jit(solution)/shard_map/ppermute | solution.py:255
  8.5 5.6 %collective-permute-start.1 = (f32[32,128]{1,0:T(8,128)S(1)}, f32[32,128]{1,0:T(8,128)S(1)}, u32[]{:S(2)}, u32[]{:S(2)}) collective-permute-start(f32[32,128]{1,0:T(8,128)S(1)} %shard_map.64), channel_id=1, source_target_pairs={{0,12},{1,13},{2,14},{3,15},{4,8},{5,9},{6,10},{7,11},{8,4},{9,5},... | collective-permute-start | bytes 49160 | tf_op jit(solution)/shard_map/ppermute | solution.py:255
  10.2 3.9 %collective-permute-start = (f32[32,128]{1,0:T(8,128)S(1)}, f32[32,128]{1,0:T(8,128)S(1)}, u32[]{:S(2)}, u32[]{:S(2)}) collective-permute-start(f32[32,128]{1,0:T(8,128)S(1)} %shard_map.64), channel_id=1, source_target_pairs={{0,5},{1,4},{2,7},{3,6},{4,1},{5,0},{6,3},{7,2},{8,13},{9,12},{10,... | collective-permute-start | bytes 49160 | tf_op jit(solution)/shard_map/ppermute | solution.py:255
  14.2 4.3 %collective-permute-start.5 = (f32[128,128]{1,0:T(8,128)S(1)}, f32[128,128]{1,0:T(8,128)S(1)}, u32[]{:S(2)}, u32[]{:S(2)}) collective-permute-start(f32[128,128]{1,0:T(8,128)S(1)} %pad_maximum_fusion.refs_0_), channel_id=1, source_target_pairs={{0,2},{1,3},{2,0},{3,1},{4,6},{5,7},{6,4},{7,5},{8,10},{9,11},{10,... | collective-permute-start | bytes 196616 | tf_op jit(solution)/shard_map/ppermute | solution.py:255
  15.7 4.2 %collective-permute-start.4 = (f32[128,128]{1,0:T(8,128)S(1)}, f32[128,128]{1,0:T(8,128)S(1)}, u32[]{:S(2)}, u32[]{:S(2)}) collective-permute-start(f32[128,128]{1,0:T(8,128)S(1)} %pad_maximum_fusion.refs_0_), channel_id=1, source_target_pairs={{0,3},{1,2},{2,1},{3,0},{4,7},{5,6},{6,5},{7,4},{8,11},{9,10},{10,... | collective-permute-start | bytes 196616 | tf_op jit(solution)/shard_map/ppermute | solution.py:255
  15.7 4.2 %collective-permute-start.3 = (f32[128,128]{1,0:T(8,128)S(1)}, f32[128,128]{1,0:T(8,128)S(1)}, u32[]{:S(2)}, u32[]{:S(2)}) collective-permute-start(f32[128,128]{1,0:T(8,128)S(1)} %pad_maximum_fusion.refs_0_), channel_id=1, source_target_pairs={{0,1},{1,0},{2,3},{3,2},{4,5},{5,4},{6,7},{7,6},{8,9},{9,8},{10,11... | collective-permute-start | bytes 196616 | tf_op jit(solution)/shard_map/ppermute | solution.py:255

commit v27 on v23

--- a/solution.py
+++ b/solution.py
@@ -103,11 +103,11 @@
     )
 
 
-def solve_first(system, scratch):
+def solve_first(system, plain, scratch):
     step = 4
 
     def spread(column):
-        return [jnp.broadcast_to(tile[:, column : column + 1], tile.shape) for tile in system]
+        return [jnp.broadcast_to(tile[:, column : column + 1], tile.shape) for tile in plain]
 
     stored = {}
 
@@ -159,7 +159,7 @@
         across = {j: [row_of(column, j) for column in columns] for j in range(first - step, first)}
         columns = forward(lower, [c[:left] for c in columns])
         following = [update(spread(j)[:left], columns, lower, inverse, across[j]) for j in across]
-        system = update(system[:left], columns, lower, inverse, [row_of(system, i) for i in pivots])
+        system = plain = update(system[:left], columns, lower, inverse, [row_of(system, i) for i in pivots])
         columns = following
     lower, inverse = factor(columns, 0)
     rows = forward(lower, [[row_of(system, i)] for i in range(step)])
@@ -196,7 +196,7 @@
     gram_ref[...] = jnp.zeros(gram_ref.shape, jnp.float32)
     slot = (query_ref[...] // per_dev) ^ lax.axis_index(axis)
     n = slot // inner
-    place = (gray((slot ^ partner(n, inner)) % inner) * outer + gray(n)) * per_dev + query_ref[...] % per_dev
+    place = ((slot ^ partner(n, inner)) % inner * outer + gray(n)) * per_dev + query_ref[...] % per_dev
     rest = LANES - examples - nq
     place = jnp.concatenate(
         [jnp.zeros((1, examples), jnp.int32), place] + ([jnp.zeros((1, rest), jnp.int32)] if rest else []), axis=1
@@ -214,11 +214,12 @@
     scale = jnp.broadcast_to(1.0 / squares, (SUBLANES, LANES))
     gram_ref[:, :examples] = gram(sketches)
     row = lax.broadcasted_iota(jnp.int32, (SUBLANES, LANES), 0)
-    system = []
+    system, plain = [], []
     for first in range(0, examples, SUBLANES):
-        tile = jnp.take_along_axis(gram_ref[first : first + SUBLANES], source, axis=1) * scale
-        system.append(jnp.where(lane == row + first, tile + damp_ratio / fisher_dim, tile))
-    solved = solve_first(system, scratch)
+        tile = gram_ref[first : first + SUBLANES] * scale
+        plain.append(jnp.where(lane == row + first, tile + damp_ratio / fisher_dim, tile))
+        system.append(jnp.where(lane < examples, plain[-1], jnp.take_along_axis(tile, source, axis=1)))
+    solved = solve_first(system, plain, scratch)
     scores = solved[0]
     for i in range(1, len(solved)):
         scores = jnp.where(row == i, solved[i], scores)
@@ -255,7 +256,7 @@
 
     rows = sorted(range(1, size // inner), key=gray)
     column = jnp.concatenate([tiles] + [swap(tiles, partner(n, inner)) for n in rows], axis=0)
-    return [column] + [swap(column, n) for n in sorted(range(1, inner), key=gray)]
+    return [column] + [swap(column, n) for n in range(1, inner)]
 
 
 def large_scores(tiles, query_index, per_dev, axis):

time: 22.1 us -> 22.2 us (level)
  waiting for transfers between devices: 7.28 us -> 7.69 us
  starting transfers between devices: 7.61 us -> 7.33 us
    ppermute x6, waiting for transfers between devices: 7.28 us -> 7.69 us  [swap(): return lax.ppermute(block, axis, [(i, i ^ slot) for i in range(size)])]
    ppermute x6, starting transfers between devices: 7.61 us -> 7.33 us  [swap(): return lax.ppermute(block, axis, [(i, i ^ slot) for i in range(size)])]
where the time goes in v27:
time: 22.2 us; the launch traced here: 22 us
  waiting for transfers between devices  7.69 us (35%)
  starting transfers between devices  7.33 us (33%)
  Pallas kernels  6.97 us (31%)
    ppermute x6, waiting for transfers between devices, swap(): return lax.ppermute(block, axis, [(i, i ^ slot) for i in range(size)])  7.69 us
    ppermute x6, starting transfers between devices, swap(): return lax.ppermute(block, axis, [(i, i ^ slot) for i in range(size)])  7.33 us
    pallas_call x1, Pallas kernels, sketch_rows(): pl.pallas_call(functools.partial(sketch_kernel, bounds, seq_len), out_sha...  4.87 us
    pallas_call x1, Pallas kernels, gram_scores(): pl.pallas_call(functools.partial(solve_kernel, per_dev, inner, axis), out...  2.1 us
  transfers between devices with their start and end apart: 6, of which 3 were waited for; matrix products, arithmetic and copies ran while one was open for 0% of the time, Pallas kernels for 0%

profile of v27, /device:TPU:0, one launch (start us, length us, event | category | flops | bytes accessed | tf_op | source)
XLA Modules:
  0.0 22.0 jit_solution(3803072688917761568)
XLA Ops:
  0.0 0.0 copy-start
  0.0 4.9 %shard_map.64 = f32[32,128]{1,0:T(8,128)S(1)} custom-call(bf16[256,8192]{1,0:T(8,128)(2,1)} %bitcast.6, bf16[256,8192]{1,0:T(8,128)(2,1)} %bitcast.7, bf16[32,8192]{1,0:T(8,128)(2,1)} %bitcast.8, bf16[32,8192]{1,0:T(8,128)(2,1)} %bitcast.9, s32[4]{0:T(128)} %lengths_hbm.1), custom_call_target="tpu_custom_call" | custom-call | tf_op jit(solution)/shard_map/pallas_call | solution.py:77
  4.9 3.5 %collective-permute-start.2 = (f32[32,128]{1,0:T(8,128)S(1)}, f32[32,128]{1,0:T(8,128)S(1)}, u32[]{:S(2)}, u32[]{:S(2)}) collective-permute-start(f32[32,128]{1,0:T(8,128)S(1)} %shard_map.64), channel_id=1, source_target_pairs={{0,9},{1,8},{2,11},{3,10},{4,13},{5,12},{6,15},{7,14},{8,1},{9,0},... | collective-permute-start | bytes 49160 | tf_op jit(solution)/shard_map/ppermute | solution.py:255
  8.4 1.7 %collective-permute-start.1 = (f32[32,128]{1,0:T(8,128)S(1)}, f32[32,128]{1,0:T(8,128)S(1)}, u32[]{:S(2)}, u32[]{:S(2)}) collective-permute-start(f32[32,128]{1,0:T(8,128)S(1)} %shard_map.64), channel_id=1, source_target_pairs={{0,12},{1,13},{2,14},{3,15},{4,8},{5,9},{6,10},{7,11},{8,4},{9,5},... | collective-permute-start | bytes 49160 | tf_op jit(solution)/shard_map/ppermute | solution.py:255
  10.1 0.2 collective-permute-start
  10.3 0.0 collective-permute-done.2
  10.3 3.7 %collective-permute-done.1 = f32[32,128]{1,0:T(8,128)S(1)} collective-permute-done((f32[32,128]{1,0:T(8,128)S(1)}, f32[32,128]{1,0:T(8,128)S(1)}, u32[]{:S(2)}, u32[]{:S(2)}) %collective-permute-start.1) | collective-permute-done | bytes 16416 | tf_op jit(solution)/shard_map/ppermute | solution.py:255
  14.0 0.0 collective-permute-done
  14.0 0.7 %collective-permute-start.5 = (f32[128,128]{1,0:T(8,128)S(1)}, f32[128,128]{1,0:T(8,128)S(1)}, u32[]{:S(2)}, u32[]{:S(2)}) collective-permute-start(f32[128,128]{1,0:T(8,128)S(1)} %pad_maximum_fusion.refs_0_), channel_id=1, source_target_pairs={{0,3},{1,2},{2,1},{3,0},{4,7},{5,6},{6,5},{7,4},{8,11},{9,10},{10,... | collective-permute-start | bytes 196616 | tf_op jit(solution)/shard_map/ppermute | solution.py:255
  14.7 0.9 %collective-permute-start.4 = (f32[128,128]{1,0:T(8,128)S(1)}, f32[128,128]{1,0:T(8,128)S(1)}, u32[]{:S(2)}, u32[]{:S(2)}) collective-permute-start(f32[128,128]{1,0:T(8,128)S(1)} %pad_maximum_fusion.refs_0_), channel_id=1, source_target_pairs={{0,2},{1,3},{2,0},{3,1},{4,6},{5,7},{6,4},{7,5},{8,10},{9,11},{10,... | collective-permute-start | bytes 196616 | tf_op jit(solution)/shard_map/ppermute | solution.py:255
  15.7 0.3 %collective-permute-start.3 = (f32[128,128]{1,0:T(8,128)S(1)}, f32[128,128]{1,0:T(8,128)S(1)}, u32[]{:S(2)}, u32[]{:S(2)}) collective-permute-start(f32[128,128]{1,0:T(8,128)S(1)} %pad_maximum_fusion.refs_0_), channel_id=1, source_target_pairs={{0,1},{1,0},{2,3},{3,2},{4,5},{5,4},{6,7},{7,6},{8,9},{9,8},{10,11... | collective-permute-start | bytes 196616 | tf_op jit(solution)/shard_map/ppermute | solution.py:255
  16.0 2.5 %collective-permute-done.5.refs_3_ = f32[128,128]{1,0:T(8,128)S(1)} collective-permute-done((f32[128,128]{1,0:T(8,128)S(1)}, f32[128,128]{1,0:T(8,128)S(1)}, u32[]{:S(2)}, u32[]{:S(2)}) %collective-permute-start.5) | collective-permute-done | bytes 65568 | tf_op jit(solution)/shard_map/ppermute | solution.py:255
  18.5 1.5 %collective-permute-done.4.refs_2_ = f32[128,128]{1,0:T(8,128)S(1)} collective-permute-done((f32[128,128]{1,0:T(8,128)S(1)}, f32[128,128]{1,0:T(8,128)S(1)}, u32[]{:S(2)}, u32[]{:S(2)}) %collective-permute-start.4) | collective-permute-done | bytes 65568 | tf_op jit(solution)/shard_map/ppermute | solution.py:255
  19.9 0.0 collective-permute-done.3.refs_1_
  19.9 0.0 copy-done
  19.9 2.1 %shard_map.65 = f32[4,16]{1,0:T(4,128)} custom-call(f32[128,128]{1,0:T(8,128)S(1)} %pad_maximum_fusion.refs_0_, f32[128,128]{1,0:T(8,128)S(1)} %collective-permute-done.3.refs_1_, f32[128,128]{1,0:T(8,128)S(1)} %collective-permute-done.4.refs_2_, f32[128,128]{1,0:T(8,128)S(1)} %collective-permute-done.5.refs_3_, s32[1,16]{1,0:T(1,128)S(1)} %bitcast.5), custom_call_target="tpu_custom_call" | custom-call | tf_op jit(solution)/shard_map/pallas_call | solution.py:232
  (1 shorter events, 0.0 us)
Async XLA Ops:
  0.0 19.9 %copy-start = (s32[16]{0:T(128)S(1)}, s32[16]{0:T(128)}, u32[]{:S(2)}) copy-start(s32[16]{0:T(128)} %param.11) | copy-start | bytes 196
  4.9 5.4 %collective-permute-start.2 = (f32[32,128]{1,0:T(8,128)S(1)}, f32[32,128]{1,0:T(8,128)S(1)}, u32[]{:S(2)}, u32[]{:S(2)}) collective-permute-start(f32[32,128]{1,0:T(8,128)S(1)} %shard_map.64), channel_id=1, source_target_pairs={{0,9},{1,8},{2,11},{3,10},{4,13},{5,12},{6,15},{7,14},{8,1},{9,0},... | collective-permute-start | bytes 49160 | tf_op jit(solution)/shard_map/ppermute | solution.py:255
  8.4 5.6 %collective-permute-start.1 = (f32[32,128]{1,0:T(8,128)S(1)}, f32[32,128]{1,0:T(8,128)S(1)}, u32[]{:S(2)}, u32[]{:S(2)}) collective-permute-start(f32[32,128]{1,0:T(8,128)S(1)} %shard_map.64), channel_id=1, source_target_pairs={{0,12},{1,13},{2,14},{3,15},{4,8},{5,9},{6,10},{7,11},{8,4},{9,5},... | collective-permute-start | bytes 49160 | tf_op jit(solution)/shard_map/ppermute | solution.py:255
  10.1 3.9 %collective-permute-start = (f32[32,128]{1,0:T(8,128)S(1)}, f32[32,128]{1,0:T(8,128)S(1)}, u32[]{:S(2)}, u32[]{:S(2)}) collective-permute-start(f32[32,128]{1,0:T(8,128)S(1)} %shard_map.64), channel_id=1, source_target_pairs={{0,5},{1,4},{2,7},{3,6},{4,1},{5,0},{6,3},{7,2},{8,13},{9,12},{10,... | collective-permute-start | bytes 49160 | tf_op jit(solution)/shard_map/ppermute | solution.py:255
  14.0 4.4 %collective-permute-start.5 = (f32[128,128]{1,0:T(8,128)S(1)}, f32[128,128]{1,0:T(8,128)S(1)}, u32[]{:S(2)}, u32[]{:S(2)}) collective-permute-start(f32[128,128]{1,0:T(8,128)S(1)} %pad_maximum_fusion.refs_0_), channel_id=1, source_target_pairs={{0,3},{1,2},{2,1},{3,0},{4,7},{5,6},{6,5},{7,4},{8,11},{9,10},{10,... | collective-permute-start | bytes 196616 | tf_op jit(solution)/shard_map/ppermute | solution.py:255
  14.7 5.2 %collective-permute-start.4 = (f32[128,128]{1,0:T(8,128)S(1)}, f32[128,128]{1,0:T(8,128)S(1)}, u32[]{:S(2)}, u32[]{:S(2)}) collective-permute-start(f32[128,128]{1,0:T(8,128)S(1)} %pad_maximum_fusion.refs_0_), channel_id=1, source_target_pairs={{0,2},{1,3},{2,0},{3,1},{4,6},{5,7},{6,4},{7,5},{8,10},{9,11},{10,... | collective-permute-start | bytes 196616 | tf_op jit(solution)/shard_map/ppermute | solution.py:255
  15.7 4.2 %collective-permute-start.3 = (f32[128,128]{1,0:T(8,128)S(1)}, f32[128,128]{1,0:T(8,128)S(1)}, u32[]{:S(2)}, u32[]{:S(2)}) collective-permute-start(f32[128,128]{1,0:T(8,128)S(1)} %pad_maximum_fusion.refs_0_), channel_id=1, source_target_pairs={{0,1},{1,0},{2,3},{3,2},{4,5},{5,4},{6,7},{7,6},{8,9},{9,8},{10,11... | collective-permute-start | bytes 196616 | tf_op jit(solution)/shard_map/ppermute | solution.py:255

commit v28 on v27

--- a/solution.py
+++ b/solution.py
@@ -196,7 +196,7 @@
     gram_ref[...] = jnp.zeros(gram_ref.shape, jnp.float32)
     slot = (query_ref[...] // per_dev) ^ lax.axis_index(axis)
     n = slot // inner
-    place = ((slot ^ partner(n, inner)) % inner * outer + gray(n)) * per_dev + query_ref[...] % per_dev
+    place = (gray((slot ^ partner(n, inner)) % inner) * outer + gray(n)) * per_dev + query_ref[...] % per_dev
     rest = LANES - examples - nq
     place = jnp.concatenate(
         [jnp.zeros((1, examples), jnp.int32), place] + ([jnp.zeros((1, rest), jnp.int32)] if rest else []), axis=1
@@ -256,7 +256,7 @@
 
     rows = sorted(range(1, size // inner), key=gray)
     column = jnp.concatenate([tiles] + [swap(tiles, partner(n, inner)) for n in rows], axis=0)
-    return [column] + [swap(column, n) for n in range(1, inner)]
+    return [column] + [swap(column, n) for n in sorted(range(1, inner), key=gray)]
 
 
 def large_scores(tiles, query_index, per_dev, axis):

time: 22.2 us -> 22 us (level)
  waiting for transfers between devices: 7.69 us -> 7.28 us
  starting transfers between devices: 7.33 us -> 7.61 us
    ppermute x6, waiting for transfers between devices: 7.69 us -> 7.28 us  [swap(): return lax.ppermute(block, axis, [(i, i ^ slot) for i in range(size)])]
    ppermute x6, starting transfers between devices: 7.33 us -> 7.61 us  [swap(): return lax.ppermute(block, axis, [(i, i ^ slot) for i in range(size)])]
where the time goes in v28:
time: 22 us; the launch traced here: 21.9 us
  starting transfers between devices  7.61 us (35%)
  waiting for transfers between devices  7.28 us (33%)
  Pallas kernels  6.97 us (32%)
    ppermute x6, starting transfers between devices, swap(): return lax.ppermute(block, axis, [(i, i ^ slot) for i in range(size)])  7.61 us
    ppermute x6, waiting for transfers between devices, swap(): return lax.ppermute(block, axis, [(i, i ^ slot) for i in range(size)])  7.28 us
    pallas_call x1, Pallas kernels, sketch_rows(): pl.pallas_call(functools.partial(sketch_kernel, bounds, seq_len), out_sha...  4.87 us
    pallas_call x1, Pallas kernels, gram_scores(): pl.pallas_call(functools.partial(solve_kernel, per_dev, inner, axis), out...  2.1 us
  transfers between devices with their start and end apart: 6, of which 3 were waited for; matrix products, arithmetic and copies ran while one was open for 0% of the time, Pallas kernels for 0%

profile of v28, /device:TPU:0, one launch (start us, length us, event | category | flops | bytes accessed | tf_op | source)
XLA Modules:
  0.0 21.9 jit_solution(727520990824774991)
XLA Ops:
  0.0 0.0 copy-start
  0.0 4.9 %shard_map.64 = f32[32,128]{1,0:T(8,128)S(1)} custom-call(bf16[256,8192]{1,0:T(8,128)(2,1)} %bitcast.6, bf16[256,8192]{1,0:T(8,128)(2,1)} %bitcast.7, bf16[32,8192]{1,0:T(8,128)(2,1)} %bitcast.8, bf16[32,8192]{1,0:T(8,128)(2,1)} %bitcast.9, s32[4]{0:T(128)} %lengths_hbm.1), custom_call_target="tpu_custom_call" | custom-call | tf_op jit(solution)/shard_map/pallas_call | solution.py:77
  4.9 3.5 %collective-permute-start.2 = (f32[32,128]{1,0:T(8,128)S(1)}, f32[32,128]{1,0:T(8,128)S(1)}, u32[]{:S(2)}, u32[]{:S(2)}) collective-permute-start(f32[32,128]{1,0:T(8,128)S(1)} %shard_map.64), channel_id=1, source_target_pairs={{0,9},{1,8},{2,11},{3,10},{4,13},{5,12},{6,15},{7,14},{8,1},{9,0},... | collective-permute-start | bytes 49160 | tf_op jit(solution)/shard_map/ppermute | solution.py:255
  8.4 1.7 %collective-permute-start.1 = (f32[32,128]{1,0:T(8,128)S(1)}, f32[32,128]{1,0:T(8,128)S(1)}, u32[]{:S(2)}, u32[]{:S(2)}) collective-permute-start(f32[32,128]{1,0:T(8,128)S(1)} %shard_map.64), channel_id=1, source_target_pairs={{0,12},{1,13},{2,14},{3,15},{4,8},{5,9},{6,10},{7,11},{8,4},{9,5},... | collective-permute-start | bytes 49160 | tf_op jit(solution)/shard_map/ppermute | solution.py:255
  10.1 0.2 collective-permute-start
  10.3 0.0 collective-permute-done.2
  10.3 3.7 %collective-permute-done.1 = f32[32,128]{1,0:T(8,128)S(1)} collective-permute-done((f32[32,128]{1,0:T(8,128)S(1)}, f32[32,128]{1,0:T(8,128)S(1)}, u32[]{:S(2)}, u32[]{:S(2)}) %collective-permute-start.1) | collective-permute-done | bytes 16416 | tf_op jit(solution)/shard_map/ppermute | solution.py:255
  14.0 0.0 collective-permute-done
  14.0 1.6 %collective-permute-start.5 = (f32[128,128]{1,0:T(8,128)S(1)}, f32[128,128]{1,0:T(8,128)S(1)}, u32[]{:S(2)}, u32[]{:S(2)}) collective-permute-start(f32[128,128]{1,0:T(8,128)S(1)} %pad_maximum_fusion.refs_0_), channel_id=1, source_target_pairs={{0,2},{1,3},{2,0},{3,1},{4,6},{5,7},{6,4},{7,5},{8,10},{9,11},{10,... | collective-permute-start | bytes 196616 | tf_op jit(solution)/shard_map/ppermute | solution.py:255
  15.6 0.0 collective-permute-start.4
  15.6 0.6 %collective-permute-start.3 = (f32[128,128]{1,0:T(8,128)S(1)}, f32[128,128]{1,0:T(8,128)S(1)}, u32[]{:S(2)}, u32[]{:S(2)}) collective-permute-start(f32[128,128]{1,0:T(8,128)S(1)} %pad_maximum_fusion.refs_0_), channel_id=1, source_target_pairs={{0,1},{1,0},{2,3},{3,2},{4,5},{5,4},{6,7},{7,6},{8,9},{9,8},{10,11... | collective-permute-start | bytes 196616 | tf_op jit(solution)/shard_map/ppermute | solution.py:255
  16.2 2.1 %collective-permute-done.5.refs_3_ = f32[128,128]{1,0:T(8,128)S(1)} collective-permute-done((f32[128,128]{1,0:T(8,128)S(1)}, f32[128,128]{1,0:T(8,128)S(1)}, u32[]{:S(2)}, u32[]{:S(2)}) %collective-permute-start.5) | collective-permute-done | bytes 65568 | tf_op jit(solution)/shard_map/ppermute | solution.py:255
  18.4 1.4 %collective-permute-done.4.refs_2_ = f32[128,128]{1,0:T(8,128)S(1)} collective-permute-done((f32[128,128]{1,0:T(8,128)S(1)}, f32[128,128]{1,0:T(8,128)S(1)}, u32[]{:S(2)}, u32[]{:S(2)}) %collective-permute-start.4) | collective-permute-done | bytes 65568 | tf_op jit(solution)/shard_map/ppermute | solution.py:255
  19.8 0.0 collective-permute-done.3.refs_1_
  19.8 0.0 copy-done
  19.8 2.1 %shard_map.65 = f32[4,16]{1,0:T(4,128)} custom-call(f32[128,128]{1,0:T(8,128)S(1)} %pad_maximum_fusion.refs_0_, f32[128,128]{1,0:T(8,128)S(1)} %collective-permute-done.3.refs_1_, f32[128,128]{1,0:T(8,128)S(1)} %collective-permute-done.4.refs_2_, f32[128,128]{1,0:T(8,128)S(1)} %collective-permute-done.5.refs_3_, s32[1,16]{1,0:T(1,128)S(1)} %bitcast.5), custom_call_target="tpu_custom_call" | custom-call | tf_op jit(solution)/shard_map/pallas_call | solution.py:232
  (1 shorter events, 0.0 us)
Async XLA Ops:
  0.0 19.8 %copy-start = (s32[16]{0:T(128)S(1)}, s32[16]{0:T(128)}, u32[]{:S(2)}) copy-start(s32[16]{0:T(128)} %param.11) | copy-start | bytes 196
  4.9 5.4 %collective-permute-start.2 = (f32[32,128]{1,0:T(8,128)S(1)}, f32[32,128]{1,0:T(8,128)S(1)}, u32[]{:S(2)}, u32[]{:S(2)}) collective-permute-start(f32[32,128]{1,0:T(8,128)S(1)} %shard_map.64), channel_id=1, source_target_pairs={{0,9},{1,8},{2,11},{3,10},{4,13},{5,12},{6,15},{7,14},{8,1},{9,0},... | collective-permute-start | bytes 49160 | tf_op jit(solution)/shard_map/ppermute | solution.py:255
  8.4 5.6 %collective-permute-start.1 = (f32[32,128]{1,0:T(8,128)S(1)}, f32[32,128]{1,0:T(8,128)S(1)}, u32[]{:S(2)}, u32[]{:S(2)}) collective-permute-start(f32[32,128]{1,0:T(8,128)S(1)} %shard_map.64), channel_id=1, source_target_pairs={{0,12},{1,13},{2,14},{3,15},{4,8},{5,9},{6,10},{7,11},{8,4},{9,5},... | collective-permute-start | bytes 49160 | tf_op jit(solution)/shard_map/ppermute | solution.py:255
  10.1 3.9 %collective-permute-start = (f32[32,128]{1,0:T(8,128)S(1)}, f32[32,128]{1,0:T(8,128)S(1)}, u32[]{:S(2)}, u32[]{:S(2)}) collective-permute-start(f32[32,128]{1,0:T(8,128)S(1)} %shard_map.64), channel_id=1, source_target_pairs={{0,5},{1,4},{2,7},{3,6},{4,1},{5,0},{6,3},{7,2},{8,13},{9,12},{10,... | collective-permute-start | bytes 49160 | tf_op jit(solution)/shard_map/ppermute | solution.py:255
  14.0 4.3 %collective-permute-start.5 = (f32[128,128]{1,0:T(8,128)S(1)}, f32[128,128]{1,0:T(8,128)S(1)}, u32[]{:S(2)}, u32[]{:S(2)}) collective-permute-start(f32[128,128]{1,0:T(8,128)S(1)} %pad_maximum_fusion.refs_0_), channel_id=1, source_target_pairs={{0,2},{1,3},{2,0},{3,1},{4,6},{5,7},{6,4},{7,5},{8,10},{9,11},{10,... | collective-permute-start | bytes 196616 | tf_op jit(solution)/shard_map/ppermute | solution.py:255
  15.6 4.2 %collective-permute-start.4 = (f32[128,128]{1,0:T(8,128)S(1)}, f32[128,128]{1,0:T(8,128)S(1)}, u32[]{:S(2)}, u32[]{:S(2)}) collective-permute-start(f32[128,128]{1,0:T(8,128)S(1)} %pad_maximum_fusion.refs_0_), channel_id=1, source_target_pairs={{0,3},{1,2},{2,1},{3,0},{4,7},{5,6},{6,5},{7,4},{8,11},{9,10},{10,... | collective-permute-start | bytes 196616 | tf_op jit(solution)/shard_map/ppermute | solution.py:255
  15.6 4.2 %collective-permute-start.3 = (f32[128,128]{1,0:T(8,128)S(1)}, f32[128,128]{1,0:T(8,128)S(1)}, u32[]{:S(2)}, u32[]{:S(2)}) collective-permute-start(f32[128,128]{1,0:T(8,128)S(1)} %pad_maximum_fusion.refs_0_), channel_id=1, source_target_pairs={{0,1},{1,0},{2,3},{3,2},{4,5},{5,4},{6,7},{7,6},{8,9},{9,8},{10,11... | collective-permute-start | bytes 196616 | tf_op jit(solution)/shard_map/ppermute | solution.py:255

commit v29 on v28

--- a/solution.py
+++ b/solution.py
@@ -247,7 +247,7 @@
 
 
 def partner(n, inner):
-    return n * inner ^ gray(n) & 1
+    return n * inner ^ (n >> 1) & ~n & 1
 
 
 def gather_xor(tiles, axis, size, inner):

time: 22 us -> 22 us (level)
  no operation moved by 1% of the time
where the time goes in v29:
time: 22 us; the launch traced here: 21.8 us
  waiting for transfers between devices  7.45 us (34%)
  starting transfers between devices  7.41 us (34%)
  Pallas kernels  6.95 us (32%)
    ppermute x6, waiting for transfers between devices, swap(): return lax.ppermute(block, axis, [(i, i ^ slot) for i in range(size)])  7.45 us
    ppermute x6, starting transfers between devices, swap(): return lax.ppermute(block, axis, [(i, i ^ slot) for i in range(size)])  7.41 us
    pallas_call x1, Pallas kernels, sketch_rows(): pl.pallas_call(functools.partial(sketch_kernel, bounds, seq_len), out_sha...  4.87 us
    pallas_call x1, Pallas kernels, gram_scores(): pl.pallas_call(functools.partial(solve_kernel, per_dev, inner, axis), out...  2.09 us
  transfers between devices with their start and end apart: 6, of which 3 were waited for; matrix products, arithmetic and copies ran while one was open for 0% of the time, Pallas kernels for 0%

profile of v29, /device:TPU:0, one launch (start us, length us, event | category | flops | bytes accessed | tf_op | source)
XLA Modules:
  0.0 21.8 jit_solution(13838908763467921042)
XLA Ops:
  0.0 0.0 copy-start
  0.0 4.9 %shard_map.64 = f32[32,128]{1,0:T(8,128)S(1)} custom-call(bf16[256,8192]{1,0:T(8,128)(2,1)} %bitcast.6, bf16[256,8192]{1,0:T(8,128)(2,1)} %bitcast.7, bf16[32,8192]{1,0:T(8,128)(2,1)} %bitcast.8, bf16[32,8192]{1,0:T(8,128)(2,1)} %bitcast.9, s32[4]{0:T(128)} %lengths_hbm.1), custom_call_target="tpu_custom_call" | custom-call | tf_op jit(solution)/shard_map/pallas_call | solution.py:77
  4.9 3.5 %collective-permute-start.2 = (f32[32,128]{1,0:T(8,128)S(1)}, f32[32,128]{1,0:T(8,128)S(1)}, u32[]{:S(2)}, u32[]{:S(2)}) collective-permute-start(f32[32,128]{1,0:T(8,128)S(1)} %shard_map.64), channel_id=1, source_target_pairs={{0,9},{1,8},{2,11},{3,10},{4,13},{5,12},{6,15},{7,14},{8,1},{9,0},... | collective-permute-start | bytes 49160 | tf_op jit(solution)/shard_map/ppermute | solution.py:255
  8.4 1.7 %collective-permute-start.1 = (f32[32,128]{1,0:T(8,128)S(1)}, f32[32,128]{1,0:T(8,128)S(1)}, u32[]{:S(2)}, u32[]{:S(2)}) collective-permute-start(f32[32,128]{1,0:T(8,128)S(1)} %shard_map.64), channel_id=1, source_target_pairs={{0,12},{1,13},{2,14},{3,15},{4,8},{5,9},{6,10},{7,11},{8,4},{9,5},... | collective-permute-start | bytes 49160 | tf_op jit(solution)/shard_map/ppermute | solution.py:255
  10.1 0.0 collective-permute-start
  10.1 0.0 collective-permute-done.2
  10.1 3.9 %collective-permute-done.1 = f32[32,128]{1,0:T(8,128)S(1)} collective-permute-done((f32[32,128]{1,0:T(8,128)S(1)}, f32[32,128]{1,0:T(8,128)S(1)}, u32[]{:S(2)}, u32[]{:S(2)}) %collective-permute-start.1) | collective-permute-done | bytes 16416 | tf_op jit(solution)/shard_map/ppermute | solution.py:255
  14.0 0.0 collective-permute-done
  14.0 1.5 %collective-permute-start.5 = (f32[128,128]{1,0:T(8,128)S(1)}, f32[128,128]{1,0:T(8,128)S(1)}, u32[]{:S(2)}, u32[]{:S(2)}) collective-permute-start(f32[128,128]{1,0:T(8,128)S(1)} %pad_maximum_fusion.refs_0_), channel_id=1, source_target_pairs={{0,2},{1,3},{2,0},{3,1},{4,6},{5,7},{6,4},{7,5},{8,10},{9,11},{10,... | collective-permute-start | bytes 196616 | tf_op jit(solution)/shard_map/ppermute | solution.py:255
  15.6 0.0 collective-permute-start.4
  15.6 0.6 %collective-permute-start.3 = (f32[128,128]{1,0:T(8,128)S(1)}, f32[128,128]{1,0:T(8,128)S(1)}, u32[]{:S(2)}, u32[]{:S(2)}) collective-permute-start(f32[128,128]{1,0:T(8,128)S(1)} %pad_maximum_fusion.refs_0_), channel_id=1, source_target_pairs={{0,1},{1,0},{2,3},{3,2},{4,5},{5,4},{6,7},{7,6},{8,9},{9,8},{10,11... | collective-permute-start | bytes 196616 | tf_op jit(solution)/shard_map/ppermute | solution.py:255
  16.2 2.1 %collective-permute-done.5.refs_3_ = f32[128,128]{1,0:T(8,128)S(1)} collective-permute-done((f32[128,128]{1,0:T(8,128)S(1)}, f32[128,128]{1,0:T(8,128)S(1)}, u32[]{:S(2)}, u32[]{:S(2)}) %collective-permute-start.5) | collective-permute-done | bytes 65568 | tf_op jit(solution)/shard_map/ppermute | solution.py:255
  18.3 1.4 %collective-permute-done.4.refs_2_ = f32[128,128]{1,0:T(8,128)S(1)} collective-permute-done((f32[128,128]{1,0:T(8,128)S(1)}, f32[128,128]{1,0:T(8,128)S(1)}, u32[]{:S(2)}, u32[]{:S(2)}) %collective-permute-start.4) | collective-permute-done | bytes 65568 | tf_op jit(solution)/shard_map/ppermute | solution.py:255
  19.7 0.0 collective-permute-done.3.refs_1_
  19.8 0.0 copy-done
  19.8 2.1 %shard_map.65 = f32[4,16]{1,0:T(4,128)} custom-call(f32[128,128]{1,0:T(8,128)S(1)} %pad_maximum_fusion.refs_0_, f32[128,128]{1,0:T(8,128)S(1)} %collective-permute-done.3.refs_1_, f32[128,128]{1,0:T(8,128)S(1)} %collective-permute-done.4.refs_2_, f32[128,128]{1,0:T(8,128)S(1)} %collective-permute-done.5.refs_3_, s32[1,16]{1,0:T(1,128)S(1)} %bitcast.5), custom_call_target="tpu_custom_call" | custom-call | tf_op jit(solution)/shard_map/pallas_call | solution.py:232
  (1 shorter events, 0.0 us)
Async XLA Ops:
  0.0 19.8 %copy-start = (s32[16]{0:T(128)S(1)}, s32[16]{0:T(128)}, u32[]{:S(2)}) copy-start(s32[16]{0:T(128)} %param.11) | copy-start | bytes 196
  4.9 5.2 %collective-permute-start.2 = (f32[32,128]{1,0:T(8,128)S(1)}, f32[32,128]{1,0:T(8,128)S(1)}, u32[]{:S(2)}, u32[]{:S(2)}) collective-permute-start(f32[32,128]{1,0:T(8,128)S(1)} %shard_map.64), channel_id=1, source_target_pairs={{0,9},{1,8},{2,11},{3,10},{4,13},{5,12},{6,15},{7,14},{8,1},{9,0},... | collective-permute-start | bytes 49160 | tf_op jit(solution)/shard_map/ppermute | solution.py:255
  8.4 5.6 %collective-permute-start.1 = (f32[32,128]{1,0:T(8,128)S(1)}, f32[32,128]{1,0:T(8,128)S(1)}, u32[]{:S(2)}, u32[]{:S(2)}) collective-permute-start(f32[32,128]{1,0:T(8,128)S(1)} %shard_map.64), channel_id=1, source_target_pairs={{0,12},{1,13},{2,14},{3,15},{4,8},{5,9},{6,10},{7,11},{8,4},{9,5},... | collective-permute-start | bytes 49160 | tf_op jit(solution)/shard_map/ppermute | solution.py:255
  10.1 3.9 %collective-permute-start = (f32[32,128]{1,0:T(8,128)S(1)}, f32[32,128]{1,0:T(8,128)S(1)}, u32[]{:S(2)}, u32[]{:S(2)}) collective-permute-start(f32[32,128]{1,0:T(8,128)S(1)} %shard_map.64), channel_id=1, source_target_pairs={{0,4},{1,5},{2,6},{3,7},{4,0},{5,1},{6,2},{7,3},{8,12},{9,13},{10,... | collective-permute-start | bytes 49160 | tf_op jit(solution)/shard_map/ppermute | solution.py:255
  14.0 4.3 %collective-permute-start.5 = (f32[128,128]{1,0:T(8,128)S(1)}, f32[128,128]{1,0:T(8,128)S(1)}, u32[]{:S(2)}, u32[]{:S(2)}) collective-permute-start(f32[128,128]{1,0:T(8,128)S(1)} %pad_maximum_fusion.refs_0_), channel_id=1, source_target_pairs={{0,2},{1,3},{2,0},{3,1},{4,6},{5,7},{6,4},{7,5},{8,10},{9,11},{10,... | collective-permute-start | bytes 196616 | tf_op jit(solution)/shard_map/ppermute | solution.py:255
  15.6 4.2 %collective-permute-start.4 = (f32[128,128]{1,0:T(8,128)S(1)}, f32[128,128]{1,0:T(8,128)S(1)}, u32[]{:S(2)}, u32[]{:S(2)}) collective-permute-start(f32[128,128]{1,0:T(8,128)S(1)} %pad_maximum_fusion.refs_0_), channel_id=1, source_target_pairs={{0,3},{1,2},{2,1},{3,0},{4,7},{5,6},{6,5},{7,4},{8,11},{9,10},{10,... | collective-permute-start | bytes 196616 | tf_op jit(solution)/shard_map/ppermute | solution.py:255
  15.6 4.2 %collective-permute-start.3 = (f32[128,128]{1,0:T(8,128)S(1)}, f32[128,128]{1,0:T(8,128)S(1)}, u32[]{:S(2)}, u32[]{:S(2)}) collective-permute-start(f32[128,128]{1,0:T(8,128)S(1)} %pad_maximum_fusion.refs_0_), channel_id=1, source_target_pairs={{0,1},{1,0},{2,3},{3,2},{4,5},{5,4},{6,7},{7,6},{8,9},{9,8},{10,11... | collective-permute-start | bytes 196616 | tf_op jit(solution)/shard_map/ppermute | solution.py:255

commit v30 on v29

--- a/solution.py
+++ b/solution.py
@@ -32,14 +32,16 @@
         )
         for copy in copies[-1]:
             copy.start()
-    feat = jnp.zeros((rows, rank_dim), jnp.float32)
-    grad = jnp.zeros((rank_dim, rows), jnp.float32)
+    feat = [jnp.zeros((rows, rank_dim), jnp.float32)] * 2
+    grad = [jnp.zeros((rank_dim, rows), jnp.float32)] * 2
     for c in range(chunks):
-        cols = slice(bounds[c], bounds[c + 1])
+        middle = (bounds[c] + bounds[c + 1]) // 2
         for copy in copies[c]:
             copy.wait()
-        feat = feat + lax.dot_general(act[:, cols], pin[:, cols], NT, preferred_element_type=jnp.float32)
-        grad = grad + lax.dot_general(pout[:, cols], out[:, cols], NT, preferred_element_type=jnp.float32)
+        for n, cols in enumerate((slice(bounds[c], middle), slice(middle, bounds[c + 1]))):
+            feat[n] = feat[n] + lax.dot_general(act[:, cols], pin[:, cols], NT, preferred_element_type=jnp.float32)
+            grad[n] = grad[n] + lax.dot_general(pout[:, cols], out[:, cols], NT, preferred_element_type=jnp.float32)
+    feat, grad = feat[0] + feat[1], grad[0] + grad[1]
     lengths_copy.wait()
     count = rows // seq_len
     reps = LANES // rank_dim

time: 22 us -> 22 us (level)
  no operation moved by 1% of the time
where the time goes in v30:
time: 22 us; the launch traced here: 21.8 us
  waiting for transfers between devices  7.45 us (34%)
  starting transfers between devices  7.41 us (34%)
  Pallas kernels  6.95 us (32%)
    ppermute x6, waiting for transfers between devices, swap(): return lax.ppermute(block, axis, [(i, i ^ slot) for i in range(size)])  7.45 us
    ppermute x6, starting transfers between devices, swap(): return lax.ppermute(block, axis, [(i, i ^ slot) for i in range(size)])  7.41 us
    pallas_call x1, Pallas kernels, sketch_rows(): pl.pallas_call(functools.partial(sketch_kernel, bounds, seq_len), out_sha...  4.87 us
    pallas_call x1, Pallas kernels, gram_scores(): pl.pallas_call(functools.partial(solve_kernel, per_dev, inner, axis), out...  2.09 us
  transfers between devices with their start and end apart: 6, of which 3 were waited for; matrix products, arithmetic and copies ran while one was open for 0% of the time, Pallas kernels for 0%

profile of v30, /device:TPU:0, one launch (start us, length us, event | category | flops | bytes accessed | tf_op | source)
XLA Modules:
  0.0 21.8 jit_solution(10803935615464232090)
XLA Ops:
  0.0 0.0 copy-start
  0.0 4.9 %shard_map.64 = f32[32,128]{1,0:T(8,128)S(1)} custom-call(bf16[256,8192]{1,0:T(8,128)(2,1)} %bitcast.6, bf16[256,8192]{1,0:T(8,128)(2,1)} %bitcast.7, bf16[32,8192]{1,0:T(8,128)(2,1)} %bitcast.8, bf16[32,8192]{1,0:T(8,128)(2,1)} %bitcast.9, s32[4]{0:T(128)} %lengths_hbm.1), custom_call_target="tpu_custom_call" | custom-call | tf_op jit(solution)/shard_map/pallas_call | solution.py:79
  4.9 3.5 %collective-permute-start.2 = (f32[32,128]{1,0:T(8,128)S(1)}, f32[32,128]{1,0:T(8,128)S(1)}, u32[]{:S(2)}, u32[]{:S(2)}) collective-permute-start(f32[32,128]{1,0:T(8,128)S(1)} %shard_map.64), channel_id=1, source_target_pairs={{0,9},{1,8},{2,11},{3,10},{4,13},{5,12},{6,15},{7,14},{8,1},{9,0},... | collective-permute-start | bytes 49160 | tf_op jit(solution)/shard_map/ppermute | solution.py:257
  8.4 1.7 %collective-permute-start.1 = (f32[32,128]{1,0:T(8,128)S(1)}, f32[32,128]{1,0:T(8,128)S(1)}, u32[]{:S(2)}, u32[]{:S(2)}) collective-permute-start(f32[32,128]{1,0:T(8,128)S(1)} %shard_map.64), channel_id=1, source_target_pairs={{0,12},{1,13},{2,14},{3,15},{4,8},{5,9},{6,10},{7,11},{8,4},{9,5},... | collective-permute-start | bytes 49160 | tf_op jit(solution)/shard_map/ppermute | solution.py:257
  10.1 0.0 collective-permute-start
  10.1 0.0 collective-permute-done.2
  10.1 3.9 %collective-permute-done.1 = f32[32,128]{1,0:T(8,128)S(1)} collective-permute-done((f32[32,128]{1,0:T(8,128)S(1)}, f32[32,128]{1,0:T(8,128)S(1)}, u32[]{:S(2)}, u32[]{:S(2)}) %collective-permute-start.1) | collective-permute-done | bytes 16416 | tf_op jit(solution)/shard_map/ppermute | solution.py:257
  14.0 0.0 collective-permute-done
  14.0 1.5 %collective-permute-start.5 = (f32[128,128]{1,0:T(8,128)S(1)}, f32[128,128]{1,0:T(8,128)S(1)}, u32[]{:S(2)}, u32[]{:S(2)}) collective-permute-start(f32[128,128]{1,0:T(8,128)S(1)} %pad_maximum_fusion.refs_0_), channel_id=1, source_target_pairs={{0,2},{1,3},{2,0},{3,1},{4,6},{5,7},{6,4},{7,5},{8,10},{9,11},{10,... | collective-permute-start | bytes 196616 | tf_op jit(solution)/shard_map/ppermute | solution.py:257
  15.6 0.0 collective-permute-start.4
  15.6 0.6 %collective-permute-start.3 = (f32[128,128]{1,0:T(8,128)S(1)}, f32[128,128]{1,0:T(8,128)S(1)}, u32[]{:S(2)}, u32[]{:S(2)}) collective-permute-start(f32[128,128]{1,0:T(8,128)S(1)} %pad_maximum_fusion.refs_0_), channel_id=1, source_target_pairs={{0,1},{1,0},{2,3},{3,2},{4,5},{5,4},{6,7},{7,6},{8,9},{9,8},{10,11... | collective-permute-start | bytes 196616 | tf_op jit(solution)/shard_map/ppermute | solution.py:257
  16.2 2.1 %collective-permute-done.5.refs_3_ = f32[128,128]{1,0:T(8,128)S(1)} collective-permute-done((f32[128,128]{1,0:T(8,128)S(1)}, f32[128,128]{1,0:T(8,128)S(1)}, u32[]{:S(2)}, u32[]{:S(2)}) %collective-permute-start.5) | collective-permute-done | bytes 65568 | tf_op jit(solution)/shard_map/ppermute | solution.py:257
  18.3 1.4 %collective-permute-done.4.refs_2_ = f32[128,128]{1,0:T(8,128)S(1)} collective-permute-done((f32[128,128]{1,0:T(8,128)S(1)}, f32[128,128]{1,0:T(8,128)S(1)}, u32[]{:S(2)}, u32[]{:S(2)}) %collective-permute-start.4) | collective-permute-done | bytes 65568 | tf_op jit(solution)/shard_map/ppermute | solution.py:257
  19.7 0.0 collective-permute-done.3.refs_1_
  19.8 0.0 copy-done
  19.8 2.1 %shard_map.65 = f32[4,16]{1,0:T(4,128)} custom-call(f32[128,128]{1,0:T(8,128)S(1)} %pad_maximum_fusion.refs_0_, f32[128,128]{1,0:T(8,128)S(1)} %collective-permute-done.3.refs_1_, f32[128,128]{1,0:T(8,128)S(1)} %collective-permute-done.4.refs_2_, f32[128,128]{1,0:T(8,128)S(1)} %collective-permute-done.5.refs_3_, s32[1,16]{1,0:T(1,128)S(1)} %bitcast.5), custom_call_target="tpu_custom_call" | custom-call | tf_op jit(solution)/shard_map/pallas_call | solution.py:234
  (1 shorter events, 0.0 us)
Async XLA Ops:
  0.0 19.8 %copy-start = (s32[16]{0:T(128)S(1)}, s32[16]{0:T(128)}, u32[]{:S(2)}) copy-start(s32[16]{0:T(128)} %param.11) | copy-start | bytes 196
  4.9 5.2 %collective-permute-start.2 = (f32[32,128]{1,0:T(8,128)S(1)}, f32[32,128]{1,0:T(8,128)S(1)}, u32[]{:S(2)}, u32[]{:S(2)}) collective-permute-start(f32[32,128]{1,0:T(8,128)S(1)} %shard_map.64), channel_id=1, source_target_pairs={{0,9},{1,8},{2,11},{3,10},{4,13},{5,12},{6,15},{7,14},{8,1},{9,0},... | collective-permute-start | bytes 49160 | tf_op jit(solution)/shard_map/ppermute | solution.py:257
  8.4 5.6 %collective-permute-start.1 = (f32[32,128]{1,0:T(8,128)S(1)}, f32[32,128]{1,0:T(8,128)S(1)}, u32[]{:S(2)}, u32[]{:S(2)}) collective-permute-start(f32[32,128]{1,0:T(8,128)S(1)} %shard_map.64), channel_id=1, source_target_pairs={{0,12},{1,13},{2,14},{3,15},{4,8},{5,9},{6,10},{7,11},{8,4},{9,5},... | collective-permute-start | bytes 49160 | tf_op jit(solution)/shard_map/ppermute | solution.py:257
  10.1 3.9 %collective-permute-start = (f32[32,128]{1,0:T(8,128)S(1)}, f32[32,128]{1,0:T(8,128)S(1)}, u32[]{:S(2)}, u32[]{:S(2)}) collective-permute-start(f32[32,128]{1,0:T(8,128)S(1)} %shard_map.64), channel_id=1, source_target_pairs={{0,4},{1,5},{2,6},{3,7},{4,0},{5,1},{6,2},{7,3},{8,12},{9,13},{10,... | collective-permute-start | bytes 49160 | tf_op jit(solution)/shard_map/ppermute | solution.py:257
  14.0 4.3 %collective-permute-start.5 = (f32[128,128]{1,0:T(8,128)S(1)}, f32[128,128]{1,0:T(8,128)S(1)}, u32[]{:S(2)}, u32[]{:S(2)}) collective-permute-start(f32[128,128]{1,0:T(8,128)S(1)} %pad_maximum_fusion.refs_0_), channel_id=1, source_target_pairs={{0,2},{1,3},{2,0},{3,1},{4,6},{5,7},{6,4},{7,5},{8,10},{9,11},{10,... | collective-permute-start | bytes 196616 | tf_op jit(solution)/shard_map/ppermute | solution.py:257
  15.6 4.2 %collective-permute-start.4 = (f32[128,128]{1,0:T(8,128)S(1)}, f32[128,128]{1,0:T(8,128)S(1)}, u32[]{:S(2)}, u32[]{:S(2)}) collective-permute-start(f32[128,128]{1,0:T(8,128)S(1)} %pad_maximum_fusion.refs_0_), channel_id=1, source_target_pairs={{0,3},{1,2},{2,1},{3,0},{4,7},{5,6},{6,5},{7,4},{8,11},{9,10},{10,... | collective-permute-start | bytes 196616 | tf_op jit(solution)/shard_map/ppermute | solution.py:257
  15.6 4.2 %collective-permute-start.3 = (f32[128,128]{1,0:T(8,128)S(1)}, f32[128,128]{1,0:T(8,128)S(1)}, u32[]{:S(2)}, u32[]{:S(2)}) collective-permute-start(f32[128,128]{1,0:T(8,128)S(1)} %pad_maximum_fusion.refs_0_), channel_id=1, source_target_pairs={{0,1},{1,0},{2,3},{3,2},{4,5},{5,4},{6,7},{7,6},{8,9},{9,8},{10,11... | collective-permute-start | bytes 196616 | tf_op jit(solution)/shard_map/ppermute | solution.py:257

commit v31 on v30

--- a/solution.py
+++ b/solution.py
@@ -109,7 +109,8 @@
     step = 4
 
     def spread(column):
-        return [jnp.broadcast_to(tile[:, column : column + 1], tile.shape) for tile in plain]
+        index = jnp.full((SUBLANES, LANES), column, jnp.int32)
+        return [jnp.take_along_axis(tile, index, axis=1) for tile in plain]
 
     stored = {}
 

time: 22 us -> 22 us (level)
  no operation moved by 1% of the time
where the time goes in v31:
time: 22 us; the launch traced here: 21.8 us
  waiting for transfers between devices  7.45 us (34%)
  starting transfers between devices  7.41 us (34%)
  Pallas kernels  6.95 us (32%)
    ppermute x6, waiting for transfers between devices, swap(): return lax.ppermute(block, axis, [(i, i ^ slot) for i in range(size)])  7.45 us
    ppermute x6, starting transfers between devices, swap(): return lax.ppermute(block, axis, [(i, i ^ slot) for i in range(size)])  7.41 us
    pallas_call x1, Pallas kernels, sketch_rows(): pl.pallas_call(functools.partial(sketch_kernel, bounds, seq_len), out_sha...  4.87 us
    pallas_call x1, Pallas kernels, gram_scores(): pl.pallas_call(functools.partial(solve_kernel, per_dev, inner, axis), out...  2.09 us
  transfers between devices with their start and end apart: 6, of which 3 were waited for; matrix products, arithmetic and copies ran while one was open for 0% of the time, Pallas kernels for 0%

profile of v31, /device:TPU:0, one launch (start us, length us, event | category | flops | bytes accessed | tf_op | source)
XLA Modules:
  0.0 21.8 jit_solution(10803935615464232090)
XLA Ops:
  0.0 0.0 copy-start
  0.0 4.9 %shard_map.64 = f32[32,128]{1,0:T(8,128)S(1)} custom-call(bf16[256,8192]{1,0:T(8,128)(2,1)} %bitcast.6, bf16[256,8192]{1,0:T(8,128)(2,1)} %bitcast.7, bf16[32,8192]{1,0:T(8,128)(2,1)} %bitcast.8, bf16[32,8192]{1,0:T(8,128)(2,1)} %bitcast.9, s32[4]{0:T(128)} %lengths_hbm.1), custom_call_target="tpu_custom_call" | custom-call | tf_op jit(solution)/shard_map/pallas_call | solution.py:79
  4.9 3.5 %collective-permute-start.2 = (f32[32,128]{1,0:T(8,128)S(1)}, f32[32,128]{1,0:T(8,128)S(1)}, u32[]{:S(2)}, u32[]{:S(2)}) collective-permute-start(f32[32,128]{1,0:T(8,128)S(1)} %shard_map.64), channel_id=1, source_target_pairs={{0,9},{1,8},{2,11},{3,10},{4,13},{5,12},{6,15},{7,14},{8,1},{9,0},... | collective-permute-start | bytes 49160 | tf_op jit(solution)/shard_map/ppermute | solution.py:258
  8.4 1.7 %collective-permute-start.1 = (f32[32,128]{1,0:T(8,128)S(1)}, f32[32,128]{1,0:T(8,128)S(1)}, u32[]{:S(2)}, u32[]{:S(2)}) collective-permute-start(f32[32,128]{1,0:T(8,128)S(1)} %shard_map.64), channel_id=1, source_target_pairs={{0,12},{1,13},{2,14},{3,15},{4,8},{5,9},{6,10},{7,11},{8,4},{9,5},... | collective-permute-start | bytes 49160 | tf_op jit(solution)/shard_map/ppermute | solution.py:258
  10.1 0.0 collective-permute-start
  10.1 0.0 collective-permute-done.2
  10.1 3.9 %collective-permute-done.1 = f32[32,128]{1,0:T(8,128)S(1)} collective-permute-done((f32[32,128]{1,0:T(8,128)S(1)}, f32[32,128]{1,0:T(8,128)S(1)}, u32[]{:S(2)}, u32[]{:S(2)}) %collective-permute-start.1) | collective-permute-done | bytes 16416 | tf_op jit(solution)/shard_map/ppermute | solution.py:258
  14.0 0.0 collective-permute-done
  14.0 1.5 %collective-permute-start.5 = (f32[128,128]{1,0:T(8,128)S(1)}, f32[128,128]{1,0:T(8,128)S(1)}, u32[]{:S(2)}, u32[]{:S(2)}) collective-permute-start(f32[128,128]{1,0:T(8,128)S(1)} %pad_maximum_fusion.refs_0_), channel_id=1, source_target_pairs={{0,2},{1,3},{2,0},{3,1},{4,6},{5,7},{6,4},{7,5},{8,10},{9,11},{10,... | collective-permute-start | bytes 196616 | tf_op jit(solution)/shard_map/ppermute | solution.py:258
  15.6 0.0 collective-permute-start.4
  15.6 0.6 %collective-permute-start.3 = (f32[128,128]{1,0:T(8,128)S(1)}, f32[128,128]{1,0:T(8,128)S(1)}, u32[]{:S(2)}, u32[]{:S(2)}) collective-permute-start(f32[128,128]{1,0:T(8,128)S(1)} %pad_maximum_fusion.refs_0_), channel_id=1, source_target_pairs={{0,1},{1,0},{2,3},{3,2},{4,5},{5,4},{6,7},{7,6},{8,9},{9,8},{10,11... | collective-permute-start | bytes 196616 | tf_op jit(solution)/shard_map/ppermute | solution.py:258
  16.2 2.1 %collective-permute-done.5.refs_3_ = f32[128,128]{1,0:T(8,128)S(1)} collective-permute-done((f32[128,128]{1,0:T(8,128)S(1)}, f32[128,128]{1,0:T(8,128)S(1)}, u32[]{:S(2)}, u32[]{:S(2)}) %collective-permute-start.5) | collective-permute-done | bytes 65568 | tf_op jit(solution)/shard_map/ppermute | solution.py:258
  18.3 1.4 %collective-permute-done.4.refs_2_ = f32[128,128]{1,0:T(8,128)S(1)} collective-permute-done((f32[128,128]{1,0:T(8,128)S(1)}, f32[128,128]{1,0:T(8,128)S(1)}, u32[]{:S(2)}, u32[]{:S(2)}) %collective-permute-start.4) | collective-permute-done | bytes 65568 | tf_op jit(solution)/shard_map/ppermute | solution.py:258
  19.7 0.0 collective-permute-done.3.refs_1_
  19.8 0.0 copy-done
  19.8 2.1 %shard_map.65 = f32[4,16]{1,0:T(4,128)} custom-call(f32[128,128]{1,0:T(8,128)S(1)} %pad_maximum_fusion.refs_0_, f32[128,128]{1,0:T(8,128)S(1)} %collective-permute-done.3.refs_1_, f32[128,128]{1,0:T(8,128)S(1)} %collective-permute-done.4.refs_2_, f32[128,128]{1,0:T(8,128)S(1)} %collective-permute-done.5.refs_3_, s32[1,16]{1,0:T(1,128)S(1)} %bitcast.5), custom_call_target="tpu_custom_call" | custom-call | tf_op jit(solution)/shard_map/pallas_call | solution.py:235
  (1 shorter events, 0.0 us)
Async XLA Ops:
  0.0 19.8 %copy-start = (s32[16]{0:T(128)S(1)}, s32[16]{0:T(128)}, u32[]{:S(2)}) copy-start(s32[16]{0:T(128)} %param.11) | copy-start | bytes 196
  4.9 5.2 %collective-permute-start.2 = (f32[32,128]{1,0:T(8,128)S(1)}, f32[32,128]{1,0:T(8,128)S(1)}, u32[]{:S(2)}, u32[]{:S(2)}) collective-permute-start(f32[32,128]{1,0:T(8,128)S(1)} %shard_map.64), channel_id=1, source_target_pairs={{0,9},{1,8},{2,11},{3,10},{4,13},{5,12},{6,15},{7,14},{8,1},{9,0},... | collective-permute-start | bytes 49160 | tf_op jit(solution)/shard_map/ppermute | solution.py:258
  8.4 5.6 %collective-permute-start.1 = (f32[32,128]{1,0:T(8,128)S(1)}, f32[32,128]{1,0:T(8,128)S(1)}, u32[]{:S(2)}, u32[]{:S(2)}) collective-permute-start(f32[32,128]{1,0:T(8,128)S(1)} %shard_map.64), channel_id=1, source_target_pairs={{0,12},{1,13},{2,14},{3,15},{4,8},{5,9},{6,10},{7,11},{8,4},{9,5},... | collective-permute-start | bytes 49160 | tf_op jit(solution)/shard_map/ppermute | solution.py:258
  10.1 3.9 %collective-permute-start = (f32[32,128]{1,0:T(8,128)S(1)}, f32[32,128]{1,0:T(8,128)S(1)}, u32[]{:S(2)}, u32[]{:S(2)}) collective-permute-start(f32[32,128]{1,0:T(8,128)S(1)} %shard_map.64), channel_id=1, source_target_pairs={{0,4},{1,5},{2,6},{3,7},{4,0},{5,1},{6,2},{7,3},{8,12},{9,13},{10,... | collective-permute-start | bytes 49160 | tf_op jit(solution)/shard_map/ppermute | solution.py:258
  14.0 4.3 %collective-permute-start.5 = (f32[128,128]{1,0:T(8,128)S(1)}, f32[128,128]{1,0:T(8,128)S(1)}, u32[]{:S(2)}, u32[]{:S(2)}) collective-permute-start(f32[128,128]{1,0:T(8,128)S(1)} %pad_maximum_fusion.refs_0_), channel_id=1, source_target_pairs={{0,2},{1,3},{2,0},{3,1},{4,6},{5,7},{6,4},{7,5},{8,10},{9,11},{10,... | collective-permute-start | bytes 196616 | tf_op jit(solution)/shard_map/ppermute | solution.py:258
  15.6 4.2 %collective-permute-start.4 = (f32[128,128]{1,0:T(8,128)S(1)}, f32[128,128]{1,0:T(8,128)S(1)}, u32[]{:S(2)}, u32[]{:S(2)}) collective-permute-start(f32[128,128]{1,0:T(8,128)S(1)} %pad_maximum_fusion.refs_0_), channel_id=1, source_target_pairs={{0,3},{1,2},{2,1},{3,0},{4,7},{5,6},{6,5},{7,4},{8,11},{9,10},{10,... | collective-permute-start | bytes 196616 | tf_op jit(solution)/shard_map/ppermute | solution.py:258
  15.6 4.2 %collective-permute-start.3 = (f32[128,128]{1,0:T(8,128)S(1)}, f32[128,128]{1,0:T(8,128)S(1)}, u32[]{:S(2)}, u32[]{:S(2)}) collective-permute-start(f32[128,128]{1,0:T(8,128)S(1)} %pad_maximum_fusion.refs_0_), channel_id=1, source_target_pairs={{0,1},{1,0},{2,3},{3,2},{4,5},{5,4},{6,7},{7,6},{8,9},{9,8},{10,11... | collective-permute-start | bytes 196616 | tf_op jit(solution)/shard_map/ppermute | solution.py:258

commit v32 on v30

--- a/solution.py
+++ b/solution.py
@@ -20,14 +20,17 @@
     lengths_copy = pltpu.make_async_copy(lengths_hbm, lengths_ref, lengths_sem)
     lengths_copy.start()
     copies = []
+    early = 2
     for c in range(chunks):
         cols = pl.ds(bounds[c], bounds[c + 1] - bounds[c])
+        operands = [(act_hbm, act, cols), (out_hbm, out, cols)]
+        if c in (0, early):
+            cols = pl.ds(bounds[c], (width if c else bounds[early]) - bounds[c])
+            operands = [(pin_hbm, pin, cols), (pout_hbm, pout, cols)] + operands
         copies.append(
             [
-                pltpu.make_async_copy(src.at[:, cols], dst.at[:, cols], sems.at[n, c])
-                for n, (src, dst) in enumerate(
-                    ((pin_hbm, pin), (act_hbm, act), (pout_hbm, pout), (out_hbm, out))
-                )
+                pltpu.make_async_copy(src.at[:, part], dst.at[:, part], sems.at[n, c])
+                for n, (src, dst, part) in enumerate(operands)
             ]
         )
         for copy in copies[-1]:

time: 22 us -> 22 us (level)
  no operation moved by 1% of the time
where the time goes in v32:
time: 22 us; the launch traced here: 21.9 us
  waiting for transfers between devices  7.45 us (34%)
  starting transfers between devices  7.41 us (34%)
  Pallas kernels  6.99 us (32%)
    ppermute x6, waiting for transfers between devices, swap(): return lax.ppermute(block, axis, [(i, i ^ slot) for i in range(size)])  7.45 us
    ppermute x6, starting transfers between devices, swap(): return lax.ppermute(block, axis, [(i, i ^ slot) for i in range(size)])  7.41 us
    pallas_call x1, Pallas kernels, sketch_rows(): pl.pallas_call(functools.partial(sketch_kernel, bounds, seq_len), out_sha...  4.9 us
    pallas_call x1, Pallas kernels, gram_scores(): pl.pallas_call(functools.partial(solve_kernel, per_dev, inner, axis), out...  2.09 us
  transfers between devices with their start and end apart: 6, of which 3 were waited for; matrix products, arithmetic and copies ran while one was open for 0% of the time, Pallas kernels for 0%

profile of v32, /device:TPU:0, one launch (start us, length us, event | category | flops | bytes accessed | tf_op | source)
XLA Modules:
  0.0 21.9 jit_solution(11125604262352236380)
XLA Ops:
  0.0 0.0 copy-start
  0.0 4.9 %shard_map.64 = f32[32,128]{1,0:T(8,128)S(1)} custom-call(bf16[256,8192]{1,0:T(8,128)(2,1)} %bitcast.6, bf16[256,8192]{1,0:T(8,128)(2,1)} %bitcast.7, bf16[32,8192]{1,0:T(8,128)(2,1)} %bitcast.8, bf16[32,8192]{1,0:T(8,128)(2,1)} %bitcast.9, s32[4]{0:T(128)} %lengths_hbm.1), custom_call_target="tpu_custom_call" | custom-call | tf_op jit(solution)/shard_map/pallas_call | solution.py:82
  4.9 3.5 %collective-permute-start.2 = (f32[32,128]{1,0:T(8,128)S(1)}, f32[32,128]{1,0:T(8,128)S(1)}, u32[]{:S(2)}, u32[]{:S(2)}) collective-permute-start(f32[32,128]{1,0:T(8,128)S(1)} %shard_map.64), channel_id=1, source_target_pairs={{0,9},{1,8},{2,11},{3,10},{4,13},{5,12},{6,15},{7,14},{8,1},{9,0},... | collective-permute-start | bytes 49160 | tf_op jit(solution)/shard_map/ppermute | solution.py:260
  8.5 1.7 %collective-permute-start.1 = (f32[32,128]{1,0:T(8,128)S(1)}, f32[32,128]{1,0:T(8,128)S(1)}, u32[]{:S(2)}, u32[]{:S(2)}) collective-permute-start(f32[32,128]{1,0:T(8,128)S(1)} %shard_map.64), channel_id=1, source_target_pairs={{0,12},{1,13},{2,14},{3,15},{4,8},{5,9},{6,10},{7,11},{8,4},{9,5},... | collective-permute-start | bytes 49160 | tf_op jit(solution)/shard_map/ppermute | solution.py:260
  10.1 0.0 collective-permute-start
  10.1 0.0 collective-permute-done.2
  10.1 3.9 %collective-permute-done.1 = f32[32,128]{1,0:T(8,128)S(1)} collective-permute-done((f32[32,128]{1,0:T(8,128)S(1)}, f32[32,128]{1,0:T(8,128)S(1)}, u32[]{:S(2)}, u32[]{:S(2)}) %collective-permute-start.1) | collective-permute-done | bytes 16416 | tf_op jit(solution)/shard_map/ppermute | solution.py:260
  14.0 0.0 collective-permute-done
  14.1 1.5 %collective-permute-start.5 = (f32[128,128]{1,0:T(8,128)S(1)}, f32[128,128]{1,0:T(8,128)S(1)}, u32[]{:S(2)}, u32[]{:S(2)}) collective-permute-start(f32[128,128]{1,0:T(8,128)S(1)} %pad_maximum_fusion.refs_0_), channel_id=1, source_target_pairs={{0,2},{1,3},{2,0},{3,1},{4,6},{5,7},{6,4},{7,5},{8,10},{9,11},{10,... | collective-permute-start | bytes 196616 | tf_op jit(solution)/shard_map/ppermute | solution.py:260
  15.6 0.0 collective-permute-start.4
  15.6 0.6 %collective-permute-start.3 = (f32[128,128]{1,0:T(8,128)S(1)}, f32[128,128]{1,0:T(8,128)S(1)}, u32[]{:S(2)}, u32[]{:S(2)}) collective-permute-start(f32[128,128]{1,0:T(8,128)S(1)} %pad_maximum_fusion.refs_0_), channel_id=1, source_target_pairs={{0,1},{1,0},{2,3},{3,2},{4,5},{5,4},{6,7},{7,6},{8,9},{9,8},{10,11... | collective-permute-start | bytes 196616 | tf_op jit(solution)/shard_map/ppermute | solution.py:260
  16.3 2.1 %collective-permute-done.5.refs_3_ = f32[128,128]{1,0:T(8,128)S(1)} collective-permute-done((f32[128,128]{1,0:T(8,128)S(1)}, f32[128,128]{1,0:T(8,128)S(1)}, u32[]{:S(2)}, u32[]{:S(2)}) %collective-permute-start.5) | collective-permute-done | bytes 65568 | tf_op jit(solution)/shard_map/ppermute | solution.py:260
  18.4 1.4 %collective-permute-done.4.refs_2_ = f32[128,128]{1,0:T(8,128)S(1)} collective-permute-done((f32[128,128]{1,0:T(8,128)S(1)}, f32[128,128]{1,0:T(8,128)S(1)}, u32[]{:S(2)}, u32[]{:S(2)}) %collective-permute-start.4) | collective-permute-done | bytes 65568 | tf_op jit(solution)/shard_map/ppermute | solution.py:260
  19.8 0.0 collective-permute-done.3.refs_1_
  19.8 0.0 copy-done
  19.8 2.1 %shard_map.65 = f32[4,16]{1,0:T(4,128)} custom-call(f32[128,128]{1,0:T(8,128)S(1)} %pad_maximum_fusion.refs_0_, f32[128,128]{1,0:T(8,128)S(1)} %collective-permute-done.3.refs_1_, f32[128,128]{1,0:T(8,128)S(1)} %collective-permute-done.4.refs_2_, f32[128,128]{1,0:T(8,128)S(1)} %collective-permute-done.5.refs_3_, s32[1,16]{1,0:T(1,128)S(1)} %bitcast.5), custom_call_target="tpu_custom_call" | custom-call | tf_op jit(solution)/shard_map/pallas_call | solution.py:237
  (1 shorter events, 0.0 us)
Async XLA Ops:
  0.0 19.8 %copy-start = (s32[16]{0:T(128)S(1)}, s32[16]{0:T(128)}, u32[]{:S(2)}) copy-start(s32[16]{0:T(128)} %param.11) | copy-start | bytes 196
  4.9 5.2 %collective-permute-start.2 = (f32[32,128]{1,0:T(8,128)S(1)}, f32[32,128]{1,0:T(8,128)S(1)}, u32[]{:S(2)}, u32[]{:S(2)}) collective-permute-start(f32[32,128]{1,0:T(8,128)S(1)} %shard_map.64), channel_id=1, source_target_pairs={{0,9},{1,8},{2,11},{3,10},{4,13},{5,12},{6,15},{7,14},{8,1},{9,0},... | collective-permute-start | bytes 49160 | tf_op jit(solution)/shard_map/ppermute | solution.py:260
  8.5 5.6 %collective-permute-start.1 = (f32[32,128]{1,0:T(8,128)S(1)}, f32[32,128]{1,0:T(8,128)S(1)}, u32[]{:S(2)}, u32[]{:S(2)}) collective-permute-start(f32[32,128]{1,0:T(8,128)S(1)} %shard_map.64), channel_id=1, source_target_pairs={{0,12},{1,13},{2,14},{3,15},{4,8},{5,9},{6,10},{7,11},{8,4},{9,5},... | collective-permute-start | bytes 49160 | tf_op jit(solution)/shard_map/ppermute | solution.py:260
  10.1 3.9 %collective-permute-start = (f32[32,128]{1,0:T(8,128)S(1)}, f32[32,128]{1,0:T(8,128)S(1)}, u32[]{:S(2)}, u32[]{:S(2)}) collective-permute-start(f32[32,128]{1,0:T(8,128)S(1)} %shard_map.64), channel_id=1, source_target_pairs={{0,4},{1,5},{2,6},{3,7},{4,0},{5,1},{6,2},{7,3},{8,12},{9,13},{10,... | collective-permute-start | bytes 49160 | tf_op jit(solution)/shard_map/ppermute | solution.py:260
  14.1 4.3 %collective-permute-start.5 = (f32[128,128]{1,0:T(8,128)S(1)}, f32[128,128]{1,0:T(8,128)S(1)}, u32[]{:S(2)}, u32[]{:S(2)}) collective-permute-start(f32[128,128]{1,0:T(8,128)S(1)} %pad_maximum_fusion.refs_0_), channel_id=1, source_target_pairs={{0,2},{1,3},{2,0},{3,1},{4,6},{5,7},{6,4},{7,5},{8,10},{9,11},{10,... | collective-permute-start | bytes 196616 | tf_op jit(solution)/shard_map/ppermute | solution.py:260
  15.6 4.2 %collective-permute-start.4 = (f32[128,128]{1,0:T(8,128)S(1)}, f32[128,128]{1,0:T(8,128)S(1)}, u32[]{:S(2)}, u32[]{:S(2)}) collective-permute-start(f32[128,128]{1,0:T(8,128)S(1)} %pad_maximum_fusion.refs_0_), channel_id=1, source_target_pairs={{0,3},{1,2},{2,1},{3,0},{4,7},{5,6},{6,5},{7,4},{8,11},{9,10},{10,... | collective-permute-start | bytes 196616 | tf_op jit(solution)/shard_map/ppermute | solution.py:260
  15.6 4.2 %collective-permute-start.3 = (f32[128,128]{1,0:T(8,128)S(1)}, f32[128,128]{1,0:T(8,128)S(1)}, u32[]{:S(2)}, u32[]{:S(2)}) collective-permute-start(f32[128,128]{1,0:T(8,128)S(1)} %pad_maximum_fusion.refs_0_), channel_id=1, source_target_pairs={{0,1},{1,0},{2,3},{3,2},{4,5},{5,4},{6,7},{7,6},{8,9},{9,8},{10,11... | collective-permute-start | bytes 196616 | tf_op jit(solution)/shard_map/ppermute | solution.py:260

commit v33 on v30

--- a/solution.py
+++ b/solution.py
@@ -249,7 +249,7 @@
 
 
 def partner(n, inner):
-    return n * inner ^ (n >> 1) & ~n & 1
+    return n * inner ^ (n >> 1) & 1
 
 
 def gather_xor(tiles, axis, size, inner):

time: 22 us -> 21.7 us (0.986)
  transfers between devices with their start and end apart: 6 -> 6, of which waited for: 3 -> 4; matrix products, arithmetic and copies ran while one was open for 0% -> 0% of each run, Pallas kernels for 0% -> 0%
where the time goes in v33:
time: 21.7 us; the launch traced here: 21.5 us
  starting transfers between devices  7.32 us (34%)
  waiting for transfers between devices  7.24 us (33%)
  Pallas kernels  6.96 us (32%)
    ppermute x6, starting transfers between devices, swap(): return lax.ppermute(block, axis, [(i, i ^ slot) for i in range(size)])  7.32 us
    ppermute x6, waiting for transfers between devices, swap(): return lax.ppermute(block, axis, [(i, i ^ slot) for i in range(size)])  7.24 us
    pallas_call x1, Pallas kernels, sketch_rows(): pl.pallas_call(functools.partial(sketch_kernel, bounds, seq_len), out_sha...  4.87 us
    pallas_call x1, Pallas kernels, gram_scores(): pl.pallas_call(functools.partial(solve_kernel, per_dev, inner, axis), out...  2.09 us
  transfers between devices with their start and end apart: 6, of which 4 were waited for; matrix products, arithmetic and copies ran while one was open for 0% of the time, Pallas kernels for 0%

profile of v33, /device:TPU:0, one launch (start us, length us, event | category | flops | bytes accessed | tf_op | source)
XLA Modules:
  0.0 21.5 jit_solution(18237838468652718422)
XLA Ops:
  0.0 0.0 copy-start
  0.0 4.9 %shard_map.64 = f32[32,128]{1,0:T(8,128)S(1)} custom-call(bf16[256,8192]{1,0:T(8,128)(2,1)} %bitcast.6, bf16[256,8192]{1,0:T(8,128)(2,1)} %bitcast.7, bf16[32,8192]{1,0:T(8,128)(2,1)} %bitcast.8, bf16[32,8192]{1,0:T(8,128)(2,1)} %bitcast.9, s32[4]{0:T(128)} %lengths_hbm.1), custom_call_target="tpu_custom_call" | custom-call | tf_op jit(solution)/shard_map/pallas_call | solution.py:79
  4.9 3.5 %collective-permute-start.2 = (f32[32,128]{1,0:T(8,128)S(1)}, f32[32,128]{1,0:T(8,128)S(1)}, u32[]{:S(2)}, u32[]{:S(2)}) collective-permute-start(f32[32,128]{1,0:T(8,128)S(1)} %shard_map.64), channel_id=1, source_target_pairs={{0,9},{1,8},{2,11},{3,10},{4,13},{5,12},{6,15},{7,14},{8,1},{9,0},... | collective-permute-start | bytes 49160 | tf_op jit(solution)/shard_map/ppermute | solution.py:257
  8.4 1.6 %collective-permute-start.1 = (f32[32,128]{1,0:T(8,128)S(1)}, f32[32,128]{1,0:T(8,128)S(1)}, u32[]{:S(2)}, u32[]{:S(2)}) collective-permute-start(f32[32,128]{1,0:T(8,128)S(1)} %shard_map.64), channel_id=1, source_target_pairs={{0,13},{1,12},{2,15},{3,14},{4,9},{5,8},{6,11},{7,10},{8,5},{9,4},... | collective-permute-start | bytes 49160 | tf_op jit(solution)/shard_map/ppermute | solution.py:257
  10.1 0.0 collective-permute-start
  10.1 0.0 collective-permute-done.2
  10.1 3.3 %collective-permute-done.1 = f32[32,128]{1,0:T(8,128)S(1)} collective-permute-done((f32[32,128]{1,0:T(8,128)S(1)}, f32[32,128]{1,0:T(8,128)S(1)}, u32[]{:S(2)}, u32[]{:S(2)}) %collective-permute-start.1) | collective-permute-done | bytes 16416 | tf_op jit(solution)/shard_map/ppermute | solution.py:257
  13.4 0.4 %collective-permute-done = f32[32,128]{1,0:T(8,128)S(1)} collective-permute-done((f32[32,128]{1,0:T(8,128)S(1)}, f32[32,128]{1,0:T(8,128)S(1)}, u32[]{:S(2)}, u32[]{:S(2)}) %collective-permute-start) | collective-permute-done | bytes 16416 | tf_op jit(solution)/shard_map/ppermute | solution.py:257
  13.8 1.5 %collective-permute-start.5 = (f32[128,128]{1,0:T(8,128)S(1)}, f32[128,128]{1,0:T(8,128)S(1)}, u32[]{:S(2)}, u32[]{:S(2)}) collective-permute-start(f32[128,128]{1,0:T(8,128)S(1)} %pad_maximum_fusion.refs_0_), channel_id=1, source_target_pairs={{0,2},{1,3},{2,0},{3,1},{4,6},{5,7},{6,4},{7,5},{8,10},{9,11},{10,... | collective-permute-start | bytes 196616 | tf_op jit(solution)/shard_map/ppermute | solution.py:257
  15.3 0.2 collective-permute-start.4
  15.5 0.4 %collective-permute-start.3 = (f32[128,128]{1,0:T(8,128)S(1)}, f32[128,128]{1,0:T(8,128)S(1)}, u32[]{:S(2)}, u32[]{:S(2)}) collective-permute-start(f32[128,128]{1,0:T(8,128)S(1)} %pad_maximum_fusion.refs_0_), channel_id=1, source_target_pairs={{0,1},{1,0},{2,3},{3,2},{4,5},{5,4},{6,7},{7,6},{8,9},{9,8},{10,11... | collective-permute-start | bytes 196616 | tf_op jit(solution)/shard_map/ppermute | solution.py:257
  15.9 2.2 %collective-permute-done.5.refs_3_ = f32[128,128]{1,0:T(8,128)S(1)} collective-permute-done((f32[128,128]{1,0:T(8,128)S(1)}, f32[128,128]{1,0:T(8,128)S(1)}, u32[]{:S(2)}, u32[]{:S(2)}) %collective-permute-start.5) | collective-permute-done | bytes 65568 | tf_op jit(solution)/shard_map/ppermute | solution.py:257
  18.1 1.3 %collective-permute-done.4.refs_2_ = f32[128,128]{1,0:T(8,128)S(1)} collective-permute-done((f32[128,128]{1,0:T(8,128)S(1)}, f32[128,128]{1,0:T(8,128)S(1)}, u32[]{:S(2)}, u32[]{:S(2)}) %collective-permute-start.4) | collective-permute-done | bytes 65568 | tf_op jit(solution)/shard_map/ppermute | solution.py:257
  19.4 0.0 collective-permute-done.3.refs_1_
  19.4 0.0 copy-done
  19.4 2.1 %shard_map.65 = f32[4,16]{1,0:T(4,128)} custom-call(f32[128,128]{1,0:T(8,128)S(1)} %pad_maximum_fusion.refs_0_, f32[128,128]{1,0:T(8,128)S(1)} %collective-permute-done.3.refs_1_, f32[128,128]{1,0:T(8,128)S(1)} %collective-permute-done.4.refs_2_, f32[128,128]{1,0:T(8,128)S(1)} %collective-permute-done.5.refs_3_, s32[1,16]{1,0:T(1,128)S(1)} %bitcast.5), custom_call_target="tpu_custom_call" | custom-call | tf_op jit(solution)/shard_map/pallas_call | solution.py:234
  (1 shorter events, 0.0 us)
Async XLA Ops:
  0.0 19.4 %copy-start = (s32[16]{0:T(128)S(1)}, s32[16]{0:T(128)}, u32[]{:S(2)}) copy-start(s32[16]{0:T(128)} %param.11) | copy-start | bytes 196
  4.9 5.2 %collective-permute-start.2 = (f32[32,128]{1,0:T(8,128)S(1)}, f32[32,128]{1,0:T(8,128)S(1)}, u32[]{:S(2)}, u32[]{:S(2)}) collective-permute-start(f32[32,128]{1,0:T(8,128)S(1)} %shard_map.64), channel_id=1, source_target_pairs={{0,9},{1,8},{2,11},{3,10},{4,13},{5,12},{6,15},{7,14},{8,1},{9,0},... | collective-permute-start | bytes 49160 | tf_op jit(solution)/shard_map/ppermute | solution.py:257
  8.4 5.0 %collective-permute-start.1 = (f32[32,128]{1,0:T(8,128)S(1)}, f32[32,128]{1,0:T(8,128)S(1)}, u32[]{:S(2)}, u32[]{:S(2)}) collective-permute-start(f32[32,128]{1,0:T(8,128)S(1)} %shard_map.64), channel_id=1, source_target_pairs={{0,13},{1,12},{2,15},{3,14},{4,9},{5,8},{6,11},{7,10},{8,5},{9,4},... | collective-permute-start | bytes 49160 | tf_op jit(solution)/shard_map/ppermute | solution.py:257
  10.1 3.7 %collective-permute-start = (f32[32,128]{1,0:T(8,128)S(1)}, f32[32,128]{1,0:T(8,128)S(1)}, u32[]{:S(2)}, u32[]{:S(2)}) collective-permute-start(f32[32,128]{1,0:T(8,128)S(1)} %shard_map.64), channel_id=1, source_target_pairs={{0,4},{1,5},{2,6},{3,7},{4,0},{5,1},{6,2},{7,3},{8,12},{9,13},{10,... | collective-permute-start | bytes 49160 | tf_op jit(solution)/shard_map/ppermute | solution.py:257
  13.8 4.3 %collective-permute-start.5 = (f32[128,128]{1,0:T(8,128)S(1)}, f32[128,128]{1,0:T(8,128)S(1)}, u32[]{:S(2)}, u32[]{:S(2)}) collective-permute-start(f32[128,128]{1,0:T(8,128)S(1)} %pad_maximum_fusion.refs_0_), channel_id=1, source_target_pairs={{0,2},{1,3},{2,0},{3,1},{4,6},{5,7},{6,4},{7,5},{8,10},{9,11},{10,... | collective-permute-start | bytes 196616 | tf_op jit(solution)/shard_map/ppermute | solution.py:257
  15.3 4.2 %collective-permute-start.4 = (f32[128,128]{1,0:T(8,128)S(1)}, f32[128,128]{1,0:T(8,128)S(1)}, u32[]{:S(2)}, u32[]{:S(2)}) collective-permute-start(f32[128,128]{1,0:T(8,128)S(1)} %pad_maximum_fusion.refs_0_), channel_id=1, source_target_pairs={{0,3},{1,2},{2,1},{3,0},{4,7},{5,6},{6,5},{7,4},{8,11},{9,10},{10,... | collective-permute-start | bytes 196616 | tf_op jit(solution)/shard_map/ppermute | solution.py:257
  15.5 4.0 %collective-permute-start.3 = (f32[128,128]{1,0:T(8,128)S(1)}, f32[128,128]{1,0:T(8,128)S(1)}, u32[]{:S(2)}, u32[]{:S(2)}) collective-permute-start(f32[128,128]{1,0:T(8,128)S(1)} %pad_maximum_fusion.refs_0_), channel_id=1, source_target_pairs={{0,1},{1,0},{2,3},{3,2},{4,5},{5,4},{6,7},{7,6},{8,9},{9,8},{10,11... | collective-permute-start | bytes 196616 | tf_op jit(solution)/shard_map/ppermute | solution.py:257

commit v34 on v33

--- a/solution.py
+++ b/solution.py
@@ -249,7 +249,7 @@
 
 
 def partner(n, inner):
-    return n * inner ^ (n >> 1) & 1
+    return n * inner ^ (n | n >> 1) & 1
 
 
 def gather_xor(tiles, axis, size, inner):

time: 21.7 us -> 21.4 us (0.986)
  waiting for transfers between devices: 7.24 us -> 6.66 us
  starting transfers between devices: 7.32 us -> 7.61 us
    ppermute x6, waiting for transfers between devices: 7.24 us -> 6.66 us  [swap(): return lax.ppermute(block, axis, [(i, i ^ slot) for i in range(size)])]
    ppermute x6, starting transfers between devices: 7.32 us -> 7.61 us  [swap(): return lax.ppermute(block, axis, [(i, i ^ slot) for i in range(size)])]
  transfers between devices with their start and end apart: 6 -> 6, of which waited for: 4 -> 3; matrix products, arithmetic and copies ran while one was open for 0% -> 0% of each run, Pallas kernels for 0% -> 0%
where the time goes in v34:
time: 21.4 us; the launch traced here: 21.3 us
  starting transfers between devices  7.61 us (36%)
  Pallas kernels  6.96 us (33%)
  waiting for transfers between devices  6.66 us (31%)
    ppermute x6, starting transfers between devices, swap(): return lax.ppermute(block, axis, [(i, i ^ slot) for i in range(size)])  7.61 us
    ppermute x6, waiting for transfers between devices, swap(): return lax.ppermute(block, axis, [(i, i ^ slot) for i in range(size)])  6.66 us
    pallas_call x1, Pallas kernels, sketch_rows(): pl.pallas_call(functools.partial(sketch_kernel, bounds, seq_len), out_sha...  4.87 us
    pallas_call x1, Pallas kernels, gram_scores(): pl.pallas_call(functools.partial(solve_kernel, per_dev, inner, axis), out...  2.09 us
  transfers between devices with their start and end apart: 6, of which 3 were waited for; matrix products, arithmetic and copies ran while one was open for 0% of the time, Pallas kernels for 0%

profile of v34, /device:TPU:0, one launch (start us, length us, event | category | flops | bytes accessed | tf_op | source)
XLA Modules:
  0.0 21.3 jit_solution(1672024552682211509)
XLA Ops:
  0.0 0.0 copy-start
  0.0 4.9 %shard_map.64 = f32[32,128]{1,0:T(8,128)S(1)} custom-call(bf16[256,8192]{1,0:T(8,128)(2,1)} %bitcast.6, bf16[256,8192]{1,0:T(8,128)(2,1)} %bitcast.7, bf16[32,8192]{1,0:T(8,128)(2,1)} %bitcast.8, bf16[32,8192]{1,0:T(8,128)(2,1)} %bitcast.9, s32[4]{0:T(128)} %lengths_hbm.1), custom_call_target="tpu_custom_call" | custom-call | tf_op jit(solution)/shard_map/pallas_call | solution.py:79
  4.9 3.5 %collective-permute-start.2 = (f32[32,128]{1,0:T(8,128)S(1)}, f32[32,128]{1,0:T(8,128)S(1)}, u32[]{:S(2)}, u32[]{:S(2)}) collective-permute-start(f32[32,128]{1,0:T(8,128)S(1)} %shard_map.64), channel_id=1, source_target_pairs={{0,9},{1,8},{2,11},{3,10},{4,13},{5,12},{6,15},{7,14},{8,1},{9,0},... | collective-permute-start | bytes 49160 | tf_op jit(solution)/shard_map/ppermute | solution.py:257
  8.4 1.6 %collective-permute-start.1 = (f32[32,128]{1,0:T(8,128)S(1)}, f32[32,128]{1,0:T(8,128)S(1)}, u32[]{:S(2)}, u32[]{:S(2)}) collective-permute-start(f32[32,128]{1,0:T(8,128)S(1)} %shard_map.64), channel_id=1, source_target_pairs={{0,13},{1,12},{2,15},{3,14},{4,9},{5,8},{6,11},{7,10},{8,5},{9,4},... | collective-permute-start | bytes 49160 | tf_op jit(solution)/shard_map/ppermute | solution.py:257
  10.1 0.2 %collective-permute-start = (f32[32,128]{1,0:T(8,128)S(1)}, f32[32,128]{1,0:T(8,128)S(1)}, u32[]{:S(2)}, u32[]{:S(2)}) collective-permute-start(f32[32,128]{1,0:T(8,128)S(1)} %shard_map.64), channel_id=1, source_target_pairs={{0,5},{1,4},{2,7},{3,6},{4,1},{5,0},{6,3},{7,2},{8,13},{9,12},{10,... | collective-permute-start | bytes 49160 | tf_op jit(solution)/shard_map/ppermute | solution.py:257
  10.3 0.0 collective-permute-done.2
  10.3 3.1 %collective-permute-done.1 = f32[32,128]{1,0:T(8,128)S(1)} collective-permute-done((f32[32,128]{1,0:T(8,128)S(1)}, f32[32,128]{1,0:T(8,128)S(1)}, u32[]{:S(2)}, u32[]{:S(2)}) %collective-permute-start.1) | collective-permute-done | bytes 16416 | tf_op jit(solution)/shard_map/ppermute | solution.py:257
  13.4 0.0 collective-permute-done
  13.4 1.6 %collective-permute-start.5 = (f32[128,128]{1,0:T(8,128)S(1)}, f32[128,128]{1,0:T(8,128)S(1)}, u32[]{:S(2)}, u32[]{:S(2)}) collective-permute-start(f32[128,128]{1,0:T(8,128)S(1)} %pad_maximum_fusion.refs_0_), channel_id=1, source_target_pairs={{0,2},{1,3},{2,0},{3,1},{4,6},{5,7},{6,4},{7,5},{8,10},{9,11},{10,... | collective-permute-start | bytes 196616 | tf_op jit(solution)/shard_map/ppermute | solution.py:257
  15.0 0.6 %collective-permute-start.4 = (f32[128,128]{1,0:T(8,128)S(1)}, f32[128,128]{1,0:T(8,128)S(1)}, u32[]{:S(2)}, u32[]{:S(2)}) collective-permute-start(f32[128,128]{1,0:T(8,128)S(1)} %pad_maximum_fusion.refs_0_), channel_id=1, source_target_pairs={{0,3},{1,2},{2,1},{3,0},{4,7},{5,6},{6,5},{7,4},{8,11},{9,10},{10,... | collective-permute-start | bytes 196616 | tf_op jit(solution)/shard_map/ppermute | solution.py:257
  15.6 0.1 collective-permute-start.3
  15.6 2.8 %collective-permute-done.5.refs_3_ = f32[128,128]{1,0:T(8,128)S(1)} collective-permute-done((f32[128,128]{1,0:T(8,128)S(1)}, f32[128,128]{1,0:T(8,128)S(1)}, u32[]{:S(2)}, u32[]{:S(2)}) %collective-permute-start.5) | collective-permute-done | bytes 65568 | tf_op jit(solution)/shard_map/ppermute | solution.py:257
  18.4 0.7 %collective-permute-done.4.refs_2_ = f32[128,128]{1,0:T(8,128)S(1)} collective-permute-done((f32[128,128]{1,0:T(8,128)S(1)}, f32[128,128]{1,0:T(8,128)S(1)}, u32[]{:S(2)}, u32[]{:S(2)}) %collective-permute-start.4) | collective-permute-done | bytes 65568 | tf_op jit(solution)/shard_map/ppermute | solution.py:257
  19.2 0.0 collective-permute-done.3.refs_1_
  19.2 0.0 copy-done
  19.2 2.1 %shard_map.65 = f32[4,16]{1,0:T(4,128)} custom-call(f32[128,128]{1,0:T(8,128)S(1)} %pad_maximum_fusion.refs_0_, f32[128,128]{1,0:T(8,128)S(1)} %collective-permute-done.3.refs_1_, f32[128,128]{1,0:T(8,128)S(1)} %collective-permute-done.4.refs_2_, f32[128,128]{1,0:T(8,128)S(1)} %collective-permute-done.5.refs_3_, s32[1,16]{1,0:T(1,128)S(1)} %bitcast.5), custom_call_target="tpu_custom_call" | custom-call | tf_op jit(solution)/shard_map/pallas_call | solution.py:234
  (1 shorter events, 0.0 us)
Async XLA Ops:
  0.0 19.2 %copy-start = (s32[16]{0:T(128)S(1)}, s32[16]{0:T(128)}, u32[]{:S(2)}) copy-start(s32[16]{0:T(128)} %param.11) | copy-start | bytes 196
  4.9 5.4 %collective-permute-start.2 = (f32[32,128]{1,0:T(8,128)S(1)}, f32[32,128]{1,0:T(8,128)S(1)}, u32[]{:S(2)}, u32[]{:S(2)}) collective-permute-start(f32[32,128]{1,0:T(8,128)S(1)} %shard_map.64), channel_id=1, source_target_pairs={{0,9},{1,8},{2,11},{3,10},{4,13},{5,12},{6,15},{7,14},{8,1},{9,0},... | collective-permute-start | bytes 49160 | tf_op jit(solution)/shard_map/ppermute | solution.py:257
  8.4 5.0 %collective-permute-start.1 = (f32[32,128]{1,0:T(8,128)S(1)}, f32[32,128]{1,0:T(8,128)S(1)}, u32[]{:S(2)}, u32[]{:S(2)}) collective-permute-start(f32[32,128]{1,0:T(8,128)S(1)} %shard_map.64), channel_id=1, source_target_pairs={{0,13},{1,12},{2,15},{3,14},{4,9},{5,8},{6,11},{7,10},{8,5},{9,4},... | collective-permute-start | bytes 49160 | tf_op jit(solution)/shard_map/ppermute | solution.py:257
  10.1 3.3 %collective-permute-start = (f32[32,128]{1,0:T(8,128)S(1)}, f32[32,128]{1,0:T(8,128)S(1)}, u32[]{:S(2)}, u32[]{:S(2)}) collective-permute-start(f32[32,128]{1,0:T(8,128)S(1)} %shard_map.64), channel_id=1, source_target_pairs={{0,5},{1,4},{2,7},{3,6},{4,1},{5,0},{6,3},{7,2},{8,13},{9,12},{10,... | collective-permute-start | bytes 49160 | tf_op jit(solution)/shard_map/ppermute | solution.py:257
  13.4 5.0 %collective-permute-start.5 = (f32[128,128]{1,0:T(8,128)S(1)}, f32[128,128]{1,0:T(8,128)S(1)}, u32[]{:S(2)}, u32[]{:S(2)}) collective-permute-start(f32[128,128]{1,0:T(8,128)S(1)} %pad_maximum_fusion.refs_0_), channel_id=1, source_target_pairs={{0,2},{1,3},{2,0},{3,1},{4,6},{5,7},{6,4},{7,5},{8,10},{9,11},{10,... | collective-permute-start | bytes 196616 | tf_op jit(solution)/shard_map/ppermute | solution.py:257
  15.0 4.2 %collective-permute-start.4 = (f32[128,128]{1,0:T(8,128)S(1)}, f32[128,128]{1,0:T(8,128)S(1)}, u32[]{:S(2)}, u32[]{:S(2)}) collective-permute-start(f32[128,128]{1,0:T(8,128)S(1)} %pad_maximum_fusion.refs_0_), channel_id=1, source_target_pairs={{0,3},{1,2},{2,1},{3,0},{4,7},{5,6},{6,5},{7,4},{8,11},{9,10},{10,... | collective-permute-start | bytes 196616 | tf_op jit(solution)/shard_map/ppermute | solution.py:257
  15.6 3.6 %collective-permute-start.3 = (f32[128,128]{1,0:T(8,128)S(1)}, f32[128,128]{1,0:T(8,128)S(1)}, u32[]{:S(2)}, u32[]{:S(2)}) collective-permute-start(f32[128,128]{1,0:T(8,128)S(1)} %pad_maximum_fusion.refs_0_), channel_id=1, source_target_pairs={{0,1},{1,0},{2,3},{3,2},{4,5},{5,4},{6,7},{7,6},{8,9},{9,8},{10,11... | collective-permute-start | bytes 196616 | tf_op jit(solution)/shard_map/ppermute | solution.py:257

commit v35 on v34

--- a/solution.py
+++ b/solution.py
@@ -198,7 +198,7 @@
     gram_ref[...] = jnp.zeros(gram_ref.shape, jnp.float32)
     slot = (query_ref[...] // per_dev) ^ lax.axis_index(axis)
     n = slot // inner
-    place = (gray((slot ^ partner(n, inner)) % inner) * outer + gray(n)) * per_dev + query_ref[...] % per_dev
+    place = ((slot ^ partner(n, inner)) % inner * outer + gray(n)) * per_dev + query_ref[...] % per_dev
     rest = LANES - examples - nq
     place = jnp.concatenate(
         [jnp.zeros((1, examples), jnp.int32), place] + ([jnp.zeros((1, rest), jnp.int32)] if rest else []), axis=1
@@ -258,7 +258,7 @@
 
     rows = sorted(range(1, size // inner), key=gray)
     column = jnp.concatenate([tiles] + [swap(tiles, partner(n, inner)) for n in rows], axis=0)
-    return [column] + [swap(column, n) for n in sorted(range(1, inner), key=gray)]
+    return [column] + [swap(column, n) for n in range(1, inner)]
 
 
 def large_scores(tiles, query_index, per_dev, axis):

time: 21.4 us -> 21.8 us (1.019)
  starting transfers between devices: 7.61 us -> 7.84 us
    ppermute x6, starting transfers between devices: 7.61 us -> 7.84 us  [swap(): return lax.ppermute(block, axis, [(i, i ^ slot) for i in range(size)])]
where the time goes in v35:
time: 21.8 us; the launch traced here: 21.7 us
  starting transfers between devices  7.84 us (36%)
  Pallas kernels  6.96 us (32%)
  waiting for transfers between devices  6.84 us (31%)
    ppermute x6, starting transfers between devices, swap(): return lax.ppermute(block, axis, [(i, i ^ slot) for i in range(size)])  7.84 us
    ppermute x6, waiting for transfers between devices, swap(): return lax.ppermute(block, axis, [(i, i ^ slot) for i in range(size)])  6.84 us
    pallas_call x1, Pallas kernels, sketch_rows(): pl.pallas_call(functools.partial(sketch_kernel, bounds, seq_len), out_sha...  4.87 us
    pallas_call x1, Pallas kernels, gram_scores(): pl.pallas_call(functools.partial(solve_kernel, per_dev, inner, axis), out...  2.09 us
  transfers between devices with their start and end apart: 6, of which 3 were waited for; matrix products, arithmetic and copies ran while one was open for 0% of the time, Pallas kernels for 0%

profile of v35, /device:TPU:0, one launch (start us, length us, event | category | flops | bytes accessed | tf_op | source)
XLA Modules:
  0.0 21.7 jit_solution(866355040429772208)
XLA Ops:
  0.0 0.0 copy-start
  0.0 4.9 %shard_map.64 = f32[32,128]{1,0:T(8,128)S(1)} custom-call(bf16[256,8192]{1,0:T(8,128)(2,1)} %bitcast.6, bf16[256,8192]{1,0:T(8,128)(2,1)} %bitcast.7, bf16[32,8192]{1,0:T(8,128)(2,1)} %bitcast.8, bf16[32,8192]{1,0:T(8,128)(2,1)} %bitcast.9, s32[4]{0:T(128)} %lengths_hbm.1), custom_call_target="tpu_custom_call" | custom-call | tf_op jit(solution)/shard_map/pallas_call | solution.py:79
  4.9 3.5 %collective-permute-start.2 = (f32[32,128]{1,0:T(8,128)S(1)}, f32[32,128]{1,0:T(8,128)S(1)}, u32[]{:S(2)}, u32[]{:S(2)}) collective-permute-start(f32[32,128]{1,0:T(8,128)S(1)} %shard_map.64), channel_id=1, source_target_pairs={{0,9},{1,8},{2,11},{3,10},{4,13},{5,12},{6,15},{7,14},{8,1},{9,0},... | collective-permute-start | bytes 49160 | tf_op jit(solution)/shard_map/ppermute | solution.py:257
  8.4 1.6 %collective-permute-start.1 = (f32[32,128]{1,0:T(8,128)S(1)}, f32[32,128]{1,0:T(8,128)S(1)}, u32[]{:S(2)}, u32[]{:S(2)}) collective-permute-start(f32[32,128]{1,0:T(8,128)S(1)} %shard_map.64), channel_id=1, source_target_pairs={{0,13},{1,12},{2,15},{3,14},{4,9},{5,8},{6,11},{7,10},{8,5},{9,4},... | collective-permute-start | bytes 49160 | tf_op jit(solution)/shard_map/ppermute | solution.py:257
  10.1 0.2 %collective-permute-start = (f32[32,128]{1,0:T(8,128)S(1)}, f32[32,128]{1,0:T(8,128)S(1)}, u32[]{:S(2)}, u32[]{:S(2)}) collective-permute-start(f32[32,128]{1,0:T(8,128)S(1)} %shard_map.64), channel_id=1, source_target_pairs={{0,5},{1,4},{2,7},{3,6},{4,1},{5,0},{6,3},{7,2},{8,13},{9,12},{10,... | collective-permute-start | bytes 49160 | tf_op jit(solution)/shard_map/ppermute | solution.py:257
  10.3 0.0 collective-permute-done.2
  10.3 3.1 %collective-permute-done.1 = f32[32,128]{1,0:T(8,128)S(1)} collective-permute-done((f32[32,128]{1,0:T(8,128)S(1)}, f32[32,128]{1,0:T(8,128)S(1)}, u32[]{:S(2)}, u32[]{:S(2)}) %collective-permute-start.1) | collective-permute-done | bytes 16416 | tf_op jit(solution)/shard_map/ppermute | solution.py:257
  13.4 0.0 collective-permute-done
  13.4 1.9 %collective-permute-start.5 = (f32[128,128]{1,0:T(8,128)S(1)}, f32[128,128]{1,0:T(8,128)S(1)}, u32[]{:S(2)}, u32[]{:S(2)}) collective-permute-start(f32[128,128]{1,0:T(8,128)S(1)} %pad_maximum_fusion.refs_0_), channel_id=1, source_target_pairs={{0,3},{1,2},{2,1},{3,0},{4,7},{5,6},{6,5},{7,4},{8,11},{9,10},{10,... | collective-permute-start | bytes 196616 | tf_op jit(solution)/shard_map/ppermute | solution.py:257
  15.3 0.5 %collective-permute-start.4 = (f32[128,128]{1,0:T(8,128)S(1)}, f32[128,128]{1,0:T(8,128)S(1)}, u32[]{:S(2)}, u32[]{:S(2)}) collective-permute-start(f32[128,128]{1,0:T(8,128)S(1)} %pad_maximum_fusion.refs_0_), channel_id=1, source_target_pairs={{0,2},{1,3},{2,0},{3,1},{4,6},{5,7},{6,4},{7,5},{8,10},{9,11},{10,... | collective-permute-start | bytes 196616 | tf_op jit(solution)/shard_map/ppermute | solution.py:257
  15.8 0.0 collective-permute-start.3
  15.8 1.7 %collective-permute-done.5.refs_3_ = f32[128,128]{1,0:T(8,128)S(1)} collective-permute-done((f32[128,128]{1,0:T(8,128)S(1)}, f32[128,128]{1,0:T(8,128)S(1)}, u32[]{:S(2)}, u32[]{:S(2)}) %collective-permute-start.5) | collective-permute-done | bytes 65568 | tf_op jit(solution)/shard_map/ppermute | solution.py:257
  17.6 2.0 %collective-permute-done.4.refs_2_ = f32[128,128]{1,0:T(8,128)S(1)} collective-permute-done((f32[128,128]{1,0:T(8,128)S(1)}, f32[128,128]{1,0:T(8,128)S(1)}, u32[]{:S(2)}, u32[]{:S(2)}) %collective-permute-start.4) | collective-permute-done | bytes 65568 | tf_op jit(solution)/shard_map/ppermute | solution.py:257
  19.6 0.0 collective-permute-done.3.refs_1_
  19.6 0.0 copy-done
  19.6 2.1 %shard_map.65 = f32[4,16]{1,0:T(4,128)} custom-call(f32[128,128]{1,0:T(8,128)S(1)} %pad_maximum_fusion.refs_0_, f32[128,128]{1,0:T(8,128)S(1)} %collective-permute-done.3.refs_1_, f32[128,128]{1,0:T(8,128)S(1)} %collective-permute-done.4.refs_2_, f32[128,128]{1,0:T(8,128)S(1)} %collective-permute-done.5.refs_3_, s32[1,16]{1,0:T(1,128)S(1)} %bitcast.5), custom_call_target="tpu_custom_call" | custom-call | tf_op jit(solution)/shard_map/pallas_call | solution.py:234
  (1 shorter events, 0.0 us)
Async XLA Ops:
  0.0 19.6 %copy-start = (s32[16]{0:T(128)S(1)}, s32[16]{0:T(128)}, u32[]{:S(2)}) copy-start(s32[16]{0:T(128)} %param.11) | copy-start | bytes 196
  4.9 5.4 %collective-permute-start.2 = (f32[32,128]{1,0:T(8,128)S(1)}, f32[32,128]{1,0:T(8,128)S(1)}, u32[]{:S(2)}, u32[]{:S(2)}) collective-permute-start(f32[32,128]{1,0:T(8,128)S(1)} %shard_map.64), channel_id=1, source_target_pairs={{0,9},{1,8},{2,11},{3,10},{4,13},{5,12},{6,15},{7,14},{8,1},{9,0},... | collective-permute-start | bytes 49160 | tf_op jit(solution)/shard_map/ppermute | solution.py:257
  8.4 5.0 %collective-permute-start.1 = (f32[32,128]{1,0:T(8,128)S(1)}, f32[32,128]{1,0:T(8,128)S(1)}, u32[]{:S(2)}, u32[]{:S(2)}) collective-permute-start(f32[32,128]{1,0:T(8,128)S(1)} %shard_map.64), channel_id=1, source_target_pairs={{0,13},{1,12},{2,15},{3,14},{4,9},{5,8},{6,11},{7,10},{8,5},{9,4},... | collective-permute-start | bytes 49160 | tf_op jit(solution)/shard_map/ppermute | solution.py:257
  10.1 3.3 %collective-permute-start = (f32[32,128]{1,0:T(8,128)S(1)}, f32[32,128]{1,0:T(8,128)S(1)}, u32[]{:S(2)}, u32[]{:S(2)}) collective-permute-start(f32[32,128]{1,0:T(8,128)S(1)} %shard_map.64), channel_id=1, source_target_pairs={{0,5},{1,4},{2,7},{3,6},{4,1},{5,0},{6,3},{7,2},{8,13},{9,12},{10,... | collective-permute-start | bytes 49160 | tf_op jit(solution)/shard_map/ppermute | solution.py:257
  13.4 4.2 %collective-permute-start.5 = (f32[128,128]{1,0:T(8,128)S(1)}, f32[128,128]{1,0:T(8,128)S(1)}, u32[]{:S(2)}, u32[]{:S(2)}) collective-permute-start(f32[128,128]{1,0:T(8,128)S(1)} %pad_maximum_fusion.refs_0_), channel_id=1, source_target_pairs={{0,3},{1,2},{2,1},{3,0},{4,7},{5,6},{6,5},{7,4},{8,11},{9,10},{10,... | collective-permute-start | bytes 196616 | tf_op jit(solution)/shard_map/ppermute | solution.py:257
  15.3 4.3 %collective-permute-start.4 = (f32[128,128]{1,0:T(8,128)S(1)}, f32[128,128]{1,0:T(8,128)S(1)}, u32[]{:S(2)}, u32[]{:S(2)}) collective-permute-start(f32[128,128]{1,0:T(8,128)S(1)} %pad_maximum_fusion.refs_0_), channel_id=1, source_target_pairs={{0,2},{1,3},{2,0},{3,1},{4,6},{5,7},{6,4},{7,5},{8,10},{9,11},{10,... | collective-permute-start | bytes 196616 | tf_op jit(solution)/shard_map/ppermute | solution.py:257
  15.8 3.7 %collective-permute-start.3 = (f32[128,128]{1,0:T(8,128)S(1)}, f32[128,128]{1,0:T(8,128)S(1)}, u32[]{:S(2)}, u32[]{:S(2)}) collective-permute-start(f32[128,128]{1,0:T(8,128)S(1)} %pad_maximum_fusion.refs_0_), channel_id=1, source_target_pairs={{0,1},{1,0},{2,3},{3,2},{4,5},{5,4},{6,7},{7,6},{8,9},{9,8},{10,11... | collective-permute-start | bytes 196616 | tf_op jit(solution)/shard_map/ppermute | solution.py:257
